TPU v7x, 32 devices: a whole 2x2x4 slice. The times are simulated.
32 devices in a mesh: dp: 4 (over z), ctx: 8 (over y, x, core).
Axes of the slice: x: 2, y: 2, z: 4, core: 2. Of those that a mesh axis runs over, the one named last changes fastest.
Arguments:
- hidden_in: bfloat16 [4, 4096, 2048], P('dp', 'ctx'), may hold values from -6 to 6
- in_gain: bfloat16 [2048], P(('dp', 'ctx')), may hold values from 0.5 to 1.5
- w_query: bfloat16 [2048, 2048], P(('dp', 'ctx')), may hold values from -0.125 to 0.125
- b_query: bfloat16 [2048], P(('dp', 'ctx')), may hold values from -1.796875 to 1.796875
- w_key: bfloat16 [2048, 2048], P(('dp', 'ctx')), may hold values from -0.125 to 0.125
- b_key: bfloat16 [2048], P(('dp', 'ctx')), may hold values from -1.796875 to 1.796875
- w_value: bfloat16 [2048, 2048], P(('dp', 'ctx')), may hold values from -0.125 to 0.125
- b_value: bfloat16 [2048], P(('dp', 'ctx')), may hold values from -1.796875 to 1.796875
- w_out: bfloat16 [2048, 2048], P(('dp', 'ctx')), may hold values from -0.375 to 0.375
- ffn_gain: bfloat16 [2048], P(('dp', 'ctx')), may hold values from 0.5 to 1.5
- w_router: bfloat16 [2048, 8], P(('dp', 'ctx')), may hold values from -0.0625 to 0.0625
- exp_gate: bfloat16 [8, 2048, 1408], P('ctx', 'dp'), may hold values from -0.125 to 0.125
- exp_up: bfloat16 [8, 2048, 1408], P('ctx', 'dp'), may hold values from -0.125 to 0.125
- exp_down: bfloat16 [8, 1408, 2048], P('ctx', None, 'dp'), may hold values from -0.3125 to 0.3125
- sh_gate: bfloat16 [2048, 5632], P(None, ('dp', 'ctx')), may hold values from -0.125 to 0.125
- sh_up: bfloat16 [2048, 5632], P(None, ('dp', 'ctx')), may hold values from -0.125 to 0.125
- sh_down: bfloat16 [5632, 2048], P(('dp', 'ctx')), may hold values from -0.15625 to 0.15625
- sh_mix: bfloat16 [2048], P(('dp', 'ctx')), may hold values from -0.125 to 0.125
- routes: int32 [4, 4096, 4], P('dp', 'ctx'), may hold values from 0 to 7, all different within a row
- priority: int32 [4, 8, 2048], P('dp', 'ctx'), may hold values from 0 to 2047, each once within a row
- blocks: int32 [4, 16], P('dp'), may hold values from 0 to 15, as said below
- cotangent: bfloat16 [4, 4096, 2048], P('dp', 'ctx'), may hold values from -6 to 6
Outputs:
- layer_out: bfloat16 [4, 4096, 2048], P('dp', 'ctx')
- grad_input: float32 [4, 4096, 2048], P('dp', 'ctx')
- grad_ingain: float32 [2048], P(('dp', 'ctx'))
- grad_wquery: float32 [2048, 2048], P(('dp', 'ctx'))
- grad_bquery: float32 [2048], P(('dp', 'ctx'))
- grad_wkey: float32 [2048, 2048], P(('dp', 'ctx'))
- grad_bkey: float32 [2048], P(('dp', 'ctx'))
- grad_wvalue: float32 [2048, 2048], P(('dp', 'ctx'))
- grad_bvalue: float32 [2048], P(('dp', 'ctx'))
- grad_wout: float32 [2048, 2048], P(('dp', 'ctx'))
- grad_ffngain: float32 [2048], P(('dp', 'ctx'))
- grad_router: float32 [2048, 8], P(('dp', 'ctx'))
- grad_expgate: float32 [8, 2048, 1408], P('ctx', 'dp')
- grad_expup: float32 [8, 2048, 1408], P('ctx', 'dp')
- grad_expdown: float32 [8, 1408, 2048], P('ctx', None, 'dp')
- grad_shgate: float32 [2048, 5632], P(None, ('dp', 'ctx'))
- grad_shup: float32 [2048, 5632], P(None, ('dp', 'ctx'))
- grad_shdown: float32 [5632, 2048], P(('dp', 'ctx'))
- grad_shmix: float32 [2048], P(('dp', 'ctx'))
Inputs may be any that keep to these rules, and one draw needn't show every extreme that they name: `blocks`: in each row, entry 2c is a block below 16/2 (prompt) and entry 2c + 1 a block of 8 or more; each row names every block once.
All inputs are finite; a program needn't handle non-finite values.
Results may differ from a plain program's by a relative error of at most 0.03.
Values may be sent and summed in bfloat16 or wider, within the bound.
A program may use at most 512 MiB of HBM per device.

v0:
```python
import jax
import jax.numpy as jnp
from jax import lax
from jax.sharding import PartitionSpec as P

D = 2048
HEADS = 16
HEAD_DIM = 128
TOP_K = 4
CONT = 256
PROMPT = 2048


rope_base = 1000000.0
epsilon = 1e-06
masked_score = -1e30


def rotate(values, cosine, sine):
    middle = values.shape[-1] // 2
    leading = values[..., :middle]
    trailing = values[..., middle:]
    return jnp.concatenate(
        [leading * cosine - trailing * sine, trailing * cosine + leading * sine], axis=-1
    )


def unrotate(values, cosine, sine):
    middle = values.shape[-1] // 2
    leading = values[..., :middle]
    trailing = values[..., middle:]
    return jnp.concatenate(
        [leading * cosine + trailing * sine, trailing * cosine - leading * sine], axis=-1
    )


def rope_tables(places):
    turned = jnp.where(places < PROMPT, places, PROMPT + (places - PROMPT) % CONT)
    frequency = rope_base ** (-2.0 * jnp.arange(HEAD_DIM // 2, dtype=jnp.float32) / HEAD_DIM)
    angles = turned.astype(jnp.float32)[:, None] * frequency[None, :]
    return (jnp.cos(angles)[:, None, :], jnp.sin(angles)[:, None, :])


def segment_of(places):
    return jnp.where(places < PROMPT, 0, 1 + (places - PROMPT) // CONT)


def visible(query_places, key_places):
    query_segment = segment_of(query_places)
    key_segment = segment_of(key_places)
    causal = key_places[None, :] <= query_places[:, None]
    same_doc = (key_segment[None, :] == 0) | (key_segment[None, :] == query_segment[:, None])
    return causal & same_doc


def local_ranks(expert_ids, order, expert_count):
    flat_ids = expert_ids.reshape(-1)
    arranged = jnp.zeros(flat_ids.shape, jnp.int32).at[order].set(flat_ids)
    member = (arranged[:, None] == jnp.arange(expert_count, dtype=jnp.int32)[None, :]).astype(
        jnp.int32
    )
    before = jnp.cumsum(member, axis=0) - member
    sorted_positions = jnp.sum(before * member, axis=1)
    return sorted_positions[order].reshape(expert_ids.shape)


def rms_scale(values):
    return lax.rsqrt(jnp.mean(values * values, axis=-1, keepdims=True) + epsilon)


def norm_back(values, scale_rows, gain_full, upstream):
    weighted = upstream * gain_full.astype(jnp.float32)[None, :]
    grad_gain = jnp.sum(upstream * values * scale_rows, axis=0)
    grad_values = scale_rows * weighted - values * scale_rows**3 * jnp.mean(
        weighted * values, axis=-1, keepdims=True
    )
    return (grad_values, grad_gain)


def silu_parts(values):
    sig_value = jax.nn.sigmoid(values)
    return (values * sig_value, sig_value * (1.0 + values * (1.0 - sig_value)))


def on_device(
    hidden_in,
    in_gain,
    w_query,
    b_query,
    w_key,
    b_key,
    w_value,
    b_value,
    w_out,
    ffn_gain,
    w_router,
    exp_gate,
    exp_up,
    exp_down,
    sh_gate,
    sh_up,
    sh_down,
    sh_mix,
    routes,
    priority,
    blocks,
    cotangent,
):
    ctx_count = lax.axis_size("ctx")
    ctx_index = lax.axis_index("ctx")
    tokens = hidden_in[0].astype(jnp.float32)
    cot_low = cotangent[0]
    cot_full = cot_low.astype(jnp.float32)
    tok_count = tokens.shape[0]
    group_len = tok_count * ctx_count
    block_len = group_len // (2 * ctx_count)
    local_experts = exp_gate.shape[0]
    experts_total = local_experts * ctx_count
    capacity = 5 * tok_count * TOP_K // (4 * experts_total)
    slot_count = experts_total * capacity
    score_scale = HEAD_DIM ** (-0.5)
    (
        gain_one,
        query_full,
        query_bias,
        key_full,
        key_bias,
        value_full,
        value_bias,
        out_full,
        gain_two,
        router_full,
        mix_full,
    ) = (
        lax.all_gather(in_gain, ("dp", "ctx"), axis=0, tiled=True),
        lax.all_gather(w_query, ("dp", "ctx"), axis=0, tiled=True),
        lax.all_gather(b_query, ("dp", "ctx"), axis=0, tiled=True),
        lax.all_gather(w_key, ("dp", "ctx"), axis=0, tiled=True),
        lax.all_gather(b_key, ("dp", "ctx"), axis=0, tiled=True),
        lax.all_gather(w_value, ("dp", "ctx"), axis=0, tiled=True),
        lax.all_gather(b_value, ("dp", "ctx"), axis=0, tiled=True),
        lax.all_gather(w_out, ("dp", "ctx"), axis=0, tiled=True),
        lax.all_gather(ffn_gain, ("dp", "ctx"), axis=0, tiled=True),
        lax.all_gather(w_router, ("dp", "ctx"), axis=0, tiled=True),
        lax.all_gather(sh_mix, ("dp", "ctx"), axis=0, tiled=True),
    )
    expert_gate, expert_up, expert_down, shared_gate_part, shared_up_part, shared_down_part = (
        lax.all_gather(exp_gate, "dp", axis=1, tiled=True),
        lax.all_gather(exp_up, "dp", axis=1, tiled=True),
        lax.all_gather(exp_down, "dp", axis=2, tiled=True),
        lax.all_gather(sh_gate, "dp", axis=1, tiled=True),
        lax.all_gather(sh_up, "dp", axis=1, tiled=True),
        lax.all_gather(sh_down, "dp", axis=0, tiled=True),
    )
    within = jnp.arange(block_len, dtype=jnp.int32)
    key_places = (blocks[0][:, None] * block_len + within[None, :]).reshape(-1)
    query_places = lax.dynamic_slice_in_dim(key_places, ctx_index * tok_count, tok_count)
    cosine, sine = rope_tables(query_places)
    allowed = visible(query_places, key_places)
    scale_one = rms_scale(tokens)
    normed_one = (tokens * scale_one * gain_one.astype(jnp.float32)[None, :]).astype(jnp.bfloat16)

    def project(weight_full, bias_full):
        return (
            jnp.dot(normed_one, weight_full, preferred_element_type=jnp.float32)
            + bias_full.astype(jnp.float32)[None, :]
        )

    head_shape = (tok_count, HEADS, HEAD_DIM)
    query_rot = (
        rotate(project(query_full, query_bias).reshape(head_shape), cosine, sine)
        .reshape(tok_count, D)
        .astype(jnp.bfloat16)
    )
    key_rot = (
        rotate(project(key_full, key_bias).reshape(head_shape), cosine, sine)
        .reshape(tok_count, D)
        .astype(jnp.bfloat16)
    )
    value_rows = project(value_full, value_bias).astype(jnp.bfloat16)
    key_all, value_all, cot_all = (
        lax.all_gather(key_rot, "ctx", axis=0, tiled=True),
        lax.all_gather(value_rows, "ctx", axis=0, tiled=True),
        lax.all_gather(cot_low, "ctx", axis=0, tiled=True),
    )

    def head_block(head_index):
        column_start = head_index * HEAD_DIM
        query_head = lax.dynamic_slice_in_dim(query_rot, column_start, HEAD_DIM, 1)
        key_head = lax.dynamic_slice_in_dim(key_all, column_start, HEAD_DIM, 1)
        value_head = lax.dynamic_slice_in_dim(value_all, column_start, HEAD_DIM, 1)
        scores = (
            jnp.einsum("qd,kd->qk", query_head, key_head, preferred_element_type=jnp.float32)
            * score_scale
        )
        return (jnp.where(allowed, scores, masked_score), query_head, key_head, value_head)

    def forward_head(head_index, loop_state):
        attended, log_totals = loop_state
        scores, query_head, key_head, value_head = head_block(head_index)
        highest = jnp.max(scores, axis=1, keepdims=True)
        weight_collection = jnp.exp(scores - highest)
        row_total = jnp.sum(weight_collection, axis=1, keepdims=True)
        weights_low = (weight_collection / row_total).astype(jnp.bfloat16)
        output = jnp.dot(weights_low, value_head, preferred_element_type=jnp.float32)
        attended = lax.dynamic_update_slice_in_dim(attended, output, head_index * HEAD_DIM, 1)
        log_totals = log_totals.at[head_index].set((highest + jnp.log(row_total))[:, 0])
        return (attended, log_totals)

    attended, log_totals = lax.fori_loop(
        0,
        HEADS,
        forward_head,
        (jnp.zeros((tok_count, D), jnp.float32), jnp.zeros((HEADS, tok_count), jnp.float32)),
    )
    attended_low = attended.astype(jnp.bfloat16)
    first_sum = tokens + jnp.dot(attended_low, out_full, preferred_element_type=jnp.float32)
    scale_two = rms_scale(first_sum)
    normed_two = (first_sum * scale_two * gain_two.astype(jnp.float32)[None, :]).astype(
        jnp.bfloat16
    )
    logits = jnp.dot(normed_two, router_full, preferred_element_type=jnp.float32)
    route_ids = routes[0]
    chosen = jnp.take_along_axis(logits, route_ids, axis=1)
    gates = jax.nn.softmax(chosen, axis=-1)
    ranks = local_ranks(route_ids, priority[0, 0], experts_total)
    keep = ranks < capacity
    slots = jnp.where(keep, route_ids * capacity + ranks, slot_count)
    slot_grid = jnp.arange(slot_count, dtype=jnp.int32)
    hits = slots[None, :, :] == slot_grid[:, None, None]
    table = jnp.any(hits, axis=2).astype(jnp.bfloat16)
    slot_gates = jnp.sum(jnp.where(hits, gates[None, :, :], 0.0), axis=(1, 2))
    send_rows = jnp.dot(table, normed_two, preferred_element_type=jnp.float32).astype(jnp.bfloat16)
    send_grads = (
        jnp.dot(table, cot_low, preferred_element_type=jnp.float32) * slot_gates[:, None]
    ).astype(jnp.bfloat16)
    owner_shape = (ctx_count, slot_count // ctx_count, D)
    arrived_rows, arrived_grads = (
        lax.all_to_all(
            send_rows.reshape(owner_shape), "ctx", split_axis=0, concat_axis=0, tiled=True
        ),
        lax.all_to_all(
            send_grads.reshape(owner_shape), "ctx", split_axis=0, concat_axis=0, tiled=True
        ),
    )
    expert_shape = (ctx_count, local_experts, capacity, D)
    received_input_rows = arrived_rows.reshape(expert_shape)
    arrived_g = arrived_grads.reshape(expert_shape)
    gate_act = jnp.einsum(
        "cjrd,jdf->cjrf", received_input_rows, expert_gate, preferred_element_type=jnp.float32
    )
    up_act = jnp.einsum(
        "cjrd,jdf->cjrf", received_input_rows, expert_up, preferred_element_type=jnp.float32
    )
    gate_silu, gate_slope = silu_parts(gate_act)
    hidden_low = (gate_silu * up_act).astype(jnp.bfloat16)
    expert_out = jnp.einsum(
        "cjrf,jfd->cjrd", hidden_low, expert_down, preferred_element_type=jnp.float32
    ).astype(jnp.bfloat16)
    hidden_grad = jnp.einsum(
        "cjrd,jfd->cjrf", arrived_g, expert_down, preferred_element_type=jnp.float32
    )
    grad_edown = jnp.einsum(
        "cjrf,cjrd->jfd", hidden_low, arrived_g, preferred_element_type=jnp.float32
    )
    gate_grad = (hidden_grad * up_act * gate_slope).astype(jnp.bfloat16)
    up_projection_gradient = (hidden_grad * gate_silu).astype(jnp.bfloat16)
    grad_egate = jnp.einsum(
        "qivk,qivo->iko", received_input_rows, gate_grad, preferred_element_type=jnp.float32
    )
    expert_up_weight_gradient = jnp.einsum(
        "qivk,qivo->iko",
        received_input_rows,
        up_projection_gradient,
        preferred_element_type=jnp.float32,
    )
    expert_dx = (
        jnp.einsum("cjrf,jdf->cjrd", gate_grad, expert_gate, preferred_element_type=jnp.float32)
        + jnp.einsum(
            "cjrf,jdf->cjrd", up_projection_gradient, expert_up, preferred_element_type=jnp.float32
        )
    ).astype(jnp.bfloat16)
    back_out, back_dx = (
        lax.all_to_all(
            expert_out.reshape(owner_shape), "ctx", split_axis=0, concat_axis=0, tiled=True
        ),
        lax.all_to_all(
            expert_dx.reshape(owner_shape), "ctx", split_axis=0, concat_axis=0, tiled=True
        ),
    )
    flat_out = back_out.reshape(slot_count, D)
    flat_dx = back_dx.reshape(slot_count, D)
    padded_out = jnp.concatenate([flat_out, jnp.zeros((1, D), jnp.bfloat16)], axis=0)
    picked = padded_out[slots].astype(jnp.float32)
    experts_sum = jnp.sum(gates[:, :, None] * picked, axis=1)
    gate_grads = jnp.sum(cot_full[:, None, :] * picked, axis=2)
    normed_grad = jnp.einsum("st,sd->td", table, flat_dx, preferred_element_type=jnp.float32)
    chosen_grad = gates * (gate_grads - jnp.sum(gates * gate_grads, axis=1, keepdims=True))
    expert_grid = jnp.arange(experts_total, dtype=jnp.int32)
    logit_grad = jnp.sum(
        jnp.where(
            route_ids[:, :, None] == expert_grid[None, None, :], chosen_grad[:, :, None], 0.0
        ),
        axis=1,
    ).astype(jnp.bfloat16)
    grad_route = jnp.einsum("td,te->de", normed_two, logit_grad, preferred_element_type=jnp.float32)
    normed_grad = normed_grad + jnp.einsum(
        "te,de->td", logit_grad, router_full, preferred_element_type=jnp.float32
    )
    mix_vector = mix_full.astype(jnp.float32)
    mix_local = jax.nn.sigmoid(jnp.dot(normed_two, mix_full, preferred_element_type=jnp.float32))
    all_normed = lax.all_gather(normed_two, "ctx", axis=0, tiled=True)
    mix_all = jax.nn.sigmoid(jnp.dot(all_normed, mix_full, preferred_element_type=jnp.float32))
    shared_g = jnp.dot(all_normed, shared_gate_part, preferred_element_type=jnp.float32)
    shared_u = jnp.dot(all_normed, shared_up_part, preferred_element_type=jnp.float32)
    shared_silu, shared_slope = silu_parts(shared_g)
    shared_low = (shared_silu * shared_u).astype(jnp.bfloat16)
    partial_sum = jnp.dot(shared_low, shared_down_part, preferred_element_type=jnp.float32)
    mix_cot = (mix_all[:, None] * cot_all.astype(jnp.float32)).astype(jnp.bfloat16)
    shared_hidden = jnp.einsum(
        "td,fd->tf", mix_cot, shared_down_part, preferred_element_type=jnp.float32
    )
    shared_dg = (shared_hidden * shared_u * shared_slope).astype(jnp.bfloat16)
    shared_du = (shared_hidden * shared_silu).astype(jnp.bfloat16)
    partial_dx = jnp.einsum(
        "tf,df->td", shared_dg, shared_gate_part, preferred_element_type=jnp.float32
    ) + jnp.einsum("tf,df->td", shared_du, shared_up_part, preferred_element_type=jnp.float32)
    grad_sgate = jnp.einsum("td,tf->df", all_normed, shared_dg, preferred_element_type=jnp.float32)
    grad_sup = jnp.einsum("td,tf->df", all_normed, shared_du, preferred_element_type=jnp.float32)
    grad_sdown = jnp.einsum("tf,td->fd", shared_low, mix_cot, preferred_element_type=jnp.float32)
    shared_sum, shared_dx = (
        lax.psum_scatter(
            partial_sum.astype(jnp.bfloat16), "ctx", scatter_dimension=0, tiled=True
        ).astype(jnp.float32),
        lax.psum_scatter(
            partial_dx.astype(jnp.bfloat16), "ctx", scatter_dimension=0, tiled=True
        ).astype(jnp.float32),
    )
    layer_out = first_sum + experts_sum + mix_local[:, None] * shared_sum
    mix_grad = jnp.sum(cot_full * shared_sum, axis=1) * mix_local * (1.0 - mix_local)
    grad_mixing = jnp.dot(mix_grad, normed_two.astype(jnp.float32))
    normed_grad = normed_grad + shared_dx + mix_grad[:, None] * mix_vector[None, :]
    norm_grad_two, grad_gain_two = norm_back(first_sum, scale_two, gain_two, normed_grad)
    first_grad = cot_full + norm_grad_two
    first_low = first_grad.astype(jnp.bfloat16)
    grad_output = jnp.einsum(
        "td,te->de", attended_low, first_low, preferred_element_type=jnp.float32
    )
    attended_grad = jnp.einsum(
        "te,de->td", first_low, out_full, preferred_element_type=jnp.float32
    ).astype(jnp.bfloat16)

    def backward_head(head_index, loop_state):
        query_grad, key_grad, value_grad = loop_state
        scores, query_head, key_head, value_head = head_block(head_index)
        column_start = head_index * HEAD_DIM
        grad_head = lax.dynamic_slice_in_dim(attended_grad, column_start, HEAD_DIM, 1)
        probs_full = jnp.exp(scores - log_totals[head_index][:, None])
        probs_low = probs_full.astype(jnp.bfloat16)
        value_part = jnp.einsum(
            "qk,qd->kd", probs_low, grad_head, preferred_element_type=jnp.float32
        )
        prob_grad = jnp.einsum(
            "qd,kd->qk", grad_head, value_head, preferred_element_type=jnp.float32
        )
        row_dot = jnp.sum(probs_full * prob_grad, axis=1, keepdims=True)
        score_grad = (probs_full * (prob_grad - row_dot)).astype(jnp.bfloat16)
        query_part = jnp.dot(score_grad, key_head, preferred_element_type=jnp.float32) * score_scale
        key_part = (
            jnp.einsum("qk,qd->kd", score_grad, query_head, preferred_element_type=jnp.float32)
            * score_scale
        )
        query_grad = lax.dynamic_update_slice_in_dim(query_grad, query_part, column_start, 1)
        key_grad = lax.dynamic_update_slice_in_dim(key_grad, key_part, column_start, 1)
        value_grad = lax.dynamic_update_slice_in_dim(value_grad, value_part, column_start, 1)
        return (query_grad, key_grad, value_grad)

    query_grad, key_grad, value_grad = lax.fori_loop(
        0,
        HEADS,
        backward_head,
        (
            jnp.zeros((tok_count, D), jnp.float32),
            jnp.zeros((group_len, D), jnp.float32),
            jnp.zeros((group_len, D), jnp.float32),
        ),
    )
    key_mine, value_mine = (
        lax.psum_scatter(
            key_grad.astype(jnp.bfloat16), "ctx", scatter_dimension=0, tiled=True
        ).astype(jnp.float32),
        lax.psum_scatter(
            value_grad.astype(jnp.bfloat16), "ctx", scatter_dimension=0, tiled=True
        ).astype(jnp.float32),
    )
    query_low = (
        unrotate(query_grad.reshape(head_shape), cosine, sine)
        .reshape(tok_count, D)
        .astype(jnp.bfloat16)
    )
    key_low = (
        unrotate(key_mine.reshape(head_shape), cosine, sine)
        .reshape(tok_count, D)
        .astype(jnp.bfloat16)
    )
    value_low = value_mine.astype(jnp.bfloat16)
    grad_query_w = jnp.einsum(
        "td,te->de", normed_one, query_low, preferred_element_type=jnp.float32
    )
    grad_key_w = jnp.einsum("td,te->de", normed_one, key_low, preferred_element_type=jnp.float32)
    grad_value_w = jnp.einsum(
        "td,te->de", normed_one, value_low, preferred_element_type=jnp.float32
    )
    grad_query_b = jnp.sum(query_low.astype(jnp.float32), axis=0)
    grad_key_b = jnp.sum(key_low.astype(jnp.float32), axis=0)
    grad_value_b = jnp.sum(value_low.astype(jnp.float32), axis=0)
    normed_one_grad = (
        jnp.einsum("te,de->td", query_low, query_full, preferred_element_type=jnp.float32)
        + jnp.einsum("te,de->td", key_low, key_full, preferred_element_type=jnp.float32)
        + jnp.einsum("te,de->td", value_low, value_full, preferred_element_type=jnp.float32)
    )
    norm_grad_one, grad_gain_one = norm_back(tokens, scale_one, gain_one, normed_one_grad)
    input_grad = first_grad + norm_grad_one
    (
        grad_ingain,
        grad_wquery,
        grad_bquery,
        grad_wkey,
        grad_bkey,
        grad_wvalue,
        grad_bvalue,
        grad_wout,
        grad_ffngain,
        grad_router,
        grad_shmix,
    ) = (
        lax.psum_scatter(grad_gain_one, ("dp", "ctx"), scatter_dimension=0, tiled=True),
        lax.psum_scatter(grad_query_w, ("dp", "ctx"), scatter_dimension=0, tiled=True),
        lax.psum_scatter(grad_query_b, ("dp", "ctx"), scatter_dimension=0, tiled=True),
        lax.psum_scatter(grad_key_w, ("dp", "ctx"), scatter_dimension=0, tiled=True),
        lax.psum_scatter(grad_key_b, ("dp", "ctx"), scatter_dimension=0, tiled=True),
        lax.psum_scatter(grad_value_w, ("dp", "ctx"), scatter_dimension=0, tiled=True),
        lax.psum_scatter(grad_value_b, ("dp", "ctx"), scatter_dimension=0, tiled=True),
        lax.psum_scatter(grad_output, ("dp", "ctx"), scatter_dimension=0, tiled=True),
        lax.psum_scatter(grad_gain_two, ("dp", "ctx"), scatter_dimension=0, tiled=True),
        lax.psum_scatter(grad_route, ("dp", "ctx"), scatter_dimension=0, tiled=True),
        lax.psum_scatter(grad_mixing, ("dp", "ctx"), scatter_dimension=0, tiled=True),
    )
    grad_expgate, grad_expup, grad_expdown, grad_shgate, grad_shup, grad_shdown = (
        lax.psum_scatter(
            grad_egate.astype(jnp.bfloat16), "dp", scatter_dimension=1, tiled=True
        ).astype(jnp.float32),
        lax.psum_scatter(
            expert_up_weight_gradient.astype(jnp.bfloat16), "dp", scatter_dimension=1, tiled=True
        ).astype(jnp.float32),
        lax.psum_scatter(
            grad_edown.astype(jnp.bfloat16), "dp", scatter_dimension=2, tiled=True
        ).astype(jnp.float32),
        lax.psum_scatter(
            grad_sgate.astype(jnp.bfloat16), "dp", scatter_dimension=1, tiled=True
        ).astype(jnp.float32),
        lax.psum_scatter(
            grad_sup.astype(jnp.bfloat16), "dp", scatter_dimension=1, tiled=True
        ).astype(jnp.float32),
        lax.psum_scatter(
            grad_sdown.astype(jnp.bfloat16), "dp", scatter_dimension=0, tiled=True
        ).astype(jnp.float32),
    )
    return (
        layer_out.astype(jnp.bfloat16)[None],
        input_grad[None],
        grad_ingain,
        grad_wquery,
        grad_bquery,
        grad_wkey,
        grad_bkey,
        grad_wvalue,
        grad_bvalue,
        grad_wout,
        grad_ffngain,
        grad_router,
        grad_expgate,
        grad_expup,
        grad_expdown,
        grad_shgate,
        grad_shup,
        grad_shdown,
        grad_shmix,
    )


def solution(mesh):
    in_specs = (
        P("dp", "ctx", None),
        P(("dp", "ctx")),
        P(("dp", "ctx"), None),
        P(("dp", "ctx")),
        P(("dp", "ctx"), None),
        P(("dp", "ctx")),
        P(("dp", "ctx"), None),
        P(("dp", "ctx")),
        P(("dp", "ctx"), None),
        P(("dp", "ctx")),
        P(("dp", "ctx"), None),
        P("ctx", "dp", None),
        P("ctx", "dp", None),
        P("ctx", None, "dp"),
        P(None, ("dp", "ctx")),
        P(None, ("dp", "ctx")),
        P(("dp", "ctx"), None),
        P(("dp", "ctx")),
        P("dp", "ctx", None),
        P("dp", "ctx", None),
        P("dp", None),
        P("dp", "ctx", None),
    )
    out_specs = (
        P("dp", "ctx", None),
        P("dp", "ctx", None),
        P(("dp", "ctx")),
        P(("dp", "ctx"), None),
        P(("dp", "ctx")),
        P(("dp", "ctx"), None),
        P(("dp", "ctx")),
        P(("dp", "ctx"), None),
        P(("dp", "ctx")),
        P(("dp", "ctx"), None),
        P(("dp", "ctx")),
        P(("dp", "ctx"), None),
        P("ctx", "dp", None),
        P("ctx", "dp", None),
        P("ctx", None, "dp"),
        P(None, ("dp", "ctx")),
        P(None, ("dp", "ctx")),
        P(("dp", "ctx"), None),
        P(("dp", "ctx")),
    )
    return jax.shard_map(
        on_device, mesh=mesh, in_specs=in_specs, out_specs=out_specs, check_vma=False
    )
```

profile of v0, /device:TPU:0, one launch (start us, length us, event | category | flops | bytes accessed | tf_op | source)
XLA Modules:
  0.0 3899.7 jit_solution(14817656109365556377)
XLA Ops:
  14.6 42.9 %all-reduce.14 = (bf16[2048]{0:T(1024)(128)(2,1)S(1)}, bf16[2048]{0:T(1024)(128)(2,1)S(1)}, bf16[2048]{0:T(1024)(128)(2,1)S(1)}, bf16[2048]{0:T(1024)(128)(2,1)S...) all-reduce(bf16[2048]{0:T(1024)(128)(2,1)S(1)} %dynamic-update-slic, ...), channel_id=1, replica_groups=mesh['dp'=4,'ctx'=8] {'dp','ctx'}, use_global_device_ids=true, to_apply=%add.2 | all-reduce | flops 12288 | bytes 49152
  60.2 30.9 all-gather.23.cloned.1.call-done
  91.1 10.0 add_convert_fusion.2
  102.6 67.4 %all-gather.19.cloned.1.call-done = bf16[2048,2048]{1,0:T(8,128)(2,1)} async-done(((bf16[64,2048]{1,0:T(8,128)(2,1)}), bf16[2048,2048]{1,0:T(8,128)(2,1)}) %all-gather.19.cloned.1.call-update) | async-done | bytes 8388624 | tf_op jit(solution)/shard_map/all_gather | solution.py:138
  179.9 69.0 %all-gather.17.cloned.1.call-done = bf16[2048,2048]{1,0:T(8,128)(2,1)} async-done(((bf16[64,2048]{1,0:T(8,128)(2,1)}), bf16[2048,2048]{1,0:T(8,128)(2,1)}) %all-gather.17.cloned.1.call-update) | async-done | bytes 8388624 | tf_op jit(solution)/shard_map/all_gather | solution.py:136
  273.5 65.7 %all-gather.25.cloned.1.call-done = bf16[4096,2048]{1,0:T(8,128)(2,1)} async-done(((bf16[512,2048]{1,0:T(8,128)(2,1)}), bf16[4096,2048]{1,0:T(8,128)(2,1)}) %all-gather.25.cloned.1.call-update) | async-done | bytes 16777232 | tf_op jit(solution)/shard_map/all_gather | solution.py:183
  339.1 92.2 %all-gather.21.cloned.1.call-done = bf16[4096,2048]{1,0:T(8,128)(2,1)} async-done(((bf16[512,2048]{1,0:T(8,128)(2,1)}), bf16[4096,2048]{1,0:T(8,128)(2,1)}) %all-gather.21.cloned.1.call-update) | async-done | bytes 16777232 | tf_op jit(solution)/shard_map/all_gather | solution.py:182
  431.3 169.9 %while.35 = (s32[]{:T(128)}, bf16[512,2048]{1,0:T(8,128)(2,1)}, f32[16,512]{1,0:T(8,128)S(1)}, bf16[512,2048]{1,0:T(8,128)(2,1)}, bf16[4096,2048]{1,0:T(8,128)(2...) while((s32[]{:T(128)}, bf16[512,2048]{1,0:T(8,128)(2,1)}, ...), condition=%wide.region_5.6_spmd.clone, body=%wide.region_1.5_spmd.clone.sunk | while | flops 1098907648 | bytes 27726060 | solution.py:210
  628.9 11.8 gather_fusion
  647.4 9.3 convolution_convert_fusion.1
  662.0 104.6 %all-gather.35.cloned.1.call-done = bf16[4096,2048]{1,0:T(8,128)(2,1)} async-done(((bf16[512,2048]{1,0:T(8,128)(2,1)}), bf16[4096,2048]{1,0:T(8,128)(2,1)}) %all-gather.35.cloned.1.call-update) | async-done | bytes 16777232 | tf_op jit(solution)/shard_map/all_gather | solution.py:312
  766.6 18.9 fusion.150
  785.5 70.2 %all-gather.37.cloned.1.call-done = bf16[2048,704]{0,1:T(8,128)(2,1)} async-done(((bf16[2048,176]{0,1:T(8,128)(2,1)}), bf16[2048,704]{0,1:T(8,128)(2,1)}) %all-gather.37.cloned.1.call-update) | async-done | bytes 2883600 | tf_op jit(solution)/shard_map/all_gather | solution.py:151
  855.8 20.5 fusion.149
  880.8 34.3 all-gather.41.cloned.1.call-done
  915.1 90.5 %all-gather.43.cloned.1.call-done = bf16[1,4096,2048]{2,1,0:T(8,128)(2,1)} async-done(((bf16[1,512,2048]{2,1,0:T(8,128)(2,1)}), bf16[1,4096,2048]{2,1,0:T(8,128)(2,1)}) %all-gather.43.cloned.1.call-update) | async-done | bytes 16777232 | tf_op jit(solution)/shard_map/all_gather | solution.py:184
  1005.6 27.0 multiply_convert_fusion.2
  1032.6 19.9 convolution_convert_fusion
  1053.2 41.7 %all-gather.1 = bf16[32,64,8]{1,2,0:T(8,128)(2,1)S(1)} all-gather(bf16[1,64,8]{1,2,0:T(8,128)(2,1)S(1)} %bitcast.363), channel_id=1, replica_groups=mesh['dp'=4,'ctx'=8] {'dp','ctx'}, dimensions={0}, use_global_device_ids=true | all-gather | bytes 33792 | tf_op jit(solution)/shard_map/all_gather | solution.py:144
  1096.8 12.7 gather_fusion.2
  1129.3 22.3 fusion.59
  1151.6 69.0 %all-gather.33.cloned.1.call-done = bf16[1,1408,2048]{2,1,0:T(8,128)(2,1)} async-done(((bf16[1,1408,512]{2,1,0:T(8,128)(2,1)}), bf16[1,1408,2048]{2,1,0:T(8,128)(2,1)}) %all-gather.33.cloned.1.call-update) | async-done | bytes 5767184 | tf_op jit(solution)/shard_map/all_gather | solution.py:150
  1220.6 25.2 all-to-all-done.2
  1245.8 22.3 fusion.54
  1268.1 22.3 fusion.153
  1290.4 23.5 add_convert_fusion
  1314.0 13.0 all-gather.29.cloned.1.call-done
  1327.0 32.2 fusion.41
  1362.2 20.0 convolution_convert_fusion.2
  1387.5 22.8 fusion.43
  1410.3 26.3 add_convert_fusion.1
  1436.6 111.2 %all-to-all-done.1 = bf16[8,320,2048]{2,1,0:T(8,128)(2,1)} async-done(((bf16[8,320,2048]{2,1,0:T(8,128)(2,1)}), bf16[8,320,2048]{2,1,0:T(8,128)(2,1)}, u32[]{:S(2)}, u32[]{:S(2)}) %all-to-all-start.1) | async-done | bytes 10485792 | tf_op jit(solution)/shard_map/all_to_all | solution.py:284
  1559.7 11.5 concatenate.27
  1571.2 22.8 gather_fusion.1
  1594.0 15.6 reshape.710
  1609.6 20.5 multiply_reduce_fusion.1
  1630.3 85.1 %all-to-all-done.3 = bf16[8,320,2048]{2,1,0:T(8,128)(2,1)} async-done(((bf16[8,320,2048]{2,1,0:T(8,128)(2,1)}), bf16[8,320,2048]{2,1,0:T(8,128)(2,1)}, u32[]{:S(2)}, u32[]{:S(2)}) %all-to-all-start.3) | async-done | bytes 10485792 | tf_op jit(solution)/shard_map/all_to_all | solution.py:287
  1715.4 9.8 fusion.151
  1727.5 10.7 reduce-scatter.20.cloned.1.call-done
  1768.3 516.1 %while.36 = (s32[]{:T(128)}, f32[512,2048]{1,0:T(8,128)}, bf16[4096,2048]{1,0:T(8,128)(2,1)}, bf16[4096,2048]{1,0:T(8,128)(2,1)}, bf16[512,2048]{1,0:T(8,128)(2,...) while((s32[]{:T(128)}, f32[512,2048]{1,0:T(8,128)}, ...), condition=%wide.region_25.26_spmd.clone, body=%wide.region_23.25_spmd.clone.sunk | while | flops 2712206848 | bytes 104652024 | solution.py:378
  2288.1 22.2 fusion.53
  2310.4 22.4 fusion.52
  2332.8 22.5 fusion.49
  2356.1 19.0 fusion.87
  2375.1 18.4 convolution_convert_fusion.3
  2394.0 18.7 convolution_convert_fusion.4
  2412.8 14.1 fusion.105
  2428.8 10.0 fusion.137
  2444.3 74.9 %reduce-scatter.22.cloned.1.call-done = bf16[512,2048]{1,0:T(8,128)(2,1)} async-done(((bf16[4096,2048]{1,0:T(8,128)(2,1)}), bf16[512,2048]{1,0:T(8,128)(2,1)}) %reduce-scatter.22.cloned.1.call-update) | async-done | bytes 2097168 | tf_op jit(solution)/shard_map/reduce_scatter | solution.py:389
  2543.0 8.9 fusion.92
  2551.9 105.0 %reduce-scatter.46.cloned.1.call-done = f32[64,8]{1,0:T(8,128)} async-done(((f32[2048,8]{1,0:T(8,128)}), f32[64,8]{1,0:T(8,128)}) %reduce-scatter.46.cloned.1.call-update) | async-done | bytes 2064
  2658.3 99.0 %reduce-scatter.38.cloned.1.call-done = bf16[1,1408,512]{2,1,0:T(8,128)(2,1)} async-done(((bf16[1,1408,2048]{2,1,0:T(8,128)(2,1)}), bf16[1,1408,512]{2,1,0:T(8,128)(2,1)}) %reduce-scatter.38.cloned.1.call-update) | async-done | bytes 1441808 | tf_op jit(solution)/shard_map/reduce_scatter | solution.py:456
  2760.7 101.9 %reduce-scatter.36.cloned.1.call-done = bf16[1,512,1408]{2,1,0:T(8,128)(2,1)} async-done(((bf16[1,2048,1408]{2,1,0:T(8,128)(2,1)}), bf16[1,512,1408]{2,1,0:T(8,128)(2,1)}) %reduce-scatter.36.cloned.1.call-update) | async-done | bytes 1441808 | tf_op jit(solution)/shard_map/reduce_scatter | solution.py:453
  2865.7 102.1 %reduce-scatter.34.cloned.1.call-done = bf16[1,512,1408]{2,1,0:T(8,128)(2,1)} async-done(((bf16[1,2048,1408]{2,1,0:T(8,128)(2,1)}), bf16[1,512,1408]{2,1,0:T(8,128)(2,1)}) %reduce-scatter.34.cloned.1.call-update) | async-done | bytes 1441808 | tf_op jit(solution)/shard_map/reduce_scatter | solution.py:450
  2970.9 56.0 %reduce-scatter.44.cloned.1.call-done = bf16[176,2048]{1,0:T(8,128)(2,1)} async-done(((bf16[704,2048]{1,0:T(8,128)(2,1)}), bf16[176,2048]{1,0:T(8,128)(2,1)}) %reduce-scatter.44.cloned.1.call-update) | async-done | bytes 720912 | tf_op jit(solution)/shard_map/reduce_scatter | solution.py:465
  3029.3 56.0 %reduce-scatter.42.cloned.1.call-done = bf16[2048,176]{0,1:T(8,128)(2,1)} async-done(((bf16[2048,704]{0,1:T(8,128)(2,1)}), bf16[2048,176]{0,1:T(8,128)(2,1)}) %reduce-scatter.42.cloned.1.call-update) | async-done | bytes 720912 | tf_op jit(solution)/shard_map/reduce_scatter | solution.py:462
  3087.6 56.1 %reduce-scatter.40.cloned.1.call-done = bf16[2048,176]{0,1:T(8,128)(2,1)} async-done(((bf16[2048,704]{0,1:T(8,128)(2,1)}), bf16[2048,176]{0,1:T(8,128)(2,1)}) %reduce-scatter.40.cloned.1.call-update) | async-done | bytes 720912 | tf_op jit(solution)/shard_map/reduce_scatter | solution.py:459
  3147.0 9.7 fusion.94
  3162.9 11.4 fusion.84
  3174.4 43.9 %all-reduce.13 = (f32[2048]{0:T(1024)S(1)}, f32[2048]{0:T(1024)S(1)}, f32[2048]{0:T(1024)S(1)}, f32[2048]{0:T(1024)S(1)}, f32[2048]{0:T(1024)S(1)}, /*index=5*/f32[2048]{0:T(1024)S(1)}) all-reduce(f32[2048]{0:T(1024)S(1)} %get-tuple-element.410, f32[2048]{0:T(1024)S(1)} %bitcast.355, ...), channel_id=7, replica_groups=mesh['dp'=4,'ctx'=8] {'dp','ctx'}, use_global_device_ids=true, to_apply=%region_30.31.clone | all-reduce | flops 12288 | bytes 98304
  3228.4 102.2 %reduce-scatter.32.cloned.1.call-done = f32[64,2048]{1,0:T(8,128)} async-done(((f32[2048,2048]{1,0:T(8,128)}), f32[64,2048]{1,0:T(8,128)}) %reduce-scatter.32.cloned.1.call-update) | async-done | bytes 524304 | tf_op jit(solution)/shard_map/reduce_scatter | solution.py:444
  3330.6 187.3 %reduce-scatter.30.cloned.1.call-done = f32[64,2048]{1,0:T(8,128)} async-done(((f32[2048,2048]{1,0:T(8,128)}), f32[64,2048]{1,0:T(8,128)}) %reduce-scatter.30.cloned.1.call-update) | async-done | bytes 524304 | tf_op jit(solution)/shard_map/reduce_scatter | solution.py:442
  3517.8 187.7 %reduce-scatter.26.cloned.1.call-done = f32[64,2048]{1,0:T(8,128)} async-done(((f32[2048,2048]{1,0:T(8,128)}), f32[64,2048]{1,0:T(8,128)}) %reduce-scatter.26.cloned.1.call-update) | async-done | bytes 524304 | tf_op jit(solution)/shard_map/reduce_scatter | solution.py:438
  3705.5 187.4 %reduce-scatter.28.cloned.1.call-done = f32[64,2048]{1,0:T(8,128)} async-done(((f32[2048,2048]{1,0:T(8,128)}), f32[64,2048]{1,0:T(8,128)}) %reduce-scatter.28.cloned.1.call-update) | async-done | bytes 524304 | tf_op jit(solution)/shard_map/reduce_scatter | solution.py:440
  (627 shorter events, 920.9 us)
Async XLA Ops:
  7.2 83.9 %all-gather.23.cloned.1.call-start = ((), (), s32[]{:S(2)}) async-start(), calls=%async_computation.22 | async-start | bytes 8650752 | tf_op jit(solution)/shard_map/all_gather | solution.py:140
  7.9 162.0 %all-gather.19.cloned.1.call-start = ((), (), s32[]{:S(2)}) async-start(), calls=%async_computation.20 | async-start | bytes 8650752 | tf_op jit(solution)/shard_map/all_gather | solution.py:138
  8.7 240.2 %all-gather.17.cloned.1.call-start = ((), (), s32[]{:S(2)}) async-start(), calls=%async_computation.19 | async-start | bytes 8650752 | tf_op jit(solution)/shard_map/all_gather | solution.py:136
  9.4 329.7 %all-gather.25.cloned.1.call-start = ((), (), s32[]{:S(2)}) async-start(), calls=%async_computation.23 | async-start | bytes 18874368 | tf_op jit(solution)/shard_map/all_gather | solution.py:183
  57.5 191.4 %copy-start.59 = (f32[2048]{0:T(1024)}, f32[2048]{0:T(1024)S(1)}, u32[]{:S(2)}) copy-start(f32[2048]{0:T(1024)S(1)} %convert_element_type.260) | copy-start | bytes 24580
  60.2 188.7 %copy-start.72 = (f32[512]{0:T(512)}, f32[512]{0:T(512)S(1)}, u32[]{:S(2)}) copy-start(f32[512]{0:T(512)S(1)} %get-tuple-element.513) | copy-start | bytes 6148
  91.1 78.9 %copy-start.15 = (bf16[1,512,2048]{2,1,0:T(8,128)(2,1)S(1)}, bf16[1,512,2048]{2,1,0:T(8,128)(2,1)}, u32[]{:S(2)}) copy-start(bf16[1,512,2048]{2,1,0:T(8,128)(2,1)} %param.28) | copy-start | bytes 6291460
  101.1 330.2 %all-gather.21.cloned.1.call-start = ((), (), s32[]{:S(2)}) async-start(), calls=%async_computation.21 | async-start | bytes 18874368 | tf_op jit(solution)/shard_map/all_gather | solution.py:182
  102.6 154.3 %copy-start.20 = (f32[512,64]{1,0:T(8,128)}, f32[512,64]{1,0:T(8,128)S(1)}, u32[]{:S(2)}) copy-start(f32[512,64]{1,0:T(8,128)S(1)} %get-tuple-element.510) | copy-start | bytes 393220
  102.6 154.3 %copy-start.22 = (f32[512,64]{1,0:T(8,128)}, f32[512,64]{1,0:T(8,128)S(1)}, u32[]{:S(2)}) copy-start(f32[512,64]{1,0:T(8,128)S(1)} %get-tuple-element.511) | copy-start | bytes 393220
  266.8 164.5 %copy-start.70 = (s32[2]{0:T(128)S(1)}, s32[2]{0:T(128)}, u32[]{:S(2)}) copy-start(s32[2]{0:T(128)} %constant.234.clone.2) | copy-start | bytes 28
  266.8 334.5 %all-gather.27.cloned.1.call-start = ((), (), s32[]{:S(2)}) async-start(), calls=%async_computation.24 | async-start | bytes 8650752 | tf_op jit(solution)/shard_map/all_gather | solution.py:142
  267.4 394.7 %all-gather.39.cloned.1.call-start = ((), (), s32[]{:S(2)}) async-start(), calls=%async_computation.30 | async-start | bytes 3604480 | tf_op jit(solution)/shard_map/all_gather | solution.py:152
  268.1 498.5 %all-gather.35.cloned.1.call-start = ((), (), s32[]{:S(2)}) async-start(), calls=%async_computation.28 | async-start | bytes 18874368 | tf_op jit(solution)/shard_map/all_gather | solution.py:312
  270.0 339.8 %copy-start.42 = (f32[2048]{0:T(1024)}, f32[2048]{0:T(1024)S(1)}, u32[]{:S(2)}) copy-start(f32[2048]{0:T(1024)S(1)} %convert_element_type.270) | copy-start | bytes 24580
  613.0 242.8 %all-gather.37.cloned.1.call-start = ((), (), s32[]{:S(2)}) async-start(), calls=%async_computation.29 | async-start | bytes 3604480 | tf_op jit(solution)/shard_map/all_gather | solution.py:151
  613.7 301.3 %all-gather.41.cloned.1.call-start = ((), (), s32[]{:S(2)}) async-start(), calls=%async_computation.31 | async-start | bytes 3604480 | tf_op jit(solution)/shard_map/all_gather | solution.py:153
  614.3 391.2 %all-gather.43.cloned.1.call-start = ((), (), s32[]{:S(2)}) async-start(), calls=%async_computation.46 | async-start | bytes 18874368 | tf_op jit(solution)/shard_map/all_gather | solution.py:184
  615.1 514.2 %all-gather.31.cloned.1.call-start = ((), (), s32[]{:S(2)}) async-start(), calls=%async_computation.26 | async-start | bytes 7208960 | tf_op jit(solution)/shard_map/all_gather | solution.py:149
  615.6 605.0 %all-gather.33.cloned.1.call-start = ((), (), s32[]{:S(2)}) async-start(), calls=%async_computation.27 | async-start | bytes 7208960 | tf_op jit(solution)/shard_map/all_gather | solution.py:150
  616.4 710.6 %all-gather.29.cloned.1.call-start = ((), (), s32[]{:S(2)}) async-start(), calls=%async_computation.25 | async-start | bytes 7208960 | tf_op jit(solution)/shard_map/all_gather | solution.py:148
  617.2 259.1 %copy-start.49 = (bf16[2048,1]{0,1:T(2,128)(2,1)}, bf16[2048,1]{0,1:T(2,128)(2,1)S(1)}, u32[]{:S(2)}) copy-start(bf16[2048,1]{0,1:T(2,128)(2,1)S(1)} %reshape.728) | copy-start | bytes 12292
  628.9 18.4 copy-start.1
  641.1 15.5 copy-start.57
  656.6 467.4 %all-to-all-start = ((bf16[8,320,2048]{2,1,0:T(8,128)(2,1)}), bf16[8,320,2048]{2,1,0:T(8,128)(2,1)}, u32[]{:S(2)}, u32[]{:S(2)}) async-start(bf16[8,320,2048]{2,1,0:T(8,128)(2,1)} %bitcast.337), calls=%async_computation | async-start | bytes 20971520 | tf_op jit(solution)/shard_map/all_to_all | solution.py:239
  661.8 1063.4 %reduce-scatter.18.cloned.1.call-start = ((), (), s32[]{:S(2)}) async-start(), calls=%async_computation.32 | async-start | bytes 18874368 | tf_op jit(solution)/shard_map/reduce_scatter | solution.py:332
  855.8 20.5 copy-start.11
  880.7 151.8 %copy-start.68 = (f32[4096]{0:T(1024)}, f32[4096]{0:T(1024)S(1)}, u32[]{:S(2)}) copy-start(f32[4096]{0:T(1024)S(1)} %add_divide_fusion.1) | copy-start | bytes 49156
  1096.7 16.8 copy-start.38
  1096.7 16.9 copy-start.58
  1096.7 19.1 copy-start.9
  1096.7 19.1 copy-start.31
  1124.1 121.7 %all-to-all-start.2 = ((bf16[8,320,2048]{2,1,0:T(8,128)(2,1)}), bf16[8,320,2048]{2,1,0:T(8,128)(2,1)}, u32[]{:S(2)}, u32[]{:S(2)}) async-start(bf16[8,320,2048]{2,1,0:T(8,128)(2,1)} %bitcast.338), calls=%async_computation.3 | async-start | bytes 20971520 | tf_op jit(solution)/shard_map/all_to_all | solution.py:242
  1129.2 609.0 %reduce-scatter.20.cloned.1.call-start = ((), (), s32[]{:S(2)}) async-start(), calls=%async_computation.33 | async-start | bytes 18874368 | tf_op jit(solution)/shard_map/reduce_scatter | solution.py:335
  1268.1 22.4 copy-start.83
  1382.1 165.6 %all-to-all-start.1 = ((bf16[8,320,2048]{2,1,0:T(8,128)(2,1)}), bf16[8,320,2048]{2,1,0:T(8,128)(2,1)}, u32[]{:S(2)}, u32[]{:S(2)}) async-start(bf16[8,320,2048]{2,1,0:T(8,128)(2,1)} %convolution_convert_fusion.2), calls=%async_computation.1 | async-start | bytes 20971520 | tf_op jit(solution)/shard_map/all_to_all | solution.py:284
  1436.6 116.5 %copy-start.65 = (bf16[2048]{0:T(1024)(128)(2,1)S(1)}, bf16[2048]{0:T(1024)(128)(2,1)}, u32[]{:S(2)}) copy-start(bf16[2048]{0:T(1024)(128)(2,1)} %get-tuple-element.473) | copy-start | bytes 12292
  1436.6 116.5 %copy-start.34 = (s32[512,4,1]{1,0,2:T(8,128)S(1)}, s32[512,4,1]{1,0,2:T(8,128)}, u32[]{:S(2)}) copy-start(s32[512,4,1]{1,0,2:T(8,128)} %get-tuple-element.509) | copy-start | bytes 24580
  1547.7 167.7 %all-to-all-start.3 = ((bf16[8,320,2048]{2,1,0:T(8,128)(2,1)}), bf16[8,320,2048]{2,1,0:T(8,128)(2,1)}, u32[]{:S(2)}, u32[]{:S(2)}) async-start(bf16[8,320,2048]{2,1,0:T(8,128)(2,1)} %add_convert_fusion.1), calls=%async_computation.4 | async-start | bytes 20971520 | tf_op jit(solution)/shard_map/all_to_all | solution.py:287
  1553.0 874.0 %reduce-scatter.24.cloned.1.call-start = ((), (), s32[]{:S(2)}) async-start(), calls=%async_computation.35 | async-start | bytes 18874368 | tf_op jit(solution)/shard_map/reduce_scatter | solution.py:392
  1594.0 15.6 copy-start.33
  1609.6 20.7 copy-start.39
  1609.6 105.9 %copy-start.32 = (pred[2560,512]{1,0:T(8,128)(4,1)S(1)}, pred[2560,512]{1,0:T(8,128)(4,1)}, u32[]{:S(2)}) copy-start(pred[2560,512]{1,0:T(8,128)(4,1)} %copy-done.30) | copy-start | bytes 3932164
  1630.3 107.9 %copy-start.47 = (bf16[512,8]{0,1:T(8,128)(2,1)}, bf16[512,8]{0,1:T(8,128)(2,1)S(1)}, u32[]{:S(2)}) copy-start(bf16[512,8]{0,1:T(8,128)(2,1)S(1)} %select_reduce_fusion.1) | copy-start | bytes 24580
  1725.2 13.0 copy-start.43
  1725.2 13.0 copy-start.56
  1727.5 16.8 copy-start.62
  2284.5 234.8 %reduce-scatter.22.cloned.1.call-start = ((), (), s32[]{:S(2)}) async-start(), calls=%async_computation.34 | async-start | bytes 18874368 | tf_op jit(solution)/shard_map/reduce_scatter | solution.py:389
  2285.0 371.8 %reduce-scatter.46.cloned.1.call-start = ((), (), s32[]{:S(2)}) async-start(), calls=%async_computation.47 | async-start | bytes 1081344
  2288.0 469.3 %reduce-scatter.38.cloned.1.call-start = ((), (), s32[]{:S(2)}) async-start(), calls=%async_computation.42 | async-start | bytes 7208960 | tf_op jit(solution)/shard_map/reduce_scatter | solution.py:456
  2310.3 552.2 %reduce-scatter.36.cloned.1.call-start = ((), (), s32[]{:S(2)}) async-start(), calls=%async_computation.41 | async-start | bytes 7208960 | tf_op jit(solution)/shard_map/reduce_scatter | solution.py:453
  2332.8 635.0 %reduce-scatter.34.cloned.1.call-start = ((), (), s32[]{:S(2)}) async-start(), calls=%async_computation.40 | async-start | bytes 7208960 | tf_op jit(solution)/shard_map/reduce_scatter | solution.py:450
  2355.4 671.5 %reduce-scatter.44.cloned.1.call-start = ((), (), s32[]{:S(2)}) async-start(), calls=%async_computation.45 | async-start | bytes 3604480 | tf_op jit(solution)/shard_map/reduce_scatter | solution.py:465
  2375.1 710.2 %reduce-scatter.42.cloned.1.call-start = ((), (), s32[]{:S(2)}) async-start(), calls=%async_computation.44 | async-start | bytes 3604480 | tf_op jit(solution)/shard_map/reduce_scatter | solution.py:462
  2393.6 19.3 copy-start.29
  2393.6 750.1 %reduce-scatter.40.cloned.1.call-start = ((), (), s32[]{:S(2)}) async-start(), calls=%async_computation.43 | async-start | bytes 3604480 | tf_op jit(solution)/shard_map/reduce_scatter | solution.py:459
  2412.8 917.8 %reduce-scatter.32.cloned.1.call-start = ((), (), s32[]{:S(2)}) async-start(), calls=%async_computation.39 | async-start | bytes 17301504 | tf_op jit(solution)/shard_map/reduce_scatter | solution.py:444
  2426.9 1090.9 %reduce-scatter.30.cloned.1.call-start = ((), (), s32[]{:S(2)}) async-start(), calls=%async_computation.38 | async-start | bytes 17301504 | tf_op jit(solution)/shard_map/reduce_scatter | solution.py:442
  2438.9 1266.7 %reduce-scatter.26.cloned.1.call-start = ((), (), s32[]{:S(2)}) async-start(), calls=%async_computation.36 | async-start | bytes 17301504 | tf_op jit(solution)/shard_map/reduce_scatter | solution.py:438
  2538.6 1354.4 %reduce-scatter.28.cloned.1.call-start = ((), (), s32[]{:S(2)}) async-start(), calls=%async_computation.37 | async-start | bytes 17301504 | tf_op jit(solution)/shard_map/reduce_scatter | solution.py:440
  2970.9 175.4 %copy-start.4 = (bf16[512,2048]{1,0:T(8,128)(2,1)S(1)}, bf16[512,2048]{1,0:T(8,128)(2,1)}, u32[]{:S(2)}) copy-start(bf16[512,2048]{1,0:T(8,128)(2,1)} %multiply_convert_fusion.5) | copy-start | bytes 6291460
  2970.9 175.4 %copy-start.63 = (f32[512]{0:T(512)S(1)}, f32[512]{0:T(512)}, u32[]{:S(2)}) copy-start(f32[512]{0:T(512)} %copy-done.62) | copy-start | bytes 6148
  3143.7 13.0 slice-start
  3162.9 58.8 %copy-start.71 = (f32[512]{0:T(512)S(1)}, f32[512]{0:T(512)}, u32[]{:S(2)}) copy-start(f32[512]{0:T(512)} %get-tuple-element.512) | copy-start | bytes 6148
  (75 other events, 464.9 us)
Sparse Core Ops, SparseCore 0:
  10.9 80.1 all-gather.22
  93.9 75.9 all-gather.18
  172.8 76.0 all-gather.16
  250.6 88.4 all-gather.24
  341.4 89.8 all-gather.20
  434.0 77.5 all-gather.26
  513.2 57.7 all-gather.38
  613.1 153.4 all-gather.34
  768.2 87.5 all-gather.36
  857.2 57.8 all-gather.40
  917.0 88.5 all-gather.42
  1007.0 106.9 all-gather.30
  1115.6 104.9 all-gather.32
  1222.0 104.9 all-gather.28
  1330.5 198.6 reduce-scatter.17
  1532.6 205.6 reduce-scatter.19
  2284.6 115.1 reduce-scatter.23
  2403.2 115.9 reduce-scatter.21
  2522.0 134.7 reduce-scatter.45
  2659.1 98.1 reduce-scatter.37
  2759.7 102.7 reduce-scatter.35
  2864.9 102.7 reduce-scatter.33
  2970.1 56.6 reduce-scatter.43
  3029.2 56.0 reduce-scatter.41
  3087.6 56.0 reduce-scatter.39
  3146.5 183.9 reduce-scatter.31
  3333.4 184.4 reduce-scatter.29
  3520.8 184.6 reduce-scatter.25
  3708.5 184.3 reduce-scatter.27
where the time goes:
time: 3910 us; the launch traced here: 3900 us
  waiting for transfers between devices  2260 us (58%)
  matrix products  1050 us (27%)
  other arithmetic  260 us (7%)
  local copies, waits for them, and re-layouts  158 us (4%)
  blocking collectives  129 us (3%)
    dot_general x32, matrix products, head_block(): jnp.einsum('qd,kd->qk', query_head, key_head, preferred_element_type=jnp....  212 us
    reduce_scatter x1, waiting for transfers between devices, on_device(): lax.psum_scatter(grad_query_w, ('dp', 'ctx'), scatter_dimension=0, tiled=...  188 us
    reduce_scatter x1, waiting for transfers between devices, on_device(): lax.psum_scatter(grad_key_w, ('dp', 'ctx'), scatter_dimension=0, tiled=True)  187 us
    reduce_scatter x1, waiting for transfers between devices, on_device(): lax.psum_scatter(grad_value_w, ('dp', 'ctx'), scatter_dimension=0, tiled=...  187 us
    convert_element_type x16, other arithmetic, backward_head(): score_grad = (probs_full * (prob_grad - row_dot)).astype(jnp.bfloat16)  127 us
    unnamed x30, waiting for transfers between devices  113 us
    all_to_all x1, waiting for transfers between devices, on_device(): lax.all_to_all(expert_out.reshape(owner_shape), 'ctx', split_axis=0, conc...  111 us
    all_gather x1, waiting for transfers between devices, on_device(): all_normed = lax.all_gather(normed_two, 'ctx', axis=0, tiled=True)  105 us
  transfers between devices with their start and end apart: 33, of which 27 were waited for; matrix products, arithmetic and copies ran while one was open for 23% of the time, Pallas kernels for 0%

commit v1 on v0

v1 whole, which is shorter than its diff:
```python
import functools

import jax
import jax.numpy as jnp
from jax import lax
from jax.experimental import pallas as pl
from jax.experimental.pallas import tpu as pltpu
from jax.sharding import PartitionSpec as P

D = 2048
HEADS = 16
HEAD_DIM = 128
TOP_K = 4
CONT = 256
PROMPT = 2048

rope_base = 1000000.0
epsilon = 1e-06
masked_score = -1e30
log2_e = 1.4426950408889634
low = jnp.bfloat16
full = jnp.float32


def dot(left, right):
    return jnp.dot(left, right, preferred_element_type=full)


def dot_nt(left, right):
    return lax.dot_general(left, right, (((1,), (1,)), ((), ())), preferred_element_type=full)


def ein(spec, left, right):
    return jnp.einsum(spec, left, right, preferred_element_type=full)


def rotate(values, cosine, sine):
    middle = values.shape[-1] // 2
    leading = values[..., :middle]
    trailing = values[..., middle:]
    return jnp.concatenate(
        [leading * cosine - trailing * sine, trailing * cosine + leading * sine], axis=-1
    )


def rope_tables(places):
    turned = jnp.where(places < PROMPT, places, PROMPT + (places - PROMPT) % CONT)
    frequency = rope_base ** (-2.0 * jnp.arange(HEAD_DIM // 2, dtype=full) / HEAD_DIM)
    angles = turned.astype(full)[:, None] * frequency[None, :]
    return (jnp.cos(angles)[:, None, :], jnp.sin(angles)[:, None, :])


def rms_scale(values):
    return lax.rsqrt(jnp.mean(values * values, axis=-1, keepdims=True) + epsilon)


def norm_back(values, scale_rows, gain_row, upstream):
    weighted = upstream * gain_row
    grad_gain = jnp.sum(upstream * values * scale_rows, axis=0)
    grad_values = scale_rows * weighted - values * scale_rows**3 * jnp.mean(
        weighted * values, axis=-1, keepdims=True
    )
    return (grad_values, grad_gain)


def silu_parts(values):
    sig_value = jax.nn.sigmoid(values)
    return (values * sig_value, sig_value * (1.0 + values * (1.0 - sig_value)))


WIDE = 4


def attend_tiles(index, chunk, carry):
    whole = jnp.minimum(index, PROMPT // CONT)
    wide = whole // WIDE
    carry = lax.fori_loop(
        0, wide, lambda step, c: chunk(step * (WIDE * CONT), WIDE * CONT, False, c), carry
    )
    carry = lax.fori_loop(
        wide * WIDE, whole, lambda step, c: chunk(step * CONT, CONT, False, c), carry
    )
    return chunk(index * CONT, CONT, True, carry)


def forward_kernel(q_ref, k_ref, vt_ref, o_ref, lse_ref):
    index = pl.program_id(1)
    query = q_ref[...]
    score_scale = HEAD_DIM ** (-0.5) * log2_e

    def chunk(start, size, diagonal, carry):
        highest, total, acc = carry
        start = pl.multiple_of(start, CONT)
        scores = dot_nt(k_ref[pl.ds(start, size), :], query) * score_scale
        if diagonal:
            keys = lax.broadcasted_iota(jnp.int32, scores.shape, 0)
            queries = lax.broadcasted_iota(jnp.int32, scores.shape, 1)
            scores = jnp.where(keys <= queries, scores, masked_score)
        newest = jnp.maximum(highest, jnp.max(scores, axis=0, keepdims=True))
        weights = jnp.exp2(scores - newest)
        shrink = jnp.exp2(highest - newest)
        total = total * shrink + jnp.sum(weights, axis=0, keepdims=True)
        acc = acc * shrink + dot(vt_ref[:, pl.ds(start, size)], weights.astype(low))
        return (newest, total, acc)

    highest, total, acc = attend_tiles(
        index,
        chunk,
        (
            jnp.full((1, CONT), masked_score, full),
            jnp.zeros((1, CONT), full),
            jnp.zeros((HEAD_DIM, CONT), full),
        ),
    )
    o_ref[...] = (acc / total).T.astype(low)
    lse_ref[...] = (highest + jnp.log2(total))[None]


def attention_forward(query, key, value_t):
    rows, width = query.shape
    heads = width // HEAD_DIM
    tile = pl.BlockSpec((CONT, HEAD_DIM), lambda h, i: (i, h))
    return pl.pallas_call(
        forward_kernel,
        grid=(heads, rows // CONT),
        in_specs=[
            tile,
            pl.BlockSpec((rows, HEAD_DIM), lambda h, i: (0, h)),
            pl.BlockSpec((HEAD_DIM, rows), lambda h, i: (h, 0)),
        ],
        out_specs=[tile, pl.BlockSpec((1, 1, CONT), lambda h, i: (h, 0, i))],
        out_shape=[
            jax.ShapeDtypeStruct((rows, width), low),
            jax.ShapeDtypeStruct((heads, 1, rows), full),
        ],
        compiler_params=pltpu.CompilerParams(vmem_limit_bytes=48 * 2**20),
        name="attend_forward",
    )(query, key, value_t)


def backward_kernel(
    q_ref, do_ref, lse_ref, delta_ref, k_ref, kt_ref, v_ref, dq_ref, dk_ref, dv_ref
):
    index = pl.program_id(1)
    query = q_ref[...]
    upstream = do_ref[...]
    lse = lse_ref[0]
    delta = delta_ref[0]
    scale = HEAD_DIM ** (-0.5)

    @pl.when(index == 0)
    def _():
        dk_ref[...] = jnp.zeros_like(dk_ref)
        dv_ref[...] = jnp.zeros_like(dv_ref)

    def chunk(start, size, diagonal, acc):
        start = pl.multiple_of(start, CONT)
        span = pl.ds(start, size)
        scores = dot_nt(k_ref[span, :], query) * (scale * log2_e) - lse
        if diagonal:
            keys = lax.broadcasted_iota(jnp.int32, scores.shape, 0)
            queries = lax.broadcasted_iota(jnp.int32, scores.shape, 1)
            scores = jnp.where(keys <= queries, scores, masked_score)
        probs = jnp.exp2(scores)
        prob_grad = dot_nt(v_ref[span, :], upstream)
        score_grad = (probs * (prob_grad - delta)).astype(low)
        dv_ref[span, :] += dot(probs.astype(low), upstream)
        dk_ref[span, :] += dot(score_grad, query) * scale
        return acc + dot(kt_ref[:, span], score_grad)

    acc = attend_tiles(index, chunk, jnp.zeros((HEAD_DIM, CONT), full))
    dq_ref[...] = acc.T * scale


def attention_backward(query, upstream, lse, delta, key, key_t, value):
    rows, width = query.shape
    heads = width // HEAD_DIM
    tile = pl.BlockSpec((CONT, HEAD_DIM), lambda h, i: (i, h))
    line = pl.BlockSpec((1, 1, CONT), lambda h, i: (h, 0, i))
    whole = pl.BlockSpec((rows, HEAD_DIM), lambda h, i: (0, h))
    grad = jax.ShapeDtypeStruct((rows, width), full)
    return pl.pallas_call(
        backward_kernel,
        grid=(heads, rows // CONT),
        in_specs=[
            tile,
            tile,
            line,
            line,
            whole,
            pl.BlockSpec((HEAD_DIM, rows), lambda h, i: (h, 0)),
            whole,
        ],
        out_specs=[tile, whole, whole],
        out_shape=[grad, grad, grad],
        compiler_params=pltpu.CompilerParams(vmem_limit_bytes=48 * 2**20),
        name="attend_backward",
    )(query, upstream, lse, delta, key, key_t, value)


def take_blocks(rows, order):
    count = order.shape[0]
    blocked = rows.reshape(count, rows.shape[0] // count, *rows.shape[1:])
    return jnp.concatenate(
        [lax.dynamic_index_in_dim(blocked, order[i], 0, keepdims=False) for i in range(count)], axis=0
    )


def gather_ctx(values):
    return lax.all_gather(values, "ctx", axis=0, tiled=True)


def scatter_ctx(values):
    return lax.psum_scatter(values, "ctx", scatter_dimension=0, tiled=True)


def swap_ctx(values):
    return lax.all_to_all(values, "ctx", split_axis=0, concat_axis=0, tiled=True)


def on_device(
    hidden_in,
    in_gain,
    w_query,
    b_query,
    w_key,
    b_key,
    w_value,
    b_value,
    w_out,
    ffn_gain,
    w_router,
    exp_gate,
    exp_up,
    exp_down,
    sh_gate,
    sh_up,
    sh_down,
    sh_mix,
    routes,
    priority,
    blocks,
    cotangent,
):
    both = ("dp", "ctx")
    ctx_count = lax.axis_size("ctx")
    ctx_index = lax.axis_index("ctx")
    dp_count = lax.axis_size("dp")
    tokens_low = hidden_in[0]
    tokens = tokens_low.astype(full)
    cot_low = cotangent[0]
    cot_full = cot_low.astype(full)
    tok_count = tokens.shape[0]
    group_len = tok_count * ctx_count
    shard = w_query.shape[0]
    experts_total = ctx_count * exp_gate.shape[0]
    capacity = 5 * tok_count * TOP_K // (4 * experts_total)
    repeat = max(1, ctx_count // HEADS)
    heads = max(1, HEADS // ctx_count)
    width = heads * HEAD_DIM
    head_sets = HEADS // heads

    def by_heads(weight):
        parts = weight.reshape(shard, head_sets, width).transpose(1, 0, 2)
        return jnp.repeat(parts, repeat, axis=0) if repeat > 1 else parts

    qkv_parts = swap_ctx(
        jnp.concatenate([by_heads(w_query), by_heads(w_key), by_heads(w_value)], axis=2)
    )
    w_qkv = lax.all_gather(
        qkv_parts.reshape(ctx_count * shard, 3 * width), "dp", axis=0, tiled=True
    )
    x_all = gather_ctx(tokens_low)
    small = jnp.concatenate(
        [
            jnp.stack([in_gain, b_query, b_key, b_value, ffn_gain, sh_mix], axis=0),
            w_router.T,
        ],
        axis=0,
    )
    small_all = (
        lax.all_gather(small, both, axis=0)
        .transpose(1, 0, 2)
        .reshape(small.shape[0], shard * dp_count * ctx_count)
        .astype(full)
    )
    gain_one, gain_two, mix_row = small_all[0:1], small_all[4:5], small_all[5:6]
    mix_router = small_all[5:].astype(low)
    out_full = lax.all_gather(w_out, both, axis=0, tiled=True)
    cot_all = gather_ctx(cot_low)
    shared_gate, shared_up, shared_down = (
        lax.all_gather(sh_gate, "dp", axis=1, tiled=True),
        lax.all_gather(sh_up, "dp", axis=1, tiled=True),
        lax.all_gather(sh_down, "dp", axis=0, tiled=True),
    )
    expert_gate, expert_up, expert_down = (
        lax.all_gather(exp_gate[0], "dp", axis=0, tiled=True),
        lax.all_gather(exp_up[0], "dp", axis=0, tiled=True),
        lax.all_gather(exp_down[0], "dp", axis=1, tiled=True),
    )

    route_ids = routes[0]
    flat_ids = route_ids.reshape(-1)
    order = priority[0, 0]
    earlier = (flat_ids[:, None] == flat_ids[None, :]) & (order[None, :] < order[:, None])
    ranks = jnp.sum(earlier.astype(jnp.int32), axis=1).reshape(route_ids.shape)
    expert_grid = jnp.arange(experts_total, dtype=jnp.int32)
    route_hits = route_ids[None, :, :] == expert_grid[:, None, None]
    code = jnp.sum(jnp.where(route_hits, ranks[None] + 1, 0), axis=2) - 1
    code_all = lax.all_gather(code, "ctx", axis=0)

    stored_to_place = blocks[0]
    block_count = stored_to_place.shape[0]
    block_grid = jnp.arange(block_count, dtype=jnp.int32)
    place_to_stored = jnp.sum(
        jnp.where(stored_to_place[None, :] == block_grid[:, None], block_grid[None, :], 0), axis=1
    )
    cosine, sine = rope_tables(jnp.arange(group_len, dtype=jnp.int32))
    my_heads = (ctx_index // repeat) * width
    x_sorted = take_blocks(x_all, place_to_stored).astype(full)
    scale_sorted = rms_scale(x_sorted)
    normed_sorted = (x_sorted * scale_sorted * gain_one).astype(low)
    bias = lax.dynamic_slice_in_dim(small_all[1:4], my_heads, width, 1)
    head_shape = (group_len, heads, HEAD_DIM)
    projected = dot(normed_sorted, w_qkv)

    def part(index):
        return projected[:, index * width : (index + 1) * width] + bias[index : index + 1]

    query = rotate(part(0).reshape(head_shape), cosine, sine).reshape(group_len, width).astype(low)
    key = rotate(part(1).reshape(head_shape), cosine, sine).reshape(group_len, width).astype(low)
    value = part(2).astype(low)
    attended_heads, lse = attention_forward(query, key, value.T)
    attended_parts = swap_ctx(
        take_blocks(attended_heads, stored_to_place).reshape(ctx_count, tok_count, width)
    )[::repeat]
    attended = attended_parts.transpose(1, 0, 2).reshape(tok_count, D)
    first_sum = tokens + dot(attended, out_full)
    scale_two = rms_scale(first_sum)
    normed_two = (first_sum * scale_two * gain_two).astype(low)
    all_normed = gather_ctx(normed_two)

    logits_all = dot_nt(all_normed, mix_router)
    mix_all = jax.nn.sigmoid(logits_all[:, 0:1])
    chosen = code_all.transpose(0, 2, 1).reshape(group_len, experts_total) >= 0
    masked = jnp.where(chosen, logits_all[:, 1:], masked_score)
    raised = jnp.where(chosen, jnp.exp(masked - jnp.max(masked, axis=1, keepdims=True)), 0.0)
    gates_all = raised / jnp.sum(raised, axis=1, keepdims=True)
    is_mine = (expert_grid == ctx_index).astype(full)
    gate_mine = jnp.sum(gates_all * is_mine[None, :], axis=1).reshape(ctx_count, tok_count)
    code_mine = lax.dynamic_index_in_dim(code_all, ctx_index, 1, keepdims=False)
    slot_grid = jnp.arange(capacity, dtype=jnp.int32)
    hits = code_mine[:, None, :] == slot_grid[None, :, None]
    table = hits.astype(low)
    gated_table = jnp.where(hits, gate_mine[:, None, :], 0.0)
    slot_gates = jnp.sum(gated_table, axis=2)
    grouped = (ctx_count, tok_count, D)
    slots = ctx_count * capacity
    expert_rows = ein("crt,ctd->crd", table, all_normed.reshape(grouped)).astype(low)
    expert_rows = expert_rows.reshape(slots, D)
    slot_grads = (
        ein("crt,ctd->crd", table, cot_all.reshape(grouped)) * slot_gates[:, :, None]
    ).astype(low)
    slot_grads = slot_grads.reshape(slots, D)

    shared_g = dot(all_normed, shared_gate)
    shared_u = dot(all_normed, shared_up)
    shared_silu, shared_slope = silu_parts(shared_g)
    shared_low = (shared_silu * shared_u).astype(low)
    mix_cot = (mix_all * cot_all.astype(full)).astype(low)
    shared_hidden = dot_nt(mix_cot, shared_down)
    shared_dg = (shared_hidden * shared_u * shared_slope).astype(low)
    shared_du = (shared_hidden * shared_silu).astype(low)
    mix_share = jnp.sum(shared_hidden * shared_silu * shared_u, axis=1)
    grad_sgate = ein("td,tf->df", all_normed, shared_dg)
    grad_sup = ein("td,tf->df", all_normed, shared_du)
    grad_sdown = ein("tf,td->fd", shared_low, mix_cot)

    gate_act = dot(expert_rows, expert_gate)
    up_act = dot(expert_rows, expert_up)
    gate_silu, gate_slope = silu_parts(gate_act)
    hidden_low = (gate_silu * up_act).astype(low)
    hidden_grad = dot_nt(slot_grads, expert_down)
    gate_grad = (hidden_grad * up_act * gate_slope).astype(low)
    up_grad = (hidden_grad * gate_silu).astype(low)
    gate_share = jnp.sum(hidden_grad * gate_silu * up_act, axis=1).reshape(ctx_count, capacity)
    expert_dx = (dot_nt(gate_grad, expert_gate) + dot_nt(up_grad, expert_up)).astype(low)
    partial_dx = (
        dot_nt(shared_dg, shared_gate)
        + dot_nt(shared_du, shared_up)
        + ein("crt,crd->ctd", table, expert_dx.reshape(ctx_count, capacity, D)).reshape(
            group_len, D
        )
    )
    dx_mine = scatter_ctx(partial_dx.astype(low)).astype(full)
    expert_out = dot(hidden_low, expert_down).astype(low)
    partial_out = mix_all * dot(shared_low, shared_down) + ein(
        "crt,crd->ctd", gated_table.astype(low), expert_out.reshape(ctx_count, capacity, D)
    ).reshape(group_len, D)
    layer_out = first_sum + scatter_ctx(partial_out.astype(low)).astype(full)
    grad_edown = ein("rf,rd->fd", hidden_low, slot_grads)
    grad_egate = ein("rd,rf->df", expert_rows, gate_grad)
    grad_eup = ein("rd,rf->df", expert_rows, up_grad)

    share_of_token = jnp.sum(jnp.where(hits, gate_share[:, :, None], 0.0), axis=1)
    shares = swap_ctx(jnp.stack([share_of_token, mix_share.reshape(ctx_count, tok_count)], axis=1))
    gates_mine = lax.dynamic_slice_in_dim(gates_all, ctx_index * tok_count, tok_count)
    mix_mine = lax.dynamic_slice_in_dim(mix_all, ctx_index * tok_count, tok_count)
    gate_shares = shares[:, 0].T
    mix_grad = jnp.sum(shares[:, 1], axis=0)[:, None] * (1.0 - mix_mine)
    logit_grad = gate_shares - gates_mine * jnp.sum(gate_shares, axis=1, keepdims=True)
    narrow_grad = jnp.concatenate([mix_grad, logit_grad], axis=1)
    narrow_low = logit_grad.astype(low)
    grad_narrow = jnp.concatenate(
        [
            jnp.sum(mix_grad * normed_two.astype(full), axis=0, keepdims=True),
            ein("te,td->ed", narrow_low, normed_two),
        ],
        axis=0,
    )
    normed_grad = dx_mine + mix_grad * mix_row + dot(narrow_low, mix_router[1:])
    norm_grad_two, grad_gain_two = norm_back(first_sum, scale_two, gain_two, normed_grad)
    first_grad = cot_full + norm_grad_two
    first_low = first_grad.astype(low)
    attended_grad = dot_nt(first_low, out_full).astype(low)
    grad_out = ein("td,te->de", attended, first_low)

    upstream_parts = attended_grad.reshape(tok_count, head_sets, width).transpose(1, 0, 2)
    if repeat > 1:
        upstream_parts = jnp.repeat(upstream_parts, repeat, axis=0)
    upstream = take_blocks(swap_ctx(upstream_parts).reshape(group_len, width), place_to_stored)
    delta = jnp.sum(
        (upstream.astype(full) * attended_heads.astype(full)).reshape(head_shape), axis=2
    ).T.reshape(heads, 1, group_len)
    query_grad, key_grad, value_grad = attention_backward(
        query, upstream, lse, delta, key, key.T, value
    )
    qkv_grad = jnp.concatenate(
        [
            rotate(query_grad.reshape(head_shape), cosine, -sine).reshape(group_len, width),
            rotate(key_grad.reshape(head_shape), cosine, -sine).reshape(group_len, width),
            value_grad,
        ],
        axis=1,
    ).astype(low)
    if repeat > 1:
        qkv_grad = jnp.where(ctx_index % repeat == 0, qkv_grad, jnp.zeros_like(qkv_grad))
    partial_one = dot_nt(qkv_grad, w_qkv).astype(low)
    grad_qkv = ein("td,te->de", normed_sorted, qkv_grad)
    bias_sums = jnp.sum(qkv_grad.astype(full), axis=0).reshape(3, width)
    grad_bias = lax.dynamic_update_slice_in_dim(
        jnp.zeros((3, D), full), bias_sums, my_heads, 1
    )
    dx_one = scatter_ctx(take_blocks(partial_one, stored_to_place)).astype(full)
    norm_grad_one, grad_gain_one = norm_back(tokens, rms_scale(tokens), gain_one, dx_one)
    input_grad = first_grad + norm_grad_one

    qkv_rows = lax.psum_scatter(
        grad_qkv.astype(low).reshape(dp_count, ctx_count, shard, 3 * width),
        "dp",
        scatter_dimension=0,
        tiled=True,
    )[0]
    qkv_mine = swap_ctx(qkv_rows)[::repeat].astype(full)
    qkv_mine = qkv_mine.reshape(head_sets, shard, 3, width).transpose(2, 1, 0, 3).reshape(3, shard, D)
    grad_wout = lax.psum_scatter(
        grad_out.astype(low), both, scatter_dimension=0, tiled=True
    ).astype(full)
    small_grads = lax.psum_scatter(
        jnp.concatenate([grad_gain_one[None], grad_bias, grad_gain_two[None], grad_narrow], axis=0).T,
        both,
        scatter_dimension=0,
        tiled=True,
    )

    def over_dp(grad, dim):
        return lax.psum_scatter(
            grad.astype(low), "dp", scatter_dimension=dim, tiled=True
        ).astype(full)

    return (
        layer_out.astype(low)[None],
        input_grad[None],
        small_grads[:, 0],
        qkv_mine[0],
        small_grads[:, 1],
        qkv_mine[1],
        small_grads[:, 2],
        qkv_mine[2],
        small_grads[:, 3],
        grad_wout,
        small_grads[:, 4],
        small_grads[:, 6:],
        over_dp(grad_egate, 0)[None],
        over_dp(grad_eup, 0)[None],
        over_dp(grad_edown, 1)[None],
        over_dp(grad_sgate, 1),
        over_dp(grad_sup, 1),
        over_dp(grad_sdown, 0),
        small_grads[:, 5],
    )


def solution(mesh):
    rows = P("dp", "ctx", None)
    flat = P(("dp", "ctx"))
    lines = P(("dp", "ctx"), None)
    columns = P(None, ("dp", "ctx"))
    deep = P("ctx", "dp", None)
    down = P("ctx", None, "dp")
    in_specs = (
        (rows, flat, lines, flat, lines, flat, lines, flat, lines, flat, lines)
        + (deep, deep, down, columns, columns, lines, flat)
        + (rows, rows, P("dp", None), rows)
    )
    out_specs = (
        (rows, rows, flat, lines, flat, lines, flat, lines, flat, lines, flat, lines)
        + (deep, deep, down, columns, columns, lines, flat)
    )
    return jax.shard_map(
        on_device, mesh=mesh, in_specs=in_specs, out_specs=out_specs, check_vma=False
    )
```

time: 3910 us -> 2330 us (0.60)
  waiting for transfers between devices: 2260 us -> 1170 us
  matrix products: 1050 us -> 607 us
  other arithmetic: 260 us -> 105 us
  Pallas kernels: 0 us -> 126 us
  between operations: 15.6 us -> 77.3 us
  blocking collectives: 129 us -> 71 us
    reduce_scatter x14 -> x11, waiting for transfers between devices: 1220 us -> 538 us  [the longest x6 183 us: over_dp(): lax.psum_scatter(grad.astype(low), 'dp', scatter_dimension=dim, tiled=True)]
    dot_general x150 -> x31, matrix products: 1050 us -> 607 us  [the longest x13 227 us: ein(): return jnp.einsum(spec, left, right, preferred_element_type=full)]
    all_gather x11 -> x8, waiting for transfers between devices: 602 us -> 400 us  [the longest x3 135 us: gather_ctx(): return lax.all_gather(values, 'ctx', axis=0, tiled=True)]
    all_to_all x4, waiting for transfers between devices: 221 us -> 49.2 us  [swap_ctx(): lax.all_to_all(values, 'ctx', split_axis=0, concat_axis=0, tiled=True)]
    convert_element_type x32 -> x9, other arithmetic: 150 us -> 14.6 us  [the longest x3 7.11 us: over_dp(): return lax.psum_scatter(grad.astype(low), 'dp', scatter_dimension=dim, ti...]
    pallas_call x0 -> x2, Pallas kernels: none -> 126 us  [the longest x1 65.7 us: attention_backward(): pl.pallas_call(backward_kernel, grid=(heads, rows // CONT), in_specs=[til...]
    unnamed x2 -> x0, blocking collectives: 86.8 us -> none
    gather x8 -> x0, local copies, waits for them, and re-layouts: 51.5 us -> none  [the longest x1 22.8 us: on_device(): picked = padded_out[slots].astype(jnp.float32)]
  transfers between devices with their start and end apart: 33 -> 27, of which waited for: 27 -> 16; matrix products, arithmetic and copies ran while one was open for 23% -> 32% of each run, Pallas kernels for 0% -> 5%
where the time goes in v1:
time: 2330 us; the launch traced here: 2320 us
  waiting for transfers between devices  1170 us (50%)
  matrix products  607 us (26%)
  local copies, waits for them, and re-layouts  144 us (6%)
  Pallas kernels  126 us (5%)
  other arithmetic  105 us (5%)
  between operations  77.3 us (3%)
  blocking collectives  71 us (3%)
    dot_general x13, matrix products, ein(): return jnp.einsum(spec, left, right, preferred_element_type=full)  227 us
    dot_general x9, matrix products, dot(): return jnp.dot(left, right, preferred_element_type=full)  195 us
    dot_general x9, matrix products, dot_nt(): lax.dot_general(left, right, (((1,), (1,)), ((), ())), preferred_element_...  185 us
    reduce_scatter x6, waiting for transfers between devices, over_dp(): lax.psum_scatter(grad.astype(low), 'dp', scatter_dimension=dim, tiled=True)  183 us
    reduce_scatter x3, waiting for transfers between devices, scatter_ctx(): return lax.psum_scatter(values, 'ctx', scatter_dimension=0, tiled=True)  160 us
    reduce_scatter x1, waiting for transfers between devices, on_device(): lax.psum_scatter(grad_out.astype(low), both, scatter_dimension=0, tiled=T...  135 us
    all_gather x3, waiting for transfers between devices, gather_ctx(): return lax.all_gather(values, 'ctx', axis=0, tiled=True)  135 us
    unnamed x24, waiting for transfers between devices  135 us
  transfers between devices with their start and end apart: 27, of which 16 were waited for; matrix products, arithmetic and copies ran while one was open for 32% of the time, Pallas kernels for 5%

profile of v1, /device:TPU:0, one launch (start us, length us, event | category | flops | bytes accessed | tf_op | source)
XLA Modules:
  0.0 2316.4 jit_solution(571968017494213254)
XLA Ops:
  11.3 21.4 all_to_all.25
  76.3 41.0 %all-gather.7 = bf16[32,14,64]{2,1,0:T(8,128)(2,1)S(1)} all-gather(bf16[1,14,64]{2,1,0:T(8,128)(2,1)S(1)} %bitcast.467), channel_id=3, replica_groups=mesh['dp'=4,'ctx'=8] {'dp','ctx'}, dimensions={0}, use_global_device_ids=true | all-gather | bytes 59136 | tf_op jit(solution)/shard_map/all_gather | solution.py:282
  117.5 4.7 fusion.52
  162.3 9.2 all-gather.20.cloned.1.call-done
  171.5 21.0 fusion.26
  192.5 9.9 fusion.70
  202.4 5.6 copy.150
  208.1 4.4 subtract_convert_fusion.2
  230.1 60.3 %attend_forward.1 = (bf16[4096,256]{1,0:T(8,128)(2,1)S(1)}, f32[2,1,4096]{2,1,0:T(1,128)S(1)}) custom-call(bf16[4096,256]{1,0:T(8,128)(2,1)S(1)} %copy.142.q_ref, bf16[4096,256]{1,0:T(8,128)(2,1)} %copy.122.k_ref, bf16[256,4096]{1,0:T(8,128)(2,1)} %copy.123.vt_ref), custom_call_target="tpu_custom_call" | custom-call | tf_op jit(solution)/shard_map/attend_forward/pallas_call | solution.py:123
  293.1 4.4 all-to-all-start.1
  297.6 26.5 %all-to-all-done.1 = bf16[8,512,256]{2,1,0:T(8,128)(2,1)} async-done(((bf16[8,512,256]{2,1,0:T(8,128)(2,1)}), bf16[8,512,256]{2,1,0:T(8,128)(2,1)}, u32[]{:S(2)}, u32[]{:S(2)}) %all-to-all-start.1) | async-done | bytes 2097184 | tf_op jit(solution)/shard_map/all_to_all | solution.py:218
  328.1 9.8 multiply_reduce_fusion.5
  350.9 8.6 all-gather.2
  359.5 70.1 %all-gather.24.cloned.1.call-done = bf16[4096,2048]{1,0:T(8,128)(2,1)} async-done(((bf16[512,2048]{1,0:T(8,128)(2,1)}), bf16[4096,2048]{1,0:T(8,128)(2,1)}) %all-gather.24.cloned.1.call-update) | async-done | bytes 16777232 | tf_op jit(solution)/shard_map/all_gather | solution.py:210
  429.6 10.2 fusion.79
  442.0 14.4 convolution_convert_fusion.6
  456.4 64.8 %all-gather.40.cloned.1.call-done = bf16[1,4096,2048]{2,1,0:T(8,128)(2,1)} async-done(((bf16[1,512,2048]{2,1,0:T(8,128)(2,1)}), bf16[1,4096,2048]{2,1,0:T(8,128)(2,1)}) %all-gather.40.cloned.1.call-update) | async-done | bytes 16777232 | tf_op jit(solution)/shard_map/all_gather | solution.py:210
  521.2 14.0 multiply_convert_fusion
  535.2 46.6 %all-gather.26.cloned.1.call-done = bf16[2048,704]{0,1:T(8,128)(2,1)} async-done(((bf16[2048,176]{0,1:T(8,128)(2,1)}), bf16[2048,704]{0,1:T(8,128)(2,1)}) %all-gather.26.cloned.1.call-update) | async-done | bytes 2883600 | tf_op jit(solution)/shard_map/all_gather | solution.py:292
  581.9 19.0 fusion.80
  600.8 88.0 %all-gather.34.cloned.1.call-done = bf16[1,2048,1408]{2,1,0:T(8,128)(2,1)} async-done(((bf16[1,512,1408]{2,1,0:T(8,128)(2,1)}), bf16[1,2048,1408]{2,1,0:T(8,128)(2,1)}) %all-gather.34.cloned.1.call-update) | async-done | bytes 5767184 | tf_op jit(solution)/shard_map/all_gather | solution.py:297
  688.9 22.7 fusion.20
  711.6 83.9 %all-gather.38.cloned.1.call-done = bf16[1,1408,2048]{2,1,0:T(8,128)(2,1)} async-done(((bf16[1,1408,512]{2,1,0:T(8,128)(2,1)}), bf16[1,1408,2048]{2,1,0:T(8,128)(2,1)}) %all-gather.38.cloned.1.call-update) | async-done | bytes 5767184 | tf_op jit(solution)/shard_map/all_gather | solution.py:299
  795.5 22.5 fusion.12
  818.0 84.1 %all-gather.36.cloned.1.call-done = bf16[1,2048,1408]{2,1,0:T(8,128)(2,1)} async-done(((bf16[1,512,1408]{2,1,0:T(8,128)(2,1)}), bf16[1,2048,1408]{2,1,0:T(8,128)(2,1)}) %all-gather.36.cloned.1.call-update) | async-done | bytes 5767184 | tf_op jit(solution)/shard_map/all_gather | solution.py:298
  902.1 35.7 %multiply_reduce_fusion = (f32[2560]{0:T(1024)}, bf16[2560,1408]{0,1:T(8,128)(2,1)}, bf16[2560,1408]{0,1:T(8,128)(2,1)}, bf16[2560,1408]{0,1:T(8,128)(2,1)}) fusion(f32[2560,1408]{0,1:T(8,128)} %fusion.12, f32[2560,1408]{0,1:T(8,128)} %fusion.20, bf16[2560,2048]{1,0:T(8,128)(2,1)} %bitcast.490, bf16[1,2048,1408]{2,1,0:T(8,128)(2,1)} %all-gather.36.cloned.1.call-done), kind=kOutput, calls=%fused_computation.15 | convolution fusion | flops 14825224192 | bytes 66725888 | tf_op jit(solution)/shard_map/dot_general | solution.py:26
  937.8 22.7 fusion.18
  960.4 26.3 %add_convert_fusion = bf16[2560,2048]{1,0:T(8,128)(2,1)} fusion(f32[2560,2048]{1,0:T(8,128)} %fusion.18, bf16[2560,1408]{0,1:T(8,128)(2,1)} %get-tuple-element.44, bf16[1,2048,1408]{2,1,0:T(8,128)(2,1)} %all-gather.36.cloned.1.call-done), kind=kOutput, calls=%fused_computation.11 | convolution fusion | flops 14774435840 | bytes 44433408 | tf_op jit(solution)/shard_map/dot_general | solution.py:30
  986.7 19.6 fusion.22
  1006.4 19.2 fusion.10
  1025.5 28.7 %multiply_reduce_fusion.1 = (f32[4096]{0:T(1024)}, bf16[4096,704]{0,1:T(8,128)(2,1)}, bf16[4096,704]{0,1:T(8,128)(2,1)}, bf16[4096,704]{0,1:T(8,128)(2,1)}) fusion(f32[4096,704]{0,1:T(8,128)} %fusion.10, f32[4096,704]{0,1:T(8,128)} %fusion.80, bf16[4096,2048]{1,0:T(8,128)(2,1)} %all-gather.24.cloned.1.call-done, ...), kind=kOutput, calls=%fused_computation.21 | convolution fusion | flops 11860176896 | bytes 60047360 | tf_op jit(solution)/shard_map/dot_general | solution.py:26
  1054.3 19.9 fusion.81
  1074.2 34.7 %fusion.4 = bf16[4096,2048]{1,0:T(8,128)(2,1)} fusion(f32[8,512,2048]{2,1,0:T(8,128)} %fusion.22, f32[4096,2048]{1,0:T(8,128)} %fusion.81, bf16[4096,704]{0,1:T(8,128)(2,1)} %get-tuple-element.46, bf16[2048,704]{0,1:T(8,128)(2,1)} %all-gather.28.cloned.1.call-done), kind=kOutput, calls=%fused_computation.8 | convolution fusion | flops 11836325888 | bytes 92536832 | tf_op jit(solution)/shard_map/dot_general | solution.py:30
  1109.0 23.2 %convolution_convert_fusion.1 = bf16[2560,2048]{1,0:T(8,128)(2,1)} fusion(bf16[2560,1408]{0,1:T(8,128)(2,1)} %get-tuple-element.45, bf16[1,1408,2048]{2,1,0:T(8,128)(2,1)} %all-gather.38.cloned.1.call-done), kind=kOutput, calls=%fused_computation.26 | convolution fusion | flops 14769192960 | bytes 23461888 | tf_op jit(solution)/shard_map/dot_general | solution.py:26
  1132.2 21.0 fusion.42
  1153.2 27.6 %fusion.5 = bf16[4096,2048]{1,0:T(8,128)(2,1)} fusion(f32[8,512,2048]{2,1,0:T(8,128)} %fusion.42, bf16[4096,704]{0,1:T(8,128)(2,1)} %get-tuple-element.47, bf16[704,2048]{1,0:T(8,128)(2,1)} %all-gather.30.cloned.1.call-done, f32[4096]{0:T(1024)S(1)} %bitcast.463), kind=kOutput, calls=%fused_computation.10 | convolution fusion | flops 11836325888 | bytes 58998784 | tf_op jit(solution)/shard_map/dot_general | solution.py:26
  1180.8 18.7 fusion.39
  1199.6 19.0 convolution_convert_fusion.8
  1218.7 18.6 convolution_convert_fusion.7
  1237.3 22.3 convolution_convert_fusion.2
  1266.5 22.5 convolution_convert_fusion.5
  1289.7 7.2 multiply_reduce_fusion.3
  1296.9 46.2 %reduce-scatter.15.cloned.1.call-done = bf16[512,2048]{1,0:T(8,128)(2,1)} async-done(((bf16[4096,2048]{1,0:T(8,128)(2,1)}), bf16[512,2048]{1,0:T(8,128)(2,1)}) %reduce-scatter.15.cloned.1.call-update) | async-done | bytes 2097168 | tf_op jit(solution)/shard_map/reduce_scatter | solution.py:214
  1343.1 6.5 convert_add_fusion.1
  1349.6 9.9 convolution_convert_fusion.9
  1369.3 22.7 all-to-all-done.3
  1410.7 6.0 reshape.379
  1416.7 9.5 reduce_sum.204
  1430.0 65.7 %attend_backward.1 = (f32[4096,256]{1,0:T(8,128)}, f32[4096,256]{1,0:T(8,128)}, f32[4096,256]{1,0:T(8,128)}) custom-call(bf16[4096,256]{1,0:T(8,128)(2,1)S(1)} %copy.142.q_ref, bf16[4096,256]{1,0:T(8,128)(2,1)S(1)} %copy-done.1, f32[2,1,4096]{2,1,0:T(1,128)S(1)} %get-tuple-element.25.lse_ref, f32[2,1,4096]{2,1,0:T(1,128)S(1)} %reshape.380.delta_ref, ...), custom_call_target="tpu_custom_call" | custom-call | tf_op jit(solution)/shard_map/attend_backward/pallas_call | solution.py:182
  1495.7 5.7 copy.147
  1503.8 6.4 copy.148
  1510.3 5.3 subtract_convert_fusion.1
  1528.1 20.8 fusion.36
  1549.0 22.1 convolution_convert_fusion.4
  1571.3 10.6 convolution_convert_fusion.3
  1582.0 19.6 convolution_convert_fusion
  1646.8 82.0 %reduce-scatter.25.cloned.1.call-done = bf16[512,1408]{1,0:T(8,128)(2,1)} async-done(((bf16[2048,1408]{1,0:T(8,128)(2,1)}), bf16[512,1408]{1,0:T(8,128)(2,1)}) %reduce-scatter.25.cloned.1.call-update) | async-done | bytes 1441808 | tf_op jit(solution)/shard_map/reduce_scatter | solution.py:477
  1732.0 60.0 %reduce-scatter.21.cloned.1.call-done = bf16[1,8,64,768]{3,2,1,0:T(8,128)(2,1)} async-done(((bf16[4,8,64,768]{3,2,1,0:T(8,128)(2,1)}), bf16[1,8,64,768]{3,2,1,0:T(8,128)(2,1)}) %reduce-scatter.21.cloned.1.call-update) | async-done | bytes 786448 | tf_op jit(solution)/shard_map/reduce_scatter | solution.py:458
  1795.9 100.5 %reduce-scatter.27.cloned.1.call-done = bf16[512,1408]{1,0:T(8,128)(2,1)} async-done(((bf16[2048,1408]{1,0:T(8,128)(2,1)}), bf16[512,1408]{1,0:T(8,128)(2,1)}) %reduce-scatter.27.cloned.1.call-update) | async-done | bytes 1441808 | tf_op jit(solution)/shard_map/reduce_scatter | solution.py:477
  1904.5 4.7 fusion.71
  1913.0 135.2 %reduce-scatter.23.cloned.1.call-done = bf16[64,2048]{1,0:T(8,128)(2,1)} async-done(((bf16[2048,2048]{1,0:T(8,128)(2,1)}), bf16[64,2048]{1,0:T(8,128)(2,1)}) %reduce-scatter.23.cloned.1.call-update) | async-done | bytes 262160 | tf_op jit(solution)/shard_map/reduce_scatter | solution.py:466
  2050.0 113.7 %reduce-scatter.19.cloned.1.call-done = bf16[512,2048]{1,0:T(8,128)(2,1)} async-done(((bf16[4096,2048]{1,0:T(8,128)(2,1)}), bf16[512,2048]{1,0:T(8,128)(2,1)}) %reduce-scatter.19.cloned.1.call-update) | async-done | bytes 2097168 | tf_op jit(solution)/shard_map/reduce_scatter | solution.py:214
  2168.4 6.0 fusion.30
  2174.5 128.9 %reduce-scatter.37.cloned.1.call-done = f32[64,14]{1,0:T(8,128)} async-done(((f32[2048,14]{1,0:T(8,128)}), f32[64,14]{1,0:T(8,128)}) %reduce-scatter.37.cloned.1.call-update) | async-done | bytes 3600
  (348 shorter events, 197.1 us)
Async XLA Ops:
  7.2 26.3 %copy-start.30 = (s32[1,16]{1,0:T(1,128)S(1)}, s32[1,16]{1,0:T(1,128)}, u32[]{:S(2)}) copy-start(s32[1,16]{1,0:T(1,128)} %param.42) | copy-start | bytes 196
  7.2 68.9 %copy-start.56 = (bf16[64]{0:T(256)(128)(2,1)S(1)}, bf16[64]{0:T(256)(128)(2,1)}, u32[]{:S(2)}) copy-start(bf16[64]{0:T(256)(128)(2,1)} %param.39) | copy-start | bytes 388
  7.2 68.9 %copy-start.50 = (bf16[64,8]{0,1:T(8,128)(2,1)S(1)}, bf16[64,8]{0,1:T(8,128)(2,1)}, u32[]{:S(2)}) copy-start(bf16[64,8]{0,1:T(8,128)(2,1)} %param.32) | copy-start | bytes 3076
  7.2 68.9 %copy-start.55 = (bf16[64]{0:T(256)(128)(2,1)S(1)}, bf16[64]{0:T(256)(128)(2,1)}, u32[]{:S(2)}) copy-start(bf16[64]{0:T(256)(128)(2,1)} %param.31) | copy-start | bytes 388
  7.2 68.9 %copy-start.54 = (bf16[64]{0:T(256)(128)(2,1)S(1)}, bf16[64]{0:T(256)(128)(2,1)}, u32[]{:S(2)}) copy-start(bf16[64]{0:T(256)(128)(2,1)} %param.29) | copy-start | bytes 388
  7.2 68.9 %copy-start.53 = (bf16[64]{0:T(256)(128)(2,1)S(1)}, bf16[64]{0:T(256)(128)(2,1)}, u32[]{:S(2)}) copy-start(bf16[64]{0:T(256)(128)(2,1)} %param.27) | copy-start | bytes 388
  7.3 68.9 %copy-start.52 = (bf16[64]{0:T(256)(128)(2,1)S(1)}, bf16[64]{0:T(256)(128)(2,1)}, u32[]{:S(2)}) copy-start(bf16[64]{0:T(256)(128)(2,1)} %param.25) | copy-start | bytes 388
  7.3 68.9 %copy-start.51 = (bf16[64]{0:T(256)(128)(2,1)S(1)}, bf16[64]{0:T(256)(128)(2,1)}, u32[]{:S(2)}) copy-start(bf16[64]{0:T(256)(128)(2,1)} %param.23) | copy-start | bytes 388
  7.3 136.5 %all-gather.32.cloned.1.call-start = ((), (), s32[]{:S(2)}) async-start(), calls=%async_computation.34 | async-start | bytes 18874368 | tf_op jit(solution)/shard_map/all_gather | solution.py:210
  8.0 163.5 %all-gather.20.cloned.1.call-start = ((), (), s32[]{:S(2)}) async-start(), calls=%async_computation.17 | async-start | bytes 3932160 | tf_op jit(solution)/shard_map/all_gather | solution.py:270
  32.7 295.4 %all-gather.22.cloned.1.call-start = ((), (), s32[]{:S(2)}) async-start(), calls=%async_computation.18 | async-start | bytes 8650752 | tf_op jit(solution)/shard_map/all_gather | solution.py:289
  117.3 229.1 %copy-start.22 = (bf16[32,14,64]{2,1,0:T(8,128)(2,1)}, bf16[32,14,64]{2,1,0:T(8,128)(2,1)S(1)}, u32[]{:S(2)}) copy-start(bf16[32,14,64]{2,1,0:T(8,128)(2,1)S(1)} %all-gather.7) | copy-start | bytes 172036
  122.2 85.8 %copy-start.11 = (f32[4096,64]{0,1:T(8,128)}, f32[4096,64]{0,1:T(8,128)S(1)}, u32[]{:S(2)}) copy-start(f32[4096,64]{0,1:T(8,128)S(1)} %get-tuple-element.80) | copy-start | bytes 3145732
  123.1 48.4 %copy-start.31 = (f32[2048]{0:T(1024)}, f32[2048]{0:T(1024)S(1)}, u32[]{:S(2)}) copy-start(f32[2048]{0:T(1024)S(1)} %mul.502) | copy-start | bytes 24580
  143.8 78.4 %copy-start.47 = (f32[1,256]{1,0:T(1,128)}, f32[1,256]{1,0:T(1,128)S(1)}, u32[]{:S(2)}) copy-start(f32[1,256]{1,0:T(1,128)S(1)} %get-tuple-element.75) | copy-start | bytes 3076
  143.8 11.7 copy-start.8
  156.4 5.8 copy-start.7
  162.3 30.2 %copy-start.43 = (f32[4096]{0:T(1024)}, f32[4096]{0:T(1024)S(1)}, u32[]{:S(2)}) copy-start(f32[4096]{0:T(1024)S(1)} %add_rsqrt_fusion) | copy-start | bytes 49156
  293.1 31.0 %all-to-all-start.1 = ((bf16[8,512,256]{2,1,0:T(8,128)(2,1)}), bf16[8,512,256]{2,1,0:T(8,128)(2,1)}, u32[]{:S(2)}, u32[]{:S(2)}) async-start(bf16[8,512,256]{2,1,0:T(8,128)(2,1)} %bitcast.426), calls=%async_computation.1 | async-start | bytes 4194304 | tf_op jit(solution)/shard_map/all_to_all | solution.py:218
  297.5 132.1 %all-gather.24.cloned.1.call-start = ((), (), s32[]{:S(2)}) async-start(), calls=%async_computation.19 | async-start | bytes 18874368 | tf_op jit(solution)/shard_map/all_gather | solution.py:210
  297.6 40.9 %copy-start.26 = (f32[2048]{0:T(1024)}, f32[2048]{0:T(1024)S(1)}, u32[]{:S(2)}) copy-start(f32[2048]{0:T(1024)S(1)} %mul.522) | copy-start | bytes 24580
  341.7 179.5 %all-gather.40.cloned.1.call-start = ((), (), s32[]{:S(2)}) async-start(), calls=%async_computation.38 | async-start | bytes 18874368 | tf_op jit(solution)/shard_map/all_gather | solution.py:210
  342.3 239.6 %all-gather.26.cloned.1.call-start = ((), (), s32[]{:S(2)}) async-start(), calls=%async_computation.20 | async-start | bytes 3604480 | tf_op jit(solution)/shard_map/all_gather | solution.py:292
  342.9 346.0 %all-gather.34.cloned.1.call-start = ((), (), s32[]{:S(2)}) async-start(), calls=%async_computation.35 | async-start | bytes 7208960 | tf_op jit(solution)/shard_map/all_gather | solution.py:297
  343.6 451.9 %all-gather.38.cloned.1.call-start = ((), (), s32[]{:S(2)}) async-start(), calls=%async_computation.37 | async-start | bytes 7208960 | tf_op jit(solution)/shard_map/all_gather | solution.py:299
  344.4 557.7 %all-gather.36.cloned.1.call-start = ((), (), s32[]{:S(2)}) async-start(), calls=%async_computation.36 | async-start | bytes 7208960 | tf_op jit(solution)/shard_map/all_gather | solution.py:298
  345.1 661.3 %all-gather.30.cloned.1.call-start = ((), (), s32[]{:S(2)}) async-start(), calls=%async_computation.22 | async-start | bytes 3604480 | tf_op jit(solution)/shard_map/all_gather | solution.py:294
  345.7 679.9 %all-gather.28.cloned.1.call-start = ((), (), s32[]{:S(2)}) async-start(), calls=%async_computation.21 | async-start | bytes 3604480 | tf_op jit(solution)/shard_map/all_gather | solution.py:293
  346.4 942.8 %reduce-scatter.17.cloned.1.call-start = ((), (), s32[]{:S(2)}) async-start(), calls=%async_computation.24 | async-start | bytes 18874368 | tf_op jit(solution)/shard_map/reduce_scatter | solution.py:214
  359.5 161.7 %copy-start.18 = (s32[8,1,512]{2,0,1:T(8,128)}, s32[8,1,512]{2,0,1:T(8,128)S(1)}, u32[]{:S(2)}) copy-start(s32[8,1,512]{2,0,1:T(8,128)S(1)} %copy.175) | copy-start | bytes 49156
  441.3 15.1 copy-start.24
  960.4 26.3 %copy-start.19 = (s32[8,1,512]{2,0,1:T(8,128)S(1)}, s32[8,1,512]{2,0,1:T(8,128)}, u32[]{:S(2)}) copy-start(s32[8,1,512]{2,0,1:T(8,128)} %copy-done.18) | copy-start | bytes 49156
  986.7 19.6 copy-start.38
  1025.5 28.7 %copy-start.57 = (bf16[2048,704]{0,1:T(8,128)(2,1)S(1)}, bf16[2048,704]{0,1:T(8,128)(2,1)}, u32[]{:S(2)}) copy-start(bf16[2048,704]{0,1:T(8,128)(2,1)} %all-gather.26.cloned.1.call-done) | copy-start | bytes 8650756
  1108.9 234.2 %reduce-scatter.15.cloned.1.call-start = ((), (), s32[]{:S(2)}) async-start(), calls=%async_computation.23 | async-start | bytes 18874368 | tf_op jit(solution)/shard_map/reduce_scatter | solution.py:214
  1109.0 23.2 %copy-start.20 = (s32[8,1,512]{2,0,1:T(8,128)S(1)}, s32[8,1,512]{2,0,1:T(8,128)}, u32[]{:S(2)}) copy-start(s32[8,1,512]{2,0,1:T(8,128)} %copy-done.18) | copy-start | bytes 49156
  1109.0 23.2 %copy-start.25 = (f32[8,512]{1,0:T(8,128)S(1)}, f32[8,512]{1,0:T(8,128)}, u32[]{:S(2)}) copy-start(f32[8,512]{1,0:T(8,128)} %copy-done.24) | copy-start | bytes 49156
  1180.8 455.5 %reduce-scatter.35.cloned.1.call-start = ((), (), s32[]{:S(2)}) async-start(), calls=%async_computation.33 | async-start | bytes 3604480 | tf_op jit(solution)/shard_map/reduce_scatter | solution.py:477
  1199.5 439.1 %reduce-scatter.31.cloned.1.call-start = ((), (), s32[]{:S(2)}) async-start(), calls=%async_computation.31 | async-start | bytes 3604480 | tf_op jit(solution)/shard_map/reduce_scatter | solution.py:477
  1218.6 422.4 %reduce-scatter.33.cloned.1.call-start = ((), (), s32[]{:S(2)}) async-start(), calls=%async_computation.32 | async-start | bytes 3604480 | tf_op jit(solution)/shard_map/reduce_scatter | solution.py:477
  1237.3 406.1 %reduce-scatter.29.cloned.1.call-start = ((), (), s32[]{:S(2)}) async-start(), calls=%async_computation.30 | async-start | bytes 7208960 | tf_op jit(solution)/shard_map/reduce_scatter | solution.py:477
  1262.7 26.4 %all-to-all-start.2 = ((f32[8,2,512]{2,1,0:T(2,128)}), f32[8,2,512]{2,1,0:T(2,128)S(1)}, u32[]{:S(2)}, u32[]{:S(2)}) async-start(f32[8,2,512]{2,1,0:T(2,128)} %pad_maximum_fusion.6), calls=%async_computation.4 | async-start | bytes 65536 | tf_op jit(solution)/shard_map/all_to_all | solution.py:218
  1266.4 462.4 %reduce-scatter.25.cloned.1.call-start = ((), (), s32[]{:S(2)}) async-start(), calls=%async_computation.28 | async-start | bytes 7208960 | tf_op jit(solution)/shard_map/reduce_scatter | solution.py:477
  1289.1 7.8 copy-start.28
  1289.1 7.8 copy-start.41
  1289.1 7.7 copy-start.39
  1289.7 53.4 %copy-start.49 = (f32[512]{0:T(512)S(1)}, f32[512]{0:T(512)}, u32[]{:S(2)}) copy-start(f32[512]{0:T(512)} %get-tuple-element.83) | copy-start | bytes 6148
  1349.6 9.9 copy-start.10
  1359.5 5.9 copy-start.48
  1361.0 31.0 %all-to-all-start.3 = ((bf16[8,512,256]{2,1,0:T(8,128)(2,1)}), bf16[8,512,256]{2,1,0:T(8,128)(2,1)}, u32[]{:S(2)}, u32[]{:S(2)}) async-start(bf16[8,512,256]{2,1,0:T(8,128)(2,1)} %bitcast.419), calls=%async_computation.5 | async-start | bytes 4194304 | tf_op jit(solution)/shard_map/all_to_all | solution.py:218
  1365.3 426.6 %reduce-scatter.21.cloned.1.call-start = ((), (), s32[]{:S(2)}) async-start(), calls=%async_computation.26 | async-start | bytes 3932160 | tf_op jit(solution)/shard_map/reduce_scatter | solution.py:458
  1392.0 14.9 copy-start.3
  1503.8 78.2 %copy-start.13 = (bf16[4096,256]{1,0:T(8,128)(2,1)}, bf16[4096,256]{1,0:T(8,128)(2,1)S(1)}, u32[]{:S(2)}) copy-start(bf16[4096,256]{1,0:T(8,128)(2,1)S(1)} %convert.46) | copy-start | bytes 6291460
  1503.8 6.5 copy-start.12
  1515.6 5.6 copy-start.16
  1521.2 6.8 copy-start.32
  1521.2 6.8 copy-start.44
  1548.9 347.5 %reduce-scatter.27.cloned.1.call-start = ((), (), s32[]{:S(2)}) async-start(), calls=%async_computation.29 | async-start | bytes 7208960 | tf_op jit(solution)/shard_map/reduce_scatter | solution.py:477
  1571.1 477.1 %reduce-scatter.23.cloned.1.call-start = ((), (), s32[]{:S(2)}) async-start(), calls=%async_computation.27 | async-start | bytes 8650752 | tf_op jit(solution)/shard_map/reduce_scatter | solution.py:466
  1581.9 581.7 %reduce-scatter.19.cloned.1.call-start = ((), (), s32[]{:S(2)}) async-start(), calls=%async_computation.25 | async-start | bytes 18874368 | tf_op jit(solution)/shard_map/reduce_scatter | solution.py:214
  1601.6 20.2 copy-start.9
  1792.0 110.7 %all-to-all-start.4 = ((bf16[8,64,768]{2,1,0:T(8,128)(2,1)}), bf16[8,64,768]{2,1,0:T(8,128)(2,1)S(1)}, u32[]{:S(2)}, u32[]{:S(2)}) async-start(bf16[8,64,768]{2,1,0:T(8,128)(2,1)} %bitcast.444), calls=%async_computation.8 | async-start | bytes 1572864 | tf_op jit(solution)/shard_map/all_to_all | solution.py:218
  1795.6 507.7 %reduce-scatter.37.cloned.1.call-start = ((), (), s32[]{:S(2)}) async-start(), calls=%async_computation.39 | async-start | bytes 1081344
  1909.5 257.3 %copy-start.37 = (f32[2048]{0:T(1024)S(1)}, f32[2048]{0:T(1024)}, u32[]{:S(2)}) copy-start(f32[2048]{0:T(1024)} %get-tuple-element.29) | copy-start | bytes 24580
  (22 other events, 48.9 us)
Sparse Core Ops, SparseCore 0:
  10.0 96.2 all-gather.31
  107.9 63.5 all-gather.19
  174.4 76.1 all-gather.21
  341.8 87.7 all-gather.23
  431.3 89.8 all-gather.39
  522.6 59.1 all-gather.25
  583.4 105.3 all-gather.33
  690.4 104.9 all-gather.37
  797.0 104.9 all-gather.35
  903.5 57.4 all-gather.29
  962.6 57.8 all-gather.27
  1109.0 114.0 reduce-scatter.16
  1226.7 116.3 reduce-scatter.14
  1345.8 56.1 reduce-scatter.34
  1404.7 56.0 reduce-scatter.30
  1463.5 56.0 reduce-scatter.32
  1521.8 102.0 reduce-scatter.28
  1626.0 102.7 reduce-scatter.24
  1731.1 60.7 reduce-scatter.20
  1794.1 102.2 reduce-scatter.26
  1898.7 149.4 reduce-scatter.22
  2051.8 111.8 reduce-scatter.18
  2168.5 134.7 reduce-scatter.36

commit v2 on v1

v2 whole, which is shorter than its diff:
```python
import functools

import jax
import jax.numpy as jnp
from jax import lax
from jax.experimental import pallas as pl
from jax.experimental.pallas import tpu as pltpu
from jax.sharding import PartitionSpec as P

D = 2048
HEADS = 16
HEAD_DIM = 128
TOP_K = 4
CONT = 256
PROMPT = 2048

rope_base = 1000000.0
epsilon = 1e-06
masked_score = -1e30
log2_e = 1.4426950408889634
low = jnp.bfloat16
full = jnp.float32


def dot(left, right):
    return jnp.dot(left, right, preferred_element_type=full)


def dot_nt(left, right):
    return lax.dot_general(left, right, (((1,), (1,)), ((), ())), preferred_element_type=full)


def ein(spec, left, right):
    return jnp.einsum(spec, left, right, preferred_element_type=full)


def rotate(values, cosine, sine):
    middle = values.shape[-1] // 2
    leading = values[..., :middle]
    trailing = values[..., middle:]
    return jnp.concatenate(
        [leading * cosine - trailing * sine, trailing * cosine + leading * sine], axis=-1
    )


def rope_tables(places):
    turned = jnp.where(places < PROMPT, places, PROMPT + (places - PROMPT) % CONT)
    frequency = rope_base ** (-2.0 * jnp.arange(HEAD_DIM // 2, dtype=full) / HEAD_DIM)
    angles = turned.astype(full)[:, None] * frequency[None, :]
    return (jnp.cos(angles)[:, None, :], jnp.sin(angles)[:, None, :])


def rms_scale(values):
    return lax.rsqrt(jnp.mean(values * values, axis=-1, keepdims=True) + epsilon)


def norm_back(values, scale_rows, gain_row, upstream):
    weighted = upstream * gain_row
    grad_gain = jnp.sum(upstream * values * scale_rows, axis=0)
    grad_values = scale_rows * weighted - values * scale_rows**3 * jnp.mean(
        weighted * values, axis=-1, keepdims=True
    )
    return (grad_values, grad_gain)


def silu_parts(values):
    sig_value = jax.nn.sigmoid(values)
    return (values * sig_value, sig_value * (1.0 + values * (1.0 - sig_value)))


WIDE = 4


def attend_tiles(index, chunk, carry):
    whole = jnp.minimum(index, PROMPT // CONT)
    wide = whole // WIDE
    carry = lax.fori_loop(
        0, wide, lambda step, c: chunk(step * (WIDE * CONT), WIDE * CONT, False, c), carry
    )
    carry = lax.fori_loop(
        wide * WIDE, whole, lambda step, c: chunk(step * CONT, CONT, False, c), carry
    )
    return chunk(index * CONT, CONT, True, carry)


def turn(values, cosine, sine):
    half = HEAD_DIM // 2
    swapped = jnp.concatenate([values[:, half:], values[:, :half]], axis=1)
    return values * cosine + swapped * sine


def project_kernel(
    place_ref, x_ref, gain_ref, w_ref, bias_ref, cos_ref, sin_ref, normed_ref, q_ref, k_ref, v_ref
):
    values = x_ref[0].astype(full)
    scale = lax.rsqrt(jnp.mean(values * values, axis=1, keepdims=True) + epsilon)
    normed = (values * scale * gain_ref[...]).astype(low)
    normed_ref[...] = normed
    width = q_ref.shape[1]
    projected = dot(normed, w_ref[...]) + bias_ref[...]
    cosine, sine = cos_ref[...], sin_ref[...]
    for start in range(0, width, HEAD_DIM):
        for kind, out in ((0, q_ref), (1, k_ref)):
            column = kind * width + start
            head = projected[:, column : column + HEAD_DIM]
            out[:, start : start + HEAD_DIM] = turn(head, cosine, sine).astype(low)
    v_ref[...] = projected[:, 2 * width :].astype(low)


def project(x_blocks, places, gain, weight, bias, cosine, sine):
    count, rows, _ = x_blocks.shape
    width = weight.shape[1] // 3
    at_place = lambda g, place: (place[g], 0)
    whole = lambda g, place: (0, 0)
    tile = pl.BlockSpec((rows, width), at_place)
    head = jax.ShapeDtypeStruct((count * rows, width), low)
    return pl.pallas_call(
        project_kernel,
        grid_spec=pltpu.PrefetchScalarGridSpec(
            num_scalar_prefetch=1,
            grid=(count,),
            in_specs=[
                pl.BlockSpec((1, rows, D), lambda g, place: (g, 0, 0)),
                pl.BlockSpec((1, D), whole),
                pl.BlockSpec((D, 3 * width), whole),
                pl.BlockSpec((1, 3 * width), whole),
                pl.BlockSpec((rows, HEAD_DIM), at_place),
                pl.BlockSpec((rows, HEAD_DIM), at_place),
            ],
            out_specs=[pl.BlockSpec((rows, D), at_place), tile, tile, tile],
        ),
        out_shape=[jax.ShapeDtypeStruct((count * rows, D), low), head, head, head],
        compiler_params=pltpu.CompilerParams(vmem_limit_bytes=40 * 2**20),
        name="project",
    )(places, x_blocks, gain, weight, bias, cosine, sine)


def unproject_kernel(place_ref, dq_ref, dk_ref, dv_ref, w_ref, odd_ref, even_ref):
    step = pl.program_id(0)
    middle = pl.num_programs(0) // 2
    width = dq_ref.shape[1]
    total = dot_nt(dq_ref[...], w_ref[:, :width])
    total += dot_nt(dk_ref[...], w_ref[:, width : 2 * width])
    total += dot_nt(dv_ref[...], w_ref[:, 2 * width :])

    @pl.when(step < middle)
    def _():
        odd_ref[...] = total.astype(low)

    @pl.when(step >= middle)
    def _():
        even_ref[...] = total.astype(low)


def unproject(grads, places, weight, per_device):
    count = places.shape[0]
    rows = grads[0].shape[0] // count
    width = weight.shape[1] // 3
    middle = count // 2

    def block_of(g):
        return odd_first(g // per_device, count // per_device) * per_device + g % per_device

    tile = pl.BlockSpec((rows, width), lambda g, place: (place[block_of(g)], 0))
    shape = jax.ShapeDtypeStruct((middle * rows, D), low)
    return pl.pallas_call(
        unproject_kernel,
        grid_spec=pltpu.PrefetchScalarGridSpec(
            num_scalar_prefetch=1,
            grid=(count,),
            in_specs=[tile, tile, tile, pl.BlockSpec((D, 3 * width), lambda g, place: (0, 0))],
            out_specs=[
                pl.BlockSpec((rows, D), lambda g, place: (jnp.minimum(g, middle - 1), 0)),
                pl.BlockSpec((rows, D), lambda g, place: (jnp.maximum(g - middle, 0), 0)),
            ],
        ),
        out_shape=[shape, shape],
        compiler_params=pltpu.CompilerParams(vmem_limit_bytes=40 * 2**20),
        name="unproject",
    )(places, *grads, weight)


def dot_tn(left, right):
    return lax.dot_general(left, right, (((0,), (0,)), ((), ())), preferred_element_type=full)


def expert_kernel(
    normed_ref, cot_ref, code_ref, gate_ref, wg_ref, wu_ref, wd_ref,
    rows_ref, sg_ref, act_ref, dg_ref, du_ref, share_ref, dx_ref, out_ref,
):
    slots = rows_ref.shape[1]
    tok = normed_ref.shape[0]
    hits = code_ref[0] == lax.broadcasted_iota(jnp.int32, (slots, tok), 0)
    table_full = jnp.where(hits, 1.0, 0.0)
    gated = jnp.where(hits, gate_ref[0], 0.0)
    table = table_full.astype(low)
    rows = dot(table, normed_ref[...]).astype(low)
    rows_ref[0] = rows
    slot_gate = jnp.sum(gated, axis=1, keepdims=True)
    slot_grad = (dot(table, cot_ref[...]) * slot_gate).astype(low)
    sg_ref[0] = slot_grad
    gate = dot(rows, wg_ref[...])
    up = dot(rows, wu_ref[...])
    hidden = dot_nt(slot_grad, wd_ref[...])
    silu, slope = silu_parts(gate)
    act_full = silu * up
    act = act_full.astype(low)
    act_ref[0] = act
    dg = (hidden * up * slope).astype(low)
    du = (hidden * silu).astype(low)
    dg_ref[0] = dg
    du_ref[0] = du
    slot_share = jnp.sum(hidden * act_full, axis=1, keepdims=True)
    share_ref[0] = jnp.sum(table_full * slot_share, axis=0, keepdims=True)
    slot_dx = (dot_nt(dg, wg_ref[...]) + dot_nt(du, wu_ref[...])).astype(low)
    dx_ref[...] = dot_tn(table, slot_dx).astype(low)
    expert_y = dot(act, wd_ref[...]).astype(low)
    out_ref[...] = dot_tn(gated.astype(low), expert_y).astype(low)


def routed_expert(all_normed, cot_all, code, gate, w_gate, w_up, w_down, slots):
    count, tok = code.shape
    ff = w_gate.shape[1]
    chunk = pl.BlockSpec((tok, D), lambda m: (m, 0))
    line = pl.BlockSpec((1, 1, tok), lambda m: (m, 0, 0))

    def fixed(array):
        return pl.BlockSpec(array.shape, lambda m: (0, 0), pipeline_mode=pl.Buffered(1))

    def per_slot(last):
        return pl.BlockSpec((1, slots, last), lambda m: (m, 0, 0))

    def shape(*dims, dtype=low):
        return jax.ShapeDtypeStruct(dims, dtype)

    return pl.pallas_call(
        expert_kernel,
        grid=(count,),
        in_specs=[chunk, chunk, line, line, fixed(w_gate), fixed(w_up), fixed(w_down)],
        out_specs=[per_slot(D), per_slot(D), per_slot(ff), per_slot(ff), per_slot(ff), line, chunk, chunk],
        out_shape=[
            shape(count, slots, D),
            shape(count, slots, D),
            shape(count, slots, ff),
            shape(count, slots, ff),
            shape(count, slots, ff),
            shape(count, 1, tok, dtype=full),
            shape(count * tok, D),
            shape(count * tok, D),
        ],
        compiler_params=pltpu.CompilerParams(vmem_limit_bytes=60 * 2**20),
        name="routed_expert",
    )(all_normed, cot_all, code[:, None, :], gate[:, None, :], w_gate, w_up, w_down)


def shared_kernel(
    normed_ref, cot_ref, mix_ref, wg_ref, wu_ref, wd_ref, dxe_ref, oute_ref,
    mixcot_ref, act_ref, dg_ref, du_ref, share_ref, dx_odd, dx_even, out_odd, out_even,
):
    step = pl.program_id(0)
    middle = pl.num_programs(0) // 2
    normed = normed_ref[...]
    mix = mix_ref[...]
    mix_cot = (mix * cot_ref[...].astype(full)).astype(low)
    mixcot_ref[...] = mix_cot
    gate = dot_nt(normed, wg_ref[...])
    up = dot_nt(normed, wu_ref[...])
    hidden = dot_nt(mix_cot, wd_ref[...])
    silu, slope = silu_parts(gate)
    act_full = silu * up
    act = act_full.astype(low)
    act_ref[...] = act
    dg = (hidden * up * slope).astype(low)
    du = (hidden * silu).astype(low)
    dg_ref[...] = dg
    du_ref[...] = du
    share_ref[...] = jnp.sum(hidden * act_full, axis=1, keepdims=True)
    dx = dot(dg, wg_ref[...]) + dot(du, wu_ref[...]) + dxe_ref[...].astype(full)
    out = mix * dot(act, wd_ref[...]) + oute_ref[...].astype(full)

    @pl.when(step < middle)
    def _():
        dx_odd[...] = dx.astype(low)
        out_odd[...] = out.astype(low)

    @pl.when(step >= middle)
    def _():
        dx_even[...] = dx.astype(low)
        out_even[...] = out.astype(low)


def shared_expert(all_normed, cot_all, mix, w_gate_t, w_up_t, w_down, dx_routed, out_routed, tok):
    rows = all_normed.shape[0]
    ff = w_down.shape[0]
    count = rows // tok
    middle = count // 2
    chunk = pl.BlockSpec((tok, D), lambda g: (odd_first(g, count), 0))
    narrow = pl.BlockSpec((tok, ff), lambda g: (odd_first(g, count), 0))
    column = pl.BlockSpec((tok, 1), lambda g: (odd_first(g, count), 0))
    odd = pl.BlockSpec((tok, D), lambda g: (jnp.minimum(g, middle - 1), 0))
    even = pl.BlockSpec((tok, D), lambda g: (jnp.maximum(g - middle, 0), 0))
    fixed = pl.BlockSpec((ff, D), lambda g: (0, 0), pipeline_mode=pl.Buffered(1))
    narrow_shape = jax.ShapeDtypeStruct((rows, ff), low)
    half_shape = jax.ShapeDtypeStruct((rows // 2, D), low)
    return pl.pallas_call(
        shared_kernel,
        grid=(count,),
        in_specs=[chunk, chunk, column, fixed, fixed, fixed, chunk, chunk],
        out_specs=[chunk, narrow, narrow, narrow, column, odd, even, odd, even],
        out_shape=[
            jax.ShapeDtypeStruct((rows, D), low),
            narrow_shape,
            narrow_shape,
            narrow_shape,
            jax.ShapeDtypeStruct((rows, 1), full),
            half_shape,
            half_shape,
            half_shape,
            half_shape,
        ],
        compiler_params=pltpu.CompilerParams(vmem_limit_bytes=60 * 2**20),
        name="shared_expert",
    )(all_normed, cot_all, mix, w_gate_t, w_up_t, w_down, dx_routed, out_routed)


def forward_kernel(at_ref, q_ref, k_ref, vt_ref, o_ref, lse_ref):
    index = pl.program_id(1)
    query = q_ref[...]
    score_scale = HEAD_DIM ** (-0.5) * log2_e

    def chunk(start, size, diagonal, carry):
        highest, total, acc = carry
        start = pl.multiple_of(start, CONT)
        scores = dot_nt(k_ref[pl.ds(start, size), :], query) * score_scale
        if diagonal:
            keys = lax.broadcasted_iota(jnp.int32, scores.shape, 0)
            queries = lax.broadcasted_iota(jnp.int32, scores.shape, 1)
            scores = jnp.where(keys <= queries, scores, masked_score)
        newest = jnp.maximum(highest, jnp.max(scores, axis=0, keepdims=True))
        weights = jnp.exp2(scores - newest)
        shrink = jnp.exp2(highest - newest)
        total = total * shrink + jnp.sum(weights, axis=0, keepdims=True)
        acc = acc * shrink + dot(vt_ref[:, pl.ds(start, size)], weights.astype(low))
        return (newest, total, acc)

    highest, total, acc = attend_tiles(
        index,
        chunk,
        (
            jnp.full((1, CONT), masked_score, full),
            jnp.zeros((1, CONT), full),
            jnp.zeros((HEAD_DIM, CONT), full),
        ),
    )
    o_ref[...] = (acc / total).T.astype(low)
    lse_ref[...] = (highest + jnp.log2(total))[None]


def attention_forward(query, key, value_t, at):
    rows, width = query.shape
    heads = width // HEAD_DIM
    return pl.pallas_call(
        forward_kernel,
        grid_spec=pltpu.PrefetchScalarGridSpec(
            num_scalar_prefetch=1,
            grid=(heads, rows // CONT),
            in_specs=[
                pl.BlockSpec((CONT, HEAD_DIM), lambda h, i, at: (i, h)),
                pl.BlockSpec((rows, HEAD_DIM), lambda h, i, at: (0, h)),
                pl.BlockSpec((HEAD_DIM, rows), lambda h, i, at: (h, 0)),
            ],
            out_specs=[
                pl.BlockSpec((CONT, HEAD_DIM), lambda h, i, at: (at[i], h)),
                pl.BlockSpec((1, 1, CONT), lambda h, i, at: (h, 0, i)),
            ],
        ),
        out_shape=[
            jax.ShapeDtypeStruct((rows, width), low),
            jax.ShapeDtypeStruct((heads, 1, rows), full),
        ],
        compiler_params=pltpu.CompilerParams(vmem_limit_bytes=48 * 2**20),
        name="attend_forward",
    )(at, query, key, value_t)


def backward_kernel(
    at_ref, q_ref, do_ref, o_ref, lse_ref, k_ref, kt_ref, v_ref, cos_ref, sin_ref,
    dq_ref, dk_ref, dv_ref, dk_sum, dv_sum,
):
    index = pl.program_id(1)
    query = q_ref[...]
    upstream = do_ref[...]
    lse = lse_ref[0]
    product = upstream.astype(full) * o_ref[...].astype(full)
    delta = jnp.sum(product.T, axis=0, keepdims=True)
    scale = HEAD_DIM ** (-0.5)
    span_now = pl.ds(pl.multiple_of(index * CONT, CONT), CONT)

    @pl.when(index == 0)
    def _():
        dk_sum[...] = jnp.zeros_like(dk_sum)
        dv_sum[...] = jnp.zeros_like(dv_sum)

    def chunk(start, size, diagonal, acc):
        start = pl.multiple_of(start, CONT)
        span = pl.ds(start, size)
        scores = dot_nt(k_ref[span, :], query) * (scale * log2_e) - lse
        if diagonal:
            keys = lax.broadcasted_iota(jnp.int32, scores.shape, 0)
            queries = lax.broadcasted_iota(jnp.int32, scores.shape, 1)
            scores = jnp.where(keys <= queries, scores, masked_score)
        probs = jnp.exp2(scores)
        prob_grad = dot_nt(v_ref[span, :], upstream)
        score_grad = (probs * (prob_grad - delta)).astype(low)
        dv_sum[span, :] += dot(probs.astype(low), upstream)
        dk_sum[span, :] += dot(score_grad, query)
        return acc + dot(kt_ref[:, span], score_grad)

    acc = attend_tiles(index, chunk, jnp.zeros((HEAD_DIM, CONT), full))
    dq_ref[...] = turn(acc.T * scale, cos_ref[span_now, :], -sin_ref[span_now, :]).astype(low)

    @pl.when(index == pl.num_programs(1) - 1)
    def _():
        def finish(step, carry):
            span = pl.ds(pl.multiple_of(step * CONT, CONT), CONT)
            dk_ref[span, :] = turn(
                dk_sum[span, :] * scale, cos_ref[span, :], -sin_ref[span, :]
            ).astype(low)
            dv_ref[span, :] = dv_sum[span, :].astype(low)
            return carry

        lax.fori_loop(0, pl.num_programs(1), finish, 0)


def attention_backward(query, upstream, attended, lse, key, key_t, value, cosine, sine, at):
    rows, width = query.shape
    heads = width // HEAD_DIM
    tile = pl.BlockSpec((CONT, HEAD_DIM), lambda h, i, at: (i, h))
    stored = pl.BlockSpec((CONT, HEAD_DIM), lambda h, i, at: (at[i], h))
    whole = pl.BlockSpec((rows, HEAD_DIM), lambda h, i, at: (0, h))
    table = pl.BlockSpec((rows, HEAD_DIM), lambda h, i, at: (0, 0))
    grad = jax.ShapeDtypeStruct((rows, width), low)
    return pl.pallas_call(
        backward_kernel,
        grid_spec=pltpu.PrefetchScalarGridSpec(
            num_scalar_prefetch=1,
            grid=(heads, rows // CONT),
            in_specs=[
                tile,
                stored,
                stored,
                pl.BlockSpec((1, 1, CONT), lambda h, i, at: (h, 0, i)),
                whole,
                pl.BlockSpec((HEAD_DIM, rows), lambda h, i, at: (h, 0)),
                whole,
                table,
                table,
            ],
            out_specs=[tile, whole, whole],
            scratch_shapes=[
                pltpu.VMEM((rows, HEAD_DIM), full),
                pltpu.VMEM((rows, HEAD_DIM), full),
            ],
        ),
        out_shape=[grad, grad, grad],
        compiler_params=pltpu.CompilerParams(vmem_limit_bytes=48 * 2**20),
        name="attend_backward",
    )(at, query, upstream, attended, lse, key, key_t, value, cosine, sine)


def take_blocks(rows, order):
    count = order.shape[0]
    blocked = rows.reshape(count, rows.shape[0] // count, *rows.shape[1:])
    return jnp.concatenate(
        [lax.dynamic_index_in_dim(blocked, order[i], 0, keepdims=False) for i in range(count)], axis=0
    )


def bit_orders(count):
    bits = [1 << i for i in range(1, count.bit_length() - 1)]
    return bits, bits[::-1]


def exchange(values, bit, count):
    return lax.ppermute(values, "ctx", [(i, i ^ bit) for i in range(count)])


def gather_plan(count):
    plan = []
    orders = bit_orders(count)
    held = [[0], [0]]
    for depth in range(len(orders[0])):
        sends = [[(half, m, orders[half][depth]) for m in held[half]] for half in (0, 1)]
        plan += [send for pair in zip(*sends) for send in pair]
        for half in (0, 1):
            held[half] = held[half] + [m ^ orders[half][depth] for m in held[half]]
    return plan, [(half, m, 1) for m in held[0] for half in (0, 1)]


def gather_kernel(count, with_small, *refs):
    if with_small:
        x_ref, small_ref, out_ref, small_out, send_sems, recv_sems, own_sems = refs
    else:
        x_ref, out_ref, send_sems, recv_sems, own_sems = refs
    me = lax.axis_index("ctx")
    dp = lax.axis_index("dp")
    bits = bit_orders(count)[0] + [1]
    rows = x_ref.shape[0] // 2
    barrier = pltpu.get_barrier_semaphore()
    for bit in bits:
        pl.semaphore_signal(
            barrier, inc=1, device_id=(dp, me ^ bit), device_id_type=pl.DeviceIdType.MESH
        )
    pl.semaphore_wait(barrier, len(bits))
    spots = [out_ref.at[i] for i in range(2 * count)]
    if with_small:
        spots += [small_out.at[m] for m in range(count)]
    own = [x_ref.at[pl.ds(0, rows)], x_ref.at[pl.ds(rows, rows)]]
    local = [pltpu.make_async_copy(own[h], spots[h], own_sems.at[h]) for h in (0, 1)]
    if with_small:
        own.append(small_ref)
        local.append(pltpu.make_async_copy(small_ref, spots[2 * count], own_sems.at[2]))
    for copy in local:
        copy.start()

    def spot(half, m):
        return 2 * count + m if half == 2 else 2 * m + half

    copies = {}
    waited = set()

    def send(half, m, bit):
        if m and (half, m) not in waited:
            copies[(half, m)].wait_recv()
            waited.add((half, m))
        lands = spot(half, m ^ bit)
        copy = pltpu.make_async_remote_copy(
            src_ref=spots[spot(half, m)] if m else own[half],
            dst_ref=spots[lands],
            send_sem=send_sems.at[lands],
            recv_sem=recv_sems.at[lands],
            device_id=(dp, me ^ bit),
            device_id_type=pl.DeviceIdType.MESH,
        )
        copy.start()
        copies[(half, m ^ bit)] = copy

    far, near = gather_plan(count)
    if with_small:
        small_far = [(2, m, bit) for half, m, bit in far if half == 0]
        small_near = [(2, m, bit) for half, m, bit in near if half == 0]
        far, near = far + small_far, near + small_near
    done = set()
    for entry in far:
        send(*entry)
        for other in near:
            if other not in done and (other[1] == 0 or (other[0], other[1]) in waited):
                done.add(other)
                send(*other)
    for other in near:
        if other not in done:
            send(*other)
    for key, copy in copies.items():
        if key not in waited:
            copy.wait_recv()
    for copy in copies.values():
        copy.wait_send()
    for copy in local:
        copy.wait()


def gather_now(values, small=None, collective_id=0):
    count = lax.axis_size("ctx")
    rows, width = values.shape
    arrays = [values] if small is None else [values, small]
    shapes = [jax.ShapeDtypeStruct((2 * count, rows // 2, width), values.dtype)]
    places = 2 * count
    if small is not None:
        shapes.append(jax.ShapeDtypeStruct((count, *small.shape), small.dtype))
        places += count
    return pl.pallas_call(
        functools.partial(gather_kernel, count, small is not None),
        in_specs=[pl.BlockSpec(memory_space=pl.ANY)] * len(arrays),
        out_specs=[pl.BlockSpec(memory_space=pl.ANY)] * len(arrays),
        out_shape=shapes,
        scratch_shapes=[
            pltpu.SemaphoreType.DMA((places,)),
            pltpu.SemaphoreType.DMA((places,)),
            pltpu.SemaphoreType.DMA((3,)),
        ],
        compiler_params=pltpu.CompilerParams(
            collective_id=collective_id, has_side_effects=True, vmem_limit_bytes=4 * 2**20
        ),
        name="gather_rows",
    )(*arrays)


def split_rows(values, parts):
    rows = values.shape[0] // parts
    return [values[i * rows : (i + 1) * rows] for i in range(parts)]


def pin(arrays, *others):
    held = lax.optimization_barrier((tuple(arrays), *others))
    return (list(held[0]), *held[1:])


def gather_steps(values):
    count = lax.axis_size("ctx")
    orders = bit_orders(count)
    names, held = [[0], [0]], [[piece] for piece in split_rows(values, 2)]
    for depth in range(len(orders[0])):
        came = []
        for half in (0, 1):
            sent = jnp.concatenate(held[half], axis=0) if depth else held[half][0]
            came.append(exchange(sent, orders[half][depth], count))
        came = yield came
        for half in (0, 1):
            held[half] = held[half] + split_rows(came[half], len(held[half]))
            names[half] = names[half] + [m ^ orders[half][depth] for m in names[half]]
    halves = [dict(zip(names[half], held[half])) for half in (0, 1)]
    own = jnp.stack(
        [jnp.concatenate([half[m] for half in halves], axis=0) for m in range(0, count, 2)]
    )
    (other,) = yield [exchange(own, 1, count)]
    return jnp.stack([own, other], axis=1).reshape(count * values.shape[0], *values.shape[1:])


def add_low(left, right):
    return (left.astype(full) + right.astype(full)).astype(low)


def scatter_steps(odd, even):
    count = lax.axis_size("ctx")
    parts = count // 2
    (came,) = yield [exchange(odd, 1, count)]
    pairs = list(zip(split_rows(even, parts), split_rows(came, parts)))
    orders = bit_orders(count)
    held = [
        {
            2 * n: add_low(split_rows(left, 2)[half], split_rows(right, 2)[half])
            for n, (left, right) in enumerate(pairs)
        }
        for half in (0, 1)
    ]
    for depth in range(len(orders[0])):
        names, came = [], []
        for half in (0, 1):
            bit = orders[half][depth]
            names.append([m for m in held[half] if m & bit])
            sent = [held[half][m] for m in names[half]]
            sent = jnp.concatenate(sent, axis=0) if len(sent) > 1 else sent[0]
            came.append(exchange(sent, bit, count))
        came = yield came
        for half in (0, 1):
            bit = orders[half][depth]
            pieces = split_rows(came[half], len(names[half]))
            held[half] = {
                m ^ bit: add_low(held[half][m ^ bit], x) for m, x in zip(names[half], pieces)
            }
    return jnp.concatenate([half[0] for half in held], axis=0)


def advance(steps, came):
    try:
        return (steps.send(came), None)
    except StopIteration as stop:
        return (None, stop.value)


def finish(steps, came):
    value = None
    while value is None:
        came, value = advance(steps, came)
    return value


def odd_first(step, count):
    return lax.rem(2 * step + 1, count + 1)


def swap_ctx(values):
    return lax.all_to_all(values, "ctx", split_axis=0, concat_axis=0, tiled=True)


def on_device(
    hidden_in,
    in_gain,
    w_query,
    b_query,
    w_key,
    b_key,
    w_value,
    b_value,
    w_out,
    ffn_gain,
    w_router,
    exp_gate,
    exp_up,
    exp_down,
    sh_gate,
    sh_up,
    sh_down,
    sh_mix,
    routes,
    priority,
    blocks,
    cotangent,
):
    both = ("dp", "ctx")
    ctx_count = lax.axis_size("ctx")
    ctx_index = lax.axis_index("ctx")
    dp_count = lax.axis_size("dp")
    dp_index = lax.axis_index("dp")
    tokens_low = hidden_in[0]
    tokens = tokens_low.astype(full)
    cot_low = cotangent[0]
    cot_full = cotangent[0].astype(full)
    tok_count = tokens.shape[0]
    group_len = tok_count * ctx_count
    shard = w_query.shape[0]
    experts_total = ctx_count * exp_gate.shape[0]
    capacity = 5 * tok_count * TOP_K // (4 * experts_total)
    repeat = max(1, ctx_count // HEADS)
    heads = max(1, HEADS // ctx_count)
    width = heads * HEAD_DIM
    head_sets = HEADS // heads

    def by_heads(weight):
        parts = weight.reshape(shard, head_sets, width).transpose(1, 0, 2)
        return jnp.repeat(parts, repeat, axis=0) if repeat > 1 else parts

    qkv_parts = swap_ctx(
        jnp.concatenate([by_heads(w_query), by_heads(w_key), by_heads(w_value)], axis=2)
    )
    w_qkv = lax.all_gather(
        qkv_parts.reshape(ctx_count * shard, 3 * width), "dp", axis=0, tiled=True
    )
    partners = jnp.arange(ctx_count, dtype=jnp.int32) ^ ctx_index
    small = jnp.concatenate(
        [
            jnp.stack([in_gain, b_query, b_key, b_value, ffn_gain, sh_mix], axis=0),
            w_router.T,
        ],
        axis=0,
    ).astype(full)
    small_count = small.shape[0]
    small_rows = -(-dp_count * small_count * shard // HEAD_DIM // 8) * 8
    around = [small] + [
        lax.ppermute(small, "dp", [(i, (i + k) % dp_count) for i in range(dp_count)])
        for k in range(1, dp_count)
    ]
    origin = (dp_index - jnp.arange(dp_count, dtype=jnp.int32)) % dp_count
    small = jnp.take(jnp.stack(around), origin, axis=0).reshape(-1)
    small = jnp.pad(small, (0, small_rows * HEAD_DIM - small.shape[0])).reshape(small_rows, HEAD_DIM)
    x_blocks, small_all = gather_now(tokens_low, small, 0)
    small_all = small_all.reshape(ctx_count, -1)[:, : dp_count * small_count * shard]
    small_all = jnp.take(small_all, partners, axis=0)
    small_all = (
        small_all.reshape(ctx_count, dp_count, small_count, shard)
        .transpose(2, 1, 0, 3)
        .reshape(small_count, shard * dp_count * ctx_count)
    )
    gain_one, gain_two, mix_row = small_all[0:1], small_all[4:5], small_all[5:6]
    mix_router = small_all[5:].astype(low)
    w_out, qkv_parts = lax.optimization_barrier((w_out, qkv_parts))
    out_mine = lax.all_gather(w_out, "dp", axis=0, tiled=True)
    (cot_low, out_mine), x_blocks = pin([cot_low, out_mine], x_blocks)
    cot_steps, out_steps = gather_steps(cot_low), gather_steps(out_mine)
    came = next(cot_steps) + next(out_steps)
    shared_gate, shared_up, shared_down = (
        lax.all_gather(sh_gate.T, "dp", axis=0, tiled=True),
        lax.all_gather(sh_up.T, "dp", axis=0, tiled=True),
        lax.all_gather(sh_down, "dp", axis=0, tiled=True),
    )
    expert_gate, expert_up, expert_down = (
        lax.all_gather(exp_gate[0], "dp", axis=0, tiled=True),
        lax.all_gather(exp_up[0], "dp", axis=0, tiled=True),
        lax.all_gather(exp_down[0], "dp", axis=1, tiled=True),
    )

    route_ids = routes[0]
    flat_ids = route_ids.reshape(-1)
    order = priority[0, 0]
    earlier = (flat_ids[:, None] == flat_ids[None, :]) & (order[None, :] < order[:, None])
    ranks = jnp.sum(earlier.astype(jnp.int32), axis=1).reshape(route_ids.shape)
    expert_grid = jnp.arange(experts_total, dtype=jnp.int32)
    route_hits = route_ids[None, :, :] == expert_grid[:, None, None]
    code = jnp.sum(jnp.where(route_hits, ranks[None] + 1, 0), axis=2) - 1

    stored_to_place = blocks[0]
    block_count = stored_to_place.shape[0]
    block_grid = jnp.arange(block_count, dtype=jnp.int32)
    place_to_stored = jnp.sum(
        jnp.where(stored_to_place[None, :] == block_grid[:, None], block_grid[None, :], 0), axis=1
    )
    per_device = block_count // ctx_count
    near = partners * per_device
    stored_near = jnp.concatenate(
        [
            lax.dynamic_slice_in_dim(stored_to_place, near[m], per_device)
            for m in range(ctx_count)
        ]
    )
    place_to_near = (place_to_stored // per_device ^ ctx_index) * per_device + (
        place_to_stored % per_device
    )
    cosine, sine = rope_tables(jnp.arange(group_len, dtype=jnp.int32))
    my_heads = (ctx_index // repeat) * width
    scale_one = rms_scale(tokens)
    bias = lax.dynamic_slice_in_dim(small_all[1:4], my_heads, width, 1).reshape(1, 3 * width)
    cosine_wide = jnp.concatenate([cosine[:, 0], cosine[:, 0]], axis=1)
    sine_wide = jnp.concatenate([-sine[:, 0], sine[:, 0]], axis=1)
    normed_sorted, query, key, value = project(
        x_blocks, stored_near, gain_one, w_qkv, bias, cosine_wide, sine_wide
    )
    tiles = group_len // CONT
    direct = block_count == tiles
    at = place_to_stored if direct else jnp.arange(tiles, dtype=jnp.int32)
    (*came, value), query = pin([*came, value], query)
    cot_came, cot_all = advance(cot_steps, came[:2])
    out_came, out_parts = advance(out_steps, came[2:])
    came = cot_came + out_came
    attended_heads, lse = attention_forward(query, key, value.T, at)
    came, attended_heads = pin(came, attended_heads)
    split = len(came) // 2
    attended_stored = attended_heads if direct else take_blocks(attended_heads, stored_to_place)
    attended_parts = swap_ctx(attended_stored.reshape(ctx_count, tok_count, width))[::repeat]
    out_parts = finish(out_steps, came[split:])
    cot_all = finish(cot_steps, came[:split])
    out_parts = out_parts.reshape(ctx_count, dp_count, shard, D)
    out_full = (
        jnp.stack(
            [lax.dynamic_index_in_dim(out_parts, partners[i], 0, False) for i in range(ctx_count)],
            axis=1,
        )
    ).reshape(D, D)
    attended = attended_parts.transpose(1, 0, 2).reshape(tok_count, D)
    first_sum = tokens + dot(attended, out_full)
    scale_two = rms_scale(first_sum)
    normed_two = (first_sum * scale_two * gain_two).astype(low)
    logits = dot_nt(normed_two, mix_router)
    mix_mine = jax.nn.sigmoid(logits[:, 0:1])
    chosen = code.T >= 0
    masked = jnp.where(chosen, logits[:, 1:], masked_score)
    raised = jnp.where(chosen, jnp.exp(masked - jnp.max(masked, axis=1, keepdims=True)), 0.0)
    gates_mine = raised / jnp.sum(raised, axis=1, keepdims=True)
    narrow = jnp.concatenate([mix_mine.T, gates_mine.T, code.astype(full)], axis=0)
    narrow = jnp.pad(narrow, ((0, -narrow.shape[0] % 8), (0, 0)))
    all_normed, narrow_all = gather_now(normed_two, narrow, 1)
    all_normed = all_normed.reshape(group_len, D)
    mix_all = narrow_all[:, 0].reshape(group_len, 1)
    gate_mine = lax.dynamic_index_in_dim(narrow_all, ctx_index + 1, 1, keepdims=False)
    code_mine = lax.dynamic_index_in_dim(
        narrow_all, ctx_index + 1 + experts_total, 1, keepdims=False
    ).astype(jnp.int32)
    code_mine = jnp.where(code_mine < capacity, code_mine, -1)
    slot_rows = -(-capacity // 32) * 32
    expert_rows, slot_grads, hidden_low, gate_grad, up_grad, gate_share, dx_routed, out_routed = (
        routed_expert(
            all_normed, cot_all, code_mine, gate_mine, expert_gate, expert_up, expert_down, slot_rows
        )
    )
    grad_egate = ein("crd,crf->df", expert_rows, gate_grad).astype(low)
    dx_routed, grad_egate = lax.optimization_barrier((dx_routed, grad_egate))
    mix_cot, shared_low, shared_dg, shared_du, mix_share, dx_odd, dx_even, out_odd, out_even = (
        shared_expert(
            all_normed, cot_all, mix_all, shared_gate, shared_up, shared_down,
            dx_routed, out_routed, tok_count,
        )
    )
    dx_steps = scatter_steps(dx_odd, dx_even)
    came = next(dx_steps)
    grad_eup = ein("crd,crf->df", expert_rows, up_grad).astype(low)
    came, grad_eup, hidden_low, shared_low, shared_dg, shared_du = pin(
        came, grad_eup, hidden_low, shared_low, shared_dg, shared_du
    )
    came, dx_mine = advance(dx_steps, came)
    grad_edown = ein("crf,crd->fd", hidden_low, slot_grads).astype(low)
    grad_sdown = ein("tf,td->fd", shared_low, mix_cot).astype(low)
    came, grad_edown, grad_sdown, shared_dg, shared_du = pin(
        came, grad_edown, grad_sdown, shared_dg, shared_du
    )
    came, dx_mine = advance(dx_steps, came)
    grad_sgate = ein("tf,td->fd", shared_dg, all_normed).astype(low)
    grad_sup = ein("tf,td->fd", shared_du, all_normed).astype(low)
    came, grad_sgate, grad_sup = pin(came, grad_sgate, grad_sup)
    dx_mine = finish(dx_steps, came).astype(full)

    shares = jnp.stack([gate_share[:, 0], mix_share.reshape(ctx_count, tok_count)], axis=1)
    shares = swap_ctx(jnp.take(shares, partners, axis=0))
    gate_shares = shares[:, 0].T
    mix_grad = jnp.sum(shares[:, 1], axis=0)[:, None] * (1.0 - mix_mine)
    logit_grad = gate_shares - gates_mine * jnp.sum(gate_shares, axis=1, keepdims=True)
    narrow_low = logit_grad.astype(low)
    grad_narrow = jnp.concatenate(
        [
            jnp.sum(mix_grad * normed_two.astype(full), axis=0, keepdims=True),
            ein("te,td->ed", narrow_low, normed_two),
        ],
        axis=0,
    )
    (out_odd,), dx_mine = pin([out_odd], dx_mine)
    add_steps = scatter_steps(out_odd, out_even)
    came = next(add_steps)
    normed_grad = dx_mine + mix_grad * mix_row + dot(narrow_low, mix_router[1:])
    norm_grad_two, grad_gain_two = norm_back(first_sum, scale_two, gain_two, normed_grad)
    first_grad = cot_full + norm_grad_two
    first_low = first_grad.astype(low)
    attended_grad = dot_nt(first_low, out_full).astype(low)
    grad_out = ein("td,te->de", attended, first_low)

    upstream_parts = attended_grad.reshape(tok_count, head_sets, width).transpose(1, 0, 2)
    if repeat > 1:
        upstream_parts = jnp.repeat(upstream_parts, repeat, axis=0)
    came, upstream_parts = pin(came, upstream_parts)
    came, added = advance(add_steps, came)
    upstream = swap_ctx(upstream_parts).reshape(group_len, width)
    if not direct:
        upstream = take_blocks(upstream, place_to_stored)
    qkv_grads = attention_backward(
        query, upstream, attended_heads, lse, key, key.T, value, cosine_wide, sine_wide, at
    )
    (*came, value_grad), key_grad, query_grad = pin([*came, qkv_grads[2]], qkv_grads[1], qkv_grads[0])
    qkv_grads = [query_grad, key_grad, value_grad]
    came, added = advance(add_steps, came)
    if repeat > 1:
        qkv_grads = [jnp.where(ctx_index % repeat == 0, g, jnp.zeros_like(g)) for g in qkv_grads]
    grad_qkv = jnp.concatenate(
        [ein("td,te->de", normed_sorted, g).astype(low) for g in qkv_grads], axis=1
    )
    bias_sums = jnp.stack([jnp.sum(g.astype(full), axis=0) for g in qkv_grads])
    grad_bias = lax.dynamic_update_slice_in_dim(
        jnp.zeros((3, D), full), bias_sums, my_heads, 1
    )
    grad_qkv, first_grads = lax.optimization_barrier((grad_qkv, qkv_grads[0]))
    odd_one, even_one = unproject([first_grads, *qkv_grads[1:]], stored_near, w_qkv, per_device)
    came, odd_one = pin(came, odd_one)
    added = finish(add_steps, came)
    layer_out = first_sum + added.astype(full)
    one_steps = scatter_steps(odd_one, even_one)
    dx_one = finish(one_steps, next(one_steps)).astype(full)
    norm_grad_one, grad_gain_one = norm_back(tokens, scale_one, gain_one, dx_one)
    input_grad = first_grad + norm_grad_one

    qkv_rows = lax.psum_scatter(
        grad_qkv.reshape(dp_count, ctx_count, shard, 3 * width),
        "dp",
        scatter_dimension=0,
        tiled=True,
    )[0]
    qkv_mine = swap_ctx(qkv_rows)[::repeat].astype(full)
    qkv_mine = qkv_mine.reshape(head_sets, shard, 3, width).transpose(2, 1, 0, 3).reshape(3, shard, D)
    out_rows = swap_ctx(
        grad_out.astype(low).reshape(dp_count, ctx_count, shard, D).transpose(1, 0, 2, 3)
    )
    out_rows = jnp.sum(out_rows.astype(full), axis=0).astype(low)
    grad_wout = lax.psum_scatter(out_rows, "dp", scatter_dimension=0, tiled=True)[0].astype(full)
    small_grads = jnp.concatenate(
        [grad_gain_one[None], grad_bias, grad_gain_two[None], grad_narrow], axis=0
    )
    small_grads = small_grads.reshape(-1, dp_count, ctx_count, shard).transpose(2, 1, 0, 3)
    small_grads = jnp.sum(swap_ctx(small_grads), axis=0)
    small_grads = jnp.sum(
        lax.all_to_all(small_grads, "dp", split_axis=0, concat_axis=0, tiled=True), axis=0
    ).T

    def over_dp(grad, dim):
        return lax.psum_scatter(
            grad.astype(low), "dp", scatter_dimension=dim, tiled=True
        ).astype(full)

    return (
        layer_out.astype(low)[None],
        input_grad[None],
        small_grads[:, 0],
        qkv_mine[0],
        small_grads[:, 1],
        qkv_mine[1],
        small_grads[:, 2],
        qkv_mine[2],
        small_grads[:, 3],
        grad_wout,
        small_grads[:, 4],
        small_grads[:, 6:],
        over_dp(grad_egate, 0)[None],
        over_dp(grad_eup, 0)[None],
        over_dp(grad_edown, 1)[None],
        over_dp(grad_sgate, 0).T,
        over_dp(grad_sup, 0).T,
        over_dp(grad_sdown, 0),
        small_grads[:, 5],
    )


def solution(mesh):
    rows = P("dp", "ctx", None)
    flat = P(("dp", "ctx"))
    lines = P(("dp", "ctx"), None)
    columns = P(None, ("dp", "ctx"))
    deep = P("ctx", "dp", None)
    down = P("ctx", None, "dp")
    in_specs = (
        (rows, flat, lines, flat, lines, flat, lines, flat, lines, flat, lines)
        + (deep, deep, down, columns, columns, lines, flat)
        + (rows, rows, P("dp", None), rows)
    )
    out_specs = (
        (rows, rows, flat, lines, flat, lines, flat, lines, flat, lines, flat, lines)
        + (deep, deep, down, columns, columns, lines, flat)
    )
    return jax.shard_map(
        on_device, mesh=mesh, in_specs=in_specs, out_specs=out_specs, check_vma=False
    )
```

time: 2330 us -> 1430 us (0.61)
  waiting for transfers between devices: 1170 us -> 281 us
  Pallas kernels: 126 us -> 580 us
  matrix products: 607 us -> 175 us
  blocking collectives: 71 us -> 17.6 us
  other arithmetic: 105 us -> 156 us
  starting transfers between devices: 17.4 us -> 56.4 us
  local copies, waits for them, and re-layouts: 144 us -> 108 us
  between operations: 77.3 us -> 47.1 us
    pallas_call x2 -> x8, Pallas kernels: 126 us -> 580 us  [the longest x2 155 us: gather_now(): pl.pallas_call(functools.partial(gather_kernel, count, small is not None)...]
    reduce_scatter x5 -> x2, waiting for transfers between devices: 355 us -> 16.3 us  [the longest x1 16.3 us: on_device(): lax.psum_scatter(grad_qkv.reshape(dp_count, ctx_count, shard, 3 * width),...]
    dot_general x9 -> x2, matrix products: 195 us -> 9.54 us  [dot(): return jnp.dot(left, right, preferred_element_type=full)]
    reduce_scatter x6, waiting for transfers between devices: 183 us -> 0.02 us  [over_dp(): lax.psum_scatter(grad.astype(low), 'dp', scatter_dimension=dim, tiled=True)]
    all_gather x6 -> x3, waiting for transfers between devices: 182 us -> 0.02 us  [the longest x1 0.02 us: on_device(): out_mine = lax.all_gather(w_out, 'dp', axis=0, tiled=True)]
    dot_general x9 -> x2, matrix products: 185 us -> 9.97 us  [dot_nt(): lax.dot_general(left, right, (((1,), (1,)), ((), ())), preferred_element_...]
    unnamed x24 -> x16, waiting for transfers between devices: 135 us -> 3.14 us
    all_to_all x4 -> x6, waiting for transfers between devices: 49.2 us -> 159 us  [swap_ctx(): lax.all_to_all(values, 'ctx', split_axis=0, concat_axis=0, tiled=True)]
  transfers between devices with their start and end apart: 27 -> 51, of which waited for: 16 -> 13; matrix products, arithmetic and copies ran while one was open for 32% -> 28% of each run, Pallas kernels for 5% -> 34%
where the time goes in v2:
time: 1430 us; the launch traced here: 1420 us
  Pallas kernels  580 us (41%)
  waiting for transfers between devices  281 us (20%)
  matrix products  175 us (12%)
  other arithmetic  156 us (11%)
  local copies, waits for them, and re-layouts  108 us (8%)
  starting transfers between devices  56.4 us (4%)
  between operations  47.1 us (3%)
  blocking collectives  17.6 us (1%)
    all_to_all x6, waiting for transfers between devices, swap_ctx(): lax.all_to_all(values, 'ctx', split_axis=0, concat_axis=0, tiled=True)  159 us
    dot_general x11, matrix products, ein(): return jnp.einsum(spec, left, right, preferred_element_type=full)  156 us
    pallas_call x2, Pallas kernels, gather_now(): pl.pallas_call(functools.partial(gather_kernel, count, small is not None)...  155 us
    pallas_call x1, Pallas kernels, routed_expert(): pl.pallas_call(expert_kernel, grid=(count,), in_specs=[chunk, chunk, line...  141 us
    pallas_call x1, Pallas kernels, shared_expert(): pl.pallas_call(shared_kernel, grid=(count,), in_specs=[chunk, chunk, colu...  103 us
    ppermute x25, waiting for transfers between devices, exchange(): return lax.ppermute(values, 'ctx', [(i, i ^ bit) for i in range(count)])  101 us
    pallas_call x1, Pallas kernels, attention_backward(): pl.pallas_call(backward_kernel, grid_spec=pltpu.PrefetchScalarGridSpec(nu...  75.8 us
    pallas_call x1, Pallas kernels, attention_forward(): pl.pallas_call(forward_kernel, grid_spec=pltpu.PrefetchScalarGridSpec(num...  61 us
  transfers between devices with their start and end apart: 51, of which 13 were waited for; matrix products, arithmetic and copies ran while one was open for 28% of the time, Pallas kernels for 34%

profile of v2, /device:TPU:0, one launch (start us, length us, event | category | flops | bytes accessed | tf_op | source)
XLA Modules:
  0.0 1420.3 jit_solution(14924124308672476417)
XLA Ops:
  9.4 17.6 %all_to_all.40 = bf16[8,64,768]{2,1,0:T(8,128)(2,1)} all-to-all(bf16[8,64,768]{2,1,0:T(8,128)(2,1)S(1)} %pad_maximum_fusion.20), channel_id=1, replica_groups=mesh['dp'=4,'ctx'=8] {'ctx'}, dimensions={0} | all-to-all | bytes 1572864 | tf_op jit(solution)/shard_map/all_to_all | solution.py:683
  30.0 3.7 collective-permute-start.2
  51.0 7.5 fusion.14
  62.8 77.2 %gather_rows.2 = (bf16[16,256,2048]{2,1,0:T(8,128)(2,1)S(1)}, f32[8,32,128]{2,1,0:T(8,128)S(1)}) custom-call(bf16[512,2048]{1,0:T(8,128)(2,1)S(1)} %bitcast.298, f32[32,128]{1,0:T(8,128)S(1)} %pad_bitcast_fusion.refs_1_), custom_call_target="tpu_custom_call" | custom-call | tf_op jit(solution)/shard_map/gather_rows/pallas_call | solution.py:581
  140.0 5.7 copy-done.10
  163.5 23.7 %project.1 = (bf16[4096,2048]{1,0:T(8,128)(2,1)}, bf16[4096,256]{1,0:T(8,128)(2,1)S(1)}, bf16[4096,256]{1,0:T(8,128)(2,1)S(1)}, bf16[4096,256]{1,0:T(8,128)(2,1)S(1)}) custom-call(s32[16]{0:T(128)S(1)} %concatenate.127.place_ref, bf16[16,256,2048]{2,1,0:T(8,128)(2,1)} %copy-done.10, f32[1,2048]{1,0:T(1,128)S(1)} %slice.435.gain_ref, ...), custom_call_target="tpu_custom_call" | custom-call | tf_op jit(solution)/shard_map/project/pallas_call | solution.py:117
  187.3 4.7 pad_maximum_fusion.9
  204.2 4.1 copy.209
  209.9 61.0 %attend_forward.1 = (bf16[4096,256]{1,0:T(8,128)(2,1)S(1)}, f32[2,1,4096]{2,1,0:T(1,128)S(1)}) custom-call(s32[16]{0:T(128)S(1)} %select_reduce_fusion.1.at_ref, bf16[4096,256]{1,0:T(8,128)(2,1)S(1)} %copy-done.14, bf16[4096,256]{1,0:T(8,128)(2,1)} %copy-done.6, bf16[256,4096]{1,0:T(8,128)(2,1)} %bitcast.316), custom_call_target="tpu_custom_call" | custom-call | tf_op jit(solution)/shard_map/attend_forward/pallas_call | solution.py:362
  276.7 3.7 fusion.40
  288.3 6.1 fusion.41
  306.3 3.5 convert_reduce_fusion
  315.7 3.9 copy.210
  319.6 4.4 all-to-all-start.1
  324.0 7.6 pad_maximum_fusion.1
  345.9 4.7 all-to-all-done.1
  350.6 7.8 multiply_reduce_fusion.3
  361.8 78.0 %gather_rows.3 = (bf16[16,256,2048]{2,1,0:T(8,128)(2,1)S(1)}, f32[8,24,512]{2,1,0:T(8,128)S(1)}) custom-call(bf16[512,2048]{1,0:T(8,128)(2,1)S(1)} %multiply_convert_fusion.refs_0_, f32[24,512]{1,0:T(8,128)S(1)} %select_maximum_fusion.refs_1_), custom_call_target="tpu_custom_call" | custom-call | tf_op jit(solution)/shard_map/gather_rows/pallas_call | solution.py:581
  439.8 5.8 copy-done
  448.9 8.0 pad_maximum_fusion
  456.9 6.6 copy.216
  463.5 140.9 %routed_expert.1 = (bf16[8,320,2048]{2,1,0:T(8,128)(2,1)}, bf16[8,320,2048]{2,1,0:T(8,128)(2,1)}, bf16[8,320,1408]{2,1,0:T(8,128)(2,1)}, bf16[8,320,1408]{2,1,0:...) custom-call(bf16[4096,2048]{1,0:T(8,128)(2,1)} %bitcast.294, ...), custom_call_target="tpu_custom_call" | custom-call | tf_op jit(solution)/shard_map/routed_expert/pallas_call | solution.py:236
  604.4 22.2 %bitcast_convert_fusion.2 = bf16[2048,1408]{1,0:T(8,128)(2,1)} fusion(bf16[8,320,2048]{2,1,0:T(8,128)(2,1)} %get-tuple-element.122, bf16[8,320,1408]{2,1,0:T(8,128)(2,1)} %get-tuple-element.123), kind=kOutput, calls=%fused_computation.7 | convolution fusion | flops 14766833664 | bytes 23461888 | tf_op jit(solution)/shard_map/crd,crf->df/dot_general | solution.py:34
  626.6 103.0 %shared_expert.1 = (bf16[4096,2048]{1,0:T(8,128)(2,1)}, bf16[4096,704]{1,0:T(8,128)(2,1)}, bf16[4096,704]{1,0:T(8,128)(2,1)}, bf16[4096,704]{1,0:T(8,128)(2,1)},...) custom-call(bf16[4096,2048]{1,0:T(8,128)(2,1)} %bitcast.295, ...), custom_call_target="tpu_custom_call" | custom-call | tf_op jit(solution)/shard_map/shared_expert/pallas_call | solution.py:305
  730.2 22.5 %bitcast_convert_fusion.1 = bf16[2048,1408]{1,0:T(8,128)(2,1)} fusion(bf16[8,320,2048]{2,1,0:T(8,128)(2,1)} %get-tuple-element.122, bf16[8,320,1408]{2,1,0:T(8,128)(2,1)} %get-tuple-element.130), kind=kOutput, calls=%fused_computation.6 | convolution fusion | flops 14766833664 | bytes 23461888 | tf_op jit(solution)/shard_map/crd,crf->df/dot_general | solution.py:34
  752.7 4.5 add_convert_fusion.39
  760.8 17.2 %convolution_convert_fusion.3 = bf16[704,2048]{1,0:T(8,128)(2,1)} fusion(bf16[4096,704]{1,0:T(8,128)(2,1)S(1)} %copy-done.72, bf16[4096,2048]{1,0:T(8,128)(2,1)} %get-tuple-element.139), kind=kOutput, calls=%fused_computation.41 | convolution fusion | flops 11812601856 | bytes 25427968 | tf_op jit(solution)/shard_map/tf,td->fd/dot_general | solution.py:34
  778.0 20.8 %bitcast_convert_fusion = bf16[1408,2048]{1,0:T(8,128)(2,1)} fusion(bf16[8,320,1408]{2,1,0:T(8,128)(2,1)} %get-tuple-element.136, bf16[8,320,2048]{2,1,0:T(8,128)(2,1)} %get-tuple-element.137), kind=kOutput, calls=%fused_computation.5 | convolution fusion | flops 14766833664 | bytes 23461888 | tf_op jit(solution)/shard_map/crf,crd->fd/dot_general | solution.py:34
  798.8 6.3 collective-permute-done.14
  808.1 5.7 add_convert_fusion.33
  815.6 18.9 %convolution_convert_fusion.2 = bf16[704,2048]{1,0:T(8,128)(2,1)} fusion(bf16[4096,704]{1,0:T(8,128)(2,1)} %get-tuple-element.144, bf16[4096,2048]{1,0:T(8,128)(2,1)} %bitcast.296), kind=kOutput, calls=%fused_computation.40 | convolution fusion | flops 11812601856 | bytes 25427968 | tf_op jit(solution)/shard_map/tf,td->fd/dot_general | solution.py:34
  834.5 18.6 %convolution_convert_fusion.1 = bf16[704,2048]{1,0:T(8,128)(2,1)} fusion(bf16[4096,704]{1,0:T(8,128)(2,1)} %get-tuple-element.145, bf16[4096,2048]{1,0:T(8,128)(2,1)} %bitcast.297), kind=kOutput, calls=%fused_computation.39 | convolution fusion | flops 11812601856 | bytes 25427968 | tf_op jit(solution)/shard_map/tf,td->fd/dot_general | solution.py:34
  857.4 3.6 all-to-all-start.2
  861.3 4.5 all-to-all-done.2
  865.8 4.9 add_convert_fusion.32
  875.9 9.9 convolution_convert_fusion
  885.7 8.4 copy.261
  894.2 4.9 all-to-all-start.7
  899.6 9.3 convolution_convert_fusion.4
  910.4 82.8 %all-to-all-done.7 = bf16[8,4,64,2048]{3,2,1,0:T(8,128)(2,1)} async-done(((bf16[8,4,64,2048]{3,2,1,0:T(8,128)(2,1)}), bf16[8,4,64,2048]{3,2,1,0:T(8,128)(2,1)}, u32[]{:S(2)}, u32[]{:S(2)}) %all-to-all-start.7) | async-done | bytes 8388640 | tf_op jit(solution)/shard_map/all_to_all | solution.py:683
  993.2 6.4 reduce_sum.192
  999.6 4.4 add_convert_fusion.25
  1008.3 4.5 all-to-all-start.3
  1016.1 61.7 %all-to-all-done.3 = bf16[8,512,256]{2,1,0:T(8,128)(2,1)} async-done(((bf16[8,512,256]{2,1,0:T(8,128)(2,1)}), bf16[8,512,256]{2,1,0:T(8,128)(2,1)}, u32[]{:S(2)}, u32[]{:S(2)}) %all-to-all-start.3) | async-done | bytes 2097184 | tf_op jit(solution)/shard_map/all_to_all | solution.py:683
  1077.8 75.8 %attend_backward.1 = (bf16[4096,256]{1,0:T(8,128)(2,1)S(1)}, bf16[4096,256]{1,0:T(8,128)(2,1)S(1)}, bf16[4096,256]{1,0:T(8,128)(2,1)}) custom-call(s32[16]{0:T(128)S(1)} %select_reduce_fusion.1.at_ref, bf16[4096,256]{1,0:T(8,128)(2,1)} %copy-done.13, bf16[4096,256]{1,0:T(8,128)(2,1)} %bitcast.99.do_ref, bf16[4096,256]{1,0:T(8,128)(2,1)} %copy-done.16, ...), custom_call_target="tpu_custom_call" | custom-call | tf_op jit(solution)/shard_map/attend_backward/pallas_call | solution.py:443
  1153.7 5.7 add_convert_fusion.19
  1160.0 8.5 convolution_convert_fusion.7
  1168.5 8.6 convolution_convert_fusion.6
  1177.1 8.3 convolution_convert_fusion.5
  1187.3 20.3 %unproject.1 = (bf16[2048,2048]{1,0:T(8,128)(2,1)}, bf16[2048,2048]{1,0:T(8,128)(2,1)}) custom-call(s32[16]{0:T(128)S(1)} %copy-done.24, bf16[4096,256]{1,0:T(8,128)(2,1)S(1)} %get-tuple-element.164.dq_ref, bf16[4096,256]{1,0:T(8,128)(2,1)S(1)} %get-tuple-element.162.dk_ref, bf16[4096,256]{1,0:T(8,128)(2,1)S(1)} %copy-done.17, bf16[2048,768]{1,0:T(8,128)(2,1)S(1)} %copy-done.12), custom_call_target="tpu_custom_call" | custom-call | tf_op jit(solution)/shard_map/unproject/pallas_call | solution.py:166
  1211.9 9.3 collective-permute-done.23
  1239.2 34.7 %collective-permute-done.24 = bf16[512,2048]{1,0:T(8,128)(2,1)} collective-permute-done((bf16[512,2048]{1,0:T(8,128)(2,1)}, bf16[512,2048]{1,0:T(8,128)(2,1)}, u32[]{:S(2)}, u32[]{:S(2)}) %collective-permute-start.24) | collective-permute-done | bytes 2097184 | tf_op jit(solution)/shard_map/ppermute | solution.py:485
  1274.0 4.7 add_convert_fusion.9
  1287.1 3.5 bitcast_convert_fusion.3
  1292.9 16.3 %reduce-scatter.9.cloned.1.call-done = bf16[1,8,64,768]{3,2,1,0:T(8,128)(2,1)} async-done(((bf16[4,8,64,768]{3,2,1,0:T(8,128)(2,1)}), bf16[1,8,64,768]{3,2,1,0:T(8,128)(2,1)}) %reduce-scatter.9.cloned.1.call-update) | async-done | bytes 786448 | tf_op jit(solution)/shard_map/reduce_scatter | solution.py:946
  1309.2 4.5 all-to-all-start.6
  1313.7 42.0 %collective-permute-done.25 = bf16[256,2048]{1,0:T(8,128)(2,1)} collective-permute-done((bf16[256,2048]{1,0:T(8,128)(2,1)S(1)}, bf16[256,2048]{1,0:T(8,128)(2,1)}, u32[]{:S(2)}, u32[]{:S(2)}) %collective-permute-start.25) | collective-permute-done | bytes 1048608 | tf_op jit(solution)/shard_map/ppermute | solution.py:485
  1355.7 5.7 add_convert_fusion.8
  1363.1 4.6 add_convert_fusion.18
  1377.5 6.0 collective-permute-done.27
  1390.1 4.0 all-to-all-start.4
  1394.1 5.4 all-to-all-done.4
  1401.8 4.0 all-to-all-start.5
  1405.8 4.8 fusion.3
  (408 shorter events, 165.6 us)
Async XLA Ops:
  7.2 139.3 %all-gather.12.cloned.1.call-start = ((), (), s32[]{:S(2)}) async-start(), calls=%async_computation.16 | async-start | bytes 1310720 | tf_op jit(solution)/shard_map/all_gather | solution.py:767
  27.1 131.4 %all-gather.14.cloned.1.call-start = ((), (), s32[]{:S(2)}) async-start(), calls=%async_computation.17 | async-start | bytes 3932160 | tf_op jit(solution)/shard_map/all_gather | solution.py:736
  27.8 435.7 %all-gather.22.cloned.1.call-start = ((), (), s32[]{:S(2)}) async-start(), calls=%async_computation.29 | async-start | bytes 7208960 | tf_op jit(solution)/shard_map/all_gather | solution.py:777
  28.5 435.0 %all-gather.24.cloned.1.call-start = ((), (), s32[]{:S(2)}) async-start(), calls=%async_computation.30 | async-start | bytes 7208960 | tf_op jit(solution)/shard_map/all_gather | solution.py:778
  29.1 434.4 %all-gather.26.cloned.1.call-start = ((), (), s32[]{:S(2)}) async-start(), calls=%async_computation.31 | async-start | bytes 7208960 | tf_op jit(solution)/shard_map/all_gather | solution.py:779
  29.7 596.9 %all-gather.16.cloned.1.call-start = ((), (), s32[]{:S(2)}) async-start(), calls=%async_computation.18 | async-start | bytes 3604480 | tf_op jit(solution)/shard_map/all_gather | solution.py:772
  30.0 32.0 %collective-permute-start.2 = (f32[14,64]{1,0:T(8,128)S(1)}, f32[14,64]{1,0:T(8,128)S(1)}, u32[]{:S(2)}, u32[]{:S(2)}) collective-permute-start(f32[14,64]{1,0:T(8,128)S(1)} %convert_element_type.512), channel_id=1, source_target_pairs={{0,24},{8,0},{16,8},{24,16},{1,25},{9,1},{17,9},{25,17},{2,26},{10... | collective-permute-start | bytes 10760 | tf_op jit(solution)/shard_map/ppermute | solution.py:750
  33.6 28.4 %collective-permute-start.1 = (f32[14,64]{1,0:T(8,128)S(1)}, f32[14,64]{1,0:T(8,128)S(1)}, u32[]{:S(2)}, u32[]{:S(2)}) collective-permute-start(f32[14,64]{1,0:T(8,128)S(1)} %convert_element_type.512), channel_id=1, source_target_pairs={{0,16},{8,24},{16,0},{24,8},{1,17},{9,25},{17,1},{25,9},{2,18},{10... | collective-permute-start | bytes 10760 | tf_op jit(solution)/shard_map/ppermute | solution.py:750
  33.6 28.4 %collective-permute-start = (f32[14,64]{1,0:T(8,128)S(1)}, f32[14,64]{1,0:T(8,128)S(1)}, u32[]{:S(2)}, u32[]{:S(2)}) collective-permute-start(f32[14,64]{1,0:T(8,128)S(1)} %convert_element_type.512), channel_id=1, source_target_pairs={{0,8},{8,16},{16,24},{24,0},{1,9},{9,17},{17,25},{25,1},{2,10},{10... | collective-permute-start | bytes 10760 | tf_op jit(solution)/shard_map/ppermute | solution.py:750
  34.6 591.9 %all-gather.18.cloned.1.call-start = ((), (), s32[]{:S(2)}) async-start(), calls=%async_computation.19 | async-start | bytes 3604480 | tf_op jit(solution)/shard_map/all_gather | solution.py:773
  34.7 120.1 %copy-start.70 = (pred[8]{0:T(512)(128)(4,1)}, pred[8]{0:T(512)(128)(4,1)S(1)}, u32[]{:S(2)}) copy-start(pred[8]{0:T(512)(128)(4,1)S(1)} %compare_and_fusion) | copy-start | bytes 28
  45.8 100.0 %copy-start.63 = (s32[1024]{0:T(1024)}, s32[1024]{0:T(1024)S(1)}, u32[]{:S(2)}) copy-start(s32[1024]{0:T(1024)S(1)} %pad_clamp_fusion) | copy-start | bytes 12292
  62.0 96.4 %copy-start.23 = (s32[16]{0:T(128)}, s32[16]{0:T(128)S(1)}, u32[]{:S(2)}) copy-start(s32[16]{0:T(128)S(1)} %concatenate.127.place_ref) | copy-start | bytes 196
  149.7 37.5 %collective-permute-start.4 = (bf16[256,2048]{1,0:T(8,128)(2,1)}, bf16[256,2048]{1,0:T(8,128)(2,1)}, u32[]{:S(2)}, u32[]{:S(2)}) collective-permute-start(bf16[256,2048]{1,0:T(8,128)(2,1)} %get-tuple-element.221), channel_id=1, source_target_pairs={{0,4},{1,5},{2,6},{3,7},{4,0},{5,1},{6,2},{7,3},{8,12},{9,13},{10,... | collective-permute-start | bytes 3145736 | tf_op jit(solution)/shard_map/ppermute | solution.py:485
  150.3 37.0 %collective-permute-start.3 = (bf16[256,2048]{1,0:T(8,128)(2,1)}, bf16[256,2048]{1,0:T(8,128)(2,1)}, u32[]{:S(2)}, u32[]{:S(2)}) collective-permute-start(bf16[256,2048]{1,0:T(8,128)(2,1)} %get-tuple-element.222), channel_id=1, source_target_pairs={{0,2},{1,3},{2,0},{3,1},{4,6},{5,7},{6,4},{7,5},{8,10},{9,11},{10,... | collective-permute-start | bytes 3145736 | tf_op jit(solution)/shard_map/ppermute | solution.py:485
  152.8 34.4 %collective-permute-start.6 = (bf16[128,2048]{1,0:T(8,128)(2,1)}, bf16[128,2048]{1,0:T(8,128)(2,1)}, u32[]{:S(2)}, u32[]{:S(2)}) collective-permute-start(bf16[128,2048]{1,0:T(8,128)(2,1)} %get-tuple-element.227), channel_id=1, source_target_pairs={{0,4},{1,5},{2,6},{3,7},{4,0},{5,1},{6,2},{7,3},{8,12},{9,13},{10,... | collective-permute-start | bytes 1572872 | tf_op jit(solution)/shard_map/ppermute | solution.py:485
  154.3 33.0 %collective-permute-start.5 = (bf16[128,2048]{1,0:T(8,128)(2,1)}, bf16[128,2048]{1,0:T(8,128)(2,1)}, u32[]{:S(2)}, u32[]{:S(2)}) collective-permute-start(bf16[128,2048]{1,0:T(8,128)(2,1)} %get-tuple-element.228), channel_id=1, source_target_pairs={{0,2},{1,3},{2,0},{3,1},{4,6},{5,7},{6,4},{7,5},{8,10},{9,11},{10,... | collective-permute-start | bytes 1572872 | tf_op jit(solution)/shard_map/ppermute | solution.py:485
  158.3 28.9 %copy-start.47 = (f32[1,4,8,64]{3,2,1,0:T(8,128)}, f32[1,4,8,64]{3,2,1,0:T(8,128)S(1)}, u32[]{:S(2)}) copy-start(f32[1,4,8,64]{3,2,1,0:T(8,128)S(1)} %copy.207) | copy-start | bytes 24580
  195.1 75.8 %collective-permute-start.8 = (bf16[512,2048]{1,0:T(8,128)(2,1)}, bf16[512,2048]{1,0:T(8,128)(2,1)}, u32[]{:S(2)}, u32[]{:S(2)}) collective-permute-start(bf16[512,2048]{1,0:T(8,128)(2,1)} %pad_maximum_fusion.6), channel_id=1, source_target_pairs={{0,2},{1,3},{2,0},{3,1},{4,6},{5,7},{6,4},{7,5},{8,10},{9,11},{10,... | collective-permute-start | bytes 6291464 | tf_op jit(solution)/shard_map/ppermute | solution.py:485
  196.6 74.3 %collective-permute-start.7 = (bf16[512,2048]{1,0:T(8,128)(2,1)}, bf16[512,2048]{1,0:T(8,128)(2,1)}, u32[]{:S(2)}, u32[]{:S(2)}) collective-permute-start(bf16[512,2048]{1,0:T(8,128)(2,1)} %pad_maximum_fusion.9), channel_id=1, source_target_pairs={{0,4},{1,5},{2,6},{3,7},{4,0},{5,1},{6,2},{7,3},{8,12},{9,13},{10,... | collective-permute-start | bytes 6291464 | tf_op jit(solution)/shard_map/ppermute | solution.py:485
  202.3 68.6 %collective-permute-start.10 = (bf16[256,2048]{1,0:T(8,128)(2,1)}, bf16[256,2048]{1,0:T(8,128)(2,1)}, u32[]{:S(2)}, u32[]{:S(2)}) collective-permute-start(bf16[256,2048]{1,0:T(8,128)(2,1)} %pad_maximum_fusion.18), channel_id=1, source_target_pairs={{0,2},{1,3},{2,0},{3,1},{4,6},{5,7},{6,4},{7,5},{8,10},{9,11},{10,... | collective-permute-start | bytes 3145736 | tf_op jit(solution)/shard_map/ppermute | solution.py:485
  202.8 68.1 %collective-permute-start.9 = (bf16[256,2048]{1,0:T(8,128)(2,1)}, bf16[256,2048]{1,0:T(8,128)(2,1)}, u32[]{:S(2)}, u32[]{:S(2)}) collective-permute-start(bf16[256,2048]{1,0:T(8,128)(2,1)} %pad_maximum_fusion.19), channel_id=1, source_target_pairs={{0,4},{1,5},{2,6},{3,7},{4,0},{5,1},{6,2},{7,3},{8,12},{9,13},{10,... | collective-permute-start | bytes 3145736 | tf_op jit(solution)/shard_map/ppermute | solution.py:485
  203.8 422.8 %all-gather.20.cloned.1.call-start = ((), (), s32[]{:S(2)}) async-start(), calls=%async_computation.20 | async-start | bytes 3604480 | tf_op jit(solution)/shard_map/all_gather | solution.py:774
  280.4 43.6 %collective-permute-start.11 = (bf16[4,256,2048]{2,1,0:T(8,128)(2,1)}, bf16[4,256,2048]{2,1,0:T(8,128)(2,1)}, u32[]{:S(2)}, u32[]{:S(2)}) collective-permute-start(bf16[4,256,2048]{2,1,0:T(8,128)(2,1)} %get-tuple-element.213), channel_id=1, source_target_pairs={{0,1},{1,0},{2,3},{3,2},{4,5},{5,4},{6,7},{7,6},{8,9},{9,8},{10,11... | collective-permute-start | bytes 12582920 | tf_op jit(solution)/shard_map/ppermute | solution.py:485
  288.3 27.1 %copy-start.40 = (bf16[14,4,8,64]{3,0,1,2:T(8,128)(2,1)S(1)}, bf16[14,4,8,64]{3,0,1,2:T(8,128)(2,1)}, u32[]{:S(2)}) copy-start(bf16[14,4,8,64]{3,0,1,2:T(8,128)(2,1)} %get-tuple-element.185) | copy-start | bytes 172036
  294.4 154.4 %collective-permute-start.12 = (bf16[4,512,2048]{2,1,0:T(8,128)(2,1)}, bf16[4,512,2048]{2,1,0:T(8,128)(2,1)}, u32[]{:S(2)}, u32[]{:S(2)}) collective-permute-start(bf16[4,512,2048]{2,1,0:T(8,128)(2,1)} %get-tuple-element.211), channel_id=1, source_target_pairs={{0,1},{1,0},{2,3},{3,2},{4,5},{5,4},{6,7},{7,6},{8,9},{9,8},{10,11... | collective-permute-start | bytes 25165832 | tf_op jit(solution)/shard_map/ppermute | solution.py:485
  315.4 43.6 %copy-start.45 = (f32[2048]{0:T(1024)}, f32[2048]{0:T(1024)S(1)}, u32[]{:S(2)}) copy-start(f32[2048]{0:T(1024)S(1)} %mul.192) | copy-start | bytes 24580
  319.6 31.0 %all-to-all-start.1 = ((bf16[8,512,256]{1,2,0:T(8,128)(2,1)}), bf16[8,512,256]{1,2,0:T(8,128)(2,1)}, u32[]{:S(2)}, u32[]{:S(2)}) async-start(bf16[8,512,256]{1,2,0:T(8,128)(2,1)} %copy.210), calls=%async_computation.1 | async-start | bytes 4194304 | tf_op jit(solution)/shard_map/all_to_all | solution.py:683
  324.0 904.9 %reduce-scatter.13.cloned.1.call-start = ((), (), s32[]{:S(2)}) async-start(), calls=%async_computation.23 | async-start | bytes 7208960 | tf_op jit(solution)/shard_map/reduce_scatter | solution.py:969
  360.4 79.4 %copy-start.1 = (bf16[512,2048]{1,0:T(8,128)(2,1)}, bf16[512,2048]{1,0:T(8,128)(2,1)S(1)}, u32[]{:S(2)}) copy-start(bf16[512,2048]{1,0:T(8,128)(2,1)S(1)} %multiply_convert_fusion.refs_0_) | copy-start | bytes 6291460
  361.1 95.8 %copy-start.54 = (f32[512]{0:T(512)}, f32[512]{0:T(512)S(1)}, u32[]{:S(2)}) copy-start(f32[512]{0:T(512)S(1)} %get-tuple-element.183) | copy-start | bytes 6148
  361.2 95.7 %copy-start.58 = (f32[512]{0:T(512)}, f32[512]{0:T(512)S(1)}, u32[]{:S(2)}) copy-start(f32[512]{0:T(512)S(1)} %fusion.22) | copy-start | bytes 6148
  729.6 23.1 %collective-permute-start.13 = (bf16[2048,2048]{1,0:T(8,128)(2,1)}, bf16[2048,2048]{1,0:T(8,128)(2,1)}, u32[]{:S(2)}, u32[]{:S(2)}) collective-permute-start(bf16[2048,2048]{1,0:T(8,128)(2,1)} %get-tuple-element.129), channel_id=1, source_target_pairs={{0,1},{1,0},{2,3},{3,2},{4,5},{5,4},{6,7},{7,6},{8,9},{9,8},{10,11... | collective-permute-start | bytes 25165832 | tf_op jit(solution)/shard_map/ppermute | solution.py:485
  730.1 502.0 %reduce-scatter.23.cloned.1.call-start = ((), (), s32[]{:S(2)}) async-start(), calls=%async_computation.28 | async-start | bytes 3604480 | tf_op jit(solution)/shard_map/reduce_scatter | solution.py:969
  757.3 47.8 %collective-permute-start.14 = (bf16[512,2048]{1,0:T(8,128)(2,1)S(1)}, bf16[512,2048]{1,0:T(8,128)(2,1)}, u32[]{:S(2)}, u32[]{:S(2)}) collective-permute-start(bf16[512,2048]{1,0:T(8,128)(2,1)S(1)} %pad_maximum_fusion.10), channel_id=1, source_target_pairs={{0,2},{1,3},{2,0},{3,1},{4,6},{5,7},{6,4},{7,5},{8,10},{9,11},{10,... | collective-permute-start | bytes 6291464 | tf_op jit(solution)/shard_map/ppermute | solution.py:485
  760.4 47.6 %collective-permute-start.15 = (bf16[512,2048]{1,0:T(8,128)(2,1)}, bf16[512,2048]{1,0:T(8,128)(2,1)}, u32[]{:S(2)}, u32[]{:S(2)}) collective-permute-start(bf16[512,2048]{1,0:T(8,128)(2,1)} %pad_maximum_fusion.11), channel_id=1, source_target_pairs={{0,4},{1,5},{2,6},{3,7},{4,0},{5,1},{6,2},{7,3},{8,12},{9,13},{10,... | collective-permute-start | bytes 6291464 | tf_op jit(solution)/shard_map/ppermute | solution.py:485
  808.0 426.5 %reduce-scatter.21.cloned.1.call-start = ((), (), s32[]{:S(2)}) async-start(), calls=%async_computation.27 | async-start | bytes 3604480 | tf_op jit(solution)/shard_map/reduce_scatter | solution.py:969
  813.7 39.4 %collective-permute-start.17 = (bf16[256,2048]{1,0:T(8,128)(2,1)}, bf16[256,2048]{1,0:T(8,128)(2,1)S(1)}, u32[]{:S(2)}, u32[]{:S(2)}) collective-permute-start(bf16[256,2048]{1,0:T(8,128)(2,1)} %get-tuple-element.204), channel_id=1, source_target_pairs={{0,2},{1,3},{2,0},{3,1},{4,6},{5,7},{6,4},{7,5},{8,10},{9,11},{10,... | collective-permute-start | bytes 3145736 | tf_op jit(solution)/shard_map/ppermute | solution.py:485
  814.4 38.7 %collective-permute-start.16 = (bf16[256,2048]{1,0:T(8,128)(2,1)}, bf16[256,2048]{1,0:T(8,128)(2,1)}, u32[]{:S(2)}, u32[]{:S(2)}) collective-permute-start(bf16[256,2048]{1,0:T(8,128)(2,1)} %get-tuple-element.205), channel_id=1, source_target_pairs={{0,4},{1,5},{2,6},{3,7},{4,0},{5,1},{6,2},{7,3},{8,12},{9,13},{10,... | collective-permute-start | bytes 3145736 | tf_op jit(solution)/shard_map/ppermute | solution.py:485
  853.1 383.7 %reduce-scatter.19.cloned.1.call-start = ((), (), s32[]{:S(2)}) async-start(), calls=%async_computation.26 | async-start | bytes 3604480 | tf_op jit(solution)/shard_map/reduce_scatter | solution.py:969
  853.7 428.1 %reduce-scatter.15.cloned.1.call-start = ((), (), s32[]{:S(2)}) async-start(), calls=%async_computation.24 | async-start | bytes 7208960 | tf_op jit(solution)/shard_map/reduce_scatter | solution.py:969
  857.4 8.3 all-to-all-start.2
  871.3 128.3 %collective-permute-start.18 = (bf16[2048,2048]{1,0:T(8,128)(2,1)}, bf16[2048,2048]{1,0:T(8,128)(2,1)}, u32[]{:S(2)}, u32[]{:S(2)}) collective-permute-start(bf16[2048,2048]{1,0:T(8,128)(2,1)} %get-tuple-element.148), channel_id=1, source_target_pairs={{0,1},{1,0},{2,3},{3,2},{4,5},{5,4},{6,7},{7,6},{8,9},{9,8},{10,11... | collective-permute-start | bytes 25165832 | tf_op jit(solution)/shard_map/ppermute | solution.py:485
  894.2 99.0 %all-to-all-start.7 = ((bf16[8,4,64,2048]{3,2,1,0:T(8,128)(2,1)}), bf16[8,4,64,2048]{3,2,1,0:T(8,128)(2,1)}, u32[]{:S(2)}, u32[]{:S(2)}) async-start(bf16[8,4,64,2048]{3,2,1,0:T(8,128)(2,1)} %bitcast.312), calls=%async_computation.8 | async-start | bytes 16777216 | tf_op jit(solution)/shard_map/all_to_all | solution.py:683
  899.1 385.9 %reduce-scatter.11.cloned.1.call-start = ((), (), s32[]{:S(2)}) async-start(), calls=%async_computation.22 | async-start | bytes 1310720 | tf_op jit(solution)/shard_map/reduce_scatter | solution.py:958
  1005.7 148.0 %collective-permute-start.19 = (bf16[512,2048]{1,0:T(8,128)(2,1)}, bf16[512,2048]{1,0:T(8,128)(2,1)}, u32[]{:S(2)}, u32[]{:S(2)}) collective-permute-start(bf16[512,2048]{1,0:T(8,128)(2,1)} %pad_maximum_fusion.12), channel_id=1, source_target_pairs={{0,2},{1,3},{2,0},{3,1},{4,6},{5,7},{6,4},{7,5},{8,10},{9,11},{10,... | collective-permute-start | bytes 6291464 | tf_op jit(solution)/shard_map/ppermute | solution.py:485
  1007.7 146.0 %collective-permute-start.20 = (bf16[512,2048]{1,0:T(8,128)(2,1)}, bf16[512,2048]{1,0:T(8,128)(2,1)}, u32[]{:S(2)}, u32[]{:S(2)}) collective-permute-start(bf16[512,2048]{1,0:T(8,128)(2,1)} %pad_maximum_fusion.13), channel_id=1, source_target_pairs={{0,4},{1,5},{2,6},{3,7},{4,0},{5,1},{6,2},{7,3},{8,12},{9,13},{10,... | collective-permute-start | bytes 6291464 | tf_op jit(solution)/shard_map/ppermute | solution.py:485
  1008.3 69.5 %all-to-all-start.3 = ((bf16[8,512,256]{2,1,0:T(8,128)(2,1)}), bf16[8,512,256]{2,1,0:T(8,128)(2,1)}, u32[]{:S(2)}, u32[]{:S(2)}) async-start(bf16[8,512,256]{2,1,0:T(8,128)(2,1)} %bitcast.318), calls=%async_computation.3 | async-start | bytes 4194304 | tf_op jit(solution)/shard_map/all_to_all | solution.py:683
  1012.8 274.3 %reduce-scatter.17.cloned.1.call-start = ((), (), s32[]{:S(2)}) async-start(), calls=%async_computation.25 | async-start | bytes 7208960 | tf_op jit(solution)/shard_map/reduce_scatter | solution.py:969
  1015.9 293.3 %reduce-scatter.9.cloned.1.call-start = ((), (), s32[]{:S(2)}) async-start(), calls=%async_computation.21 | async-start | bytes 3932160 | tf_op jit(solution)/shard_map/reduce_scatter | solution.py:946
  1153.7 32.2 %copy-start.19 = (bf16[4096,256]{1,0:T(8,128)(2,1)}, bf16[4096,256]{1,0:T(8,128)(2,1)S(1)}, u32[]{:S(2)}) copy-start(bf16[4096,256]{1,0:T(8,128)(2,1)S(1)} %get-tuple-element.162.dk_ref) | copy-start | bytes 6291460
  1153.7 32.2 %copy-start.21 = (bf16[4096,256]{1,0:T(8,128)(2,1)}, bf16[4096,256]{1,0:T(8,128)(2,1)S(1)}, u32[]{:S(2)}) copy-start(bf16[4096,256]{1,0:T(8,128)(2,1)S(1)} %get-tuple-element.164.dq_ref) | copy-start | bytes 6291460
  1159.4 48.2 %collective-permute-start.22 = (bf16[256,2048]{1,0:T(8,128)(2,1)S(1)}, bf16[256,2048]{1,0:T(8,128)(2,1)S(1)}, u32[]{:S(2)}, u32[]{:S(2)}) collective-permute-start(bf16[256,2048]{1,0:T(8,128)(2,1)S(1)} %get-tuple-element.196), channel_id=1, source_target_pairs={{0,2},{1,3},{2,0},{3,1},{4,6},{5,7},{6,4},{7,5},{8,10},{9,11},{10,... | collective-permute-start | bytes 3145736 | tf_op jit(solution)/shard_map/ppermute | solution.py:485
  1159.7 47.9 %collective-permute-start.21 = (bf16[256,2048]{1,0:T(8,128)(2,1)S(1)}, bf16[256,2048]{1,0:T(8,128)(2,1)S(1)}, u32[]{:S(2)}, u32[]{:S(2)}) collective-permute-start(bf16[256,2048]{1,0:T(8,128)(2,1)S(1)} %get-tuple-element.197), channel_id=1, source_target_pairs={{0,4},{1,5},{2,6},{3,7},{4,0},{5,1},{6,2},{7,3},{8,12},{9,13},{10,... | collective-permute-start | bytes 3145736 | tf_op jit(solution)/shard_map/ppermute | solution.py:485
  1207.6 13.6 collective-permute-start.23
  1225.9 48.1 %collective-permute-start.24 = (bf16[512,2048]{1,0:T(8,128)(2,1)}, bf16[512,2048]{1,0:T(8,128)(2,1)}, u32[]{:S(2)}, u32[]{:S(2)}) collective-permute-start(bf16[512,2048]{1,0:T(8,128)(2,1)} %pad_maximum_fusion.14), channel_id=1, source_target_pairs={{0,2},{1,3},{2,0},{3,1},{4,6},{5,7},{6,4},{7,5},{8,10},{9,11},{10,... | collective-permute-start | bytes 6291464 | tf_op jit(solution)/shard_map/ppermute | solution.py:485
  1280.1 75.6 %collective-permute-start.26 = (bf16[512,2048]{1,0:T(8,128)(2,1)}, bf16[512,2048]{1,0:T(8,128)(2,1)}, u32[]{:S(2)}, u32[]{:S(2)}) collective-permute-start(bf16[512,2048]{1,0:T(8,128)(2,1)} %pad_maximum_fusion.15), channel_id=1, source_target_pairs={{0,4},{1,5},{2,6},{3,7},{4,0},{5,1},{6,2},{7,3},{8,12},{9,13},{10,... | collective-permute-start | bytes 6291464 | tf_op jit(solution)/shard_map/ppermute | solution.py:485
  1286.8 68.9 %collective-permute-start.25 = (bf16[256,2048]{1,0:T(8,128)(2,1)S(1)}, bf16[256,2048]{1,0:T(8,128)(2,1)}, u32[]{:S(2)}, u32[]{:S(2)}) collective-permute-start(bf16[256,2048]{1,0:T(8,128)(2,1)S(1)} %get-tuple-element.189), channel_id=1, source_target_pairs={{0,4},{1,5},{2,6},{3,7},{4,0},{5,1},{6,2},{7,3},{8,12},{9,13},{10,... | collective-permute-start | bytes 3145736 | tf_op jit(solution)/shard_map/ppermute | solution.py:485
  1309.2 60.5 %all-to-all-start.6 = ((bf16[8,64,768]{2,1,0:T(8,128)(2,1)}), bf16[8,64,768]{2,1,0:T(8,128)(2,1)}, u32[]{:S(2)}, u32[]{:S(2)}) async-start(bf16[8,64,768]{2,1,0:T(8,128)(2,1)} %bitcast.330), calls=%async_computation.7 | async-start | bytes 1572864 | tf_op jit(solution)/shard_map/all_to_all | solution.py:683
  1313.7 49.4 %copy-start.37 = (bf16[256,2048]{1,0:T(8,128)(2,1)S(1)}, bf16[256,2048]{1,0:T(8,128)(2,1)}, u32[]{:S(2)}) copy-start(bf16[256,2048]{1,0:T(8,128)(2,1)} %copy-done.36) | copy-start | bytes 3145732
  1313.7 49.4 %copy-start.39 = (bf16[256,2048]{1,0:T(8,128)(2,1)S(1)}, bf16[256,2048]{1,0:T(8,128)(2,1)}, u32[]{:S(2)}) copy-start(bf16[256,2048]{1,0:T(8,128)(2,1)} %copy-done.38) | copy-start | bytes 3145732
  1361.4 22.2 %collective-permute-start.27 = (bf16[256,2048]{1,0:T(8,128)(2,1)}, bf16[256,2048]{1,0:T(8,128)(2,1)}, u32[]{:S(2)}, u32[]{:S(2)}) collective-permute-start(bf16[256,2048]{1,0:T(8,128)(2,1)} %get-tuple-element.188), channel_id=1, source_target_pairs={{0,2},{1,3},{2,0},{3,1},{4,6},{5,7},{6,4},{7,5},{8,10},{9,11},{10,... | collective-permute-start | bytes 3145736 | tf_op jit(solution)/shard_map/ppermute | solution.py:485
  1390.1 9.4 all-to-all-start.4
  1401.8 9.6 all-to-all-start.5
  (61 other events, 280.2 us)
Sparse Core Ops, SparseCore 0:
  27.2 27.8 all-gather.11
  56.7 62.4 all-gather.13
  120.7 105.3 all-gather.21
  227.5 105.0 all-gather.23
  334.0 104.9 all-gather.25
  440.5 57.4 all-gather.15
  499.5 57.8 all-gather.17
  559.0 57.8 all-gather.19
  730.2 101.7 reduce-scatter.12
  834.2 56.7 reduce-scatter.22
  893.8 56.0 reduce-scatter.20
  952.6 56.0 reduce-scatter.18
  1011.0 102.0 reduce-scatter.14
  1115.3 27.6 reduce-scatter.10
  1145.2 100.9 reduce-scatter.16
  1248.4 60.7 reduce-scatter.8

commit v3 on v2

--- a/solution.py
+++ b/solution.py
@@ -2,6 +2,7 @@
 
 import jax
 import jax.numpy as jnp
+import numpy as np
 from jax import lax
 from jax.experimental import pallas as pl
 from jax.experimental.pallas import tpu as pltpu
@@ -43,11 +44,14 @@
     )
 
 
-def rope_tables(places):
-    turned = jnp.where(places < PROMPT, places, PROMPT + (places - PROMPT) % CONT)
-    frequency = rope_base ** (-2.0 * jnp.arange(HEAD_DIM // 2, dtype=full) / HEAD_DIM)
-    angles = turned.astype(full)[:, None] * frequency[None, :]
-    return (jnp.cos(angles)[:, None, :], jnp.sin(angles)[:, None, :])
+def rope_tables(rows):
+    places = np.arange(rows)
+    turned = np.where(places < PROMPT, places, PROMPT + (places - PROMPT) % CONT)
+    frequency = rope_base ** (-2.0 * np.arange(HEAD_DIM // 2, dtype=np.float64) / HEAD_DIM)
+    angles = turned.astype(np.float64)[:, None] * frequency[None, :]
+    cosine, sine = np.cos(angles), np.sin(angles)
+    wide = np.concatenate([cosine, cosine], axis=1), np.concatenate([-sine, sine], axis=1)
+    return tuple(jnp.asarray(table.astype(np.float32)) for table in wide)
 
 
 def rms_scale(values):
@@ -66,6 +70,14 @@
 def silu_parts(values):
     sig_value = jax.nn.sigmoid(values)
     return (values * sig_value, sig_value * (1.0 + values * (1.0 - sig_value)))
+
+
+def cost(microseconds):
+    return pl.CostEstimate(
+        flops=int(microseconds * 1.1e9),
+        bytes_accessed=int(microseconds * 3.3e6),
+        transcendentals=0,
+    )
 
 
 WIDE = 4
@@ -131,17 +143,22 @@
         ),
         out_shape=[jax.ShapeDtypeStruct((count * rows, D), low), head, head, head],
         compiler_params=pltpu.CompilerParams(vmem_limit_bytes=40 * 2**20),
+        cost_estimate=cost(24),
         name="project",
     )(places, x_blocks, gain, weight, bias, cosine, sine)
 
 
-def unproject_kernel(place_ref, dq_ref, dk_ref, dv_ref, w_ref, odd_ref, even_ref):
+def unproject_kernel(place_ref, grad_ref, w_ref, normed_ref, odd_ref, even_ref, gain_ref):
     step = pl.program_id(0)
     middle = pl.num_programs(0) // 2
-    width = dq_ref.shape[1]
-    total = dot_nt(dq_ref[...], w_ref[:, :width])
-    total += dot_nt(dk_ref[...], w_ref[:, width : 2 * width])
-    total += dot_nt(dv_ref[...], w_ref[:, 2 * width :])
+    total = dot_nt(grad_ref[...], w_ref[...])
+    gain_part = jnp.sum(total * normed_ref[...].astype(full), axis=0, keepdims=True)
+
+    @pl.when(step == 0)
+    def _():
+        gain_ref[...] = jnp.zeros_like(gain_ref)
+
+    gain_ref[...] += gain_part
 
     @pl.when(step < middle)
     def _():
@@ -152,32 +169,38 @@
         even_ref[...] = total.astype(low)
 
 
-def unproject(grads, places, weight, per_device):
+def unproject(grads, places, weight, normed, per_device):
     count = places.shape[0]
-    rows = grads[0].shape[0] // count
-    width = weight.shape[1] // 3
+    rows = grads.shape[0] // count
+    width = weight.shape[1]
     middle = count // 2
 
-    def block_of(g):
-        return odd_first(g // per_device, count // per_device) * per_device + g % per_device
-
-    tile = pl.BlockSpec((rows, width), lambda g, place: (place[block_of(g)], 0))
+    def at_place(g, place):
+        block = odd_first(g // per_device, count // per_device) * per_device + g % per_device
+        return (place[block], 0)
+
     shape = jax.ShapeDtypeStruct((middle * rows, D), low)
     return pl.pallas_call(
         unproject_kernel,
         grid_spec=pltpu.PrefetchScalarGridSpec(
             num_scalar_prefetch=1,
             grid=(count,),
-            in_specs=[tile, tile, tile, pl.BlockSpec((D, 3 * width), lambda g, place: (0, 0))],
+            in_specs=[
+                pl.BlockSpec((rows, width), at_place),
+                pl.BlockSpec((D, width), lambda g, place: (0, 0)),
+                pl.BlockSpec((rows, D), at_place),
+            ],
             out_specs=[
                 pl.BlockSpec((rows, D), lambda g, place: (jnp.minimum(g, middle - 1), 0)),
                 pl.BlockSpec((rows, D), lambda g, place: (jnp.maximum(g - middle, 0), 0)),
+                pl.BlockSpec((1, D), lambda g, place: (0, 0)),
             ],
         ),
-        out_shape=[shape, shape],
+        out_shape=[shape, shape, jax.ShapeDtypeStruct((1, D), full)],
         compiler_params=pltpu.CompilerParams(vmem_limit_bytes=40 * 2**20),
+        cost_estimate=cost(20),
         name="unproject",
-    )(places, *grads, weight)
+    )(places, grads, weight, normed)
 
 
 def dot_tn(left, right):
@@ -249,6 +272,7 @@
             shape(count * tok, D),
         ],
         compiler_params=pltpu.CompilerParams(vmem_limit_bytes=60 * 2**20),
+        cost_estimate=cost(140),
         name="routed_expert",
     )(all_normed, cot_all, code[:, None, :], gate[:, None, :], w_gate, w_up, w_down)
 
@@ -319,12 +343,13 @@
             half_shape,
         ],
         compiler_params=pltpu.CompilerParams(vmem_limit_bytes=60 * 2**20),
+        cost_estimate=cost(103),
         name="shared_expert",
     )(all_normed, cot_all, mix, w_gate_t, w_up_t, w_down, dx_routed, out_routed)
 
 
 def forward_kernel(at_ref, q_ref, k_ref, vt_ref, o_ref, lse_ref):
-    index = pl.program_id(1)
+    index = pl.program_id(0)
     query = q_ref[...]
     score_scale = HEAD_DIM ** (-0.5) * log2_e
 
@@ -353,32 +378,32 @@
         ),
     )
     o_ref[...] = (acc / total).T.astype(low)
-    lse_ref[...] = (highest + jnp.log2(total))[None]
-
-
-def attention_forward(query, key, value_t, at):
-    rows, width = query.shape
-    heads = width // HEAD_DIM
+    lse_ref[...] = highest + jnp.log2(total)
+
+
+def attention_forward(query, key, value_t, at, head):
+    rows = query.shape[0]
     return pl.pallas_call(
         forward_kernel,
         grid_spec=pltpu.PrefetchScalarGridSpec(
             num_scalar_prefetch=1,
-            grid=(heads, rows // CONT),
+            grid=(rows // CONT,),
             in_specs=[
-                pl.BlockSpec((CONT, HEAD_DIM), lambda h, i, at: (i, h)),
-                pl.BlockSpec((rows, HEAD_DIM), lambda h, i, at: (0, h)),
-                pl.BlockSpec((HEAD_DIM, rows), lambda h, i, at: (h, 0)),
+                pl.BlockSpec((CONT, HEAD_DIM), lambda i, at: (i, head)),
+                pl.BlockSpec((rows, HEAD_DIM), lambda i, at: (0, head)),
+                pl.BlockSpec((HEAD_DIM, rows), lambda i, at: (head, 0)),
             ],
             out_specs=[
-                pl.BlockSpec((CONT, HEAD_DIM), lambda h, i, at: (at[i], h)),
-                pl.BlockSpec((1, 1, CONT), lambda h, i, at: (h, 0, i)),
+                pl.BlockSpec((CONT, HEAD_DIM), lambda i, at: (at[i], 0)),
+                pl.BlockSpec((1, CONT), lambda i, at: (0, i)),
             ],
         ),
         out_shape=[
-            jax.ShapeDtypeStruct((rows, width), low),
-            jax.ShapeDtypeStruct((heads, 1, rows), full),
+            jax.ShapeDtypeStruct((rows, HEAD_DIM), low),
+            jax.ShapeDtypeStruct((1, rows), full),
         ],
-        compiler_params=pltpu.CompilerParams(vmem_limit_bytes=48 * 2**20),
+        compiler_params=pltpu.CompilerParams(vmem_limit_bytes=32 * 2**20),
+        cost_estimate=cost(30),
         name="attend_forward",
     )(at, query, key, value_t)
 
@@ -387,10 +412,10 @@
     at_ref, q_ref, do_ref, o_ref, lse_ref, k_ref, kt_ref, v_ref, cos_ref, sin_ref,
     dq_ref, dk_ref, dv_ref, dk_sum, dv_sum,
 ):
-    index = pl.program_id(1)
+    index = pl.program_id(0)
     query = q_ref[...]
     upstream = do_ref[...]
-    lse = lse_ref[0]
+    lse = lse_ref[...]
     product = upstream.astype(full) * o_ref[...].astype(full)
     delta = jnp.sum(product.T, axis=0, keepdims=True)
     scale = HEAD_DIM ** (-0.5)
@@ -419,7 +444,7 @@
     acc = attend_tiles(index, chunk, jnp.zeros((HEAD_DIM, CONT), full))
     dq_ref[...] = turn(acc.T * scale, cos_ref[span_now, :], -sin_ref[span_now, :]).astype(low)
 
-    @pl.when(index == pl.num_programs(1) - 1)
+    @pl.when(index == pl.num_programs(0) - 1)
     def _():
         def finish(step, carry):
             span = pl.ds(pl.multiple_of(step * CONT, CONT), CONT)
@@ -429,34 +454,33 @@
             dv_ref[span, :] = dv_sum[span, :].astype(low)
             return carry
 
-        lax.fori_loop(0, pl.num_programs(1), finish, 0)
-
-
-def attention_backward(query, upstream, attended, lse, key, key_t, value, cosine, sine, at):
-    rows, width = query.shape
-    heads = width // HEAD_DIM
-    tile = pl.BlockSpec((CONT, HEAD_DIM), lambda h, i, at: (i, h))
-    stored = pl.BlockSpec((CONT, HEAD_DIM), lambda h, i, at: (at[i], h))
-    whole = pl.BlockSpec((rows, HEAD_DIM), lambda h, i, at: (0, h))
-    table = pl.BlockSpec((rows, HEAD_DIM), lambda h, i, at: (0, 0))
-    grad = jax.ShapeDtypeStruct((rows, width), low)
+        lax.fori_loop(0, pl.num_programs(0), finish, 0)
+
+
+def attention_backward(query, upstream, attended, lse, key, key_t, value, cosine, sine, at, head):
+    rows = query.shape[0]
+    tile = pl.BlockSpec((CONT, HEAD_DIM), lambda i, at: (i, head))
+    stored = pl.BlockSpec((CONT, HEAD_DIM), lambda i, at: (at[i], 0))
+    whole = pl.BlockSpec((rows, HEAD_DIM), lambda i, at: (0, head))
+    table = pl.BlockSpec((rows, HEAD_DIM), lambda i, at: (0, 0))
+    grad = jax.ShapeDtypeStruct((rows, HEAD_DIM), low)
     return pl.pallas_call(
         backward_kernel,
         grid_spec=pltpu.PrefetchScalarGridSpec(
             num_scalar_prefetch=1,
-            grid=(heads, rows // CONT),
+            grid=(rows // CONT,),
             in_specs=[
                 tile,
                 stored,
                 stored,
-                pl.BlockSpec((1, 1, CONT), lambda h, i, at: (h, 0, i)),
+                pl.BlockSpec((1, CONT), lambda i, at: (0, i)),
                 whole,
-                pl.BlockSpec((HEAD_DIM, rows), lambda h, i, at: (h, 0)),
+                pl.BlockSpec((HEAD_DIM, rows), lambda i, at: (head, 0)),
                 whole,
                 table,
                 table,
             ],
-            out_specs=[tile, whole, whole],
+            out_specs=[pl.BlockSpec((CONT, HEAD_DIM), lambda i, at: (i, 0)), table, table],
             scratch_shapes=[
                 pltpu.VMEM((rows, HEAD_DIM), full),
                 pltpu.VMEM((rows, HEAD_DIM), full),
@@ -464,6 +488,7 @@
         ),
         out_shape=[grad, grad, grad],
         compiler_params=pltpu.CompilerParams(vmem_limit_bytes=48 * 2**20),
+        cost_estimate=cost(38),
         name="attend_backward",
     )(at, query, upstream, attended, lse, key, key_t, value, cosine, sine)
 
@@ -497,59 +522,61 @@
     return plan, [(half, m, 1) for m in held[0] for half in (0, 1)]
 
 
-def gather_kernel(count, with_small, *refs):
-    if with_small:
-        x_ref, small_ref, out_ref, small_out, send_sems, recv_sems, own_sems = refs
-    else:
-        x_ref, out_ref, send_sems, recv_sems, own_sems = refs
+def gather_kernel(count, big, with_small, *refs):
+    ins = refs[: big + with_small]
+    outs = refs[big + with_small : 2 * (big + with_small)]
+    send_sems, recv_sems, own_sems = refs[2 * (big + with_small) :]
     me = lax.axis_index("ctx")
     dp = lax.axis_index("dp")
     bits = bit_orders(count)[0] + [1]
-    rows = x_ref.shape[0] // 2
+    rows = ins[0].shape[0] // 2
     barrier = pltpu.get_barrier_semaphore()
     for bit in bits:
         pl.semaphore_signal(
             barrier, inc=1, device_id=(dp, me ^ bit), device_id_type=pl.DeviceIdType.MESH
         )
     pl.semaphore_wait(barrier, len(bits))
-    spots = [out_ref.at[i] for i in range(2 * count)]
+    own, spots = [], []
+    for a in range(big):
+        for half in (0, 1):
+            own.append(ins[a].at[pl.ds(half * rows, rows)])
+            spots.append([outs[a].at[2 * m + half] for m in range(count)])
     if with_small:
-        spots += [small_out.at[m] for m in range(count)]
-    own = [x_ref.at[pl.ds(0, rows)], x_ref.at[pl.ds(rows, rows)]]
-    local = [pltpu.make_async_copy(own[h], spots[h], own_sems.at[h]) for h in (0, 1)]
-    if with_small:
-        own.append(small_ref)
-        local.append(pltpu.make_async_copy(small_ref, spots[2 * count], own_sems.at[2]))
+        own.append(ins[big])
+        spots.append([outs[big].at[m] for m in range(count)])
+    local = [
+        pltpu.make_async_copy(own[t], spots[t][0], own_sems.at[t]) for t in range(len(own))
+    ]
     for copy in local:
         copy.start()
-
-    def spot(half, m):
-        return 2 * count + m if half == 2 else 2 * m + half
-
     copies = {}
     waited = set()
 
-    def send(half, m, bit):
-        if m and (half, m) not in waited:
-            copies[(half, m)].wait_recv()
-            waited.add((half, m))
-        lands = spot(half, m ^ bit)
+    def send(track, m, bit):
+        if m and (track, m) not in waited:
+            copies[(track, m)].wait_recv()
+            waited.add((track, m))
+        lands = track * count + (m ^ bit)
         copy = pltpu.make_async_remote_copy(
-            src_ref=spots[spot(half, m)] if m else own[half],
-            dst_ref=spots[lands],
+            src_ref=spots[track][m] if m else own[track],
+            dst_ref=spots[track][m ^ bit],
             send_sem=send_sems.at[lands],
             recv_sem=recv_sems.at[lands],
             device_id=(dp, me ^ bit),
             device_id_type=pl.DeviceIdType.MESH,
         )
         copy.start()
-        copies[(half, m ^ bit)] = copy
-
-    far, near = gather_plan(count)
+        copies[(track, m ^ bit)] = copy
+
+    plan_far, plan_near = gather_plan(count)
+    far, near = [], []
     if with_small:
-        small_far = [(2, m, bit) for half, m, bit in far if half == 0]
-        small_near = [(2, m, bit) for half, m, bit in near if half == 0]
-        far, near = far + small_far, near + small_near
+        far += [(2 * big, m, bit) for half, m, bit in plan_far if half == 0]
+        near += [(2 * big, m, bit) for half, m, bit in plan_near if half == 0]
+    for half, m, bit in plan_far:
+        far += [(2 * a + half, m, bit) for a in range(big)]
+    for half, m, bit in plan_near:
+        near += [(2 * a + half, m, bit) for a in range(big)]
     done = set()
     for entry in far:
         send(*entry)
@@ -569,30 +596,30 @@
         copy.wait()
 
 
-def gather_now(values, small=None, collective_id=0):
+def gather_now(arrays, small, collective_id, microseconds):
     count = lax.axis_size("ctx")
-    rows, width = values.shape
-    arrays = [values] if small is None else [values, small]
-    shapes = [jax.ShapeDtypeStruct((2 * count, rows // 2, width), values.dtype)]
-    places = 2 * count
-    if small is not None:
-        shapes.append(jax.ShapeDtypeStruct((count, *small.shape), small.dtype))
-        places += count
+    shapes = [
+        jax.ShapeDtypeStruct((2 * count, x.shape[0] // 2, x.shape[1]), x.dtype) for x in arrays
+    ]
+    shapes.append(jax.ShapeDtypeStruct((count, *small.shape), small.dtype))
+    tracks = 2 * len(arrays) + 1
     return pl.pallas_call(
-        functools.partial(gather_kernel, count, small is not None),
-        in_specs=[pl.BlockSpec(memory_space=pl.ANY)] * len(arrays),
-        out_specs=[pl.BlockSpec(memory_space=pl.ANY)] * len(arrays),
+        functools.partial(gather_kernel, count, len(arrays), 1),
+        in_specs=[pl.BlockSpec(memory_space=pl.ANY)] * len(shapes),
+        out_specs=[pl.BlockSpec(memory_space=pltpu.HBM)] * len(arrays)
+        + [pl.BlockSpec(memory_space=pl.ANY)],
         out_shape=shapes,
         scratch_shapes=[
-            pltpu.SemaphoreType.DMA((places,)),
-            pltpu.SemaphoreType.DMA((places,)),
-            pltpu.SemaphoreType.DMA((3,)),
+            pltpu.SemaphoreType.DMA((tracks * count,)),
+            pltpu.SemaphoreType.DMA((tracks * count,)),
+            pltpu.SemaphoreType.DMA((tracks,)),
         ],
         compiler_params=pltpu.CompilerParams(
             collective_id=collective_id, has_side_effects=True, vmem_limit_bytes=4 * 2**20
         ),
+        cost_estimate=cost(microseconds),
         name="gather_rows",
-    )(*arrays)
+    )(*arrays, small)
 
 
 def split_rows(values, parts):
@@ -661,6 +688,116 @@
     return jnp.concatenate([half[0] for half in held], axis=0)
 
 
+def scatter_kernel(count, odd_ref, even_ref, out_ref, sums, came, near_sems, far_send, far_recv):
+    me = lax.axis_index("ctx")
+    dp = lax.axis_index("dp")
+    orders = bit_orders(count)
+    bits = orders[0] + [1]
+    parts = count // 2
+    rows = even_ref.shape[2]
+    tile = min(32, rows)
+    barrier = pltpu.get_barrier_semaphore()
+    for bit in bits:
+        pl.semaphore_signal(
+            barrier, inc=1, device_id=(dp, me ^ bit), device_id_type=pl.DeviceIdType.MESH
+        )
+    pl.semaphore_wait(barrier, len(bits))
+    first = sorted(range(parts), key=lambda n: -bin(n).count("1"))
+    near = {}
+    for n in first:
+        near[n] = pltpu.make_async_remote_copy(
+            src_ref=odd_ref.at[n],
+            dst_ref=sums.at[n],
+            send_sem=near_sems.at[0, n],
+            recv_sem=near_sems.at[1, n],
+            device_id=(dp, me ^ 1),
+            device_id_type=pl.DeviceIdType.MESH,
+        )
+        near[n].start()
+
+    def add(into, left, right):
+        def body(step, carry):
+            span = pl.ds(pl.multiple_of(step * tile, tile), tile)
+            total = left[span, :].astype(full) + right[span, :].astype(full)
+            into[span, :] = total.astype(into.dtype)
+            return carry
+
+        lax.fori_loop(0, rows // tile, body, 0)
+
+    far = []
+    used = [0, 0]
+
+    def send(half, n, bit):
+        place = used[half]
+        used[half] += 1
+        copy = pltpu.make_async_remote_copy(
+            src_ref=sums.at[n, half],
+            dst_ref=came.at[half, place],
+            send_sem=far_send.at[half, place],
+            recv_sem=far_recv.at[half, place],
+            device_id=(dp, me ^ bit),
+            device_id_type=pl.DeviceIdType.MESH,
+        )
+        copy.start()
+        far.append(copy)
+        return copy, place
+
+    pending = [{}, {}]
+    for n in first:
+        near[n].wait_recv()
+        for half in (0, 1):
+            add(sums.at[n, half], sums.at[n, half], even_ref.at[n, half])
+            bit = orders[half][0]
+            if 2 * n & bit:
+                pending[half][n] = send(half, n, bit)
+    depth_count = len(orders[0])
+    for depth in range(depth_count):
+        later = [{}, {}]
+        waiting = [(half, n) for k in range(parts) for half in (0, 1) for n in list(pending[half])[k : k + 1]]
+        for half, n in waiting:
+            copy, place = pending[half][n]
+            keep = n ^ (orders[half][depth] >> 1)
+            copy.wait_recv()
+            if depth + 1 == depth_count:
+                add(out_ref.at[half], sums.at[keep, half], came.at[half, place])
+            else:
+                add(sums.at[keep, half], sums.at[keep, half], came.at[half, place])
+                bit = orders[half][depth + 1]
+                if 2 * keep & bit:
+                    later[half][keep] = send(half, keep, bit)
+        pending = later
+    for n in first:
+        near[n].wait_send()
+    for copy in far:
+        copy.wait_send()
+
+
+def scatter_now(odd, even, collective_id):
+    count = lax.axis_size("ctx")
+    parts = count // 2
+    rows = odd.shape[0] // parts // 2
+    shape = (parts, 2, rows, odd.shape[1])
+    out = pl.pallas_call(
+        functools.partial(scatter_kernel, count),
+        in_specs=[pl.BlockSpec(memory_space=pl.ANY), pl.BlockSpec(memory_space=pltpu.VMEM)],
+        out_specs=pl.BlockSpec(memory_space=pltpu.VMEM),
+        out_shape=jax.ShapeDtypeStruct((2, rows, odd.shape[1]), full),
+        scratch_shapes=[
+            pltpu.VMEM(shape, low),
+            pltpu.VMEM((2, parts - 1, rows, odd.shape[1]), low),
+            pltpu.SemaphoreType.DMA((2, parts)),
+            pltpu.SemaphoreType.DMA((2, parts - 1)),
+            pltpu.SemaphoreType.DMA((2, parts - 1)),
+        ],
+        compiler_params=pltpu.CompilerParams(
+            collective_id=collective_id, has_side_effects=True, vmem_limit_bytes=40 * 2**20
+        ),
+        cost_estimate=cost(90),
+        name="scatter_rows",
+    )(odd.reshape(shape), even.reshape(shape))
+    return out.reshape(2 * rows, odd.shape[1])
+
+
 def advance(steps, came):
     try:
         return (steps.send(came), None)
@@ -673,6 +810,10 @@
     while value is None:
         came, value = advance(steps, came)
     return value
+
+
+def over_dp(grad, dim):
+    return lax.psum_scatter(grad, "dp", scatter_dimension=dim, tiled=True)
 
 
 def odd_first(step, count):
@@ -753,7 +894,16 @@
     origin = (dp_index - jnp.arange(dp_count, dtype=jnp.int32)) % dp_count
     small = jnp.take(jnp.stack(around), origin, axis=0).reshape(-1)
     small = jnp.pad(small, (0, small_rows * HEAD_DIM - small.shape[0])).reshape(small_rows, HEAD_DIM)
-    x_blocks, small_all = gather_now(tokens_low, small, 0)
+    w_out, small = lax.optimization_barrier((w_out, small))
+    out_around = jnp.stack(
+        [w_out]
+        + [
+            lax.ppermute(w_out, "dp", [(i, (i + k) % dp_count) for i in range(dp_count)])
+            for k in range(1, dp_count)
+        ]
+    )
+    x_blocks, cot_all, small_all = gather_now([tokens_low, cot_low], small, 0, 145)
+    cot_all = cot_all.reshape(group_len, D)
     small_all = small_all.reshape(ctx_count, -1)[:, : dp_count * small_count * shard]
     small_all = jnp.take(small_all, partners, axis=0)
     small_all = (
@@ -763,11 +913,12 @@
     )
     gain_one, gain_two, mix_row = small_all[0:1], small_all[4:5], small_all[5:6]
     mix_router = small_all[5:].astype(low)
-    w_out, qkv_parts = lax.optimization_barrier((w_out, qkv_parts))
-    out_mine = lax.all_gather(w_out, "dp", axis=0, tiled=True)
-    (cot_low, out_mine), x_blocks = pin([cot_low, out_mine], x_blocks)
-    cot_steps, out_steps = gather_steps(cot_low), gather_steps(out_mine)
-    came = next(cot_steps) + next(out_steps)
+    out_mine = jnp.concatenate(
+        [lax.dynamic_index_in_dim(out_around, origin[p], 0, False) for p in range(dp_count)], axis=0
+    )
+    (out_mine,), x_blocks = pin([out_mine], x_blocks)
+    out_steps = gather_steps(out_mine)
+    out_came = next(out_steps)
     shared_gate, shared_up, shared_down = (
         lax.all_gather(sh_gate.T, "dp", axis=0, tiled=True),
         lax.all_gather(sh_up.T, "dp", axis=0, tiled=True),
@@ -805,29 +956,32 @@
     place_to_near = (place_to_stored // per_device ^ ctx_index) * per_device + (
         place_to_stored % per_device
     )
-    cosine, sine = rope_tables(jnp.arange(group_len, dtype=jnp.int32))
+    cosine_wide, sine_wide = rope_tables(group_len)
     my_heads = (ctx_index // repeat) * width
     scale_one = rms_scale(tokens)
     bias = lax.dynamic_slice_in_dim(small_all[1:4], my_heads, width, 1).reshape(1, 3 * width)
-    cosine_wide = jnp.concatenate([cosine[:, 0], cosine[:, 0]], axis=1)
-    sine_wide = jnp.concatenate([-sine[:, 0], sine[:, 0]], axis=1)
     normed_sorted, query, key, value = project(
         x_blocks, stored_near, gain_one, w_qkv, bias, cosine_wide, sine_wide
     )
     tiles = group_len // CONT
     direct = block_count == tiles
     at = place_to_stored if direct else jnp.arange(tiles, dtype=jnp.int32)
-    (*came, value), query = pin([*came, value], query)
-    cot_came, cot_all = advance(cot_steps, came[:2])
-    out_came, out_parts = advance(out_steps, came[2:])
-    came = cot_came + out_came
-    attended_heads, lse = attention_forward(query, key, value.T, at)
-    came, attended_heads = pin(came, attended_heads)
-    split = len(came) // 2
-    attended_stored = attended_heads if direct else take_blocks(attended_heads, stored_to_place)
-    attended_parts = swap_ctx(attended_stored.reshape(ctx_count, tok_count, width))[::repeat]
-    out_parts = finish(out_steps, came[split:])
-    cot_all = finish(cot_steps, came[:split])
+    out_came, query = pin(out_came, query)
+    out_came, out_parts = advance(out_steps, out_came)
+    attended_heads, lses, parts = [], [], []
+    value_t = value.T
+    for head in range(heads):
+        one_head, lse = attention_forward(query, key, value_t, at, head)
+        if head == 0:
+            (*out_came, query), one_head = pin([*out_came, query], one_head)
+            out_came, out_parts = advance(out_steps, out_came)
+        attended_heads.append(one_head)
+        lses.append(lse)
+        stored_head = one_head if direct else take_blocks(one_head, stored_to_place)
+        parts.append(swap_ctx(stored_head.reshape(ctx_count, tok_count, HEAD_DIM))[::repeat])
+    if out_parts is None:
+        out_came, parts[-1] = pin(out_came, parts[-1]) if heads == 1 else (out_came, parts[-1])
+        out_parts = finish(out_steps, out_came)
     out_parts = out_parts.reshape(ctx_count, dp_count, shard, D)
     out_full = (
         jnp.stack(
@@ -835,6 +989,7 @@
             axis=1,
         )
     ).reshape(D, D)
+    attended_parts = jnp.stack(parts, axis=2).reshape(head_sets, tok_count, width)
     attended = attended_parts.transpose(1, 0, 2).reshape(tok_count, D)
     first_sum = tokens + dot(attended, out_full)
     scale_two = rms_scale(first_sum)
@@ -847,7 +1002,7 @@
     gates_mine = raised / jnp.sum(raised, axis=1, keepdims=True)
     narrow = jnp.concatenate([mix_mine.T, gates_mine.T, code.astype(full)], axis=0)
     narrow = jnp.pad(narrow, ((0, -narrow.shape[0] % 8), (0, 0)))
-    all_normed, narrow_all = gather_now(normed_two, narrow, 1)
+    all_normed, narrow_all = gather_now([normed_two], narrow, 1, 75)
     all_normed = all_normed.reshape(group_len, D)
     mix_all = narrow_all[:, 0].reshape(group_len, 1)
     gate_mine = lax.dynamic_index_in_dim(narrow_all, ctx_index + 1, 1, keepdims=False)
@@ -862,7 +1017,9 @@
         )
     )
     grad_egate = ein("crd,crf->df", expert_rows, gate_grad).astype(low)
-    dx_routed, grad_egate = lax.optimization_barrier((dx_routed, grad_egate))
+    grad_eup = ein("crd,crf->df", expert_rows, up_grad).astype(low)
+    dx_routed, grad_egate, grad_eup = lax.optimization_barrier((dx_routed, grad_egate, grad_eup))
+    sum_egate, sum_eup = over_dp(grad_egate, 0), over_dp(grad_eup, 0)
     mix_cot, shared_low, shared_dg, shared_du, mix_share, dx_odd, dx_even, out_odd, out_even = (
         shared_expert(
             all_normed, cot_all, mix_all, shared_gate, shared_up, shared_down,
@@ -871,20 +1028,20 @@
     )
     dx_steps = scatter_steps(dx_odd, dx_even)
     came = next(dx_steps)
-    grad_eup = ein("crd,crf->df", expert_rows, up_grad).astype(low)
-    came, grad_eup, hidden_low, shared_low, shared_dg, shared_du = pin(
-        came, grad_eup, hidden_low, shared_low, shared_dg, shared_du
-    )
+    grad_edown = ein("crf,crd->fd", hidden_low, slot_grads).astype(low)
+    came, grad_edown, sum_egate, shared_low, shared_dg, shared_du = pin(
+        came, grad_edown, sum_egate, shared_low, shared_dg, shared_du
+    )
+    sum_edown = over_dp(grad_edown, 1)
     came, dx_mine = advance(dx_steps, came)
-    grad_edown = ein("crf,crd->fd", hidden_low, slot_grads).astype(low)
     grad_sdown = ein("tf,td->fd", shared_low, mix_cot).astype(low)
-    came, grad_edown, grad_sdown, shared_dg, shared_du = pin(
-        came, grad_edown, grad_sdown, shared_dg, shared_du
-    )
+    grad_sgate = ein("tf,td->fd", shared_dg, all_normed).astype(low)
+    came, grad_sdown, grad_sgate, shared_du = pin(came, grad_sdown, grad_sgate, shared_du)
+    sum_sdown, sum_sgate = over_dp(grad_sdown, 0), over_dp(grad_sgate, 0)
     came, dx_mine = advance(dx_steps, came)
-    grad_sgate = ein("tf,td->fd", shared_dg, all_normed).astype(low)
     grad_sup = ein("tf,td->fd", shared_du, all_normed).astype(low)
-    came, grad_sgate, grad_sup = pin(came, grad_sgate, grad_sup)
+    came, grad_sup = pin(came, grad_sup)
+    sum_sup = over_dp(grad_sup, 0)
     dx_mine = finish(dx_steps, came).astype(full)
 
     shares = jnp.stack([gate_share[:, 0], mix_share.reshape(ctx_count, tok_count)], axis=1)
@@ -908,54 +1065,86 @@
     first_grad = cot_full + norm_grad_two
     first_low = first_grad.astype(low)
     attended_grad = dot_nt(first_low, out_full).astype(low)
-    grad_out = ein("td,te->de", attended, first_low)
-
-    upstream_parts = attended_grad.reshape(tok_count, head_sets, width).transpose(1, 0, 2)
+    grad_out = ein("td,te->de", attended, first_low).astype(low)
+
+    upstream_parts = attended_grad.reshape(tok_count, head_sets, heads, HEAD_DIM)
+    upstream_parts = [upstream_parts[:, :, head].transpose(1, 0, 2) for head in range(heads)]
     if repeat > 1:
-        upstream_parts = jnp.repeat(upstream_parts, repeat, axis=0)
-    came, upstream_parts = pin(came, upstream_parts)
+        upstream_parts = [jnp.repeat(part, repeat, axis=0) for part in upstream_parts]
+    came, upstream_parts[0], sum_eup = pin(came, upstream_parts[0], sum_eup)
     came, added = advance(add_steps, came)
-    upstream = swap_ctx(upstream_parts).reshape(group_len, width)
-    if not direct:
-        upstream = take_blocks(upstream, place_to_stored)
-    qkv_grads = attention_backward(
-        query, upstream, attended_heads, lse, key, key.T, value, cosine_wide, sine_wide, at
-    )
-    (*came, value_grad), key_grad, query_grad = pin([*came, qkv_grads[2]], qkv_grads[1], qkv_grads[0])
-    qkv_grads = [query_grad, key_grad, value_grad]
+    upstreams = [swap_ctx(part).reshape(group_len, HEAD_DIM) for part in upstream_parts]
+    (grad_out,), upstreams[0] = pin([grad_out], upstreams[0])
+    grad_out = grad_out.reshape(dp_count, ctx_count, shard, D)
+
+    def out_rows_of(first):
+        return jnp.concatenate(
+            [
+                lax.dynamic_index_in_dim(grad_out, partners[m], 1, False).reshape(-1, D)
+                for m in range(first, ctx_count, 2)
+            ],
+            axis=0,
+        )
+
+    wout_steps = scatter_steps(out_rows_of(1), out_rows_of(0))
+    wout_came = next(wout_steps)
+    key_t = key.T
+    head_grads = []
+    for head in range(heads):
+        upstream = upstreams[head] if direct else take_blocks(upstreams[head], place_to_stored)
+        grads = attention_backward(
+            query, upstream, attended_heads[head], lses[head], key, key_t, value,
+            cosine_wide, sine_wide, at, head,
+        )
+        grads = list(grads)
+        if head == 0:
+            wout_came, grads[0] = pin(wout_came, grads[0])
+            wout_came, wout = advance(wout_steps, wout_came)
+        head_grads.append(grads)
+    came, last, sum_edown = pin(came, head_grads[-1][0], sum_edown)
+    head_grads[-1][0] = last
     came, added = advance(add_steps, came)
+    qkv_grads = jnp.concatenate(
+        [head_grads[head][kind] for kind in range(3) for head in range(heads)], axis=1
+    )
     if repeat > 1:
-        qkv_grads = [jnp.where(ctx_index % repeat == 0, g, jnp.zeros_like(g)) for g in qkv_grads]
-    grad_qkv = jnp.concatenate(
-        [ein("td,te->de", normed_sorted, g).astype(low) for g in qkv_grads], axis=1
-    )
-    bias_sums = jnp.stack([jnp.sum(g.astype(full), axis=0) for g in qkv_grads])
+        qkv_grads = jnp.where(ctx_index % repeat == 0, qkv_grads, jnp.zeros_like(qkv_grads))
+    wout_came, qkv_grads = pin(wout_came, qkv_grads)
+    wout_came, wout = advance(wout_steps, wout_came)
+    grad_qkv = ein("td,te->de", normed_sorted, qkv_grads).astype(low)
+    bias_sums = jnp.sum(qkv_grads.astype(full), axis=0).reshape(3, width)
     grad_bias = lax.dynamic_update_slice_in_dim(
         jnp.zeros((3, D), full), bias_sums, my_heads, 1
     )
-    grad_qkv, first_grads = lax.optimization_barrier((grad_qkv, qkv_grads[0]))
-    odd_one, even_one = unproject([first_grads, *qkv_grads[1:]], stored_near, w_qkv, per_device)
-    came, odd_one = pin(came, odd_one)
+    came, grad_qkv, qkv_grads = pin(came, grad_qkv, qkv_grads)
+    odd_one, even_one, gain_sums = unproject(
+        qkv_grads, stored_near, w_qkv, normed_sorted, per_device
+    )
+    grad_gain_one = gain_sums[0] / gain_one[0]
     added = finish(add_steps, came)
     layer_out = first_sum + added.astype(full)
-    one_steps = scatter_steps(odd_one, even_one)
-    dx_one = finish(one_steps, next(one_steps)).astype(full)
-    norm_grad_one, grad_gain_one = norm_back(tokens, scale_one, gain_one, dx_one)
-    input_grad = first_grad + norm_grad_one
-
+    wout_came, odd_one = pin(wout_came, odd_one)
+    wout = finish(wout_steps, wout_came)
+    (wout,), odd_one, sum_sdown = pin([wout], odd_one, sum_sdown)
     qkv_rows = lax.psum_scatter(
         grad_qkv.reshape(dp_count, ctx_count, shard, 3 * width),
         "dp",
         scatter_dimension=0,
         tiled=True,
     )[0]
+    wout_rows = lax.psum_scatter(
+        wout.reshape(dp_count, shard, D), "dp", scatter_dimension=0, tiled=True
+    )[0]
+    dx_one = scatter_now(odd_one, even_one, 2)
+    (sum_sgate, sum_sup, qkv_rows, wout_rows), dx_one = pin(
+        [sum_sgate, sum_sup, qkv_rows, wout_rows], dx_one
+    )
+    norm_grad_one, _ = norm_back(tokens, scale_one, gain_one, dx_one)
+    input_grad = first_grad + norm_grad_one
+
     qkv_mine = swap_ctx(qkv_rows)[::repeat].astype(full)
     qkv_mine = qkv_mine.reshape(head_sets, shard, 3, width).transpose(2, 1, 0, 3).reshape(3, shard, D)
-    out_rows = swap_ctx(
-        grad_out.astype(low).reshape(dp_count, ctx_count, shard, D).transpose(1, 0, 2, 3)
-    )
-    out_rows = jnp.sum(out_rows.astype(full), axis=0).astype(low)
-    grad_wout = lax.psum_scatter(out_rows, "dp", scatter_dimension=0, tiled=True)[0].astype(full)
+    grad_wout = wout_rows.astype(full)
     small_grads = jnp.concatenate(
         [grad_gain_one[None], grad_bias, grad_gain_two[None], grad_narrow], axis=0
     )
@@ -964,11 +1153,6 @@
     small_grads = jnp.sum(
         lax.all_to_all(small_grads, "dp", split_axis=0, concat_axis=0, tiled=True), axis=0
     ).T
-
-    def over_dp(grad, dim):
-        return lax.psum_scatter(
-            grad.astype(low), "dp", scatter_dimension=dim, tiled=True
-        ).astype(full)
 
     return (
         layer_out.astype(low)[None],
@@ -983,12 +1167,12 @@
         grad_wout,
         small_grads[:, 4],
         small_grads[:, 6:],
-        over_dp(grad_egate, 0)[None],
-        over_dp(grad_eup, 0)[None],
-        over_dp(grad_edown, 1)[None],
-        over_dp(grad_sgate, 0).T,
-        over_dp(grad_sup, 0).T,
-        over_dp(grad_sdown, 0),
+        sum_egate.astype(full)[None],
+        sum_eup.astype(full)[None],
+        sum_edown.astype(full)[None],
+        sum_sgate.astype(full).T,
+        sum_sup.astype(full).T,
+        sum_sdown.astype(full),
         small_grads[:, 5],
     )
 

time: 1430 us -> 1340 us (0.937)
  waiting for transfers between devices: 281 us -> 67.6 us
  Pallas kernels: 580 us -> 731 us
  other arithmetic: 156 us -> 113 us
    all_to_all x6 -> x7, waiting for transfers between devices: 159 us -> 10.7 us  [swap_ctx(): lax.all_to_all(values, 'ctx', split_axis=0, concat_axis=0, tiled=True)]
    pallas_call x2 -> x3, Pallas kernels: 155 us -> 302 us  [the longest x2 223 us: gather_now(): pl.pallas_call(functools.partial(gather_kernel, count, len(arrays), 1), i...]
    ppermute x25 -> x20, waiting for transfers between devices: 101 us -> 52.2 us  [exchange(): return lax.ppermute(values, 'ctx', [(i, i ^ bit) for i in range(count)])]
    unnamed x171 -> x246, local copies, waits for them, and re-layouts: 46.8 us -> 69.7 us
    reduce_scatter x1, waiting for transfers between devices: 16.3 us -> 0.02 us  [on_device(): lax.psum_scatter(grad_qkv.reshape(dp_count, ctx_count, shard, 3 * width),...]
    convert_element_type x10 -> x9, other arithmetic: 46.1 us -> 38 us  [add_low(): return (left.astype(full) + right.astype(full)).astype(low)]
    dot_general x11 -> x9, matrix products: 156 us -> 152 us  [ein(): return jnp.einsum(spec, left, right, preferred_element_type=full)]
    pallas_call x1 -> x2, Pallas kernels: 61 us -> 59.3 us  [attention_forward(): pl.pallas_call(forward_kernel, grid_spec=pltpu.PrefetchScalarGridSpec(num...]
  transfers between devices with their start and end apart: 51 -> 49, of which waited for: 13 -> 10; matrix products, arithmetic and copies ran while one was open for 28% -> 25% of each run, Pallas kernels for 34% -> 55%
where the time goes in v3:
time: 1340 us; the launch traced here: 1330 us
  Pallas kernels  731 us (55%)
  matrix products  165 us (12%)
  local copies, waits for them, and re-layouts  117 us (9%)
  other arithmetic  113 us (8%)
  waiting for transfers between devices  67.6 us (5%)
  starting transfers between devices  61.7 us (5%)
  between operations  54.9 us (4%)
  blocking collectives  17.8 us (1%)
    pallas_call x2, Pallas kernels, gather_now(): pl.pallas_call(functools.partial(gather_kernel, count, len(arrays), 1), i...  223 us
    dot_general x9, matrix products, ein(): return jnp.einsum(spec, left, right, preferred_element_type=full)  152 us
    pallas_call x1, Pallas kernels, routed_expert(): pl.pallas_call(expert_kernel, grid=(count,), in_specs=[chunk, chunk, line...  141 us
    pallas_call x1, Pallas kernels, shared_expert(): pl.pallas_call(shared_kernel, grid=(count,), in_specs=[chunk, chunk, colu...  104 us
    pallas_call x1, Pallas kernels, scatter_now(): pl.pallas_call(functools.partial(scatter_kernel, count), in_specs=[pl.Blo...  79.1 us
    pallas_call x2, Pallas kernels, attention_backward(): pl.pallas_call(backward_kernel, grid_spec=pltpu.PrefetchScalarGridSpec(nu...  76.2 us
    unnamed x246, local copies, waits for them, and re-layouts  69.7 us
    pallas_call x2, Pallas kernels, attention_forward(): pl.pallas_call(forward_kernel, grid_spec=pltpu.PrefetchScalarGridSpec(num...  59.3 us
  transfers between devices with their start and end apart: 49, of which 10 were waited for; matrix products, arithmetic and copies ran while one was open for 25% of the time, Pallas kernels for 55%

profile of v3, /device:TPU:0, one launch (start us, length us, event | category | flops | bytes accessed | tf_op | source)
XLA Modules:
  0.0 1328.5 jit_solution(3624879051780933011)
XLA Ops:
  9.5 17.8 %all_to_all.45 = bf16[8,64,768]{2,1,0:T(8,128)(2,1)} all-to-all(bf16[8,64,768]{2,1,0:T(8,128)(2,1)S(1)} %pad_maximum_fusion.16), channel_id=1, replica_groups=mesh['dp'=4,'ctx'=8] {'ctx'}, dimensions={0} | all-to-all | bytes 1572864 | tf_op jit(solution)/shard_map/all_to_all | solution.py:824
  30.1 3.7 collective-permute-start.2
  62.3 2.8 collective-permute-start.5
  67.9 145.3 %gather_rows.2 = (bf16[16,256,2048]{2,1,0:T(8,128)(2,1)S(1)}, bf16[16,256,2048]{2,1,0:T(8,128)(2,1)S(1)}, f32[8,32,128]{2,1,0:T(8,128)S(1)}) custom-call(bf16[512,2048]{1,0:T(8,128)(2,1)S(1)} %bitcast.332, bf16[512,2048]{1,0:T(8,128)(2,1)S(1)} %bitcast.335, f32[32,128]{1,0:T(8,128)S(1)} %pad_bitcast_fusion.refs_2_), custom_call_target="tpu_custom_call" | custom-call | flops 159499993088 | bytes 478500000 | tf_op jit(solution)/shard_map/gather_rows/pallas_call | solution.py:606
  213.2 5.8 copy-done.33
  218.9 5.8 copy-done.38
  239.5 23.5 %project.1 = (bf16[4096,2048]{1,0:T(8,128)(2,1)}, bf16[4096,256]{1,0:T(8,128)(2,1)S(1)}, bf16[4096,256]{1,0:T(8,128)(2,1)S(1)}, bf16[4096,256]{1,0:T(8,128)(2,1)S(1)}) custom-call(s32[16]{0:T(128)S(1)} %concatenate.111.place_ref, bf16[16,256,2048]{2,1,0:T(8,128)(2,1)} %copy-done.38, f32[1,2048]{1,0:T(1,128)S(1)} %slice.440.gain_ref, ...), custom_call_target="tpu_custom_call" | custom-call | flops 26400000000 | bytes 79200000 | tf_op jit(solution)/shard_map/project/pallas_call | solution.py:129
  267.0 2.5 pad_maximum_fusion.12
  272.8 4.1 copy.186
  281.7 29.6 %attend_forward.2 = (bf16[4096,128]{1,0:T(8,128)(2,1)S(1)}, f32[1,4096]{1,0:T(1,128)S(1)}) custom-call(s32[16]{0:T(128)S(1)} %select_reduce_fusion.1.at_ref, bf16[4096,256]{1,0:T(8,128)(2,1)S(1)} %copy-done.40, bf16[4096,256]{1,0:T(8,128)(2,1)S(1)} %copy-done.8, bf16[256,4096]{1,0:T(8,128)(2,1)S(1)} %bitcast.333), custom_call_target="tpu_custom_call" | custom-call | flops 32999999488 | bytes 99000000 | tf_op jit(solution)/shard_map/attend_forward/pallas_call | solution.py:386
  315.4 3.7 fusion.39
  319.1 29.6 %attend_forward.3 = (bf16[4096,128]{1,0:T(8,128)(2,1)S(1)}, f32[1,4096]{1,0:T(1,128)S(1)}) custom-call(s32[16]{0:T(128)S(1)} %select_reduce_fusion.1.at_ref, bf16[4096,256]{1,0:T(8,128)(2,1)S(1)} %copy-done.40, bf16[4096,256]{1,0:T(8,128)(2,1)S(1)} %copy-done.8, bf16[256,4096]{1,0:T(8,128)(2,1)S(1)} %bitcast.334), custom_call_target="tpu_custom_call" | custom-call | flops 32999999488 | bytes 99000000 | tf_op jit(solution)/shard_map/attend_forward/pallas_call | solution.py:386
  352.0 4.4 all-to-all-start.2
  371.8 4.2 all-to-all-start.1
  376.3 3.5 convert_reduce_fusion
  386.6 4.9 all-to-all-done.1
  393.3 8.3 pad_maximum_fusion
  407.8 5.1 multiply_reduce_fusion.3
  415.4 77.7 %gather_rows.3 = (bf16[16,256,2048]{2,1,0:T(8,128)(2,1)S(1)}, f32[8,24,512]{2,1,0:T(8,128)S(1)}) custom-call(bf16[512,2048]{1,0:T(8,128)(2,1)S(1)} %multiply_convert_fusion.refs_0_, f32[24,512]{1,0:T(8,128)S(1)} %select_maximum_fusion.refs_1_), custom_call_target="tpu_custom_call" | custom-call | flops 82500001792 | bytes 247500000 | tf_op jit(solution)/shard_map/gather_rows/pallas_call | solution.py:606
  493.1 6.0 copy-done.34
  500.4 140.8 %routed_expert.1 = (bf16[8,320,2048]{2,1,0:T(8,128)(2,1)}, bf16[8,320,2048]{2,1,0:T(8,128)(2,1)}, bf16[8,320,1408]{2,1,0:T(8,128)(2,1)}, bf16[8,320,1408]{2,1,0:...) custom-call(bf16[4096,2048]{1,0:T(8,128)(2,1)} %bitcast.344, ...), custom_call_target="tpu_custom_call" | custom-call | flops 153999998976 | bytes 462000000 | tf_op jit(solution)/shard_map/routed_expert/pallas_call | solution.py:259
  641.2 22.2 %bitcast_convert_fusion.2 = bf16[2048,1408]{1,0:T(8,128)(2,1)} fusion(bf16[8,320,2048]{2,1,0:T(8,128)(2,1)} %get-tuple-element.139, bf16[8,320,1408]{2,1,0:T(8,128)(2,1)} %get-tuple-element.140), kind=kOutput, calls=%fused_computation.7 | convolution fusion | flops 14766833664 | bytes 23461888 | tf_op jit(solution)/shard_map/crd,crf->df/dot_general | solution.py:35
  663.4 22.1 %bitcast_convert_fusion.1 = bf16[2048,1408]{1,0:T(8,128)(2,1)} fusion(bf16[8,320,2048]{2,1,0:T(8,128)(2,1)} %get-tuple-element.139, bf16[8,320,1408]{2,1,0:T(8,128)(2,1)} %get-tuple-element.141), kind=kOutput, calls=%fused_computation.6 | convolution fusion | flops 14766833664 | bytes 23461888 | tf_op jit(solution)/shard_map/crd,crf->df/dot_general | solution.py:35
  688.3 104.1 %shared_expert.1 = (bf16[4096,2048]{1,0:T(8,128)(2,1)}, bf16[4096,704]{1,0:T(8,128)(2,1)}, bf16[4096,704]{1,0:T(8,128)(2,1)}, bf16[4096,704]{1,0:T(8,128)(2,1)},...) custom-call(bf16[4096,2048]{1,0:T(8,128)(2,1)} %bitcast.345, ...), custom_call_target="tpu_custom_call" | custom-call | flops 113299996672 | bytes 339900000 | tf_op jit(solution)/shard_map/shared_expert/pallas_call | solution.py:329
  792.9 20.8 %bitcast_convert_fusion = bf16[1408,2048]{1,0:T(8,128)(2,1)} fusion(bf16[8,320,1408]{2,1,0:T(8,128)(2,1)} %get-tuple-element.148, bf16[8,320,2048]{2,1,0:T(8,128)(2,1)} %get-tuple-element.149), kind=kOutput, calls=%fused_computation.5 | convolution fusion | flops 14766833664 | bytes 23461888 | tf_op jit(solution)/shard_map/crf,crd->fd/dot_general | solution.py:35
  813.8 4.8 add_convert_fusion.25
  824.0 17.2 %convolution_convert_fusion.3 = bf16[704,2048]{1,0:T(8,128)(2,1)} fusion(bf16[4096,704]{1,0:T(8,128)(2,1)S(1)} %bitcast.426, bf16[4096,2048]{1,0:T(8,128)(2,1)} %bitcast.346), kind=kOutput, calls=%fused_computation.32 | convolution fusion | flops 11812601856 | bytes 25427968 | tf_op jit(solution)/shard_map/tf,td->fd/dot_general | solution.py:35
  841.2 18.8 %convolution_convert_fusion.4 = bf16[704,2048]{1,0:T(8,128)(2,1)} fusion(bf16[4096,704]{1,0:T(8,128)(2,1)} %get-tuple-element.155, bf16[4096,2048]{1,0:T(8,128)(2,1)} %get-tuple-element.156), kind=kOutput, calls=%fused_computation.33 | convolution fusion | flops 11812601856 | bytes 25427968 | tf_op jit(solution)/shard_map/tf,td->fd/dot_general | solution.py:35
  860.1 8.1 collective-permute-done.12
  872.4 3.7 all-to-all-start.3
  877.2 4.3 copy.200
  881.6 2.8 multiply_reduce_fusion
  886.3 5.5 add_convert_fusion.19
  895.3 18.9 %convolution_convert_fusion.2 = bf16[704,2048]{1,0:T(8,128)(2,1)} fusion(bf16[4096,704]{1,0:T(8,128)(2,1)} %get-tuple-element.161, bf16[4096,2048]{1,0:T(8,128)(2,1)} %bitcast.347), kind=kOutput, calls=%fused_computation.31 | convolution fusion | flops 11812601856 | bytes 25427968 | tf_op jit(solution)/shard_map/tf,td->fd/dot_general | solution.py:35
  914.2 3.4 collective-permute-done.15
  918.9 4.6 add_convert_fusion.18
  930.7 5.7 convolution_convert_fusion.5
  936.4 3.2 reshape.458
  939.6 3.8 fusion.42
  944.8 3.6 all-to-all-start.4
  948.7 3.2 bitcast_convert_fusion.5
  952.5 3.0 copy.239
  955.5 10.8 convolution_convert_fusion
  968.5 37.7 %attend_backward.2 = (bf16[4096,128]{1,0:T(8,128)(2,1)S(1)}, bf16[4096,128]{1,0:T(8,128)(2,1)S(1)}, bf16[4096,128]{1,0:T(8,128)(2,1)S(1)}) custom-call(s32[16]{0:T(128)S(1)} %select_reduce_fusion.1.at_ref, bf16[4096,256]{1,0:T(8,128)(2,1)} %copy-done.39, bf16[4096,128]{1,0:T(8,128)(2,1)S(1)} %bitcast.339, bf16[4096,128]{1,0:T(8,128)(2,1)S(1)} %copy-done.14, ...), custom_call_target="tpu_custom_call" | custom-call | flops 41799999488 | bytes 125400000 | tf_op jit(solution)/shard_map/attend_backward/pallas_call | solution.py:467
  1008.1 4.1 all-to-all-start.5
  1012.7 4.4 add_convert_fusion.11
  1025.5 2.7 all-to-all-done.5
  1028.2 3.1 constant_dynamic-slice_fusion.9
  1033.7 38.5 %attend_backward.3 = (bf16[4096,128]{1,0:T(8,128)(2,1)S(1)}, bf16[4096,128]{1,0:T(8,128)(2,1)S(1)}, bf16[4096,128]{1,0:T(8,128)(2,1)S(1)}) custom-call(s32[16]{0:T(128)S(1)} %select_reduce_fusion.1.at_ref, bf16[4096,256]{1,0:T(8,128)(2,1)} %copy-done.39, bf16[4096,128]{1,0:T(8,128)(2,1)S(1)} %bitcast.338, bf16[4096,128]{1,0:T(8,128)(2,1)S(1)} %get-tuple-element.130.o_ref, ...), custom_call_target="tpu_custom_call" | custom-call | flops 41799999488 | bytes 125400000 | tf_op jit(solution)/shard_map/attend_backward/pallas_call | solution.py:467
  1076.0 5.7 add_convert_fusion.5
  1092.2 37.3 %collective-permute-done.22 = bf16[256,2048]{1,0:T(8,128)(2,1)S(1)} collective-permute-done((bf16[256,2048]{1,0:T(8,128)(2,1)S(1)}, bf16[256,2048]{1,0:T(8,128)(2,1)S(1)}, u32[]{:S(2)}, u32[]{:S(2)}) %collective-permute-start.22) | collective-permute-done | bytes 1048608 | tf_op jit(solution)/shard_map/ppermute | solution.py:510
  1131.7 3.0 add_convert_fusion.32
  1136.3 20.5 %convolution_convert_fusion.1 = bf16[2048,768]{1,0:T(8,128)(2,1)} fusion(bf16[4096,2048]{1,0:T(8,128)(2,1)} %get-tuple-element.175.normed_ref, bf16[4096,768]{1,0:T(8,128)(2,1)} %copy-done.4), kind=kOutput, calls=%fused_computation.30 | convolution fusion | flops 12886474752 | bytes 26214400 | tf_op jit(solution)/shard_map/td,te->de/dot_general | solution.py:35
  1156.8 25.2 %unproject.1 = (bf16[2048,2048]{1,0:T(8,128)(2,1)}, bf16[2048,2048]{1,0:T(8,128)(2,1)}, f32[1,2048]{1,0:T(1,128)S(1)}) custom-call(s32[16]{0:T(128)S(1)} %copy-done.30, bf16[4096,768]{1,0:T(8,128)(2,1)S(1)} %bitcast.331, bf16[2048,768]{1,0:T(8,128)(2,1)S(1)} %copy-done.32, bf16[4096,2048]{1,0:T(8,128)(2,1)} %get-tuple-element.175.normed_ref), custom_call_target="tpu_custom_call" | custom-call | flops 22000001024 | bytes 66000000 | tf_op jit(solution)/shard_map/unproject/pallas_call | solution.py:183
  1186.4 3.4 all-to-all-start.6
  1189.8 5.4 add_convert_fusion.4
  1197.5 5.1 all-to-all-start.7
  1202.8 4.3 fusion.6
  1211.6 3.4 copy-done.35
  1215.1 79.1 %scatter_rows.1 = f32[2,256,2048]{2,1,0:T(8,128)S(1)} custom-call(bf16[4,2,256,2048]{3,2,1,0:T(8,128)(2,1)S(1)} %bitcast.348, bf16[4,2,256,2048]{3,2,1,0:T(8,128)(2,1)} %bitcast.424), custom_call_target="tpu_custom_call" | custom-call | flops 99000000512 | bytes 297000000 | tf_op jit(solution)/shard_map/scatter_rows/pallas_call | solution.py:780
  1296.3 3.1 fusion
  1299.5 3.6 all-to-all-start.8
  1303.9 3.0 convert_bitcast_fusion.1
  1309.2 5.3 fusion.4
  (475 shorter events, 151.9 us)
Async XLA Ops:
  7.2 227.2 %all-gather.11.cloned.1.call-start = ((), (), s32[]{:S(2)}) async-start(), calls=%async_computation.17 | async-start | bytes 3932160 | tf_op jit(solution)/shard_map/all_gather | solution.py:877
  9.4 56.8 %copy-start.5 = (bf16[1,512,2048]{2,1,0:T(8,128)(2,1)S(1)}, bf16[1,512,2048]{2,1,0:T(8,128)(2,1)}, u32[]{:S(2)}) copy-start(bf16[1,512,2048]{2,1,0:T(8,128)(2,1)} %param.24) | copy-start | bytes 6291460
  27.2 473.1 %all-gather.19.cloned.1.call-start = ((), (), s32[]{:S(2)}) async-start(), calls=%async_computation.29 | async-start | bytes 7208960 | tf_op jit(solution)/shard_map/all_gather | solution.py:928
  28.0 472.4 %all-gather.21.cloned.1.call-start = ((), (), s32[]{:S(2)}) async-start(), calls=%async_computation.30 | async-start | bytes 7208960 | tf_op jit(solution)/shard_map/all_gather | solution.py:929
  28.7 471.6 %all-gather.23.cloned.1.call-start = ((), (), s32[]{:S(2)}) async-start(), calls=%async_computation.31 | async-start | bytes 7208960 | tf_op jit(solution)/shard_map/all_gather | solution.py:930
  29.3 659.0 %all-gather.13.cloned.1.call-start = ((), (), s32[]{:S(2)}) async-start(), calls=%async_computation.18 | async-start | bytes 3604480 | tf_op jit(solution)/shard_map/all_gather | solution.py:923
  29.9 658.4 %all-gather.15.cloned.1.call-start = ((), (), s32[]{:S(2)}) async-start(), calls=%async_computation.19 | async-start | bytes 3604480 | tf_op jit(solution)/shard_map/all_gather | solution.py:924
  30.1 31.4 %collective-permute-start.2 = (f32[14,64]{1,0:T(8,128)S(1)}, f32[14,64]{1,0:T(8,128)S(1)}, u32[]{:S(2)}, u32[]{:S(2)}) collective-permute-start(f32[14,64]{1,0:T(8,128)S(1)} %convert_element_type.503), channel_id=1, source_target_pairs={{0,24},{8,0},{16,8},{24,16},{1,25},{9,1},{17,9},{25,17},{2,26},{10... | collective-permute-start | bytes 10760 | tf_op jit(solution)/shard_map/ppermute | solution.py:891
  33.8 27.8 %collective-permute-start.1 = (f32[14,64]{1,0:T(8,128)S(1)}, f32[14,64]{1,0:T(8,128)S(1)}, u32[]{:S(2)}, u32[]{:S(2)}) collective-permute-start(f32[14,64]{1,0:T(8,128)S(1)} %convert_element_type.503), channel_id=1, source_target_pairs={{0,16},{8,24},{16,0},{24,8},{1,17},{9,25},{17,1},{25,9},{2,18},{10... | collective-permute-start | bytes 10760 | tf_op jit(solution)/shard_map/ppermute | solution.py:891
  33.8 27.8 %collective-permute-start = (f32[14,64]{1,0:T(8,128)S(1)}, f32[14,64]{1,0:T(8,128)S(1)}, u32[]{:S(2)}, u32[]{:S(2)}) collective-permute-start(f32[14,64]{1,0:T(8,128)S(1)} %convert_element_type.503), channel_id=1, source_target_pairs={{0,8},{8,16},{16,24},{24,0},{1,9},{9,17},{17,25},{25,1},{2,10},{10... | collective-permute-start | bytes 10760 | tf_op jit(solution)/shard_map/ppermute | solution.py:891
  61.6 172.8 %copy-start.29 = (s32[16]{0:T(128)}, s32[16]{0:T(128)S(1)}, u32[]{:S(2)}) copy-start(s32[16]{0:T(128)S(1)} %concatenate.111.place_ref) | copy-start | bytes 196
  62.3 165.0 %collective-permute-start.5 = (bf16[64,2048]{1,0:T(8,128)(2,1)}, bf16[64,2048]{1,0:T(8,128)(2,1)}, u32[]{:S(2)}, u32[]{:S(2)}) collective-permute-start(bf16[64,2048]{1,0:T(8,128)(2,1)} %param.32), channel_id=1, source_target_pairs={{0,24},{8,0},{16,8},{24,16},{1,25},{9,1},{17,9},{25,17},{2,26},{10... | collective-permute-start | bytes 786440 | tf_op jit(solution)/shard_map/ppermute | solution.py:901
  65.1 162.2 %collective-permute-start.4 = (bf16[64,2048]{1,0:T(8,128)(2,1)}, bf16[64,2048]{1,0:T(8,128)(2,1)}, u32[]{:S(2)}, u32[]{:S(2)}) collective-permute-start(bf16[64,2048]{1,0:T(8,128)(2,1)} %param.32), channel_id=1, source_target_pairs={{0,16},{8,24},{16,0},{24,8},{1,17},{9,25},{17,1},{25,9},{2,18},{10... | collective-permute-start | bytes 786440 | tf_op jit(solution)/shard_map/ppermute | solution.py:901
  66.3 161.1 %collective-permute-start.3 = (bf16[64,2048]{1,0:T(8,128)(2,1)}, bf16[64,2048]{1,0:T(8,128)(2,1)}, u32[]{:S(2)}, u32[]{:S(2)}) collective-permute-start(bf16[64,2048]{1,0:T(8,128)(2,1)} %param.32), channel_id=1, source_target_pairs={{0,8},{8,16},{16,24},{24,0},{1,9},{9,17},{17,25},{25,1},{2,10},{10... | collective-permute-start | bytes 786440 | tf_op jit(solution)/shard_map/ppermute | solution.py:901
  67.9 157.8 %copy-start.97 = (pred[8]{0:T(512)(128)(4,1)S(1)}, pred[8]{0:T(512)(128)(4,1)}, u32[]{:S(2)}) copy-start(pred[8]{0:T(512)(128)(4,1)} %compare_and_fusion) | copy-start | bytes 28
  231.5 35.5 %collective-permute-start.7 = (bf16[128,2048]{1,0:T(8,128)(2,1)}, bf16[128,2048]{1,0:T(8,128)(2,1)S(1)}, u32[]{:S(2)}, u32[]{:S(2)}) collective-permute-start(bf16[128,2048]{1,0:T(8,128)(2,1)} %get-tuple-element.272), channel_id=1, source_target_pairs={{0,4},{1,5},{2,6},{3,7},{4,0},{5,1},{6,2},{7,3},{8,12},{9,13},{10,... | collective-permute-start | bytes 1572872 | tf_op jit(solution)/shard_map/ppermute | solution.py:510
  232.9 34.1 %collective-permute-start.6 = (bf16[128,2048]{1,0:T(8,128)(2,1)}, bf16[128,2048]{1,0:T(8,128)(2,1)}, u32[]{:S(2)}, u32[]{:S(2)}) collective-permute-start(bf16[128,2048]{1,0:T(8,128)(2,1)} %get-tuple-element.273), channel_id=1, source_target_pairs={{0,2},{1,3},{2,0},{3,1},{4,6},{5,7},{6,4},{7,5},{8,10},{9,11},{10,... | collective-permute-start | bytes 1572872 | tf_op jit(solution)/shard_map/ppermute | solution.py:510
  271.6 39.7 %collective-permute-start.9 = (bf16[256,2048]{1,0:T(8,128)(2,1)}, bf16[256,2048]{1,0:T(8,128)(2,1)}, u32[]{:S(2)}, u32[]{:S(2)}) collective-permute-start(bf16[256,2048]{1,0:T(8,128)(2,1)} %pad_maximum_fusion.9), channel_id=1, source_target_pairs={{0,2},{1,3},{2,0},{3,1},{4,6},{5,7},{6,4},{7,5},{8,10},{9,11},{10,... | collective-permute-start | bytes 3145736 | tf_op jit(solution)/shard_map/ppermute | solution.py:510
  272.2 39.1 %collective-permute-start.8 = (bf16[256,2048]{1,0:T(8,128)(2,1)}, bf16[256,2048]{1,0:T(8,128)(2,1)}, u32[]{:S(2)}, u32[]{:S(2)}) collective-permute-start(bf16[256,2048]{1,0:T(8,128)(2,1)} %pad_maximum_fusion.12), channel_id=1, source_target_pairs={{0,4},{1,5},{2,6},{3,7},{4,0},{5,1},{6,2},{7,3},{8,12},{9,13},{10,... | collective-permute-start | bytes 3145736 | tf_op jit(solution)/shard_map/ppermute | solution.py:510
  319.1 74.1 %collective-permute-start.10 = (bf16[4,256,2048]{2,1,0:T(8,128)(2,1)}, bf16[4,256,2048]{2,1,0:T(8,128)(2,1)}, u32[]{:S(2)}, u32[]{:S(2)}) collective-permute-start(bf16[4,256,2048]{2,1,0:T(8,128)(2,1)} %get-tuple-element.262), channel_id=1, source_target_pairs={{0,1},{1,0},{2,3},{3,2},{4,5},{5,4},{6,7},{7,6},{8,9},{9,8},{10,11... | collective-permute-start | bytes 12582920 | tf_op jit(solution)/shard_map/ppermute | solution.py:510
  352.0 19.8 %all-to-all-start.2 = ((bf16[8,512,128]{1,2,0:T(8,128)(2,1)}), bf16[8,512,128]{1,2,0:T(8,128)(2,1)}, u32[]{:S(2)}, u32[]{:S(2)}) async-start(bf16[8,512,128]{1,2,0:T(8,128)(2,1)} %copy.188), calls=%async_computation.2 | async-start | bytes 2097152 | tf_op jit(solution)/shard_map/all_to_all | solution.py:824
  356.4 331.9 %all-gather.17.cloned.1.call-start = ((), (), s32[]{:S(2)}) async-start(), calls=%async_computation.20 | async-start | bytes 3604480 | tf_op jit(solution)/shard_map/all_gather | solution.py:925
  371.8 19.7 %all-to-all-start.1 = ((bf16[8,512,128]{1,2,0:T(8,128)(2,1)}), bf16[8,512,128]{1,2,0:T(8,128)(2,1)}, u32[]{:S(2)}, u32[]{:S(2)}) async-start(bf16[8,512,128]{1,2,0:T(8,128)(2,1)} %copy.187), calls=%async_computation.1 | async-start | bytes 2097152 | tf_op jit(solution)/shard_map/all_to_all | solution.py:824
  376.1 437.7 %reduce-scatter.9.cloned.1.call-start = ((), (), s32[]{:S(2)}) async-start(), calls=%async_computation.21 | async-start | bytes 7208960 | tf_op jit(solution)/shard_map/reduce_scatter | solution.py:816
  414.5 78.5 %copy-start = (bf16[512,2048]{1,0:T(8,128)(2,1)}, bf16[512,2048]{1,0:T(8,128)(2,1)S(1)}, u32[]{:S(2)}) copy-start(bf16[512,2048]{1,0:T(8,128)(2,1)S(1)} %multiply_convert_fusion.refs_0_) | copy-start | bytes 6291460
  415.2 77.9 %copy-start.64 = (f32[512,9]{0,1:T(8,128)}, f32[512,9]{0,1:T(8,128)S(1)}, u32[]{:S(2)}) copy-start(f32[512,9]{0,1:T(8,128)S(1)} %fusion.53) | copy-start | bytes 55300
  415.2 77.8 %copy-start.72 = (pred[8,512]{1,0:T(8,128)(4,1)}, pred[8,512]{1,0:T(8,128)(4,1)S(1)}, u32[]{:S(2)}) copy-start(pred[8,512]{1,0:T(8,128)(4,1)S(1)} %get-tuple-element.222) | copy-start | bytes 12292
  415.2 77.8 %copy-start.81 = (f32[512]{0:T(512)}, f32[512]{0:T(512)S(1)}, u32[]{:S(2)}) copy-start(f32[512]{0:T(512)S(1)} %get-tuple-element.221) | copy-start | bytes 6148
  415.3 77.8 %copy-start.86 = (f32[512]{0:T(512)}, f32[512]{0:T(512)S(1)}, u32[]{:S(2)}) copy-start(f32[512]{0:T(512)S(1)} %fusion.21) | copy-start | bytes 6148
  685.5 322.6 %reduce-scatter.11.cloned.1.call-start = ((), (), s32[]{:S(2)}) async-start(), calls=%async_computation.22 | async-start | bytes 7208960 | tf_op jit(solution)/shard_map/reduce_scatter | solution.py:816
  688.2 387.8 %reduce-scatter.13.cloned.1.call-start = ((), (), s32[]{:S(2)}) async-start(), calls=%async_computation.23 | async-start | bytes 7208960 | tf_op jit(solution)/shard_map/reduce_scatter | solution.py:816
  792.5 21.3 %collective-permute-start.11 = (bf16[2048,2048]{1,0:T(8,128)(2,1)}, bf16[2048,2048]{1,0:T(8,128)(2,1)}, u32[]{:S(2)}, u32[]{:S(2)}) collective-permute-start(bf16[2048,2048]{1,0:T(8,128)(2,1)} %get-tuple-element.147), channel_id=1, source_target_pairs={{0,1},{1,0},{2,3},{3,2},{4,5},{5,4},{6,7},{7,6},{8,9},{9,8},{10,11... | collective-permute-start | bytes 25165832 | tf_op jit(solution)/shard_map/ppermute | solution.py:510
  813.8 371.6 %reduce-scatter.21.cloned.1.call-start = ((), (), s32[]{:S(2)}) async-start(), calls=%async_computation.27 | async-start | bytes 3604480 | tf_op jit(solution)/shard_map/reduce_scatter | solution.py:816
  820.3 48.0 %collective-permute-start.12 = (bf16[512,2048]{1,0:T(8,128)(2,1)}, bf16[512,2048]{1,0:T(8,128)(2,1)}, u32[]{:S(2)}, u32[]{:S(2)}) collective-permute-start(bf16[512,2048]{1,0:T(8,128)(2,1)} %pad_maximum_fusion.4), channel_id=1, source_target_pairs={{0,2},{1,3},{2,0},{3,1},{4,6},{5,7},{6,4},{7,5},{8,10},{9,11},{10,... | collective-permute-start | bytes 6291464 | tf_op jit(solution)/shard_map/ppermute | solution.py:510
  822.5 47.8 %collective-permute-start.13 = (bf16[512,2048]{1,0:T(8,128)(2,1)}, bf16[512,2048]{1,0:T(8,128)(2,1)}, u32[]{:S(2)}, u32[]{:S(2)}) collective-permute-start(bf16[512,2048]{1,0:T(8,128)(2,1)} %pad_maximum_fusion.5), channel_id=1, source_target_pairs={{0,4},{1,5},{2,6},{3,7},{4,0},{5,1},{6,2},{7,3},{8,12},{9,13},{10,... | collective-permute-start | bytes 6291464 | tf_op jit(solution)/shard_map/ppermute | solution.py:510
  872.4 9.1 all-to-all-start.3
  876.2 420.1 %reduce-scatter.15.cloned.1.call-start = ((), (), s32[]{:S(2)}) async-start(), calls=%async_computation.24 | async-start | bytes 3604480 | tf_op jit(solution)/shard_map/reduce_scatter | solution.py:816
  891.8 25.7 %collective-permute-start.15 = (bf16[256,2048]{1,0:T(8,128)(2,1)}, bf16[256,2048]{1,0:T(8,128)(2,1)S(1)}, u32[]{:S(2)}, u32[]{:S(2)}) collective-permute-start(bf16[256,2048]{1,0:T(8,128)(2,1)} %get-tuple-element.235), channel_id=1, source_target_pairs={{0,2},{1,3},{2,0},{3,1},{4,6},{5,7},{6,4},{7,5},{8,10},{9,11},{10,... | collective-permute-start | bytes 3145736 | tf_op jit(solution)/shard_map/ppermute | solution.py:510
  893.8 25.1 %collective-permute-start.14 = (bf16[256,2048]{1,0:T(8,128)(2,1)}, bf16[256,2048]{1,0:T(8,128)(2,1)S(1)}, u32[]{:S(2)}, u32[]{:S(2)}) collective-permute-start(bf16[256,2048]{1,0:T(8,128)(2,1)} %get-tuple-element.236), channel_id=1, source_target_pairs={{0,4},{1,5},{2,6},{3,7},{4,0},{5,1},{6,2},{7,3},{8,12},{9,13},{10,... | collective-permute-start | bytes 3145736 | tf_op jit(solution)/shard_map/ppermute | solution.py:510
  924.0 84.1 %collective-permute-start.16 = (bf16[2048,2048]{1,0:T(8,128)(2,1)}, bf16[2048,2048]{1,0:T(8,128)(2,1)}, u32[]{:S(2)}, u32[]{:S(2)}) collective-permute-start(bf16[2048,2048]{1,0:T(8,128)(2,1)} %get-tuple-element.164), channel_id=1, source_target_pairs={{0,1},{1,0},{2,3},{3,2},{4,5},{5,4},{6,7},{7,6},{8,9},{9,8},{10,11... | collective-permute-start | bytes 25165832 | tf_op jit(solution)/shard_map/ppermute | solution.py:510
  944.8 21.4 %all-to-all-start.4 = ((bf16[8,512,128]{2,1,0:T(8,128)(2,1)}), bf16[8,512,128]{2,1,0:T(8,128)(2,1)S(1)}, u32[]{:S(2)}, u32[]{:S(2)}) async-start(bf16[8,512,128]{2,1,0:T(8,128)(2,1)} %bitcast.323), calls=%async_computation.6 | async-start | bytes 2097152 | tf_op jit(solution)/shard_map/all_to_all | solution.py:824
  948.4 347.9 %reduce-scatter.17.cloned.1.call-start = ((), (), s32[]{:S(2)}) async-start(), calls=%async_computation.25 | async-start | bytes 3604480 | tf_op jit(solution)/shard_map/reduce_scatter | solution.py:816
  1008.1 20.0 %all-to-all-start.5 = ((bf16[8,512,128]{2,1,0:T(8,128)(2,1)}), bf16[8,512,128]{2,1,0:T(8,128)(2,1)S(1)}, u32[]{:S(2)}, u32[]{:S(2)}) async-start(bf16[8,512,128]{2,1,0:T(8,128)(2,1)} %bitcast.363), calls=%async_computation.8 | async-start | bytes 2097152 | tf_op jit(solution)/shard_map/all_to_all | solution.py:824
  1012.2 284.0 %reduce-scatter.23.cloned.1.call-start = ((), (), s32[]{:S(2)}) async-start(), calls=%async_computation.28 | async-start | bytes 1310720 | tf_op jit(solution)/shard_map/reduce_scatter | solution.py:1135
  1018.7 57.3 %collective-permute-start.17 = (bf16[512,2048]{1,0:T(8,128)(2,1)}, bf16[512,2048]{1,0:T(8,128)(2,1)}, u32[]{:S(2)}, u32[]{:S(2)}) collective-permute-start(bf16[512,2048]{1,0:T(8,128)(2,1)} %pad_maximum_fusion.6), channel_id=1, source_target_pairs={{0,2},{1,3},{2,0},{3,1},{4,6},{5,7},{6,4},{7,5},{8,10},{9,11},{10,... | collective-permute-start | bytes 6291464 | tf_op jit(solution)/shard_map/ppermute | solution.py:510
  1022.2 53.7 %collective-permute-start.18 = (bf16[512,2048]{1,0:T(8,128)(2,1)}, bf16[512,2048]{1,0:T(8,128)(2,1)}, u32[]{:S(2)}, u32[]{:S(2)}) collective-permute-start(bf16[512,2048]{1,0:T(8,128)(2,1)} %pad_maximum_fusion.7), channel_id=1, source_target_pairs={{0,4},{1,5},{2,6},{3,7},{4,0},{5,1},{6,2},{7,3},{8,12},{9,13},{10,... | collective-permute-start | bytes 6291464 | tf_op jit(solution)/shard_map/ppermute | solution.py:510
  1031.3 42.9 %slice-start.2 = ((s8[8388608]{0:T(1024)(128)(4,1)}), s8[4194304]{0:T(1024)(128)(4,1)S(1)}, s32[]{:S(2)}) async-start(s8[8388608]{0:T(1024)(128)(4,1)} %bitcast.359), calls=%async_computation.34 | async-start | bytes 8388608
  1033.7 51.1 %collective-permute-start.21 = (bf16[1024,2048]{1,0:T(8,128)(2,1)}, bf16[1024,2048]{1,0:T(8,128)(2,1)}, u32[]{:S(2)}, u32[]{:S(2)}) collective-permute-start(bf16[1024,2048]{1,0:T(8,128)(2,1)} %pad_maximum_fusion.2), channel_id=1, source_target_pairs={{0,1},{1,0},{2,3},{3,2},{4,5},{5,4},{6,7},{7,6},{8,9},{9,8},{10,11... | collective-permute-start | bytes 12582920 | tf_op jit(solution)/shard_map/ppermute | solution.py:510
  1033.7 40.5 %slice-start.3 = ((s8[8388608]{0:T(1024)(128)(4,1)}), s8[4194304]{0:T(1024)(128)(4,1)S(1)}, s32[]{:S(2)}) async-start(s8[8388608]{0:T(1024)(128)(4,1)} %bitcast.359), calls=%async_computation.35 | async-start | bytes 8388608
  1081.7 75.1 %collective-permute-start.20 = (bf16[256,2048]{1,0:T(8,128)(2,1)}, bf16[256,2048]{1,0:T(8,128)(2,1)}, u32[]{:S(2)}, u32[]{:S(2)}) collective-permute-start(bf16[256,2048]{1,0:T(8,128)(2,1)} %get-tuple-element.227), channel_id=1, source_target_pairs={{0,2},{1,3},{2,0},{3,1},{4,6},{5,7},{6,4},{7,5},{8,10},{9,11},{10,... | collective-permute-start | bytes 3145736 | tf_op jit(solution)/shard_map/ppermute | solution.py:510
  1082.0 74.8 %collective-permute-start.19 = (bf16[256,2048]{1,0:T(8,128)(2,1)}, bf16[256,2048]{1,0:T(8,128)(2,1)}, u32[]{:S(2)}, u32[]{:S(2)}) collective-permute-start(bf16[256,2048]{1,0:T(8,128)(2,1)} %get-tuple-element.228), channel_id=1, source_target_pairs={{0,4},{1,5},{2,6},{3,7},{4,0},{5,1},{6,2},{7,3},{8,12},{9,13},{10,... | collective-permute-start | bytes 3145736 | tf_op jit(solution)/shard_map/ppermute | solution.py:510
  1087.5 42.0 %collective-permute-start.22 = (bf16[256,2048]{1,0:T(8,128)(2,1)S(1)}, bf16[256,2048]{1,0:T(8,128)(2,1)S(1)}, u32[]{:S(2)}, u32[]{:S(2)}) collective-permute-start(bf16[256,2048]{1,0:T(8,128)(2,1)S(1)} %pad_maximum_fusion.13), channel_id=1, source_target_pairs={{0,2},{1,3},{2,0},{3,1},{4,6},{5,7},{6,4},{7,5},{8,10},{9,11},{10,... | collective-permute-start | bytes 3145736 | tf_op jit(solution)/shard_map/ppermute | solution.py:510
  1089.1 41.4 %collective-permute-start.23 = (bf16[256,2048]{1,0:T(8,128)(2,1)S(1)}, bf16[256,2048]{1,0:T(8,128)(2,1)}, u32[]{:S(2)}, u32[]{:S(2)}) collective-permute-start(bf16[256,2048]{1,0:T(8,128)(2,1)S(1)} %pad_maximum_fusion.14), channel_id=1, source_target_pairs={{0,4},{1,5},{2,6},{3,7},{4,0},{5,1},{6,2},{7,3},{8,12},{9,13},{10,... | collective-permute-start | bytes 3145736 | tf_op jit(solution)/shard_map/ppermute | solution.py:510
  1091.9 39.6 %copy-start.53 = (bf16[2,1,64,2048]{3,2,1,0:T(8,128)(2,1)S(1)}, bf16[2,1,64,2048]{3,2,1,0:T(8,128)(2,1)}, u32[]{:S(2)}) copy-start(bf16[2,1,64,2048]{3,2,1,0:T(8,128)(2,1)} %get-tuple-element.246) | copy-start | bytes 1572868
  1091.9 39.6 %copy-start.54 = (bf16[2,1,64,2048]{3,2,1,0:T(8,128)(2,1)S(1)}, bf16[2,1,64,2048]{3,2,1,0:T(8,128)(2,1)}, u32[]{:S(2)}) copy-start(bf16[2,1,64,2048]{3,2,1,0:T(8,128)(2,1)} %get-tuple-element.248) | copy-start | bytes 1572868
  1092.2 38.3 %copy-start.4 = (bf16[4096,768]{1,0:T(8,128)(2,1)}, bf16[4096,768]{1,0:T(8,128)(2,1)S(1)}, u32[]{:S(2)}) copy-start(bf16[4096,768]{1,0:T(8,128)(2,1)S(1)} %constant_dynamic-update-slice_fusion.grad_ref) | copy-start | bytes 18874372
  1134.8 47.4 %collective-permute-start.25 = (bf16[128,2048]{1,0:T(8,128)(2,1)}, bf16[128,2048]{1,0:T(8,128)(2,1)S(1)}, u32[]{:S(2)}, u32[]{:S(2)}) collective-permute-start(bf16[128,2048]{1,0:T(8,128)(2,1)} %get-tuple-element.255), channel_id=1, source_target_pairs={{0,2},{1,3},{2,0},{3,1},{4,6},{5,7},{6,4},{7,5},{8,10},{9,11},{10,... | collective-permute-start | bytes 1572872 | tf_op jit(solution)/shard_map/ppermute | solution.py:510
  1135.7 46.5 %collective-permute-start.24 = (bf16[128,2048]{1,0:T(8,128)(2,1)}, bf16[128,2048]{1,0:T(8,128)(2,1)S(1)}, u32[]{:S(2)}, u32[]{:S(2)}) collective-permute-start(bf16[128,2048]{1,0:T(8,128)(2,1)} %get-tuple-element.256), channel_id=1, source_target_pairs={{0,4},{1,5},{2,6},{3,7},{4,0},{5,1},{6,2},{7,3},{8,12},{9,13},{10,... | collective-permute-start | bytes 1572872 | tf_op jit(solution)/shard_map/ppermute | solution.py:510
  1186.4 8.7 all-to-all-start.6
  1197.5 11.0 all-to-all-start.7
  1202.6 93.7 %reduce-scatter.19.cloned.1.call-start = ((), (), s32[]{:S(2)}) async-start(), calls=%async_computation.26 | async-start | bytes 3932160 | tf_op jit(solution)/shard_map/reduce_scatter | solution.py:1129
  1215.1 81.2 %copy-start.6 = (bf16[1,512,2048]{2,1,0:T(8,128)(2,1)S(1)}, bf16[1,512,2048]{2,1,0:T(8,128)(2,1)}, u32[]{:S(2)}) copy-start(bf16[1,512,2048]{2,1,0:T(8,128)(2,1)} %param.24) | copy-start | bytes 6291460
  1215.1 81.2 %copy-start.74 = (f32[2048]{0:T(1024)S(1)}, f32[2048]{0:T(1024)}, u32[]{:S(2)}) copy-start(f32[2048]{0:T(1024)} %mul.166) | copy-start | bytes 24580
  1299.5 16.1 %all-to-all-start.8 = ((bf16[8,64,768]{2,1,0:T(8,128)(2,1)}), bf16[8,64,768]{2,1,0:T(8,128)(2,1)S(1)}, u32[]{:S(2)}, u32[]{:S(2)}) async-start(bf16[8,64,768]{2,1,0:T(8,128)(2,1)} %bitcast.379), calls=%async_computation.16 | async-start | bytes 1572864 | tf_op jit(solution)/shard_map/all_to_all | solution.py:824
  (93 other events, 751.5 us)
Sparse Core Ops, SparseCore 0:
  27.4 85.1 all-gather.10
  114.1 105.1 all-gather.18
  220.9 104.9 all-gather.20
  327.4 104.9 all-gather.22
  433.9 57.4 all-gather.12
  492.8 57.8 all-gather.14
  552.3 57.8 all-gather.16
  685.6 102.9 reduce-scatter.8
  790.9 102.7 reduce-scatter.10
  895.9 102.7 reduce-scatter.12
  1001.0 56.7 reduce-scatter.20
  1059.9 56.0 reduce-scatter.14
  1118.2 56.0 reduce-scatter.16
  1185.5 28.4 reduce-scatter.22
  1216.3 58.8 reduce-scatter.18

commit v4 on v3

--- a/solution.py
+++ b/solution.py
@@ -121,7 +121,7 @@
 
 def project(x_blocks, places, gain, weight, bias, cosine, sine):
     count, rows, _ = x_blocks.shape
-    width = weight.shape[1] // 3
+    width = bias.shape[1] // 3
     at_place = lambda g, place: (place[g], 0)
     whole = lambda g, place: (0, 0)
     tile = pl.BlockSpec((rows, width), at_place)
@@ -172,7 +172,7 @@
 def unproject(grads, places, weight, normed, per_device):
     count = places.shape[0]
     rows = grads.shape[0] // count
-    width = weight.shape[1]
+    width = grads.shape[1]
     middle = count // 2
 
     def at_place(g, place):
@@ -601,13 +601,16 @@
     shapes = [
         jax.ShapeDtypeStruct((2 * count, x.shape[0] // 2, x.shape[1]), x.dtype) for x in arrays
     ]
-    shapes.append(jax.ShapeDtypeStruct((count, *small.shape), small.dtype))
-    tracks = 2 * len(arrays) + 1
+    inputs = list(arrays)
+    if small is not None:
+        inputs.append(small)
+        shapes.append(jax.ShapeDtypeStruct((count, *small.shape), small.dtype))
+    tracks = len(arrays) + len(inputs)
     return pl.pallas_call(
-        functools.partial(gather_kernel, count, len(arrays), 1),
+        functools.partial(gather_kernel, count, len(arrays), len(inputs) - len(arrays)),
         in_specs=[pl.BlockSpec(memory_space=pl.ANY)] * len(shapes),
         out_specs=[pl.BlockSpec(memory_space=pltpu.HBM)] * len(arrays)
-        + [pl.BlockSpec(memory_space=pl.ANY)],
+        + [pl.BlockSpec(memory_space=pl.ANY)] * (len(inputs) - len(arrays)),
         out_shape=shapes,
         scratch_shapes=[
             pltpu.SemaphoreType.DMA((tracks * count,)),
@@ -615,11 +618,11 @@
             pltpu.SemaphoreType.DMA((tracks,)),
         ],
         compiler_params=pltpu.CompilerParams(
-            collective_id=collective_id, has_side_effects=True, vmem_limit_bytes=4 * 2**20
+            collective_id=collective_id, has_side_effects=True, vmem_limit_bytes=58 * 2**20
         ),
         cost_estimate=cost(microseconds),
         name="gather_rows",
-    )(*arrays, small)
+    )(*inputs)
 
 
 def split_rows(values, parts):
@@ -871,30 +874,34 @@
         parts = weight.reshape(shard, head_sets, width).transpose(1, 0, 2)
         return jnp.repeat(parts, repeat, axis=0) if repeat > 1 else parts
 
-    qkv_parts = swap_ctx(
-        jnp.concatenate([by_heads(w_query), by_heads(w_key), by_heads(w_value)], axis=2)
-    )
-    w_qkv = lax.all_gather(
-        qkv_parts.reshape(ctx_count * shard, 3 * width), "dp", axis=0, tiled=True
-    )
-    partners = jnp.arange(ctx_count, dtype=jnp.int32) ^ ctx_index
     small = jnp.concatenate(
         [
-            jnp.stack([in_gain, b_query, b_key, b_value, ffn_gain, sh_mix], axis=0),
-            w_router.T,
+            jnp.stack([in_gain, b_query, b_key, b_value, ffn_gain, sh_mix], axis=1),
+            w_router,
         ],
-        axis=0,
-    ).astype(full)
-    small_count = small.shape[0]
-    small_rows = -(-dp_count * small_count * shard // HEAD_DIM // 8) * 8
-    around = [small] + [
-        lax.ppermute(small, "dp", [(i, (i + k) % dp_count) for i in range(dp_count)])
-        for k in range(1, dp_count)
-    ]
+        axis=1,
+    )
+    small_count = small.shape[1]
+    small = jnp.pad(small, ((0, 0), (0, -small_count % HEAD_DIM)))
+    qkv_parts = swap_ctx(
+        jnp.concatenate(
+            [
+                by_heads(w_query),
+                by_heads(w_key),
+                by_heads(w_value),
+                jnp.broadcast_to(small[None], (ctx_count, *small.shape)),
+            ],
+            axis=2,
+        )
+    )
+    w_qkv = lax.all_gather(
+        qkv_parts.reshape(ctx_count * shard, qkv_parts.shape[2]), "dp", axis=0, tiled=True
+    )
+    small_all = w_qkv[:, 3 * width : 3 * width + small_count].astype(full).T
+    gain_one, gain_two, mix_row = small_all[0:1], small_all[4:5], small_all[5:6]
+    mix_router = small_all[5:].astype(low)
+    partners = jnp.arange(ctx_count, dtype=jnp.int32) ^ ctx_index
     origin = (dp_index - jnp.arange(dp_count, dtype=jnp.int32)) % dp_count
-    small = jnp.take(jnp.stack(around), origin, axis=0).reshape(-1)
-    small = jnp.pad(small, (0, small_rows * HEAD_DIM - small.shape[0])).reshape(small_rows, HEAD_DIM)
-    w_out, small = lax.optimization_barrier((w_out, small))
     out_around = jnp.stack(
         [w_out]
         + [
@@ -902,17 +909,8 @@
             for k in range(1, dp_count)
         ]
     )
-    x_blocks, cot_all, small_all = gather_now([tokens_low, cot_low], small, 0, 145)
+    x_blocks, cot_all = gather_now([tokens_low, cot_low], None, 0, 145)
     cot_all = cot_all.reshape(group_len, D)
-    small_all = small_all.reshape(ctx_count, -1)[:, : dp_count * small_count * shard]
-    small_all = jnp.take(small_all, partners, axis=0)
-    small_all = (
-        small_all.reshape(ctx_count, dp_count, small_count, shard)
-        .transpose(2, 1, 0, 3)
-        .reshape(small_count, shard * dp_count * ctx_count)
-    )
-    gain_one, gain_two, mix_row = small_all[0:1], small_all[4:5], small_all[5:6]
-    mix_router = small_all[5:].astype(low)
     out_mine = jnp.concatenate(
         [lax.dynamic_index_in_dim(out_around, origin[p], 0, False) for p in range(dp_count)], axis=0
     )
@@ -975,6 +973,8 @@
         if head == 0:
             (*out_came, query), one_head = pin([*out_came, query], one_head)
             out_came, out_parts = advance(out_steps, out_came)
+        if head == 1:
+            (parts[0],), one_head = pin([parts[0]], one_head)
         attended_heads.append(one_head)
         lses.append(lse)
         stored_head = one_head if direct else take_blocks(one_head, stored_to_place)
@@ -1098,10 +1098,13 @@
         )
         grads = list(grads)
         if head == 0:
-            wout_came, grads[0] = pin(wout_came, grads[0])
+            (*wout_came, upstreams[-1]), grads[0] = pin([*wout_came, upstreams[-1]], grads[0])
             wout_came, wout = advance(wout_steps, wout_came)
         head_grads.append(grads)
     came, last, sum_edown = pin(came, head_grads[-1][0], sum_edown)
+    if wout is None:
+        wout_came, last = pin(wout_came, last)
+        wout_came, wout = advance(wout_steps, wout_came)
     head_grads[-1][0] = last
     came, added = advance(add_steps, came)
     qkv_grads = jnp.concatenate(
@@ -1109,18 +1112,17 @@
     )
     if repeat > 1:
         qkv_grads = jnp.where(ctx_index % repeat == 0, qkv_grads, jnp.zeros_like(qkv_grads))
-    wout_came, qkv_grads = pin(wout_came, qkv_grads)
-    wout_came, wout = advance(wout_steps, wout_came)
     grad_qkv = ein("td,te->de", normed_sorted, qkv_grads).astype(low)
     bias_sums = jnp.sum(qkv_grads.astype(full), axis=0).reshape(3, width)
     grad_bias = lax.dynamic_update_slice_in_dim(
         jnp.zeros((3, D), full), bias_sums, my_heads, 1
     )
-    came, grad_qkv, qkv_grads = pin(came, grad_qkv, qkv_grads)
+    grad_qkv, qkv_grads = lax.optimization_barrier((grad_qkv, qkv_grads))
     odd_one, even_one, gain_sums = unproject(
         qkv_grads, stored_near, w_qkv, normed_sorted, per_device
     )
     grad_gain_one = gain_sums[0] / gain_one[0]
+    came, odd_one = pin(came, odd_one)
     added = finish(add_steps, came)
     layer_out = first_sum + added.astype(full)
     wout_came, odd_one = pin(wout_came, odd_one)

time: 1340 us -> 1300 us (0.970)
  local copies, waits for them, and re-layouts: 117 us -> 88.4 us
  waiting for transfers between devices: 67.6 us -> 52.8 us
    unnamed x246 -> x201, local copies, waits for them, and re-layouts: 69.7 us -> 41.4 us
    ppermute x20, waiting for transfers between devices: 52.2 us -> 30.1 us  [exchange(): return lax.ppermute(values, 'ctx', [(i, i ^ bit) for i in range(count)])]
  transfers between devices with their start and end apart: 49 -> 46, of which waited for: 10 -> 13; matrix products, arithmetic and copies ran while one was open for 25% -> 26% of each run, Pallas kernels for 55% -> 57%
where the time goes in v4:
time: 1300 us; the launch traced here: 1290 us
  Pallas kernels  732 us (56%)
  matrix products  169 us (13%)
  other arithmetic  119 us (9%)
  local copies, waits for them, and re-layouts  88.4 us (7%)
  between operations  55 us (4%)
  starting transfers between devices  54.9 us (4%)
  waiting for transfers between devices  52.8 us (4%)
  blocking collectives  19 us (1%)
    pallas_call x2, Pallas kernels, gather_now(): pl.pallas_call(functools.partial(gather_kernel, count, len(arrays), len(i...  222 us
    dot_general x9, matrix products, ein(): return jnp.einsum(spec, left, right, preferred_element_type=full)  149 us
    pallas_call x1, Pallas kernels, routed_expert(): pl.pallas_call(expert_kernel, grid=(count,), in_specs=[chunk, chunk, line...  141 us
    pallas_call x1, Pallas kernels, shared_expert(): pl.pallas_call(shared_kernel, grid=(count,), in_specs=[chunk, chunk, colu...  104 us
    pallas_call x1, Pallas kernels, scatter_now(): pl.pallas_call(functools.partial(scatter_kernel, count), in_specs=[pl.Blo...  79.2 us
    pallas_call x2, Pallas kernels, attention_backward(): pl.pallas_call(backward_kernel, grid_spec=pltpu.PrefetchScalarGridSpec(nu...  76.3 us
    pallas_call x2, Pallas kernels, attention_forward(): pl.pallas_call(forward_kernel, grid_spec=pltpu.PrefetchScalarGridSpec(num...  59.3 us
    unnamed x201, local copies, waits for them, and re-layouts  41.4 us
  transfers between devices with their start and end apart: 46, of which 13 were waited for; matrix products, arithmetic and copies ran while one was open for 26% of the time, Pallas kernels for 57%

profile of v4, /device:TPU:0, one launch (start us, length us, event | category | flops | bytes accessed | tf_op | source)
XLA Modules:
  0.0 1290.0 jit_solution(15414137224480321610)
XLA Ops:
  11.1 19.0 %all_to_all.45 = bf16[8,64,896]{2,1,0:T(8,128)(2,1)} all-to-all(bf16[8,64,896]{2,1,0:T(8,128)(2,1)S(1)} %pad_maximum_fusion.16), channel_id=1, replica_groups=mesh['dp'=4,'ctx'=8] {'ctx'}, dimensions={0} | all-to-all | bytes 1835008 | tf_op jit(solution)/shard_map/all_to_all | solution.py:827
  40.0 143.3 %gather_rows.2 = (bf16[16,256,2048]{2,1,0:T(8,128)(2,1)}, bf16[16,256,2048]{2,1,0:T(8,128)(2,1)}) custom-call(bf16[512,2048]{1,0:T(8,128)(2,1)} %bitcast.314, bf16[512,2048]{1,0:T(8,128)(2,1)} %bitcast.330), custom_call_target="tpu_custom_call" | custom-call | flops 159499993088 | bytes 478500000 | tf_op jit(solution)/shard_map/gather_rows/pallas_call | solution.py:609
  232.9 25.8 %project.1 = (bf16[4096,2048]{1,0:T(8,128)(2,1)}, bf16[4096,256]{1,0:T(8,128)(2,1)S(1)}, bf16[4096,256]{1,0:T(8,128)(2,1)S(1)}, bf16[4096,256]{1,0:T(8,128)(2,1)S(1)}) custom-call(s32[16]{0:T(128)S(1)} %concatenate.79.place_ref, bf16[16,256,2048]{2,1,0:T(8,128)(2,1)} %get-tuple-element.120.x_ref, f32[1,2048]{1,0:T(1,128)S(1)} %copy.179.gain_ref, ...), custom_call_target="tpu_custom_call" | custom-call | flops 26400000000 | bytes 79200000 | tf_op jit(solution)/shard_map/project/pallas_call | solution.py:129
  261.4 3.0 pad_maximum_fusion.12
  268.5 4.1 copy.180
  275.8 29.6 %attend_forward.2 = (bf16[4096,128]{1,0:T(8,128)(2,1)S(1)}, f32[1,4096]{1,0:T(1,128)S(1)}) custom-call(s32[16]{0:T(128)S(1)} %select_reduce_fusion.1.at_ref, bf16[4096,256]{1,0:T(8,128)(2,1)S(1)} %copy-done.26, bf16[4096,256]{1,0:T(8,128)(2,1)S(1)} %get-tuple-element.125.k_ref, bf16[256,4096]{1,0:T(8,128)(2,1)S(1)} %bitcast.294), custom_call_target="tpu_custom_call" | custom-call | flops 32999999488 | bytes 99000000 | tf_op jit(solution)/shard_map/attend_forward/pallas_call | solution.py:386
  311.0 4.2 all-to-all-start.1
  318.0 4.1 fusion.40
  322.4 29.6 %attend_forward.3 = (bf16[4096,128]{1,0:T(8,128)(2,1)S(1)}, f32[1,4096]{1,0:T(1,128)S(1)}) custom-call(s32[16]{0:T(128)S(1)} %select_reduce_fusion.1.at_ref, bf16[4096,256]{1,0:T(8,128)(2,1)S(1)} %copy-done.27, bf16[4096,256]{1,0:T(8,128)(2,1)S(1)} %get-tuple-element.125.k_ref, bf16[256,4096]{1,0:T(8,128)(2,1)S(1)} %bitcast.295), custom_call_target="tpu_custom_call" | custom-call | flops 32999999488 | bytes 99000000 | tf_op jit(solution)/shard_map/attend_forward/pallas_call | solution.py:386
  355.3 4.3 all-to-all-start.2
  360.1 3.5 convert_reduce_fusion
  369.2 5.8 all-to-all-done.2
  376.7 8.4 pad_maximum_fusion
  392.8 5.1 multiply_reduce_fusion.3
  401.0 78.3 %gather_rows.3 = (bf16[16,256,2048]{2,1,0:T(8,128)(2,1)}, f32[8,24,512]{2,1,0:T(8,128)}) custom-call(bf16[512,2048]{1,0:T(8,128)(2,1)} %copy-done.33, f32[24,512]{1,0:T(8,128)} %select_maximum_fusion.refs_1_), custom_call_target="tpu_custom_call" | custom-call | flops 82500001792 | bytes 247500000 | tf_op jit(solution)/shard_map/gather_rows/pallas_call | solution.py:609
  482.6 140.7 %routed_expert.1 = (bf16[8,320,2048]{2,1,0:T(8,128)(2,1)}, bf16[8,320,2048]{2,1,0:T(8,128)(2,1)}, bf16[8,320,1408]{2,1,0:T(8,128)(2,1)}, bf16[8,320,1408]{2,1,0:...) custom-call(bf16[4096,2048]{1,0:T(8,128)(2,1)} %bitcast.366, ...), custom_call_target="tpu_custom_call" | custom-call | flops 153999998976 | bytes 462000000 | tf_op jit(solution)/shard_map/routed_expert/pallas_call | solution.py:259
  623.3 22.1 %bitcast_convert_fusion.2 = bf16[2048,1408]{1,0:T(8,128)(2,1)} fusion(bf16[8,320,2048]{2,1,0:T(8,128)(2,1)} %get-tuple-element.139, bf16[8,320,1408]{2,1,0:T(8,128)(2,1)} %get-tuple-element.140), kind=kOutput, calls=%fused_computation.5 | convolution fusion | flops 14766833664 | bytes 23461888 | tf_op jit(solution)/shard_map/crd,crf->df/dot_general | solution.py:35
  645.4 22.1 %bitcast_convert_fusion.1 = bf16[2048,1408]{1,0:T(8,128)(2,1)} fusion(bf16[8,320,2048]{2,1,0:T(8,128)(2,1)} %get-tuple-element.139, bf16[8,320,1408]{2,1,0:T(8,128)(2,1)} %get-tuple-element.141), kind=kOutput, calls=%fused_computation.4 | convolution fusion | flops 14766833664 | bytes 23461888 | tf_op jit(solution)/shard_map/crd,crf->df/dot_general | solution.py:35
  670.3 104.2 %shared_expert.1 = (bf16[4096,2048]{1,0:T(8,128)(2,1)}, bf16[4096,704]{1,0:T(8,128)(2,1)}, bf16[4096,704]{1,0:T(8,128)(2,1)}, bf16[4096,704]{1,0:T(8,128)(2,1)},...) custom-call(bf16[4096,2048]{1,0:T(8,128)(2,1)} %bitcast.367, ...), custom_call_target="tpu_custom_call" | custom-call | flops 113299996672 | bytes 339900000 | tf_op jit(solution)/shard_map/shared_expert/pallas_call | solution.py:329
  775.0 21.8 %bitcast_convert_fusion = bf16[1408,2048]{1,0:T(8,128)(2,1)} fusion(bf16[8,320,1408]{2,1,0:T(8,128)(2,1)} %get-tuple-element.148, bf16[8,320,2048]{2,1,0:T(8,128)(2,1)} %get-tuple-element.149), kind=kOutput, calls=%fused_computation.3 | convolution fusion | flops 14766833664 | bytes 23461888 | tf_op jit(solution)/shard_map/crf,crd->fd/dot_general | solution.py:35
  797.0 4.7 add_convert_fusion.25
  806.2 17.0 %convolution_convert_fusion.3 = bf16[704,2048]{1,0:T(8,128)(2,1)} fusion(bf16[4096,704]{1,0:T(8,128)(2,1)S(1)} %bitcast.372, bf16[4096,2048]{1,0:T(8,128)(2,1)} %bitcast.368), kind=kOutput, calls=%fused_computation.30 | convolution fusion | flops 11812601856 | bytes 25427968 | tf_op jit(solution)/shard_map/tf,td->fd/dot_general | solution.py:35
  823.3 18.8 %convolution_convert_fusion.4 = bf16[704,2048]{1,0:T(8,128)(2,1)} fusion(bf16[4096,704]{1,0:T(8,128)(2,1)} %get-tuple-element.155, bf16[4096,2048]{1,0:T(8,128)(2,1)} %get-tuple-element.156), kind=kOutput, calls=%fused_computation.31 | convolution fusion | flops 11812601856 | bytes 25427968 | tf_op jit(solution)/shard_map/tf,td->fd/dot_general | solution.py:35
  842.1 9.0 collective-permute-done.9
  852.9 5.5 add_convert_fusion.19
  860.5 18.7 %convolution_convert_fusion.2 = bf16[704,2048]{1,0:T(8,128)(2,1)} fusion(bf16[4096,704]{1,0:T(8,128)(2,1)} %get-tuple-element.161, bf16[4096,2048]{1,0:T(8,128)(2,1)} %bitcast.369), kind=kOutput, calls=%fused_computation.29 | convolution fusion | flops 11812601856 | bytes 25427968 | tf_op jit(solution)/shard_map/tf,td->fd/dot_general | solution.py:35
  879.2 3.9 collective-permute-done.12
  884.2 5.2 add_convert_fusion.18
  889.4 2.5 maximum_convert_fusion
  895.5 3.3 all-to-all-start.3
  899.4 3.0 copy.190
  902.3 2.9 all-to-all-done.3
  905.4 2.8 multiply_reduce_fusion
  910.0 3.3 bitcast_convert_fusion.5
  913.3 4.2 multiply_reduce_fusion.1
  920.7 9.3 convolution_convert_fusion.5
  930.0 3.2 reshape.273
  933.9 3.0 fusion.42
  939.7 8.8 convolution_convert_fusion
  948.6 3.6 all-to-all-start.4
  952.1 4.3 add_convert_fusion.11
  964.7 3.2 all-to-all-done.4
  968.0 4.2 all-to-all-start.5
  972.5 2.7 constant_dynamic-slice_fusion.10
  975.2 2.4 pad_maximum_fusion.2
  978.0 38.3 %attend_backward.2 = (bf16[4096,128]{1,0:T(8,128)(2,1)S(1)}, bf16[4096,128]{1,0:T(8,128)(2,1)S(1)}, bf16[4096,128]{1,0:T(8,128)(2,1)S(1)}) custom-call(s32[16]{0:T(128)S(1)} %select_reduce_fusion.1.at_ref, bf16[4096,256]{1,0:T(8,128)(2,1)} %copy-done.25, bf16[4096,128]{1,0:T(8,128)(2,1)S(1)} %bitcast.298, bf16[4096,128]{1,0:T(8,128)(2,1)S(1)} %get-tuple-element.128.o_ref, ...), custom_call_target="tpu_custom_call" | custom-call | flops 41799999488 | bytes 125400000 | tf_op jit(solution)/shard_map/attend_backward/pallas_call | solution.py:467
  1019.4 4.5 all-to-all-done.5
  1023.8 38.0 %attend_backward.3 = (bf16[4096,128]{1,0:T(8,128)(2,1)S(1)}, bf16[4096,128]{1,0:T(8,128)(2,1)S(1)}, bf16[4096,128]{1,0:T(8,128)(2,1)S(1)}) custom-call(s32[16]{0:T(128)S(1)} %select_reduce_fusion.1.at_ref, bf16[4096,256]{1,0:T(8,128)(2,1)} %copy-done.25, bf16[4096,128]{1,0:T(8,128)(2,1)} %bitcast.107.do_ref, bf16[4096,128]{1,0:T(8,128)(2,1)S(1)} %copy-done.7, ...), custom_call_target="tpu_custom_call" | custom-call | flops 41799999488 | bytes 125400000 | tf_op jit(solution)/shard_map/attend_backward/pallas_call | solution.py:467
  1064.9 3.0 fusion.13
  1069.2 5.6 add_convert_fusion.5
  1080.0 14.1 %collective-permute-done.19 = bf16[256,2048]{1,0:T(8,128)(2,1)S(1)} collective-permute-done((bf16[256,2048]{1,0:T(8,128)(2,1)S(1)}, bf16[256,2048]{1,0:T(8,128)(2,1)S(1)}, u32[]{:S(2)}, u32[]{:S(2)}) %collective-permute-start.19) | collective-permute-done | bytes 1048608 | tf_op jit(solution)/shard_map/ppermute | solution.py:510
  1094.5 3.2 add_convert_fusion.32
  1101.3 19.4 %convolution_convert_fusion.1 = bf16[2048,768]{1,0:T(8,128)(2,1)} fusion(bf16[4096,2048]{1,0:T(8,128)(2,1)} %get-tuple-element.181.normed_ref, bf16[4096,768]{1,0:T(8,128)(2,1)S(1)} %constant_dynamic-update-slice_fusion.grad_ref), kind=kOutput, calls=%fused_computation.28 | convolution fusion | flops 12886474752 | bytes 26214400 | tf_op jit(solution)/shard_map/td,te->de/dot_general | solution.py:35
  1120.7 25.1 %unproject.1 = (bf16[2048,2048]{1,0:T(8,128)(2,1)}, bf16[2048,2048]{1,0:T(8,128)(2,1)}, f32[1,2048]{1,0:T(1,128)S(1)}) custom-call(s32[16]{0:T(128)S(1)} %copy-done.21, bf16[4096,768]{1,0:T(8,128)(2,1)S(1)} %constant_dynamic-update-slice_fusion.grad_ref, bf16[2048,896]{1,0:T(8,128)(2,1)S(1)} %copy-done.19, bf16[4096,2048]{1,0:T(8,128)(2,1)} %get-tuple-element.181.normed_ref), custom_call_target="tpu_custom_call" | custom-call | flops 22000001024 | bytes 66000000 | tf_op jit(solution)/shard_map/unproject/pallas_call | solution.py:183
  1148.1 2.6 add_convert_fusion.31
  1152.7 3.6 all-to-all-start.6
  1156.4 5.2 add_convert_fusion.4
  1164.0 3.3 all-to-all-start.7
  1167.3 4.3 fusion.6
  1176.1 3.4 copy-done.22
  1179.5 79.2 %scatter_rows.1 = f32[2,256,2048]{2,1,0:T(8,128)S(1)} custom-call(bf16[4,2,256,2048]{3,2,1,0:T(8,128)(2,1)S(1)} %bitcast.300, bf16[4,2,256,2048]{3,2,1,0:T(8,128)(2,1)} %bitcast.370), custom_call_target="tpu_custom_call" | custom-call | flops 99000000512 | bytes 297000000 | tf_op jit(solution)/shard_map/scatter_rows/pallas_call | solution.py:783
  1260.7 3.6 all-to-all-start.8
  1266.2 3.3 fusion
  1272.0 3.1 fusion.4
  (399 shorter events, 143.6 us)
Async XLA Ops:
  7.2 216.0 %all-gather.11.cloned.1.call-start = ((), (), s32[]{:S(2)}) async-start(), calls=%async_computation.17 | async-start | bytes 4587520 | tf_op jit(solution)/shard_map/all_gather | solution.py:897
  30.2 452.4 %all-gather.19.cloned.1.call-start = ((), (), s32[]{:S(2)}) async-start(), calls=%async_computation.29 | async-start | bytes 7208960 | tf_op jit(solution)/shard_map/all_gather | solution.py:926
  30.9 451.6 %all-gather.21.cloned.1.call-start = ((), (), s32[]{:S(2)}) async-start(), calls=%async_computation.30 | async-start | bytes 7208960 | tf_op jit(solution)/shard_map/all_gather | solution.py:927
  31.7 450.9 %all-gather.23.cloned.1.call-start = ((), (), s32[]{:S(2)}) async-start(), calls=%async_computation.31 | async-start | bytes 7208960 | tf_op jit(solution)/shard_map/all_gather | solution.py:928
  32.2 638.0 %all-gather.13.cloned.1.call-start = ((), (), s32[]{:S(2)}) async-start(), calls=%async_computation.18 | async-start | bytes 3604480 | tf_op jit(solution)/shard_map/all_gather | solution.py:921
  32.8 637.5 %all-gather.15.cloned.1.call-start = ((), (), s32[]{:S(2)}) async-start(), calls=%async_computation.19 | async-start | bytes 3604480 | tf_op jit(solution)/shard_map/all_gather | solution.py:922
  33.4 636.9 %all-gather.17.cloned.1.call-start = ((), (), s32[]{:S(2)}) async-start(), calls=%async_computation.20 | async-start | bytes 3604480 | tf_op jit(solution)/shard_map/all_gather | solution.py:923
  33.4 184.9 %collective-permute-start = (bf16[64,2048]{1,0:T(8,128)(2,1)}, bf16[64,2048]{1,0:T(8,128)(2,1)}, u32[]{:S(2)}, u32[]{:S(2)}) collective-permute-start(bf16[64,2048]{1,0:T(8,128)(2,1)} %param.32), channel_id=1, source_target_pairs={{0,8},{8,16},{16,24},{24,0},{1,9},{9,17},{17,25},{25,1},{2,10},{10... | collective-permute-start | bytes 786440 | tf_op jit(solution)/shard_map/ppermute | solution.py:908
  35.1 183.3 %collective-permute-start.2 = (bf16[64,2048]{1,0:T(8,128)(2,1)}, bf16[64,2048]{1,0:T(8,128)(2,1)}, u32[]{:S(2)}, u32[]{:S(2)}) collective-permute-start(bf16[64,2048]{1,0:T(8,128)(2,1)} %param.32), channel_id=1, source_target_pairs={{0,24},{8,0},{16,8},{24,16},{1,25},{9,1},{17,9},{25,17},{2,26},{10... | collective-permute-start | bytes 786440 | tf_op jit(solution)/shard_map/ppermute | solution.py:908
  37.3 181.0 %collective-permute-start.1 = (bf16[64,2048]{1,0:T(8,128)(2,1)}, bf16[64,2048]{1,0:T(8,128)(2,1)}, u32[]{:S(2)}, u32[]{:S(2)}) collective-permute-start(bf16[64,2048]{1,0:T(8,128)(2,1)} %param.32), channel_id=1, source_target_pairs={{0,16},{8,24},{16,0},{24,8},{1,17},{9,25},{17,1},{25,9},{2,18},{10... | collective-permute-start | bytes 786440 | tf_op jit(solution)/shard_map/ppermute | solution.py:908
  40.0 143.4 %copy-start.80 = (s32[4]{0:T(128)S(1)}, s32[4]{0:T(128)}, u32[]{:S(2)}) copy-start(s32[4]{0:T(128)} %and_select_fusion) | copy-start | bytes 52
  40.0 170.0 %copy-start.74 = (s32[1,512,4]{1,2,0:T(4,128)S(1)}, s32[1,512,4]{1,2,0:T(4,128)}, u32[]{:S(2)}) copy-start(s32[1,512,4]{1,2,0:T(4,128)} %param.42) | copy-start | bytes 24580
  40.0 178.1 %copy-start.73 = (s32[1,16]{1,0:T(1,128)S(1)}, s32[1,16]{1,0:T(1,128)}, u32[]{:S(2)}) copy-start(s32[1,16]{1,0:T(1,128)} %param.44) | copy-start | bytes 196
  221.1 40.2 %collective-permute-start.4 = (bf16[128,2048]{1,0:T(8,128)(2,1)}, bf16[128,2048]{1,0:T(8,128)(2,1)}, u32[]{:S(2)}, u32[]{:S(2)}) collective-permute-start(bf16[128,2048]{1,0:T(8,128)(2,1)} %get-tuple-element.279), channel_id=1, source_target_pairs={{0,4},{1,5},{2,6},{3,7},{4,0},{5,1},{6,2},{7,3},{8,12},{9,13},{10,... | collective-permute-start | bytes 1572872 | tf_op jit(solution)/shard_map/ppermute | solution.py:510
  222.6 38.8 %collective-permute-start.3 = (bf16[128,2048]{1,0:T(8,128)(2,1)}, bf16[128,2048]{1,0:T(8,128)(2,1)}, u32[]{:S(2)}, u32[]{:S(2)}) collective-permute-start(bf16[128,2048]{1,0:T(8,128)(2,1)} %get-tuple-element.280), channel_id=1, source_target_pairs={{0,2},{1,3},{2,0},{3,1},{4,6},{5,7},{6,4},{7,5},{8,10},{9,11},{10,... | collective-permute-start | bytes 1572872 | tf_op jit(solution)/shard_map/ppermute | solution.py:510
  227.0 171.5 %copy-start.61 = (f32[2048]{0:T(1024)}, f32[2048]{0:T(1024)S(1)}, u32[]{:S(2)}) copy-start(f32[2048]{0:T(1024)S(1)} %get-tuple-element.224) | copy-start | bytes 24580
  261.4 638.0 %copy-start.2 = (bf16[4096,256]{1,0:T(8,128)(2,1)}, bf16[4096,256]{1,0:T(8,128)(2,1)S(1)}, u32[]{:S(2)}) copy-start(bf16[4096,256]{1,0:T(8,128)(2,1)S(1)} %get-tuple-element.125.k_ref) | copy-start | bytes 6291460
  266.7 38.7 %collective-permute-start.6 = (bf16[256,2048]{1,0:T(8,128)(2,1)}, bf16[256,2048]{1,0:T(8,128)(2,1)}, u32[]{:S(2)}, u32[]{:S(2)}) collective-permute-start(bf16[256,2048]{1,0:T(8,128)(2,1)} %pad_maximum_fusion.9), channel_id=1, source_target_pairs={{0,2},{1,3},{2,0},{3,1},{4,6},{5,7},{6,4},{7,5},{8,10},{9,11},{10,... | collective-permute-start | bytes 3145736 | tf_op jit(solution)/shard_map/ppermute | solution.py:510
  268.0 37.5 %collective-permute-start.5 = (bf16[256,2048]{1,0:T(8,128)(2,1)}, bf16[256,2048]{1,0:T(8,128)(2,1)}, u32[]{:S(2)}, u32[]{:S(2)}) collective-permute-start(bf16[256,2048]{1,0:T(8,128)(2,1)} %pad_maximum_fusion.12), channel_id=1, source_target_pairs={{0,4},{1,5},{2,6},{3,7},{4,0},{5,1},{6,2},{7,3},{8,12},{9,13},{10,... | collective-permute-start | bytes 3145736 | tf_op jit(solution)/shard_map/ppermute | solution.py:510
  311.0 42.1 %all-to-all-start.1 = ((bf16[8,512,128]{1,2,0:T(8,128)(2,1)}), bf16[8,512,128]{1,2,0:T(8,128)(2,1)}, u32[]{:S(2)}, u32[]{:S(2)}) async-start(bf16[8,512,128]{1,2,0:T(8,128)(2,1)} %copy.181), calls=%async_computation.1 | async-start | bytes 2097152 | tf_op jit(solution)/shard_map/all_to_all | solution.py:827
  322.1 54.7 %collective-permute-start.7 = (bf16[4,256,2048]{2,1,0:T(8,128)(2,1)}, bf16[4,256,2048]{2,1,0:T(8,128)(2,1)}, u32[]{:S(2)}, u32[]{:S(2)}) collective-permute-start(bf16[4,256,2048]{2,1,0:T(8,128)(2,1)} %get-tuple-element.266), channel_id=1, source_target_pairs={{0,1},{1,0},{2,3},{3,2},{4,5},{5,4},{6,7},{7,6},{8,9},{9,8},{10,11... | collective-permute-start | bytes 12582920 | tf_op jit(solution)/shard_map/ppermute | solution.py:510
  355.3 19.7 %all-to-all-start.2 = ((bf16[8,512,128]{1,2,0:T(8,128)(2,1)}), bf16[8,512,128]{1,2,0:T(8,128)(2,1)}, u32[]{:S(2)}, u32[]{:S(2)}) async-start(bf16[8,512,128]{1,2,0:T(8,128)(2,1)} %copy.182), calls=%async_computation.2 | async-start | bytes 2097152 | tf_op jit(solution)/shard_map/all_to_all | solution.py:827
  359.6 437.3 %reduce-scatter.9.cloned.1.call-start = ((), (), s32[]{:S(2)}) async-start(), calls=%async_computation.21 | async-start | bytes 7208960 | tf_op jit(solution)/shard_map/reduce_scatter | solution.py:819
  376.7 14.6 %copy-start.45 = (bf16[8,512,2,128]{1,3,2,0:T(8,128)(2,1)}, bf16[8,512,2,128]{1,3,2,0:T(8,128)(2,1)S(1)}, u32[]{:S(2)}) copy-start(bf16[8,512,2,128]{1,3,2,0:T(8,128)(2,1)S(1)} %pad_maximum_fusion.3) | copy-start | bytes 6291460
  400.2 79.1 %copy-start.59 = (f32[512,9]{0,1:T(8,128)}, f32[512,9]{0,1:T(8,128)S(1)}, u32[]{:S(2)}) copy-start(f32[512,9]{0,1:T(8,128)S(1)} %fusion.19) | copy-start | bytes 55300
  400.2 79.1 %copy-start.64 = (pred[8,512]{1,0:T(8,128)(4,1)}, pred[8,512]{1,0:T(8,128)(4,1)S(1)}, u32[]{:S(2)}) copy-start(pred[8,512]{1,0:T(8,128)(4,1)S(1)} %get-tuple-element.228) | copy-start | bytes 12292
  400.3 79.1 %copy-start.71 = (f32[512]{0:T(512)}, f32[512]{0:T(512)S(1)}, u32[]{:S(2)}) copy-start(f32[512]{0:T(512)S(1)} %get-tuple-element.227) | copy-start | bytes 6148
  400.3 79.0 %copy-start.76 = (f32[512]{0:T(512)}, f32[512]{0:T(512)S(1)}, u32[]{:S(2)}) copy-start(f32[512]{0:T(512)S(1)} %fusion.24) | copy-start | bytes 6148
  667.5 281.0 %reduce-scatter.11.cloned.1.call-start = ((), (), s32[]{:S(2)}) async-start(), calls=%async_computation.22 | async-start | bytes 7208960 | tf_op jit(solution)/shard_map/reduce_scatter | solution.py:819
  670.2 394.7 %reduce-scatter.13.cloned.1.call-start = ((), (), s32[]{:S(2)}) async-start(), calls=%async_computation.23 | async-start | bytes 7208960 | tf_op jit(solution)/shard_map/reduce_scatter | solution.py:819
  774.6 22.3 %collective-permute-start.8 = (bf16[2048,2048]{1,0:T(8,128)(2,1)}, bf16[2048,2048]{1,0:T(8,128)(2,1)}, u32[]{:S(2)}, u32[]{:S(2)}) collective-permute-start(bf16[2048,2048]{1,0:T(8,128)(2,1)} %get-tuple-element.147), channel_id=1, source_target_pairs={{0,1},{1,0},{2,3},{3,2},{4,5},{5,4},{6,7},{7,6},{8,9},{9,8},{10,11... | collective-permute-start | bytes 25165832 | tf_op jit(solution)/shard_map/ppermute | solution.py:510
  796.9 354.8 %reduce-scatter.21.cloned.1.call-start = ((), (), s32[]{:S(2)}) async-start(), calls=%async_computation.27 | async-start | bytes 3604480 | tf_op jit(solution)/shard_map/reduce_scatter | solution.py:819
  803.2 47.9 %collective-permute-start.9 = (bf16[512,2048]{1,0:T(8,128)(2,1)}, bf16[512,2048]{1,0:T(8,128)(2,1)}, u32[]{:S(2)}, u32[]{:S(2)}) collective-permute-start(bf16[512,2048]{1,0:T(8,128)(2,1)} %pad_maximum_fusion.4), channel_id=1, source_target_pairs={{0,2},{1,3},{2,0},{3,1},{4,6},{5,7},{6,4},{7,5},{8,10},{9,11},{10,... | collective-permute-start | bytes 6291464 | tf_op jit(solution)/shard_map/ppermute | solution.py:510
  804.8 47.9 %collective-permute-start.10 = (bf16[512,2048]{1,0:T(8,128)(2,1)}, bf16[512,2048]{1,0:T(8,128)(2,1)}, u32[]{:S(2)}, u32[]{:S(2)}) collective-permute-start(bf16[512,2048]{1,0:T(8,128)(2,1)} %pad_maximum_fusion.5), channel_id=1, source_target_pairs={{0,4},{1,5},{2,6},{3,7},{4,0},{5,1},{6,2},{7,3},{8,12},{9,13},{10,... | collective-permute-start | bytes 6291464 | tf_op jit(solution)/shard_map/ppermute | solution.py:510
  852.7 408.1 %reduce-scatter.15.cloned.1.call-start = ((), (), s32[]{:S(2)}) async-start(), calls=%async_computation.24 | async-start | bytes 3604480 | tf_op jit(solution)/shard_map/reduce_scatter | solution.py:819
  858.5 24.6 %collective-permute-start.12 = (bf16[256,2048]{1,0:T(8,128)(2,1)}, bf16[256,2048]{1,0:T(8,128)(2,1)}, u32[]{:S(2)}, u32[]{:S(2)}) collective-permute-start(bf16[256,2048]{1,0:T(8,128)(2,1)} %get-tuple-element.239), channel_id=1, source_target_pairs={{0,2},{1,3},{2,0},{3,1},{4,6},{5,7},{6,4},{7,5},{8,10},{9,11},{10,... | collective-permute-start | bytes 3145736 | tf_op jit(solution)/shard_map/ppermute | solution.py:510
  860.2 24.0 %collective-permute-start.11 = (bf16[256,2048]{1,0:T(8,128)(2,1)}, bf16[256,2048]{1,0:T(8,128)(2,1)}, u32[]{:S(2)}, u32[]{:S(2)}) collective-permute-start(bf16[256,2048]{1,0:T(8,128)(2,1)} %get-tuple-element.240), channel_id=1, source_target_pairs={{0,4},{1,5},{2,6},{3,7},{4,0},{5,1},{6,2},{7,3},{8,12},{9,13},{10,... | collective-permute-start | bytes 3145736 | tf_op jit(solution)/shard_map/ppermute | solution.py:510
  891.9 56.7 %collective-permute-start.13 = (bf16[2048,2048]{1,0:T(8,128)(2,1)}, bf16[2048,2048]{1,0:T(8,128)(2,1)}, u32[]{:S(2)}, u32[]{:S(2)}) collective-permute-start(bf16[2048,2048]{1,0:T(8,128)(2,1)} %get-tuple-element.164), channel_id=1, source_target_pairs={{0,1},{1,0},{2,3},{3,2},{4,5},{5,4},{6,7},{7,6},{8,9},{9,8},{10,11... | collective-permute-start | bytes 25165832 | tf_op jit(solution)/shard_map/ppermute | solution.py:510
  895.5 9.7 all-to-all-start.3
  898.9 361.9 %reduce-scatter.17.cloned.1.call-start = ((), (), s32[]{:S(2)}) async-start(), calls=%async_computation.25 | async-start | bytes 3604480 | tf_op jit(solution)/shard_map/reduce_scatter | solution.py:819
  948.6 19.4 %all-to-all-start.4 = ((bf16[8,512,128]{2,1,0:T(8,128)(2,1)}), bf16[8,512,128]{2,1,0:T(8,128)(2,1)S(1)}, u32[]{:S(2)}, u32[]{:S(2)}) async-start(bf16[8,512,128]{2,1,0:T(8,128)(2,1)} %bitcast.289), calls=%async_computation.6 | async-start | bytes 2097152 | tf_op jit(solution)/shard_map/all_to_all | solution.py:827
  958.0 106.9 %collective-permute-start.14 = (bf16[512,2048]{1,0:T(8,128)(2,1)}, bf16[512,2048]{1,0:T(8,128)(2,1)}, u32[]{:S(2)}, u32[]{:S(2)}) collective-permute-start(bf16[512,2048]{1,0:T(8,128)(2,1)} %pad_maximum_fusion.6), channel_id=1, source_target_pairs={{0,2},{1,3},{2,0},{3,1},{4,6},{5,7},{6,4},{7,5},{8,10},{9,11},{10,... | collective-permute-start | bytes 6291464 | tf_op jit(solution)/shard_map/ppermute | solution.py:510
  961.5 103.4 %collective-permute-start.15 = (bf16[512,2048]{1,0:T(8,128)(2,1)}, bf16[512,2048]{1,0:T(8,128)(2,1)}, u32[]{:S(2)}, u32[]{:S(2)}) collective-permute-start(bf16[512,2048]{1,0:T(8,128)(2,1)} %pad_maximum_fusion.7), channel_id=1, source_target_pairs={{0,4},{1,5},{2,6},{3,7},{4,0},{5,1},{6,2},{7,3},{8,12},{9,13},{10,... | collective-permute-start | bytes 6291464 | tf_op jit(solution)/shard_map/ppermute | solution.py:510
  968.0 55.9 %all-to-all-start.5 = ((bf16[8,512,128]{2,1,0:T(8,128)(2,1)}), bf16[8,512,128]{2,1,0:T(8,128)(2,1)}, u32[]{:S(2)}, u32[]{:S(2)}) async-start(bf16[8,512,128]{2,1,0:T(8,128)(2,1)} %bitcast.288), calls=%async_computation.7 | async-start | bytes 2097152 | tf_op jit(solution)/shard_map/all_to_all | solution.py:827
  972.2 288.5 %reduce-scatter.23.cloned.1.call-start = ((), (), s32[]{:S(2)}) async-start(), calls=%async_computation.28 | async-start | bytes 1310720 | tf_op jit(solution)/shard_map/reduce_scatter | solution.py:1137
  975.2 42.1 %slice-start = ((s8[8388608]{0:T(1024)(128)(4,1)}), s8[4194304]{0:T(1024)(128)(4,1)S(1)}, s32[]{:S(2)}) async-start(s8[8388608]{0:T(1024)(128)(4,1)} %bitcast.311), calls=%async_computation.32 | async-start | bytes 8388608
  977.6 46.2 %collective-permute-start.16 = (bf16[1024,2048]{1,0:T(8,128)(2,1)}, bf16[1024,2048]{1,0:T(8,128)(2,1)}, u32[]{:S(2)}, u32[]{:S(2)}) collective-permute-start(bf16[1024,2048]{1,0:T(8,128)(2,1)} %pad_maximum_fusion.2), channel_id=1, source_target_pairs={{0,1},{1,0},{2,3},{3,2},{4,5},{5,4},{6,7},{7,6},{8,9},{9,8},{10,11... | collective-permute-start | bytes 12582920 | tf_op jit(solution)/shard_map/ppermute | solution.py:510
  978.0 39.3 %slice-start.1 = ((s8[8388608]{0:T(1024)(128)(4,1)}), s8[4194304]{0:T(1024)(128)(4,1)S(1)}, s32[]{:S(2)}) async-start(s8[8388608]{0:T(1024)(128)(4,1)} %bitcast.311), calls=%async_computation.33 | async-start | bytes 8388608
  1068.0 26.2 %collective-permute-start.19 = (bf16[256,2048]{1,0:T(8,128)(2,1)S(1)}, bf16[256,2048]{1,0:T(8,128)(2,1)S(1)}, u32[]{:S(2)}, u32[]{:S(2)}) collective-permute-start(bf16[256,2048]{1,0:T(8,128)(2,1)S(1)} %pad_maximum_fusion.13), channel_id=1, source_target_pairs={{0,2},{1,3},{2,0},{3,1},{4,6},{5,7},{6,4},{7,5},{8,10},{9,11},{10,... | collective-permute-start | bytes 3145736 | tf_op jit(solution)/shard_map/ppermute | solution.py:510
  1068.4 26.1 %collective-permute-start.20 = (bf16[256,2048]{1,0:T(8,128)(2,1)S(1)}, bf16[256,2048]{1,0:T(8,128)(2,1)S(1)}, u32[]{:S(2)}, u32[]{:S(2)}) collective-permute-start(bf16[256,2048]{1,0:T(8,128)(2,1)S(1)} %pad_maximum_fusion.14), channel_id=1, source_target_pairs={{0,4},{1,5},{2,6},{3,7},{4,0},{5,1},{6,2},{7,3},{8,12},{9,13},{10,... | collective-permute-start | bytes 3145736 | tf_op jit(solution)/shard_map/ppermute | solution.py:510
  1074.8 19.7 %copy-start.48 = (bf16[2,1,64,2048]{3,2,1,0:T(8,128)(2,1)S(1)}, bf16[2,1,64,2048]{3,2,1,0:T(8,128)(2,1)}, u32[]{:S(2)}) copy-start(bf16[2,1,64,2048]{3,2,1,0:T(8,128)(2,1)} %get-tuple-element.250) | copy-start | bytes 1572868
  1074.8 19.7 %copy-start.49 = (bf16[2,1,64,2048]{3,2,1,0:T(8,128)(2,1)S(1)}, bf16[2,1,64,2048]{3,2,1,0:T(8,128)(2,1)}, u32[]{:S(2)}) copy-start(bf16[2,1,64,2048]{3,2,1,0:T(8,128)(2,1)} %get-tuple-element.252) | copy-start | bytes 1572868
  1074.8 73.1 %collective-permute-start.18 = (bf16[256,2048]{1,0:T(8,128)(2,1)}, bf16[256,2048]{1,0:T(8,128)(2,1)}, u32[]{:S(2)}, u32[]{:S(2)}) collective-permute-start(bf16[256,2048]{1,0:T(8,128)(2,1)} %get-tuple-element.231), channel_id=1, source_target_pairs={{0,2},{1,3},{2,0},{3,1},{4,6},{5,7},{6,4},{7,5},{8,10},{9,11},{10,... | collective-permute-start | bytes 3145736 | tf_op jit(solution)/shard_map/ppermute | solution.py:510
  1076.5 71.4 %collective-permute-start.17 = (bf16[256,2048]{1,0:T(8,128)(2,1)}, bf16[256,2048]{1,0:T(8,128)(2,1)}, u32[]{:S(2)}, u32[]{:S(2)}) collective-permute-start(bf16[256,2048]{1,0:T(8,128)(2,1)} %get-tuple-element.232), channel_id=1, source_target_pairs={{0,4},{1,5},{2,6},{3,7},{4,0},{5,1},{6,2},{7,3},{8,12},{9,13},{10,... | collective-permute-start | bytes 3145736 | tf_op jit(solution)/shard_map/ppermute | solution.py:510
  1078.1 21.9 %copy-start.15 = (bf16[4096,128]{1,0:T(8,128)(2,1)S(1)}, bf16[4096,128]{1,0:T(8,128)(2,1)}, u32[]{:S(2)}) copy-start(bf16[4096,128]{1,0:T(8,128)(2,1)} %copy-done.14) | copy-start | bytes 3145732
  1097.7 50.3 %collective-permute-start.22 = (bf16[128,2048]{1,0:T(8,128)(2,1)}, bf16[128,2048]{1,0:T(8,128)(2,1)}, u32[]{:S(2)}, u32[]{:S(2)}) collective-permute-start(bf16[128,2048]{1,0:T(8,128)(2,1)} %get-tuple-element.259), channel_id=1, source_target_pairs={{0,2},{1,3},{2,0},{3,1},{4,6},{5,7},{6,4},{7,5},{8,10},{9,11},{10,... | collective-permute-start | bytes 1572872 | tf_op jit(solution)/shard_map/ppermute | solution.py:510
  1099.5 48.5 %collective-permute-start.21 = (bf16[128,2048]{1,0:T(8,128)(2,1)}, bf16[128,2048]{1,0:T(8,128)(2,1)}, u32[]{:S(2)}, u32[]{:S(2)}) collective-permute-start(bf16[128,2048]{1,0:T(8,128)(2,1)} %get-tuple-element.260), channel_id=1, source_target_pairs={{0,4},{1,5},{2,6},{3,7},{4,0},{5,1},{6,2},{7,3},{8,12},{9,13},{10,... | collective-permute-start | bytes 1572872 | tf_op jit(solution)/shard_map/ppermute | solution.py:510
  1101.3 19.4 %copy-start.19 = (bf16[2048,896]{1,0:T(8,128)(2,1)S(1)}, bf16[2048,896]{1,0:T(8,128)(2,1)}, u32[]{:S(2)}) copy-start(bf16[2048,896]{1,0:T(8,128)(2,1)} %all-gather.11.cloned.1.call-done.w_ref) | copy-start | bytes 11010052
  1101.3 19.4 %copy-start.21 = (s32[16]{0:T(128)S(1)}, s32[16]{0:T(128)}, u32[]{:S(2)}) copy-start(s32[16]{0:T(128)} %copy-done.20) | copy-start | bytes 196
  1152.7 8.9 all-to-all-start.6
  1164.0 8.9 all-to-all-start.7
  1167.2 93.5 %reduce-scatter.19.cloned.1.call-start = ((), (), s32[]{:S(2)}) async-start(), calls=%async_computation.26 | async-start | bytes 3932160 | tf_op jit(solution)/shard_map/reduce_scatter | solution.py:1131
  1179.5 86.7 %copy-start.40 = (bf16[1,512,2048]{2,1,0:T(8,128)(2,1)S(1)}, bf16[1,512,2048]{2,1,0:T(8,128)(2,1)}, u32[]{:S(2)}) copy-start(bf16[1,512,2048]{2,1,0:T(8,128)(2,1)} %param.24) | copy-start | bytes 6291460
  1260.7 16.1 %all-to-all-start.8 = ((bf16[8,64,768]{2,1,0:T(8,128)(2,1)}), bf16[8,64,768]{2,1,0:T(8,128)(2,1)S(1)}, u32[]{:S(2)}, u32[]{:S(2)}) async-start(bf16[8,64,768]{2,1,0:T(8,128)(2,1)} %bitcast.332), calls=%async_computation.16 | async-start | bytes 1572864 | tf_op jit(solution)/shard_map/all_to_all | solution.py:827
  (68 other events, 304.9 us)
Sparse Core Ops, SparseCore 0:
  30.3 89.5 all-gather.10
  121.5 104.2 all-gather.18
  227.3 105.0 all-gather.20
  333.8 105.1 all-gather.22
  440.4 57.4 all-gather.12
  499.4 57.8 all-gather.14
  558.8 57.8 all-gather.16
  667.6 101.2 reduce-scatter.8
  771.2 102.7 reduce-scatter.10
  876.2 102.7 reduce-scatter.12
  981.3 56.7 reduce-scatter.20
  1040.2 56.0 reduce-scatter.14
  1098.5 56.0 reduce-scatter.16
  1157.3 27.2 reduce-scatter.22
  1186.8 58.9 reduce-scatter.18

commit v5 on v4

--- a/solution.py
+++ b/solution.py
@@ -901,7 +901,6 @@
     gain_one, gain_two, mix_row = small_all[0:1], small_all[4:5], small_all[5:6]
     mix_router = small_all[5:].astype(low)
     partners = jnp.arange(ctx_count, dtype=jnp.int32) ^ ctx_index
-    origin = (dp_index - jnp.arange(dp_count, dtype=jnp.int32)) % dp_count
     out_around = jnp.stack(
         [w_out]
         + [
@@ -912,7 +911,8 @@
     x_blocks, cot_all = gather_now([tokens_low, cot_low], None, 0, 145)
     cot_all = cot_all.reshape(group_len, D)
     out_mine = jnp.concatenate(
-        [lax.dynamic_index_in_dim(out_around, origin[p], 0, False) for p in range(dp_count)], axis=0
+        [lax.dynamic_index_in_dim(out_around, (dp_index + dp_count - p) % dp_count, 0, False)
+            for p in range(dp_count)], axis=0
     )
     (out_mine,), x_blocks = pin([out_mine], x_blocks)
     out_steps = gather_steps(out_mine)
@@ -944,15 +944,9 @@
         jnp.where(stored_to_place[None, :] == block_grid[:, None], block_grid[None, :], 0), axis=1
     )
     per_device = block_count // ctx_count
-    near = partners * per_device
-    stored_near = jnp.concatenate(
-        [
-            lax.dynamic_slice_in_dim(stored_to_place, near[m], per_device)
-            for m in range(ctx_count)
-        ]
-    )
-    place_to_near = (place_to_stored // per_device ^ ctx_index) * per_device + (
-        place_to_stored % per_device
+    near = (block_grid // per_device ^ ctx_index) * per_device + block_grid % per_device
+    stored_near = jnp.sum(
+        jnp.where(near[:, None] == block_grid[None, :], stored_to_place[None, :], 0), axis=1
     )
     cosine_wide, sine_wide = rope_tables(group_len)
     my_heads = (ctx_index // repeat) * width
@@ -985,10 +979,11 @@
     out_parts = out_parts.reshape(ctx_count, dp_count, shard, D)
     out_full = (
         jnp.stack(
-            [lax.dynamic_index_in_dim(out_parts, partners[i], 0, False) for i in range(ctx_count)],
+            [lax.dynamic_index_in_dim(out_parts, ctx_index ^ i, 0, False) for i in range(ctx_count)],
             axis=1,
         )
     ).reshape(D, D)
+    parts, out_full = pin(parts, out_full)
     attended_parts = jnp.stack(parts, axis=2).reshape(head_sets, tok_count, width)
     attended = attended_parts.transpose(1, 0, 2).reshape(tok_count, D)
     first_sum = tokens + dot(attended, out_full)
@@ -1080,7 +1075,7 @@
     def out_rows_of(first):
         return jnp.concatenate(
             [
-                lax.dynamic_index_in_dim(grad_out, partners[m], 1, False).reshape(-1, D)
+                lax.dynamic_index_in_dim(grad_out, ctx_index ^ m, 1, False).reshape(-1, D)
                 for m in range(first, ctx_count, 2)
             ],
             axis=0,

time: 1300 us -> 1280 us (0.985)
  between operations: 55 us -> 15.7 us
    unnamed x201 -> x193, local copies, waits for them, and re-layouts: 41.4 us -> 50.9 us
  transfers between devices with their start and end apart: 46 -> 46, of which waited for: 13 -> 12; matrix products, arithmetic and copies ran while one was open for 26% -> 27% of each run, Pallas kernels for 57% -> 58%
where the time goes in v5:
time: 1280 us; the launch traced here: 1270 us
  Pallas kernels  733 us (57%)
  matrix products  172 us (13%)
  other arithmetic  117 us (9%)
  local copies, waits for them, and re-layouts  96.1 us (8%)
  starting transfers between devices  65.8 us (5%)
  waiting for transfers between devices  47 us (4%)
  blocking collectives  19 us (1%)
  between operations  15.7 us (1%)
    pallas_call x2, Pallas kernels, gather_now(): pl.pallas_call(functools.partial(gather_kernel, count, len(arrays), len(i...  223 us
    dot_general x9, matrix products, ein(): return jnp.einsum(spec, left, right, preferred_element_type=full)  150 us
    pallas_call x1, Pallas kernels, routed_expert(): pl.pallas_call(expert_kernel, grid=(count,), in_specs=[chunk, chunk, line...  141 us
    pallas_call x1, Pallas kernels, shared_expert(): pl.pallas_call(shared_kernel, grid=(count,), in_specs=[chunk, chunk, colu...  104 us
    pallas_call x1, Pallas kernels, scatter_now(): pl.pallas_call(functools.partial(scatter_kernel, count), in_specs=[pl.Blo...  79 us
    pallas_call x2, Pallas kernels, attention_backward(): pl.pallas_call(backward_kernel, grid_spec=pltpu.PrefetchScalarGridSpec(nu...  76.3 us
    pallas_call x2, Pallas kernels, attention_forward(): pl.pallas_call(forward_kernel, grid_spec=pltpu.PrefetchScalarGridSpec(num...  59.3 us
    unnamed x193, local copies, waits for them, and re-layouts  50.9 us
  transfers between devices with their start and end apart: 46, of which 12 were waited for; matrix products, arithmetic and copies ran while one was open for 27% of the time, Pallas kernels for 58%

profile of v5, /device:TPU:0, one launch (start us, length us, event | category | flops | bytes accessed | tf_op | source)
XLA Modules:
  0.0 1265.6 jit_solution(10930155851630015017)
XLA Ops:
  11.1 19.0 %all_to_all.45 = bf16[8,64,896]{2,1,0:T(8,128)(2,1)} all-to-all(bf16[8,64,896]{2,1,0:T(8,128)(2,1)S(1)} %pad_maximum_fusion.16), channel_id=1, replica_groups=mesh['dp'=4,'ctx'=8] {'ctx'}, dimensions={0} | all-to-all | bytes 1835008 | tf_op jit(solution)/shard_map/all_to_all | solution.py:827
  37.6 143.3 %gather_rows.2 = (bf16[16,256,2048]{2,1,0:T(8,128)(2,1)}, bf16[16,256,2048]{2,1,0:T(8,128)(2,1)}) custom-call(bf16[512,2048]{1,0:T(8,128)(2,1)} %bitcast.278, bf16[512,2048]{1,0:T(8,128)(2,1)} %bitcast.294), custom_call_target="tpu_custom_call" | custom-call | flops 159499993088 | bytes 478500000 | tf_op jit(solution)/shard_map/gather_rows/pallas_call | solution.py:609
  195.6 25.6 %project.1 = (bf16[4096,2048]{1,0:T(8,128)(2,1)}, bf16[4096,256]{1,0:T(8,128)(2,1)S(1)}, bf16[4096,256]{1,0:T(8,128)(2,1)S(1)}, bf16[4096,256]{1,0:T(8,128)(2,1)S(1)}) custom-call(s32[16]{0:T(128)S(1)} %get-tuple-element.234.place_ref, bf16[16,256,2048]{2,1,0:T(8,128)(2,1)} %get-tuple-element.123.x_ref, f32[1,2048]{1,0:T(1,128)S(1)} %copy.179.gain_ref, ...), custom_call_target="tpu_custom_call" | custom-call | flops 26400000000 | bytes 79200000 | tf_op jit(solution)/shard_map/project/pallas_call | solution.py:129
  223.8 3.0 pad_maximum_fusion.12
  231.1 4.2 copy.180
  238.7 29.6 %attend_forward.2 = (bf16[4096,128]{1,0:T(8,128)(2,1)S(1)}, f32[1,4096]{1,0:T(1,128)S(1)}) custom-call(s32[16]{0:T(128)S(1)} %get-tuple-element.233.at_ref, bf16[4096,256]{1,0:T(8,128)(2,1)S(1)} %copy-done.26, bf16[4096,256]{1,0:T(8,128)(2,1)S(1)} %get-tuple-element.128.k_ref, bf16[256,4096]{1,0:T(8,128)(2,1)S(1)} %bitcast.258), custom_call_target="tpu_custom_call" | custom-call | flops 32999999488 | bytes 99000000 | tf_op jit(solution)/shard_map/attend_forward/pallas_call | solution.py:386
  273.5 3.7 fusion.34
  277.6 3.5 convert_reduce_fusion
  282.8 4.2 all-to-all-start.1
  290.2 29.6 %attend_forward.3 = (bf16[4096,128]{1,0:T(8,128)(2,1)S(1)}, f32[1,4096]{1,0:T(1,128)S(1)}) custom-call(s32[16]{0:T(128)S(1)} %get-tuple-element.233.at_ref, bf16[4096,256]{1,0:T(8,128)(2,1)S(1)} %copy-done.27, bf16[4096,256]{1,0:T(8,128)(2,1)S(1)} %get-tuple-element.128.k_ref, bf16[256,4096]{1,0:T(8,128)(2,1)S(1)} %bitcast.259), custom_call_target="tpu_custom_call" | custom-call | flops 32999999488 | bytes 99000000 | tf_op jit(solution)/shard_map/attend_forward/pallas_call | solution.py:386
  323.1 4.2 all-to-all-start.2
  327.4 12.0 reduce-scatter.9.cloned.1.call-start
  339.3 8.3 pad_maximum_fusion
  347.6 2.5 bitcast_dynamic-update-slice_fusion.7
  350.1 3.0 bitcast_dynamic-update-slice_fusion.6
  364.4 7.6 multiply_reduce_fusion.3
  375.1 79.8 %gather_rows.3 = (bf16[16,256,2048]{2,1,0:T(8,128)(2,1)}, f32[8,24,512]{2,1,0:T(8,128)}) custom-call(bf16[512,2048]{1,0:T(8,128)(2,1)} %copy-done.33, f32[24,512]{1,0:T(8,128)} %select_maximum_fusion.refs_1_), custom_call_target="tpu_custom_call" | custom-call | flops 82500001792 | bytes 247500000 | tf_op jit(solution)/shard_map/gather_rows/pallas_call | solution.py:609
  458.2 140.7 %routed_expert.1 = (bf16[8,320,2048]{2,1,0:T(8,128)(2,1)}, bf16[8,320,2048]{2,1,0:T(8,128)(2,1)}, bf16[8,320,1408]{2,1,0:T(8,128)(2,1)}, bf16[8,320,1408]{2,1,0:...) custom-call(bf16[4096,2048]{1,0:T(8,128)(2,1)} %bitcast.328, ...), custom_call_target="tpu_custom_call" | custom-call | flops 153999998976 | bytes 462000000 | tf_op jit(solution)/shard_map/routed_expert/pallas_call | solution.py:259
  598.9 22.2 %bitcast_convert_fusion.2 = bf16[2048,1408]{1,0:T(8,128)(2,1)} fusion(bf16[8,320,2048]{2,1,0:T(8,128)(2,1)} %get-tuple-element.145, bf16[8,320,1408]{2,1,0:T(8,128)(2,1)} %get-tuple-element.146), kind=kOutput, calls=%fused_computation.5 | convolution fusion | flops 14766833664 | bytes 23461888 | tf_op jit(solution)/shard_map/crd,crf->df/dot_general | solution.py:35
  621.0 22.2 %bitcast_convert_fusion.1 = bf16[2048,1408]{1,0:T(8,128)(2,1)} fusion(bf16[8,320,2048]{2,1,0:T(8,128)(2,1)} %get-tuple-element.145, bf16[8,320,1408]{2,1,0:T(8,128)(2,1)} %get-tuple-element.147), kind=kOutput, calls=%fused_computation.4 | convolution fusion | flops 14766833664 | bytes 23461888 | tf_op jit(solution)/shard_map/crd,crf->df/dot_general | solution.py:35
  646.0 104.0 %shared_expert.1 = (bf16[4096,2048]{1,0:T(8,128)(2,1)}, bf16[4096,704]{1,0:T(8,128)(2,1)}, bf16[4096,704]{1,0:T(8,128)(2,1)}, bf16[4096,704]{1,0:T(8,128)(2,1)},...) custom-call(bf16[4096,2048]{1,0:T(8,128)(2,1)} %bitcast.329, ...), custom_call_target="tpu_custom_call" | custom-call | flops 113299996672 | bytes 339900000 | tf_op jit(solution)/shard_map/shared_expert/pallas_call | solution.py:329
  750.5 21.8 %bitcast_convert_fusion = bf16[1408,2048]{1,0:T(8,128)(2,1)} fusion(bf16[8,320,1408]{2,1,0:T(8,128)(2,1)} %get-tuple-element.154, bf16[8,320,2048]{2,1,0:T(8,128)(2,1)} %get-tuple-element.155), kind=kOutput, calls=%fused_computation.3 | convolution fusion | flops 14766833664 | bytes 23461888 | tf_op jit(solution)/shard_map/crf,crd->fd/dot_general | solution.py:35
  772.5 4.7 add_convert_fusion.25
  781.4 17.1 %convolution_convert_fusion.3 = bf16[704,2048]{1,0:T(8,128)(2,1)} fusion(bf16[4096,704]{1,0:T(8,128)(2,1)S(1)} %bitcast.334, bf16[4096,2048]{1,0:T(8,128)(2,1)} %bitcast.330), kind=kOutput, calls=%fused_computation.30 | convolution fusion | flops 11812601856 | bytes 25427968 | tf_op jit(solution)/shard_map/tf,td->fd/dot_general | solution.py:35
  798.5 18.8 %convolution_convert_fusion.4 = bf16[704,2048]{1,0:T(8,128)(2,1)} fusion(bf16[4096,704]{1,0:T(8,128)(2,1)} %get-tuple-element.161, bf16[4096,2048]{1,0:T(8,128)(2,1)} %get-tuple-element.162), kind=kOutput, calls=%fused_computation.31 | convolution fusion | flops 11812601856 | bytes 25427968 | tf_op jit(solution)/shard_map/tf,td->fd/dot_general | solution.py:35
  817.3 9.3 collective-permute-done.9
  829.4 5.5 add_convert_fusion.19
  836.9 18.7 %convolution_convert_fusion.2 = bf16[704,2048]{1,0:T(8,128)(2,1)} fusion(bf16[4096,704]{1,0:T(8,128)(2,1)} %get-tuple-element.167, bf16[4096,2048]{1,0:T(8,128)(2,1)} %bitcast.331), kind=kOutput, calls=%fused_computation.29 | convolution fusion | flops 11812601856 | bytes 25427968 | tf_op jit(solution)/shard_map/tf,td->fd/dot_general | solution.py:35
  855.7 3.5 collective-permute-done.12
  859.8 5.2 add_convert_fusion.18
  871.1 3.3 all-to-all-start.3
  874.7 3.0 copy.190
  877.7 3.1 all-to-all-done.3
  880.9 2.8 multiply_reduce_fusion
  885.6 3.3 bitcast_convert_fusion.5
  888.9 4.2 multiply_reduce_fusion.1
  896.4 9.3 convolution_convert_fusion.5
  905.7 3.2 reshape.288
  909.7 3.0 fusion.36
  915.4 8.8 convolution_convert_fusion
  924.3 3.6 all-to-all-start.4
  927.8 4.3 add_convert_fusion.11
  940.5 3.2 all-to-all-done.4
  943.7 4.3 all-to-all-start.5
  948.2 2.7 constant_dynamic-slice_fusion.10
  953.7 38.3 %attend_backward.2 = (bf16[4096,128]{1,0:T(8,128)(2,1)S(1)}, bf16[4096,128]{1,0:T(8,128)(2,1)S(1)}, bf16[4096,128]{1,0:T(8,128)(2,1)S(1)}) custom-call(s32[16]{0:T(128)S(1)} %get-tuple-element.233.at_ref, bf16[4096,256]{1,0:T(8,128)(2,1)} %copy-done.25, bf16[4096,128]{1,0:T(8,128)(2,1)S(1)} %bitcast.262, bf16[4096,128]{1,0:T(8,128)(2,1)S(1)} %get-tuple-element.131.o_ref, ...), custom_call_target="tpu_custom_call" | custom-call | flops 41799999488 | bytes 125400000 | tf_op jit(solution)/shard_map/attend_backward/pallas_call | solution.py:467
  995.1 4.4 all-to-all-done.5
  999.6 38.0 %attend_backward.3 = (bf16[4096,128]{1,0:T(8,128)(2,1)S(1)}, bf16[4096,128]{1,0:T(8,128)(2,1)S(1)}, bf16[4096,128]{1,0:T(8,128)(2,1)S(1)}) custom-call(s32[16]{0:T(128)S(1)} %get-tuple-element.233.at_ref, bf16[4096,256]{1,0:T(8,128)(2,1)} %copy-done.25, bf16[4096,128]{1,0:T(8,128)(2,1)} %bitcast.79.do_ref, bf16[4096,128]{1,0:T(8,128)(2,1)S(1)} %copy-done.7, ...), custom_call_target="tpu_custom_call" | custom-call | flops 41799999488 | bytes 125400000 | tf_op jit(solution)/shard_map/attend_backward/pallas_call | solution.py:467
  1040.5 3.0 fusion.13
  1044.9 5.6 add_convert_fusion.5
  1055.7 14.1 %collective-permute-done.19 = bf16[256,2048]{1,0:T(8,128)(2,1)S(1)} collective-permute-done((bf16[256,2048]{1,0:T(8,128)(2,1)S(1)}, bf16[256,2048]{1,0:T(8,128)(2,1)S(1)}, u32[]{:S(2)}, u32[]{:S(2)}) %collective-permute-start.19) | collective-permute-done | bytes 1048608 | tf_op jit(solution)/shard_map/ppermute | solution.py:510
  1070.2 3.2 add_convert_fusion.32
  1077.0 19.8 %convolution_convert_fusion.1 = bf16[2048,768]{1,0:T(8,128)(2,1)} fusion(bf16[4096,2048]{1,0:T(8,128)(2,1)} %get-tuple-element.187.normed_ref, bf16[4096,768]{1,0:T(8,128)(2,1)S(1)} %constant_dynamic-update-slice_fusion.grad_ref), kind=kOutput, calls=%fused_computation.28 | convolution fusion | flops 12886474752 | bytes 26214400 | tf_op jit(solution)/shard_map/td,te->de/dot_general | solution.py:35
  1096.7 25.1 %unproject.1 = (bf16[2048,2048]{1,0:T(8,128)(2,1)}, bf16[2048,2048]{1,0:T(8,128)(2,1)}, f32[1,2048]{1,0:T(1,128)S(1)}) custom-call(s32[16]{0:T(128)S(1)} %copy-done.21, bf16[4096,768]{1,0:T(8,128)(2,1)S(1)} %constant_dynamic-update-slice_fusion.grad_ref, bf16[2048,896]{1,0:T(8,128)(2,1)S(1)} %copy-done.19, bf16[4096,2048]{1,0:T(8,128)(2,1)} %get-tuple-element.187.normed_ref), custom_call_target="tpu_custom_call" | custom-call | flops 22000001024 | bytes 66000000 | tf_op jit(solution)/shard_map/unproject/pallas_call | solution.py:183
  1124.0 2.6 add_convert_fusion.31
  1128.7 3.5 all-to-all-start.6
  1132.3 5.2 add_convert_fusion.4
  1139.9 3.3 all-to-all-start.7
  1143.2 4.3 fusion.6
  1152.1 3.4 copy-done.22
  1155.6 79.0 %scatter_rows.1 = f32[2,256,2048]{2,1,0:T(8,128)S(1)} custom-call(bf16[4,2,256,2048]{3,2,1,0:T(8,128)(2,1)S(1)} %bitcast.264, bf16[4,2,256,2048]{3,2,1,0:T(8,128)(2,1)} %bitcast.332), custom_call_target="tpu_custom_call" | custom-call | flops 99000000512 | bytes 297000000 | tf_op jit(solution)/shard_map/scatter_rows/pallas_call | solution.py:783
  1236.6 3.6 all-to-all-start.8
  1242.1 3.3 fusion
  1247.9 3.1 fusion.4
  (385 shorter events, 148.3 us)
Async XLA Ops:
  7.2 178.9 %all-gather.11.cloned.1.call-start = ((), (), s32[]{:S(2)}) async-start(), calls=%async_computation.17 | async-start | bytes 4587520 | tf_op jit(solution)/shard_map/all_gather | solution.py:897
  30.2 428.0 %all-gather.19.cloned.1.call-start = ((), (), s32[]{:S(2)}) async-start(), calls=%async_computation.29 | async-start | bytes 7208960 | tf_op jit(solution)/shard_map/all_gather | solution.py:926
  30.9 427.3 %all-gather.21.cloned.1.call-start = ((), (), s32[]{:S(2)}) async-start(), calls=%async_computation.30 | async-start | bytes 7208960 | tf_op jit(solution)/shard_map/all_gather | solution.py:927
  31.7 426.5 %all-gather.23.cloned.1.call-start = ((), (), s32[]{:S(2)}) async-start(), calls=%async_computation.31 | async-start | bytes 7208960 | tf_op jit(solution)/shard_map/all_gather | solution.py:928
  32.2 613.7 %all-gather.13.cloned.1.call-start = ((), (), s32[]{:S(2)}) async-start(), calls=%async_computation.18 | async-start | bytes 3604480 | tf_op jit(solution)/shard_map/all_gather | solution.py:921
  32.8 613.2 %all-gather.15.cloned.1.call-start = ((), (), s32[]{:S(2)}) async-start(), calls=%async_computation.19 | async-start | bytes 3604480 | tf_op jit(solution)/shard_map/all_gather | solution.py:922
  32.9 148.4 %collective-permute-start = (bf16[64,2048]{1,0:T(8,128)(2,1)}, bf16[64,2048]{1,0:T(8,128)(2,1)}, u32[]{:S(2)}, u32[]{:S(2)}) collective-permute-start(bf16[64,2048]{1,0:T(8,128)(2,1)} %param.32), channel_id=1, source_target_pairs={{0,8},{8,16},{16,24},{24,0},{1,9},{9,17},{17,25},{25,1},{2,10},{10... | collective-permute-start | bytes 786440 | tf_op jit(solution)/shard_map/ppermute | solution.py:907
  34.5 146.7 %collective-permute-start.2 = (bf16[64,2048]{1,0:T(8,128)(2,1)}, bf16[64,2048]{1,0:T(8,128)(2,1)}, u32[]{:S(2)}, u32[]{:S(2)}) collective-permute-start(bf16[64,2048]{1,0:T(8,128)(2,1)} %param.32), channel_id=1, source_target_pairs={{0,24},{8,0},{16,8},{24,16},{1,25},{9,1},{17,9},{25,17},{2,26},{10... | collective-permute-start | bytes 786440 | tf_op jit(solution)/shard_map/ppermute | solution.py:907
  36.7 144.5 %collective-permute-start.1 = (bf16[64,2048]{1,0:T(8,128)(2,1)}, bf16[64,2048]{1,0:T(8,128)(2,1)}, u32[]{:S(2)}, u32[]{:S(2)}) collective-permute-start(bf16[64,2048]{1,0:T(8,128)(2,1)} %param.32), channel_id=1, source_target_pairs={{0,16},{8,24},{16,0},{24,8},{1,17},{9,25},{17,1},{25,9},{2,18},{10... | collective-permute-start | bytes 786440 | tf_op jit(solution)/shard_map/ppermute | solution.py:907
  37.6 608.5 %all-gather.17.cloned.1.call-start = ((), (), s32[]{:S(2)}) async-start(), calls=%async_computation.20 | async-start | bytes 3604480 | tf_op jit(solution)/shard_map/all_gather | solution.py:923
  37.6 143.4 %copy-start.76 = (s32[1,16]{1,0:T(1,128)S(1)}, s32[1,16]{1,0:T(1,128)}, u32[]{:S(2)}) copy-start(s32[1,16]{1,0:T(1,128)} %param.44) | copy-start | bytes 196
  184.0 39.8 %collective-permute-start.4 = (bf16[128,2048]{1,0:T(8,128)(2,1)}, bf16[128,2048]{1,0:T(8,128)(2,1)}, u32[]{:S(2)}, u32[]{:S(2)}) collective-permute-start(bf16[128,2048]{1,0:T(8,128)(2,1)} %get-tuple-element.287), channel_id=1, source_target_pairs={{0,4},{1,5},{2,6},{3,7},{4,0},{5,1},{6,2},{7,3},{8,12},{9,13},{10,... | collective-permute-start | bytes 1572872 | tf_op jit(solution)/shard_map/ppermute | solution.py:510
  185.5 38.3 %collective-permute-start.3 = (bf16[128,2048]{1,0:T(8,128)(2,1)}, bf16[128,2048]{1,0:T(8,128)(2,1)}, u32[]{:S(2)}, u32[]{:S(2)}) collective-permute-start(bf16[128,2048]{1,0:T(8,128)(2,1)} %get-tuple-element.288), channel_id=1, source_target_pairs={{0,2},{1,3},{2,0},{3,1},{4,6},{5,7},{6,4},{7,5},{8,10},{9,11},{10,... | collective-permute-start | bytes 1572872 | tf_op jit(solution)/shard_map/ppermute | solution.py:510
  189.9 182.7 %copy-start.59 = (f32[2048]{0:T(1024)}, f32[2048]{0:T(1024)S(1)}, u32[]{:S(2)}) copy-start(f32[2048]{0:T(1024)S(1)} %get-tuple-element.230) | copy-start | bytes 24580
  223.8 650.9 %copy-start.2 = (bf16[4096,256]{1,0:T(8,128)(2,1)}, bf16[4096,256]{1,0:T(8,128)(2,1)S(1)}, u32[]{:S(2)}) copy-start(bf16[4096,256]{1,0:T(8,128)(2,1)S(1)} %get-tuple-element.128.k_ref) | copy-start | bytes 6291460
  229.1 39.2 %collective-permute-start.6 = (bf16[256,2048]{1,0:T(8,128)(2,1)}, bf16[256,2048]{1,0:T(8,128)(2,1)}, u32[]{:S(2)}, u32[]{:S(2)}) collective-permute-start(bf16[256,2048]{1,0:T(8,128)(2,1)} %pad_maximum_fusion.9), channel_id=1, source_target_pairs={{0,2},{1,3},{2,0},{3,1},{4,6},{5,7},{6,4},{7,5},{8,10},{9,11},{10,... | collective-permute-start | bytes 3145736 | tf_op jit(solution)/shard_map/ppermute | solution.py:510
  230.6 37.8 %collective-permute-start.5 = (bf16[256,2048]{1,0:T(8,128)(2,1)}, bf16[256,2048]{1,0:T(8,128)(2,1)}, u32[]{:S(2)}, u32[]{:S(2)}) collective-permute-start(bf16[256,2048]{1,0:T(8,128)(2,1)} %pad_maximum_fusion.12), channel_id=1, source_target_pairs={{0,4},{1,5},{2,6},{3,7},{4,0},{5,1},{6,2},{7,3},{8,12},{9,13},{10,... | collective-permute-start | bytes 3145736 | tf_op jit(solution)/shard_map/ppermute | solution.py:510
  277.2 62.2 %collective-permute-start.7 = (bf16[4,256,2048]{2,1,0:T(8,128)(2,1)}, bf16[4,256,2048]{2,1,0:T(8,128)(2,1)}, u32[]{:S(2)}, u32[]{:S(2)}) collective-permute-start(bf16[4,256,2048]{2,1,0:T(8,128)(2,1)} %get-tuple-element.274), channel_id=1, source_target_pairs={{0,1},{1,0},{2,3},{3,2},{4,5},{5,4},{6,7},{7,6},{8,9},{9,8},{10,11... | collective-permute-start | bytes 12582920 | tf_op jit(solution)/shard_map/ppermute | solution.py:510
  282.8 38.1 %all-to-all-start.1 = ((bf16[8,512,128]{1,2,0:T(8,128)(2,1)}), bf16[8,512,128]{1,2,0:T(8,128)(2,1)}, u32[]{:S(2)}, u32[]{:S(2)}) async-start(bf16[8,512,128]{1,2,0:T(8,128)(2,1)} %copy.181), calls=%async_computation.1 | async-start | bytes 2097152 | tf_op jit(solution)/shard_map/all_to_all | solution.py:827
  323.1 39.0 %all-to-all-start.2 = ((bf16[8,512,128]{1,2,0:T(8,128)(2,1)}), bf16[8,512,128]{1,2,0:T(8,128)(2,1)}, u32[]{:S(2)}, u32[]{:S(2)}) async-start(bf16[8,512,128]{1,2,0:T(8,128)(2,1)} %copy.182), calls=%async_computation.2 | async-start | bytes 2097152 | tf_op jit(solution)/shard_map/all_to_all | solution.py:827
  327.4 445.0 %reduce-scatter.9.cloned.1.call-start = ((), (), s32[]{:S(2)}) async-start(), calls=%async_computation.21 | async-start | bytes 7208960 | tf_op jit(solution)/shard_map/reduce_scatter | solution.py:819
  374.3 80.7 %copy-start.57 = (f32[512,9]{0,1:T(8,128)}, f32[512,9]{0,1:T(8,128)S(1)}, u32[]{:S(2)}) copy-start(f32[512,9]{0,1:T(8,128)S(1)} %fusion.19) | copy-start | bytes 55300
  374.4 80.6 %copy-start.61 = (pred[8,512]{1,0:T(8,128)(4,1)}, pred[8,512]{1,0:T(8,128)(4,1)S(1)}, u32[]{:S(2)}) copy-start(pred[8,512]{1,0:T(8,128)(4,1)S(1)} %get-tuple-element.236) | copy-start | bytes 12292
  374.4 80.6 %copy-start.68 = (f32[512]{0:T(512)}, f32[512]{0:T(512)S(1)}, u32[]{:S(2)}) copy-start(f32[512]{0:T(512)S(1)} %get-tuple-element.235) | copy-start | bytes 6148
  374.4 80.6 %copy-start.72 = (f32[512]{0:T(512)}, f32[512]{0:T(512)S(1)}, u32[]{:S(2)}) copy-start(f32[512]{0:T(512)S(1)} %fusion.24) | copy-start | bytes 6148
  643.2 281.1 %reduce-scatter.11.cloned.1.call-start = ((), (), s32[]{:S(2)}) async-start(), calls=%async_computation.22 | async-start | bytes 7208960 | tf_op jit(solution)/shard_map/reduce_scatter | solution.py:819
  645.9 394.6 %reduce-scatter.13.cloned.1.call-start = ((), (), s32[]{:S(2)}) async-start(), calls=%async_computation.23 | async-start | bytes 7208960 | tf_op jit(solution)/shard_map/reduce_scatter | solution.py:819
  750.0 22.4 %collective-permute-start.8 = (bf16[2048,2048]{1,0:T(8,128)(2,1)}, bf16[2048,2048]{1,0:T(8,128)(2,1)}, u32[]{:S(2)}, u32[]{:S(2)}) collective-permute-start(bf16[2048,2048]{1,0:T(8,128)(2,1)} %get-tuple-element.153), channel_id=1, source_target_pairs={{0,1},{1,0},{2,3},{3,2},{4,5},{5,4},{6,7},{7,6},{8,9},{9,8},{10,11... | collective-permute-start | bytes 25165832 | tf_op jit(solution)/shard_map/ppermute | solution.py:510
  772.4 355.3 %reduce-scatter.21.cloned.1.call-start = ((), (), s32[]{:S(2)}) async-start(), calls=%async_computation.27 | async-start | bytes 3604480 | tf_op jit(solution)/shard_map/reduce_scatter | solution.py:819
  778.7 47.8 %collective-permute-start.9 = (bf16[512,2048]{1,0:T(8,128)(2,1)}, bf16[512,2048]{1,0:T(8,128)(2,1)}, u32[]{:S(2)}, u32[]{:S(2)}) collective-permute-start(bf16[512,2048]{1,0:T(8,128)(2,1)} %pad_maximum_fusion.4), channel_id=1, source_target_pairs={{0,2},{1,3},{2,0},{3,1},{4,6},{5,7},{6,4},{7,5},{8,10},{9,11},{10,... | collective-permute-start | bytes 6291464 | tf_op jit(solution)/shard_map/ppermute | solution.py:510
  781.3 47.6 %collective-permute-start.10 = (bf16[512,2048]{1,0:T(8,128)(2,1)}, bf16[512,2048]{1,0:T(8,128)(2,1)}, u32[]{:S(2)}, u32[]{:S(2)}) collective-permute-start(bf16[512,2048]{1,0:T(8,128)(2,1)} %pad_maximum_fusion.5), channel_id=1, source_target_pairs={{0,4},{1,5},{2,6},{3,7},{4,0},{5,1},{6,2},{7,3},{8,12},{9,13},{10,... | collective-permute-start | bytes 6291464 | tf_op jit(solution)/shard_map/ppermute | solution.py:510
  828.9 407.7 %reduce-scatter.15.cloned.1.call-start = ((), (), s32[]{:S(2)}) async-start(), calls=%async_computation.24 | async-start | bytes 3604480 | tf_op jit(solution)/shard_map/reduce_scatter | solution.py:819
  834.9 24.2 %collective-permute-start.12 = (bf16[256,2048]{1,0:T(8,128)(2,1)}, bf16[256,2048]{1,0:T(8,128)(2,1)}, u32[]{:S(2)}, u32[]{:S(2)}) collective-permute-start(bf16[256,2048]{1,0:T(8,128)(2,1)} %get-tuple-element.247), channel_id=1, source_target_pairs={{0,2},{1,3},{2,0},{3,1},{4,6},{5,7},{6,4},{7,5},{8,10},{9,11},{10,... | collective-permute-start | bytes 3145736 | tf_op jit(solution)/shard_map/ppermute | solution.py:510
  835.9 23.9 %collective-permute-start.11 = (bf16[256,2048]{1,0:T(8,128)(2,1)}, bf16[256,2048]{1,0:T(8,128)(2,1)}, u32[]{:S(2)}, u32[]{:S(2)}) collective-permute-start(bf16[256,2048]{1,0:T(8,128)(2,1)} %get-tuple-element.248), channel_id=1, source_target_pairs={{0,4},{1,5},{2,6},{3,7},{4,0},{5,1},{6,2},{7,3},{8,12},{9,13},{10,... | collective-permute-start | bytes 3145736 | tf_op jit(solution)/shard_map/ppermute | solution.py:510
  867.5 56.8 %collective-permute-start.13 = (bf16[2048,2048]{1,0:T(8,128)(2,1)}, bf16[2048,2048]{1,0:T(8,128)(2,1)}, u32[]{:S(2)}, u32[]{:S(2)}) collective-permute-start(bf16[2048,2048]{1,0:T(8,128)(2,1)} %get-tuple-element.170), channel_id=1, source_target_pairs={{0,1},{1,0},{2,3},{3,2},{4,5},{5,4},{6,7},{7,6},{8,9},{9,8},{10,11... | collective-permute-start | bytes 25165832 | tf_op jit(solution)/shard_map/ppermute | solution.py:510
  869.7 11.2 copy-start.58
  869.7 11.2 copy-start.60
  869.7 11.2 copy-start.67
  871.1 9.7 all-to-all-start.3
  874.4 362.2 %reduce-scatter.17.cloned.1.call-start = ((), (), s32[]{:S(2)}) async-start(), calls=%async_computation.25 | async-start | bytes 3604480 | tf_op jit(solution)/shard_map/reduce_scatter | solution.py:819
  924.3 19.4 %all-to-all-start.4 = ((bf16[8,512,128]{2,1,0:T(8,128)(2,1)}), bf16[8,512,128]{2,1,0:T(8,128)(2,1)S(1)}, u32[]{:S(2)}, u32[]{:S(2)}) async-start(bf16[8,512,128]{2,1,0:T(8,128)(2,1)} %bitcast.253), calls=%async_computation.6 | async-start | bytes 2097152 | tf_op jit(solution)/shard_map/all_to_all | solution.py:827
  933.7 106.8 %collective-permute-start.14 = (bf16[512,2048]{1,0:T(8,128)(2,1)}, bf16[512,2048]{1,0:T(8,128)(2,1)}, u32[]{:S(2)}, u32[]{:S(2)}) collective-permute-start(bf16[512,2048]{1,0:T(8,128)(2,1)} %pad_maximum_fusion.6), channel_id=1, source_target_pairs={{0,2},{1,3},{2,0},{3,1},{4,6},{5,7},{6,4},{7,5},{8,10},{9,11},{10,... | collective-permute-start | bytes 6291464 | tf_op jit(solution)/shard_map/ppermute | solution.py:510
  937.2 103.3 %collective-permute-start.15 = (bf16[512,2048]{1,0:T(8,128)(2,1)}, bf16[512,2048]{1,0:T(8,128)(2,1)}, u32[]{:S(2)}, u32[]{:S(2)}) collective-permute-start(bf16[512,2048]{1,0:T(8,128)(2,1)} %pad_maximum_fusion.7), channel_id=1, source_target_pairs={{0,4},{1,5},{2,6},{3,7},{4,0},{5,1},{6,2},{7,3},{8,12},{9,13},{10,... | collective-permute-start | bytes 6291464 | tf_op jit(solution)/shard_map/ppermute | solution.py:510
  943.7 55.9 %all-to-all-start.5 = ((bf16[8,512,128]{2,1,0:T(8,128)(2,1)}), bf16[8,512,128]{2,1,0:T(8,128)(2,1)}, u32[]{:S(2)}, u32[]{:S(2)}) async-start(bf16[8,512,128]{2,1,0:T(8,128)(2,1)} %bitcast.252), calls=%async_computation.7 | async-start | bytes 2097152 | tf_op jit(solution)/shard_map/all_to_all | solution.py:827
  948.0 288.7 %reduce-scatter.23.cloned.1.call-start = ((), (), s32[]{:S(2)}) async-start(), calls=%async_computation.28 | async-start | bytes 1310720 | tf_op jit(solution)/shard_map/reduce_scatter | solution.py:1132
  951.0 42.1 %slice-start = ((s8[8388608]{0:T(1024)(128)(4,1)}), s8[4194304]{0:T(1024)(128)(4,1)S(1)}, s32[]{:S(2)}) async-start(s8[8388608]{0:T(1024)(128)(4,1)} %bitcast.275), calls=%async_computation.32 | async-start | bytes 8388608
  953.4 46.2 %collective-permute-start.16 = (bf16[1024,2048]{1,0:T(8,128)(2,1)}, bf16[1024,2048]{1,0:T(8,128)(2,1)}, u32[]{:S(2)}, u32[]{:S(2)}) collective-permute-start(bf16[1024,2048]{1,0:T(8,128)(2,1)} %pad_maximum_fusion.2), channel_id=1, source_target_pairs={{0,1},{1,0},{2,3},{3,2},{4,5},{5,4},{6,7},{7,6},{8,9},{9,8},{10,11... | collective-permute-start | bytes 12582920 | tf_op jit(solution)/shard_map/ppermute | solution.py:510
  953.7 39.3 %slice-start.1 = ((s8[8388608]{0:T(1024)(128)(4,1)}), s8[4194304]{0:T(1024)(128)(4,1)S(1)}, s32[]{:S(2)}) async-start(s8[8388608]{0:T(1024)(128)(4,1)} %bitcast.275), calls=%async_computation.33 | async-start | bytes 8388608
  1043.6 26.2 %collective-permute-start.19 = (bf16[256,2048]{1,0:T(8,128)(2,1)S(1)}, bf16[256,2048]{1,0:T(8,128)(2,1)S(1)}, u32[]{:S(2)}, u32[]{:S(2)}) collective-permute-start(bf16[256,2048]{1,0:T(8,128)(2,1)S(1)} %pad_maximum_fusion.13), channel_id=1, source_target_pairs={{0,2},{1,3},{2,0},{3,1},{4,6},{5,7},{6,4},{7,5},{8,10},{9,11},{10,... | collective-permute-start | bytes 3145736 | tf_op jit(solution)/shard_map/ppermute | solution.py:510
  1044.1 26.1 %collective-permute-start.20 = (bf16[256,2048]{1,0:T(8,128)(2,1)S(1)}, bf16[256,2048]{1,0:T(8,128)(2,1)S(1)}, u32[]{:S(2)}, u32[]{:S(2)}) collective-permute-start(bf16[256,2048]{1,0:T(8,128)(2,1)S(1)} %pad_maximum_fusion.14), channel_id=1, source_target_pairs={{0,4},{1,5},{2,6},{3,7},{4,0},{5,1},{6,2},{7,3},{8,12},{9,13},{10,... | collective-permute-start | bytes 3145736 | tf_op jit(solution)/shard_map/ppermute | solution.py:510
  1050.5 19.7 %copy-start.47 = (bf16[2,1,64,2048]{3,2,1,0:T(8,128)(2,1)S(1)}, bf16[2,1,64,2048]{3,2,1,0:T(8,128)(2,1)}, u32[]{:S(2)}) copy-start(bf16[2,1,64,2048]{3,2,1,0:T(8,128)(2,1)} %get-tuple-element.258) | copy-start | bytes 1572868
  1050.5 19.7 %copy-start.48 = (bf16[2,1,64,2048]{3,2,1,0:T(8,128)(2,1)S(1)}, bf16[2,1,64,2048]{3,2,1,0:T(8,128)(2,1)}, u32[]{:S(2)}) copy-start(bf16[2,1,64,2048]{3,2,1,0:T(8,128)(2,1)} %get-tuple-element.260) | copy-start | bytes 1572868
  1050.5 73.4 %collective-permute-start.18 = (bf16[256,2048]{1,0:T(8,128)(2,1)}, bf16[256,2048]{1,0:T(8,128)(2,1)}, u32[]{:S(2)}, u32[]{:S(2)}) collective-permute-start(bf16[256,2048]{1,0:T(8,128)(2,1)} %get-tuple-element.239), channel_id=1, source_target_pairs={{0,2},{1,3},{2,0},{3,1},{4,6},{5,7},{6,4},{7,5},{8,10},{9,11},{10,... | collective-permute-start | bytes 3145736 | tf_op jit(solution)/shard_map/ppermute | solution.py:510
  1052.2 71.7 %collective-permute-start.17 = (bf16[256,2048]{1,0:T(8,128)(2,1)}, bf16[256,2048]{1,0:T(8,128)(2,1)}, u32[]{:S(2)}, u32[]{:S(2)}) collective-permute-start(bf16[256,2048]{1,0:T(8,128)(2,1)} %get-tuple-element.240), channel_id=1, source_target_pairs={{0,4},{1,5},{2,6},{3,7},{4,0},{5,1},{6,2},{7,3},{8,12},{9,13},{10,... | collective-permute-start | bytes 3145736 | tf_op jit(solution)/shard_map/ppermute | solution.py:510
  1053.7 21.9 %copy-start.15 = (bf16[4096,128]{1,0:T(8,128)(2,1)S(1)}, bf16[4096,128]{1,0:T(8,128)(2,1)}, u32[]{:S(2)}) copy-start(bf16[4096,128]{1,0:T(8,128)(2,1)} %copy-done.14) | copy-start | bytes 3145732
  1073.4 50.5 %collective-permute-start.22 = (bf16[128,2048]{1,0:T(8,128)(2,1)}, bf16[128,2048]{1,0:T(8,128)(2,1)}, u32[]{:S(2)}, u32[]{:S(2)}) collective-permute-start(bf16[128,2048]{1,0:T(8,128)(2,1)} %get-tuple-element.267), channel_id=1, source_target_pairs={{0,2},{1,3},{2,0},{3,1},{4,6},{5,7},{6,4},{7,5},{8,10},{9,11},{10,... | collective-permute-start | bytes 1572872 | tf_op jit(solution)/shard_map/ppermute | solution.py:510
  1075.2 48.8 %collective-permute-start.21 = (bf16[128,2048]{1,0:T(8,128)(2,1)}, bf16[128,2048]{1,0:T(8,128)(2,1)}, u32[]{:S(2)}, u32[]{:S(2)}) collective-permute-start(bf16[128,2048]{1,0:T(8,128)(2,1)} %get-tuple-element.268), channel_id=1, source_target_pairs={{0,4},{1,5},{2,6},{3,7},{4,0},{5,1},{6,2},{7,3},{8,12},{9,13},{10,... | collective-permute-start | bytes 1572872 | tf_op jit(solution)/shard_map/ppermute | solution.py:510
  1076.9 19.8 %copy-start.19 = (bf16[2048,896]{1,0:T(8,128)(2,1)S(1)}, bf16[2048,896]{1,0:T(8,128)(2,1)}, u32[]{:S(2)}) copy-start(bf16[2048,896]{1,0:T(8,128)(2,1)} %all-gather.11.cloned.1.call-done.w_ref) | copy-start | bytes 11010052
  1076.9 19.8 %copy-start.21 = (s32[16]{0:T(128)S(1)}, s32[16]{0:T(128)}, u32[]{:S(2)}) copy-start(s32[16]{0:T(128)} %copy-done.20) | copy-start | bytes 196
  1128.7 8.8 all-to-all-start.6
  1139.9 9.1 all-to-all-start.7
  1143.1 93.5 %reduce-scatter.19.cloned.1.call-start = ((), (), s32[]{:S(2)}) async-start(), calls=%async_computation.26 | async-start | bytes 3932160 | tf_op jit(solution)/shard_map/reduce_scatter | solution.py:1126
  1155.6 86.6 %copy-start.40 = (bf16[1,512,2048]{2,1,0:T(8,128)(2,1)S(1)}, bf16[1,512,2048]{2,1,0:T(8,128)(2,1)}, u32[]{:S(2)}) copy-start(bf16[1,512,2048]{2,1,0:T(8,128)(2,1)} %param.24) | copy-start | bytes 6291460
  1236.6 16.1 %all-to-all-start.8 = ((bf16[8,64,768]{2,1,0:T(8,128)(2,1)}), bf16[8,64,768]{2,1,0:T(8,128)(2,1)S(1)}, u32[]{:S(2)}, u32[]{:S(2)}) async-start(bf16[8,64,768]{2,1,0:T(8,128)(2,1)} %bitcast.296), calls=%async_computation.16 | async-start | bytes 1572864 | tf_op jit(solution)/shard_map/all_to_all | solution.py:827
  (64 other events, 268.7 us)
Sparse Core Ops, SparseCore 0:
  30.3 88.9 all-gather.10
  120.9 104.2 all-gather.18
  226.8 104.9 all-gather.20
  333.3 104.9 all-gather.22
  439.7 57.4 all-gather.12
  498.6 57.8 all-gather.14
  558.1 57.8 all-gather.16
  643.3 101.0 reduce-scatter.8
  746.7 102.7 reduce-scatter.10
  851.6 102.7 reduce-scatter.12
  956.8 56.7 reduce-scatter.20
  1015.7 56.0 reduce-scatter.14
  1074.0 56.0 reduce-scatter.16
  1132.8 27.2 reduce-scatter.22
  1162.3 58.9 reduce-scatter.18

commit v6 on v5

--- a/solution.py
+++ b/solution.py
@@ -1012,9 +1012,11 @@
         )
     )
     grad_egate = ein("crd,crf->df", expert_rows, gate_grad).astype(low)
+    grad_egate, up_grad = lax.optimization_barrier((grad_egate, up_grad))
     grad_eup = ein("crd,crf->df", expert_rows, up_grad).astype(low)
-    dx_routed, grad_egate, grad_eup = lax.optimization_barrier((dx_routed, grad_egate, grad_eup))
-    sum_egate, sum_eup = over_dp(grad_egate, 0), over_dp(grad_eup, 0)
+    sum_egate = over_dp(grad_egate, 0)
+    dx_routed, grad_eup = lax.optimization_barrier((dx_routed, grad_eup))
+    sum_eup = over_dp(grad_eup, 0)
     mix_cot, shared_low, shared_dg, shared_du, mix_share, dx_odd, dx_even, out_odd, out_even = (
         shared_expert(
             all_normed, cot_all, mix_all, shared_gate, shared_up, shared_down,
@@ -1096,10 +1098,11 @@
             (*wout_came, upstreams[-1]), grads[0] = pin([*wout_came, upstreams[-1]], grads[0])
             wout_came, wout = advance(wout_steps, wout_came)
         head_grads.append(grads)
-    came, last, sum_edown = pin(came, head_grads[-1][0], sum_edown)
+    last = head_grads[-1][0]
     if wout is None:
         wout_came, last = pin(wout_came, last)
         wout_came, wout = advance(wout_steps, wout_came)
+    came, last, sum_edown = pin(came, last, sum_edown)
     head_grads[-1][0] = last
     came, added = advance(add_steps, came)
     qkv_grads = jnp.concatenate(

time: 1280 us -> 1260 us (0.984)
    ppermute x20, waiting for transfers between devices: 30.3 us -> 15.6 us  [exchange(): return lax.ppermute(values, 'ctx', [(i, i ^ bit) for i in range(count)])]
  transfers between devices with their start and end apart: 46 -> 46, of which waited for: 12 -> 10; matrix products, arithmetic and copies ran while one was open for 27% -> 28% of each run, Pallas kernels for 58% -> 58%
where the time goes in v6:
time: 1260 us; the launch traced here: 1250 us
  Pallas kernels  730 us (58%)
  matrix products  171 us (14%)
  other arithmetic  117 us (9%)
  local copies, waits for them, and re-layouts  92.7 us (7%)
  starting transfers between devices  65.9 us (5%)
  waiting for transfers between devices  40.3 us (3%)
  blocking collectives  19 us (2%)
  between operations  15.7 us (1%)
    pallas_call x2, Pallas kernels, gather_now(): pl.pallas_call(functools.partial(gather_kernel, count, len(arrays), len(i...  223 us
    dot_general x9, matrix products, ein(): return jnp.einsum(spec, left, right, preferred_element_type=full)  149 us
    pallas_call x1, Pallas kernels, routed_expert(): pl.pallas_call(expert_kernel, grid=(count,), in_specs=[chunk, chunk, line...  141 us
    pallas_call x1, Pallas kernels, shared_expert(): pl.pallas_call(shared_kernel, grid=(count,), in_specs=[chunk, chunk, colu...  103 us
    pallas_call x1, Pallas kernels, scatter_now(): pl.pallas_call(functools.partial(scatter_kernel, count), in_specs=[pl.Blo...  77 us
    pallas_call x2, Pallas kernels, attention_backward(): pl.pallas_call(backward_kernel, grid_spec=pltpu.PrefetchScalarGridSpec(nu...  76.1 us
    pallas_call x2, Pallas kernels, attention_forward(): pl.pallas_call(forward_kernel, grid_spec=pltpu.PrefetchScalarGridSpec(num...  59.3 us
    unnamed x193, local copies, waits for them, and re-layouts  47.8 us
  transfers between devices with their start and end apart: 46, of which 10 were waited for; matrix products, arithmetic and copies ran while one was open for 28% of the time, Pallas kernels for 58%

profile of v6, /device:TPU:0, one launch (start us, length us, event | category | flops | bytes accessed | tf_op | source)
XLA Modules:
  0.0 1251.6 jit_solution(16229638947397190454)
XLA Ops:
  11.1 19.0 %all_to_all.45 = bf16[8,64,896]{2,1,0:T(8,128)(2,1)} all-to-all(bf16[8,64,896]{2,1,0:T(8,128)(2,1)S(1)} %pad_maximum_fusion.16), channel_id=1, replica_groups=mesh['dp'=4,'ctx'=8] {'ctx'}, dimensions={0} | all-to-all | bytes 1835008 | tf_op jit(solution)/shard_map/all_to_all | solution.py:827
  37.6 143.3 %gather_rows.2 = (bf16[16,256,2048]{2,1,0:T(8,128)(2,1)}, bf16[16,256,2048]{2,1,0:T(8,128)(2,1)}) custom-call(bf16[512,2048]{1,0:T(8,128)(2,1)} %bitcast.282, bf16[512,2048]{1,0:T(8,128)(2,1)} %bitcast.298), custom_call_target="tpu_custom_call" | custom-call | flops 159499993088 | bytes 478500000 | tf_op jit(solution)/shard_map/gather_rows/pallas_call | solution.py:609
  195.6 25.5 %project.1 = (bf16[4096,2048]{1,0:T(8,128)(2,1)}, bf16[4096,256]{1,0:T(8,128)(2,1)S(1)}, bf16[4096,256]{1,0:T(8,128)(2,1)S(1)}, bf16[4096,256]{1,0:T(8,128)(2,1)S(1)}) custom-call(s32[16]{0:T(128)S(1)} %get-tuple-element.236.place_ref, bf16[16,256,2048]{2,1,0:T(8,128)(2,1)} %get-tuple-element.124.x_ref, f32[1,2048]{1,0:T(1,128)S(1)} %copy.179.gain_ref, ...), custom_call_target="tpu_custom_call" | custom-call | flops 26400000000 | bytes 79200000 | tf_op jit(solution)/shard_map/project/pallas_call | solution.py:129
  223.8 3.0 pad_maximum_fusion.12
  231.1 4.2 copy.180
  238.7 29.6 %attend_forward.2 = (bf16[4096,128]{1,0:T(8,128)(2,1)S(1)}, f32[1,4096]{1,0:T(1,128)S(1)}) custom-call(s32[16]{0:T(128)S(1)} %get-tuple-element.235.at_ref, bf16[4096,256]{1,0:T(8,128)(2,1)S(1)} %copy-done.23, bf16[4096,256]{1,0:T(8,128)(2,1)S(1)} %get-tuple-element.129.k_ref, bf16[256,4096]{1,0:T(8,128)(2,1)S(1)} %bitcast.260), custom_call_target="tpu_custom_call" | custom-call | flops 32999999488 | bytes 99000000 | tf_op jit(solution)/shard_map/attend_forward/pallas_call | solution.py:386
  273.5 3.7 fusion.34
  277.6 3.5 convert_reduce_fusion
  282.8 4.2 all-to-all-start.1
  290.2 29.6 %attend_forward.3 = (bf16[4096,128]{1,0:T(8,128)(2,1)S(1)}, f32[1,4096]{1,0:T(1,128)S(1)}) custom-call(s32[16]{0:T(128)S(1)} %get-tuple-element.235.at_ref, bf16[4096,256]{1,0:T(8,128)(2,1)S(1)} %copy-done.24, bf16[4096,256]{1,0:T(8,128)(2,1)S(1)} %get-tuple-element.129.k_ref, bf16[256,4096]{1,0:T(8,128)(2,1)S(1)} %bitcast.261), custom_call_target="tpu_custom_call" | custom-call | flops 32999999488 | bytes 99000000 | tf_op jit(solution)/shard_map/attend_forward/pallas_call | solution.py:386
  323.1 4.3 all-to-all-start.2
  327.4 12.0 reduce-scatter.9.cloned.1.call-start
  339.4 8.3 pad_maximum_fusion
  347.6 2.5 bitcast_dynamic-update-slice_fusion.7
  350.1 3.0 bitcast_dynamic-update-slice_fusion.6
  364.3 7.6 multiply_reduce_fusion.3
  375.0 79.8 %gather_rows.3 = (bf16[16,256,2048]{2,1,0:T(8,128)(2,1)}, f32[8,24,512]{2,1,0:T(8,128)}) custom-call(bf16[512,2048]{1,0:T(8,128)(2,1)} %copy-done.31, f32[24,512]{1,0:T(8,128)} %select_maximum_fusion.refs_1_), custom_call_target="tpu_custom_call" | custom-call | flops 82500001792 | bytes 247500000 | tf_op jit(solution)/shard_map/gather_rows/pallas_call | solution.py:609
  458.1 140.7 %routed_expert.1 = (bf16[8,320,2048]{2,1,0:T(8,128)(2,1)}, bf16[8,320,2048]{2,1,0:T(8,128)(2,1)}, bf16[8,320,1408]{2,1,0:T(8,128)(2,1)}, bf16[8,320,1408]{2,1,0:...) custom-call(bf16[4096,2048]{1,0:T(8,128)(2,1)} %bitcast.332, ...), custom_call_target="tpu_custom_call" | custom-call | flops 153999998976 | bytes 462000000 | tf_op jit(solution)/shard_map/routed_expert/pallas_call | solution.py:259
  598.8 22.2 %bitcast_convert_fusion.2 = bf16[2048,1408]{1,0:T(8,128)(2,1)} fusion(bf16[8,320,2048]{2,1,0:T(8,128)(2,1)} %get-tuple-element.146, bf16[8,320,1408]{2,1,0:T(8,128)(2,1)} %get-tuple-element.147), kind=kOutput, calls=%fused_computation.5 | convolution fusion | flops 14766833664 | bytes 23461888 | tf_op jit(solution)/shard_map/crd,crf->df/dot_general | solution.py:35
  623.6 23.2 %bitcast_convert_fusion.1 = bf16[2048,1408]{1,0:T(8,128)(2,1)} fusion(bf16[8,320,2048]{2,1,0:T(8,128)(2,1)} %get-tuple-element.146, bf16[8,320,1408]{2,1,0:T(8,128)(2,1)} %get-tuple-element.149), kind=kOutput, calls=%fused_computation.4 | convolution fusion | flops 14766833664 | bytes 23461888 | tf_op jit(solution)/shard_map/crd,crf->df/dot_general | solution.py:35
  647.0 103.0 %shared_expert.1 = (bf16[4096,2048]{1,0:T(8,128)(2,1)}, bf16[4096,704]{1,0:T(8,128)(2,1)}, bf16[4096,704]{1,0:T(8,128)(2,1)}, bf16[4096,704]{1,0:T(8,128)(2,1)},...) custom-call(bf16[4096,2048]{1,0:T(8,128)(2,1)} %bitcast.333, ...), custom_call_target="tpu_custom_call" | custom-call | flops 113299996672 | bytes 339900000 | tf_op jit(solution)/shard_map/shared_expert/pallas_call | solution.py:329
  750.6 20.8 %bitcast_convert_fusion = bf16[1408,2048]{1,0:T(8,128)(2,1)} fusion(bf16[8,320,1408]{2,1,0:T(8,128)(2,1)} %get-tuple-element.156, bf16[8,320,2048]{2,1,0:T(8,128)(2,1)} %get-tuple-element.157), kind=kOutput, calls=%fused_computation.3 | convolution fusion | flops 14766833664 | bytes 23461888 | tf_op jit(solution)/shard_map/crf,crd->fd/dot_general | solution.py:35
  771.5 4.7 add_convert_fusion.25
  780.8 17.1 %convolution_convert_fusion.3 = bf16[704,2048]{1,0:T(8,128)(2,1)} fusion(bf16[4096,704]{1,0:T(8,128)(2,1)S(1)} %bitcast.338, bf16[4096,2048]{1,0:T(8,128)(2,1)} %bitcast.334), kind=kOutput, calls=%fused_computation.30 | convolution fusion | flops 11812601856 | bytes 25427968 | tf_op jit(solution)/shard_map/tf,td->fd/dot_general | solution.py:35
  797.9 18.6 %convolution_convert_fusion.4 = bf16[704,2048]{1,0:T(8,128)(2,1)} fusion(bf16[4096,704]{1,0:T(8,128)(2,1)} %get-tuple-element.163, bf16[4096,2048]{1,0:T(8,128)(2,1)} %get-tuple-element.164), kind=kOutput, calls=%fused_computation.31 | convolution fusion | flops 11812601856 | bytes 25427968 | tf_op jit(solution)/shard_map/tf,td->fd/dot_general | solution.py:35
  816.5 9.2 collective-permute-done.9
  825.7 2.7 collective-permute-done.10
  828.8 5.5 add_convert_fusion.19
  836.3 19.0 %convolution_convert_fusion.2 = bf16[704,2048]{1,0:T(8,128)(2,1)} fusion(bf16[4096,704]{1,0:T(8,128)(2,1)} %get-tuple-element.169, bf16[4096,2048]{1,0:T(8,128)(2,1)} %bitcast.335), kind=kOutput, calls=%fused_computation.29 | convolution fusion | flops 11812601856 | bytes 25427968 | tf_op jit(solution)/shard_map/tf,td->fd/dot_general | solution.py:35
  855.3 3.3 collective-permute-done.12
  859.0 5.2 add_convert_fusion.18
  870.4 3.3 all-to-all-start.3
  874.0 3.0 copy.190
  877.0 3.1 all-to-all-done.3
  880.2 2.8 multiply_reduce_fusion
  884.9 3.3 bitcast_convert_fusion.5
  888.1 4.2 multiply_reduce_fusion.1
  895.7 9.2 convolution_convert_fusion.5
  904.9 3.2 reshape.288
  908.8 3.0 fusion.36
  914.5 8.8 convolution_convert_fusion
  923.4 3.6 all-to-all-start.4
  926.9 4.3 add_convert_fusion.11
  937.8 5.0 all-to-all-done.4
  942.8 4.3 all-to-all-start.5
  947.3 2.7 constant_dynamic-slice_fusion.9
  952.9 38.2 %attend_backward.2 = (bf16[4096,128]{1,0:T(8,128)(2,1)S(1)}, bf16[4096,128]{1,0:T(8,128)(2,1)S(1)}, bf16[4096,128]{1,0:T(8,128)(2,1)S(1)}) custom-call(s32[16]{0:T(128)S(1)} %get-tuple-element.235.at_ref, bf16[4096,256]{1,0:T(8,128)(2,1)} %copy-done.22, bf16[4096,128]{1,0:T(8,128)(2,1)S(1)} %bitcast.264, bf16[4096,128]{1,0:T(8,128)(2,1)S(1)} %get-tuple-element.132.o_ref, ...), custom_call_target="tpu_custom_call" | custom-call | flops 41799999488 | bytes 125400000 | tf_op jit(solution)/shard_map/attend_backward/pallas_call | solution.py:467
  993.9 4.8 all-to-all-done.5
  998.7 3.3 fusion.13
  1003.0 37.9 %attend_backward.3 = (bf16[4096,128]{1,0:T(8,128)(2,1)S(1)}, bf16[4096,128]{1,0:T(8,128)(2,1)S(1)}, bf16[4096,128]{1,0:T(8,128)(2,1)S(1)}) custom-call(s32[16]{0:T(128)S(1)} %get-tuple-element.235.at_ref, bf16[4096,256]{1,0:T(8,128)(2,1)} %copy-done.22, bf16[4096,128]{1,0:T(8,128)(2,1)} %bitcast.80.do_ref, bf16[4096,128]{1,0:T(8,128)(2,1)S(1)} %copy-done.7, ...), custom_call_target="tpu_custom_call" | custom-call | flops 41799999488 | bytes 125400000 | tf_op jit(solution)/shard_map/attend_backward/pallas_call | solution.py:467
  1044.6 3.6 add_convert_fusion.32
  1051.6 5.5 add_convert_fusion.5
  1059.4 19.2 %convolution_convert_fusion.1 = bf16[2048,768]{1,0:T(8,128)(2,1)} fusion(bf16[4096,2048]{1,0:T(8,128)(2,1)} %get-tuple-element.191.normed_ref, bf16[4096,768]{1,0:T(8,128)(2,1)S(1)} %constant_dynamic-update-slice_fusion.grad_ref), kind=kOutput, calls=%fused_computation.28 | convolution fusion | flops 12886474752 | bytes 26214400 | tf_op jit(solution)/shard_map/td,te->de/dot_general | solution.py:35
  1078.6 25.1 %unproject.1 = (bf16[2048,2048]{1,0:T(8,128)(2,1)}, bf16[2048,2048]{1,0:T(8,128)(2,1)}, f32[1,2048]{1,0:T(1,128)S(1)}) custom-call(s32[16]{0:T(128)S(1)} %copy-done.19, bf16[4096,768]{1,0:T(8,128)(2,1)S(1)} %constant_dynamic-update-slice_fusion.grad_ref, bf16[2048,896]{1,0:T(8,128)(2,1)S(1)} %copy-done.17, bf16[4096,2048]{1,0:T(8,128)(2,1)} %get-tuple-element.191.normed_ref), custom_call_target="tpu_custom_call" | custom-call | flops 22000001024 | bytes 66000000 | tf_op jit(solution)/shard_map/unproject/pallas_call | solution.py:183
  1106.0 2.7 add_convert_fusion.31
  1110.8 3.8 all-to-all-start.6
  1116.4 3.6 all-to-all-done.6
  1122.3 3.4 all-to-all-start.7
  1127.8 3.8 all-to-all-done.7
  1134.7 6.2 add_convert_fusion.4
  1143.0 77.0 %scatter_rows.1 = f32[2,256,2048]{2,1,0:T(8,128)S(1)} custom-call(bf16[4,2,256,2048]{3,2,1,0:T(8,128)(2,1)S(1)} %bitcast.268, bf16[4,2,256,2048]{3,2,1,0:T(8,128)(2,1)} %bitcast.336), custom_call_target="tpu_custom_call" | custom-call | flops 99000000512 | bytes 297000000 | tf_op jit(solution)/shard_map/scatter_rows/pallas_call | solution.py:783
  1222.0 4.1 all-to-all-start.8
  1228.0 3.3 fusion
  1233.8 3.1 fusion.4
  (387 shorter events, 145.1 us)
Async XLA Ops:
  7.2 178.9 %all-gather.11.cloned.1.call-start = ((), (), s32[]{:S(2)}) async-start(), calls=%async_computation.17 | async-start | bytes 4587520 | tf_op jit(solution)/shard_map/all_gather | solution.py:897
  30.2 427.9 %all-gather.19.cloned.1.call-start = ((), (), s32[]{:S(2)}) async-start(), calls=%async_computation.29 | async-start | bytes 7208960 | tf_op jit(solution)/shard_map/all_gather | solution.py:926
  30.9 427.2 %all-gather.21.cloned.1.call-start = ((), (), s32[]{:S(2)}) async-start(), calls=%async_computation.30 | async-start | bytes 7208960 | tf_op jit(solution)/shard_map/all_gather | solution.py:927
  31.7 426.5 %all-gather.23.cloned.1.call-start = ((), (), s32[]{:S(2)}) async-start(), calls=%async_computation.31 | async-start | bytes 7208960 | tf_op jit(solution)/shard_map/all_gather | solution.py:928
  32.2 614.7 %all-gather.13.cloned.1.call-start = ((), (), s32[]{:S(2)}) async-start(), calls=%async_computation.18 | async-start | bytes 3604480 | tf_op jit(solution)/shard_map/all_gather | solution.py:921
  32.8 614.1 %all-gather.15.cloned.1.call-start = ((), (), s32[]{:S(2)}) async-start(), calls=%async_computation.19 | async-start | bytes 3604480 | tf_op jit(solution)/shard_map/all_gather | solution.py:922
  32.9 148.4 %collective-permute-start = (bf16[64,2048]{1,0:T(8,128)(2,1)}, bf16[64,2048]{1,0:T(8,128)(2,1)}, u32[]{:S(2)}, u32[]{:S(2)}) collective-permute-start(bf16[64,2048]{1,0:T(8,128)(2,1)} %param.32), channel_id=1, source_target_pairs={{0,8},{8,16},{16,24},{24,0},{1,9},{9,17},{17,25},{25,1},{2,10},{10... | collective-permute-start | bytes 786440 | tf_op jit(solution)/shard_map/ppermute | solution.py:907
  34.5 146.7 %collective-permute-start.2 = (bf16[64,2048]{1,0:T(8,128)(2,1)}, bf16[64,2048]{1,0:T(8,128)(2,1)}, u32[]{:S(2)}, u32[]{:S(2)}) collective-permute-start(bf16[64,2048]{1,0:T(8,128)(2,1)} %param.32), channel_id=1, source_target_pairs={{0,24},{8,0},{16,8},{24,16},{1,25},{9,1},{17,9},{25,17},{2,26},{10... | collective-permute-start | bytes 786440 | tf_op jit(solution)/shard_map/ppermute | solution.py:907
  36.7 144.5 %collective-permute-start.1 = (bf16[64,2048]{1,0:T(8,128)(2,1)}, bf16[64,2048]{1,0:T(8,128)(2,1)}, u32[]{:S(2)}, u32[]{:S(2)}) collective-permute-start(bf16[64,2048]{1,0:T(8,128)(2,1)} %param.32), channel_id=1, source_target_pairs={{0,16},{8,24},{16,0},{24,8},{1,17},{9,25},{17,1},{25,9},{2,18},{10... | collective-permute-start | bytes 786440 | tf_op jit(solution)/shard_map/ppermute | solution.py:907
  37.6 609.4 %all-gather.17.cloned.1.call-start = ((), (), s32[]{:S(2)}) async-start(), calls=%async_computation.20 | async-start | bytes 3604480 | tf_op jit(solution)/shard_map/all_gather | solution.py:923
  37.6 143.4 %copy-start.72 = (s32[1,16]{1,0:T(1,128)S(1)}, s32[1,16]{1,0:T(1,128)}, u32[]{:S(2)}) copy-start(s32[1,16]{1,0:T(1,128)} %param.44) | copy-start | bytes 196
  184.0 39.7 %collective-permute-start.4 = (bf16[128,2048]{1,0:T(8,128)(2,1)}, bf16[128,2048]{1,0:T(8,128)(2,1)}, u32[]{:S(2)}, u32[]{:S(2)}) collective-permute-start(bf16[128,2048]{1,0:T(8,128)(2,1)} %get-tuple-element.289), channel_id=1, source_target_pairs={{0,4},{1,5},{2,6},{3,7},{4,0},{5,1},{6,2},{7,3},{8,12},{9,13},{10,... | collective-permute-start | bytes 1572872 | tf_op jit(solution)/shard_map/ppermute | solution.py:510
  185.5 38.3 %collective-permute-start.3 = (bf16[128,2048]{1,0:T(8,128)(2,1)}, bf16[128,2048]{1,0:T(8,128)(2,1)}, u32[]{:S(2)}, u32[]{:S(2)}) collective-permute-start(bf16[128,2048]{1,0:T(8,128)(2,1)} %get-tuple-element.290), channel_id=1, source_target_pairs={{0,2},{1,3},{2,0},{3,1},{4,6},{5,7},{6,4},{7,5},{8,10},{9,11},{10,... | collective-permute-start | bytes 1572872 | tf_op jit(solution)/shard_map/ppermute | solution.py:510
  189.9 182.7 %copy-start.55 = (f32[2048]{0:T(1024)}, f32[2048]{0:T(1024)S(1)}, u32[]{:S(2)}) copy-start(f32[2048]{0:T(1024)S(1)} %get-tuple-element.232) | copy-start | bytes 24580
  223.8 650.2 %copy-start.2 = (bf16[4096,256]{1,0:T(8,128)(2,1)}, bf16[4096,256]{1,0:T(8,128)(2,1)S(1)}, u32[]{:S(2)}) copy-start(bf16[4096,256]{1,0:T(8,128)(2,1)S(1)} %get-tuple-element.129.k_ref) | copy-start | bytes 6291460
  229.1 39.3 %collective-permute-start.6 = (bf16[256,2048]{1,0:T(8,128)(2,1)}, bf16[256,2048]{1,0:T(8,128)(2,1)}, u32[]{:S(2)}, u32[]{:S(2)}) collective-permute-start(bf16[256,2048]{1,0:T(8,128)(2,1)} %pad_maximum_fusion.9), channel_id=1, source_target_pairs={{0,2},{1,3},{2,0},{3,1},{4,6},{5,7},{6,4},{7,5},{8,10},{9,11},{10,... | collective-permute-start | bytes 3145736 | tf_op jit(solution)/shard_map/ppermute | solution.py:510
  230.6 37.8 %collective-permute-start.5 = (bf16[256,2048]{1,0:T(8,128)(2,1)}, bf16[256,2048]{1,0:T(8,128)(2,1)}, u32[]{:S(2)}, u32[]{:S(2)}) collective-permute-start(bf16[256,2048]{1,0:T(8,128)(2,1)} %pad_maximum_fusion.12), channel_id=1, source_target_pairs={{0,4},{1,5},{2,6},{3,7},{4,0},{5,1},{6,2},{7,3},{8,12},{9,13},{10,... | collective-permute-start | bytes 3145736 | tf_op jit(solution)/shard_map/ppermute | solution.py:510
  277.2 62.2 %collective-permute-start.7 = (bf16[4,256,2048]{2,1,0:T(8,128)(2,1)}, bf16[4,256,2048]{2,1,0:T(8,128)(2,1)}, u32[]{:S(2)}, u32[]{:S(2)}) collective-permute-start(bf16[4,256,2048]{2,1,0:T(8,128)(2,1)} %get-tuple-element.276), channel_id=1, source_target_pairs={{0,1},{1,0},{2,3},{3,2},{4,5},{5,4},{6,7},{7,6},{8,9},{9,8},{10,11... | collective-permute-start | bytes 12582920 | tf_op jit(solution)/shard_map/ppermute | solution.py:510
  282.8 38.1 %all-to-all-start.1 = ((bf16[8,512,128]{1,2,0:T(8,128)(2,1)}), bf16[8,512,128]{1,2,0:T(8,128)(2,1)}, u32[]{:S(2)}, u32[]{:S(2)}) async-start(bf16[8,512,128]{1,2,0:T(8,128)(2,1)} %copy.181), calls=%async_computation.1 | async-start | bytes 2097152 | tf_op jit(solution)/shard_map/all_to_all | solution.py:827
  323.1 38.9 %all-to-all-start.2 = ((bf16[8,512,128]{1,2,0:T(8,128)(2,1)}), bf16[8,512,128]{1,2,0:T(8,128)(2,1)}, u32[]{:S(2)}, u32[]{:S(2)}) async-start(bf16[8,512,128]{1,2,0:T(8,128)(2,1)} %copy.182), calls=%async_computation.2 | async-start | bytes 2097152 | tf_op jit(solution)/shard_map/all_to_all | solution.py:827
  327.4 444.0 %reduce-scatter.9.cloned.1.call-start = ((), (), s32[]{:S(2)}) async-start(), calls=%async_computation.21 | async-start | bytes 7208960 | tf_op jit(solution)/shard_map/reduce_scatter | solution.py:819
  374.2 80.6 %copy-start.53 = (f32[512,9]{0,1:T(8,128)}, f32[512,9]{0,1:T(8,128)S(1)}, u32[]{:S(2)}) copy-start(f32[512,9]{0,1:T(8,128)S(1)} %fusion.19) | copy-start | bytes 55300
  374.3 80.6 %copy-start.57 = (pred[8,512]{1,0:T(8,128)(4,1)}, pred[8,512]{1,0:T(8,128)(4,1)S(1)}, u32[]{:S(2)}) copy-start(pred[8,512]{1,0:T(8,128)(4,1)S(1)} %get-tuple-element.238) | copy-start | bytes 12292
  374.3 80.6 %copy-start.64 = (f32[512]{0:T(512)}, f32[512]{0:T(512)S(1)}, u32[]{:S(2)}) copy-start(f32[512]{0:T(512)S(1)} %get-tuple-element.237) | copy-start | bytes 6148
  374.4 80.5 %copy-start.68 = (f32[512]{0:T(512)}, f32[512]{0:T(512)S(1)}, u32[]{:S(2)}) copy-start(f32[512]{0:T(512)S(1)} %fusion.24) | copy-start | bytes 6148
  621.0 302.4 %reduce-scatter.11.cloned.1.call-start = ((), (), s32[]{:S(2)}) async-start(), calls=%async_computation.22 | async-start | bytes 7208960 | tf_op jit(solution)/shard_map/reduce_scatter | solution.py:819
  646.9 397.7 %reduce-scatter.13.cloned.1.call-start = ((), (), s32[]{:S(2)}) async-start(), calls=%async_computation.23 | async-start | bytes 7208960 | tf_op jit(solution)/shard_map/reduce_scatter | solution.py:819
  750.0 21.4 %collective-permute-start.8 = (bf16[2048,2048]{1,0:T(8,128)(2,1)}, bf16[2048,2048]{1,0:T(8,128)(2,1)}, u32[]{:S(2)}, u32[]{:S(2)}) collective-permute-start(bf16[2048,2048]{1,0:T(8,128)(2,1)} %get-tuple-element.155), channel_id=1, source_target_pairs={{0,1},{1,0},{2,3},{3,2},{4,5},{5,4},{6,7},{7,6},{8,9},{9,8},{10,11... | collective-permute-start | bytes 25165832 | tf_op jit(solution)/shard_map/ppermute | solution.py:510
  771.5 338.3 %reduce-scatter.21.cloned.1.call-start = ((), (), s32[]{:S(2)}) async-start(), calls=%async_computation.27 | async-start | bytes 3604480 | tf_op jit(solution)/shard_map/reduce_scatter | solution.py:819
  777.8 47.9 %collective-permute-start.9 = (bf16[512,2048]{1,0:T(8,128)(2,1)}, bf16[512,2048]{1,0:T(8,128)(2,1)}, u32[]{:S(2)}, u32[]{:S(2)}) collective-permute-start(bf16[512,2048]{1,0:T(8,128)(2,1)} %pad_maximum_fusion.4), channel_id=1, source_target_pairs={{0,2},{1,3},{2,0},{3,1},{4,6},{5,7},{6,4},{7,5},{8,10},{9,11},{10,... | collective-permute-start | bytes 6291464 | tf_op jit(solution)/shard_map/ppermute | solution.py:510
  780.8 47.6 %collective-permute-start.10 = (bf16[512,2048]{1,0:T(8,128)(2,1)}, bf16[512,2048]{1,0:T(8,128)(2,1)}, u32[]{:S(2)}, u32[]{:S(2)}) collective-permute-start(bf16[512,2048]{1,0:T(8,128)(2,1)} %pad_maximum_fusion.5), channel_id=1, source_target_pairs={{0,4},{1,5},{2,6},{3,7},{4,0},{5,1},{6,2},{7,3},{8,12},{9,13},{10,... | collective-permute-start | bytes 6291464 | tf_op jit(solution)/shard_map/ppermute | solution.py:510
  828.4 393.6 %reduce-scatter.15.cloned.1.call-start = ((), (), s32[]{:S(2)}) async-start(), calls=%async_computation.24 | async-start | bytes 3604480 | tf_op jit(solution)/shard_map/reduce_scatter | solution.py:819
  834.4 24.2 %collective-permute-start.12 = (bf16[256,2048]{1,0:T(8,128)(2,1)}, bf16[256,2048]{1,0:T(8,128)(2,1)}, u32[]{:S(2)}, u32[]{:S(2)}) collective-permute-start(bf16[256,2048]{1,0:T(8,128)(2,1)} %get-tuple-element.249), channel_id=1, source_target_pairs={{0,2},{1,3},{2,0},{3,1},{4,6},{5,7},{6,4},{7,5},{8,10},{9,11},{10,... | collective-permute-start | bytes 3145736 | tf_op jit(solution)/shard_map/ppermute | solution.py:510
  835.1 24.0 %collective-permute-start.11 = (bf16[256,2048]{1,0:T(8,128)(2,1)}, bf16[256,2048]{1,0:T(8,128)(2,1)}, u32[]{:S(2)}, u32[]{:S(2)}) collective-permute-start(bf16[256,2048]{1,0:T(8,128)(2,1)} %get-tuple-element.250), channel_id=1, source_target_pairs={{0,4},{1,5},{2,6},{3,7},{4,0},{5,1},{6,2},{7,3},{8,12},{9,13},{10,... | collective-permute-start | bytes 3145736 | tf_op jit(solution)/shard_map/ppermute | solution.py:510
  866.7 56.7 %collective-permute-start.13 = (bf16[2048,2048]{1,0:T(8,128)(2,1)}, bf16[2048,2048]{1,0:T(8,128)(2,1)}, u32[]{:S(2)}, u32[]{:S(2)}) collective-permute-start(bf16[2048,2048]{1,0:T(8,128)(2,1)} %get-tuple-element.172), channel_id=1, source_target_pairs={{0,1},{1,0},{2,3},{3,2},{4,5},{5,4},{6,7},{7,6},{8,9},{9,8},{10,11... | collective-permute-start | bytes 25165832 | tf_op jit(solution)/shard_map/ppermute | solution.py:510
  869.0 11.2 copy-start.56
  869.0 11.2 copy-start.63
  870.4 9.7 all-to-all-start.3
  873.7 348.3 %reduce-scatter.17.cloned.1.call-start = ((), (), s32[]{:S(2)}) async-start(), calls=%async_computation.25 | async-start | bytes 3604480 | tf_op jit(solution)/shard_map/reduce_scatter | solution.py:819
  923.4 19.4 %all-to-all-start.4 = ((bf16[8,512,128]{2,1,0:T(8,128)(2,1)}), bf16[8,512,128]{2,1,0:T(8,128)(2,1)S(1)}, u32[]{:S(2)}, u32[]{:S(2)}) async-start(bf16[8,512,128]{2,1,0:T(8,128)(2,1)} %bitcast.253), calls=%async_computation.6 | async-start | bytes 2097152 | tf_op jit(solution)/shard_map/all_to_all | solution.py:827
  932.8 111.7 %collective-permute-start.14 = (bf16[512,2048]{1,0:T(8,128)(2,1)}, bf16[512,2048]{1,0:T(8,128)(2,1)}, u32[]{:S(2)}, u32[]{:S(2)}) collective-permute-start(bf16[512,2048]{1,0:T(8,128)(2,1)} %pad_maximum_fusion.6), channel_id=1, source_target_pairs={{0,2},{1,3},{2,0},{3,1},{4,6},{5,7},{6,4},{7,5},{8,10},{9,11},{10,... | collective-permute-start | bytes 6291464 | tf_op jit(solution)/shard_map/ppermute | solution.py:510
  936.3 108.3 %collective-permute-start.15 = (bf16[512,2048]{1,0:T(8,128)(2,1)}, bf16[512,2048]{1,0:T(8,128)(2,1)}, u32[]{:S(2)}, u32[]{:S(2)}) collective-permute-start(bf16[512,2048]{1,0:T(8,128)(2,1)} %pad_maximum_fusion.7), channel_id=1, source_target_pairs={{0,4},{1,5},{2,6},{3,7},{4,0},{5,1},{6,2},{7,3},{8,12},{9,13},{10,... | collective-permute-start | bytes 6291464 | tf_op jit(solution)/shard_map/ppermute | solution.py:510
  942.8 55.9 %all-to-all-start.5 = ((bf16[8,512,128]{2,1,0:T(8,128)(2,1)}), bf16[8,512,128]{2,1,0:T(8,128)(2,1)}, u32[]{:S(2)}, u32[]{:S(2)}) async-start(bf16[8,512,128]{2,1,0:T(8,128)(2,1)} %bitcast.252), calls=%async_computation.7 | async-start | bytes 2097152 | tf_op jit(solution)/shard_map/all_to_all | solution.py:827
  947.1 275.0 %reduce-scatter.23.cloned.1.call-start = ((), (), s32[]{:S(2)}) async-start(), calls=%async_computation.28 | async-start | bytes 1310720 | tf_op jit(solution)/shard_map/reduce_scatter | solution.py:1135
  950.1 42.0 %slice-start.4 = ((s8[8388608]{0:T(1024)(128)(4,1)}), s8[4194304]{0:T(1024)(128)(4,1)S(1)}, s32[]{:S(2)}) async-start(s8[8388608]{0:T(1024)(128)(4,1)} %bitcast.279), calls=%async_computation.36 | async-start | bytes 8388608
  952.5 46.1 %collective-permute-start.16 = (bf16[1024,2048]{1,0:T(8,128)(2,1)}, bf16[1024,2048]{1,0:T(8,128)(2,1)}, u32[]{:S(2)}, u32[]{:S(2)}) collective-permute-start(bf16[1024,2048]{1,0:T(8,128)(2,1)} %pad_maximum_fusion.2), channel_id=1, source_target_pairs={{0,1},{1,0},{2,3},{3,2},{4,5},{5,4},{6,7},{7,6},{8,9},{9,8},{10,11... | collective-permute-start | bytes 12582920 | tf_op jit(solution)/shard_map/ppermute | solution.py:510
  952.9 39.2 %slice-start.5 = ((s8[8388608]{0:T(1024)(128)(4,1)}), s8[4194304]{0:T(1024)(128)(4,1)S(1)}, s32[]{:S(2)}) async-start(s8[8388608]{0:T(1024)(128)(4,1)} %bitcast.279), calls=%async_computation.37 | async-start | bytes 8388608
  1002.1 40.1 %collective-permute-start.17 = (bf16[256,2048]{1,0:T(8,128)(2,1)S(1)}, bf16[256,2048]{1,0:T(8,128)(2,1)S(1)}, u32[]{:S(2)}, u32[]{:S(2)}) collective-permute-start(bf16[256,2048]{1,0:T(8,128)(2,1)S(1)} %pad_maximum_fusion.13), channel_id=1, source_target_pairs={{0,2},{1,3},{2,0},{3,1},{4,6},{5,7},{6,4},{7,5},{8,10},{9,11},{10,... | collective-permute-start | bytes 3145736 | tf_op jit(solution)/shard_map/ppermute | solution.py:510
  1002.3 40.3 %collective-permute-start.18 = (bf16[256,2048]{1,0:T(8,128)(2,1)S(1)}, bf16[256,2048]{1,0:T(8,128)(2,1)S(1)}, u32[]{:S(2)}, u32[]{:S(2)}) collective-permute-start(bf16[256,2048]{1,0:T(8,128)(2,1)S(1)} %pad_maximum_fusion.14), channel_id=1, source_target_pairs={{0,4},{1,5},{2,6},{3,7},{4,0},{5,1},{6,2},{7,3},{8,12},{9,13},{10,... | collective-permute-start | bytes 3145736 | tf_op jit(solution)/shard_map/ppermute | solution.py:510
  1003.0 37.9 %copy-start.9 = (bf16[4096,128]{1,0:T(8,128)(2,1)S(1)}, bf16[4096,128]{1,0:T(8,128)(2,1)}, u32[]{:S(2)}) copy-start(bf16[4096,128]{1,0:T(8,128)(2,1)} %copy-done.8) | copy-start | bytes 3145732
  1044.5 13.6 %slice-start = ((s8[6291456]{0:T(1024)(128)(4,1)}), s8[4194304]{0:T(1024)(128)(4,1)S(1)}, s32[]{:S(2)}) async-start(s8[6291456]{0:T(1024)(128)(4,1)} %bitcast.258), calls=%async_computation.32 | async-start | bytes 8388608
  1048.1 57.8 %collective-permute-start.22 = (bf16[128,2048]{1,0:T(8,128)(2,1)}, bf16[128,2048]{1,0:T(8,128)(2,1)}, u32[]{:S(2)}, u32[]{:S(2)}) collective-permute-start(bf16[128,2048]{1,0:T(8,128)(2,1)} %get-tuple-element.269), channel_id=1, source_target_pairs={{0,2},{1,3},{2,0},{3,1},{4,6},{5,7},{6,4},{7,5},{8,10},{9,11},{10,... | collective-permute-start | bytes 1572872 | tf_op jit(solution)/shard_map/ppermute | solution.py:510
  1049.6 56.3 %collective-permute-start.21 = (bf16[128,2048]{1,0:T(8,128)(2,1)}, bf16[128,2048]{1,0:T(8,128)(2,1)}, u32[]{:S(2)}, u32[]{:S(2)}) collective-permute-start(bf16[128,2048]{1,0:T(8,128)(2,1)} %get-tuple-element.270), channel_id=1, source_target_pairs={{0,4},{1,5},{2,6},{3,7},{4,0},{5,1},{6,2},{7,3},{8,12},{9,13},{10,... | collective-permute-start | bytes 1572872 | tf_op jit(solution)/shard_map/ppermute | solution.py:510
  1057.1 48.8 %collective-permute-start.20 = (bf16[256,2048]{1,0:T(8,128)(2,1)}, bf16[256,2048]{1,0:T(8,128)(2,1)}, u32[]{:S(2)}, u32[]{:S(2)}) collective-permute-start(bf16[256,2048]{1,0:T(8,128)(2,1)} %get-tuple-element.241), channel_id=1, source_target_pairs={{0,2},{1,3},{2,0},{3,1},{4,6},{5,7},{6,4},{7,5},{8,10},{9,11},{10,... | collective-permute-start | bytes 3145736 | tf_op jit(solution)/shard_map/ppermute | solution.py:510
  1057.2 48.7 %collective-permute-start.19 = (bf16[256,2048]{1,0:T(8,128)(2,1)}, bf16[256,2048]{1,0:T(8,128)(2,1)}, u32[]{:S(2)}, u32[]{:S(2)}) collective-permute-start(bf16[256,2048]{1,0:T(8,128)(2,1)} %get-tuple-element.242), channel_id=1, source_target_pairs={{0,4},{1,5},{2,6},{3,7},{4,0},{5,1},{6,2},{7,3},{8,12},{9,13},{10,... | collective-permute-start | bytes 3145736 | tf_op jit(solution)/shard_map/ppermute | solution.py:510
  1059.4 19.2 %copy-start.17 = (bf16[2048,896]{1,0:T(8,128)(2,1)S(1)}, bf16[2048,896]{1,0:T(8,128)(2,1)}, u32[]{:S(2)}) copy-start(bf16[2048,896]{1,0:T(8,128)(2,1)} %all-gather.11.cloned.1.call-done.w_ref) | copy-start | bytes 11010052
  1059.4 19.2 %copy-start.19 = (s32[16]{0:T(128)S(1)}, s32[16]{0:T(128)}, u32[]{:S(2)}) copy-start(s32[16]{0:T(128)} %copy-done.18) | copy-start | bytes 196
  1109.7 16.0 %copy-start.46 = (bf16[1408,512]{1,0:T(8,128)(2,1)S(1)}, bf16[1408,512]{1,0:T(8,128)(2,1)}, u32[]{:S(2)}) copy-start(bf16[1408,512]{1,0:T(8,128)(2,1)} %reduce-scatter.13.cloned.1.call-done) | copy-start | bytes 4325380
  1110.8 9.2 all-to-all-start.6
  1121.4 12.1 copy-start.49
  1122.3 9.3 all-to-all-start.7
  1125.7 96.3 %reduce-scatter.19.cloned.1.call-start = ((), (), s32[]{:S(2)}) async-start(), calls=%async_computation.26 | async-start | bytes 3932160 | tf_op jit(solution)/shard_map/reduce_scatter | solution.py:1129
  1143.0 85.0 %copy-start.38 = (bf16[1,512,2048]{2,1,0:T(8,128)(2,1)S(1)}, bf16[1,512,2048]{2,1,0:T(8,128)(2,1)}, u32[]{:S(2)}) copy-start(bf16[1,512,2048]{2,1,0:T(8,128)(2,1)} %param.24) | copy-start | bytes 6291460
  1222.0 16.7 %all-to-all-start.8 = ((bf16[8,64,768]{2,1,0:T(8,128)(2,1)}), bf16[8,64,768]{2,1,0:T(8,128)(2,1)S(1)}, u32[]{:S(2)}, u32[]{:S(2)}) async-start(bf16[8,64,768]{2,1,0:T(8,128)(2,1)} %bitcast.300), calls=%async_computation.16 | async-start | bytes 1572864 | tf_op jit(solution)/shard_map/all_to_all | solution.py:827
  (64 other events, 275.1 us)
Sparse Core Ops, SparseCore 0:
  30.3 88.9 all-gather.10
  120.9 104.2 all-gather.18
  226.8 104.9 all-gather.20
  333.3 104.9 all-gather.22
  439.7 57.4 all-gather.12
  498.6 57.8 all-gather.14
  558.1 57.8 all-gather.16
  621.1 101.0 reduce-scatter.8
  724.5 102.7 reduce-scatter.10
  829.4 102.7 reduce-scatter.12
  935.1 56.7 reduce-scatter.20
  994.0 56.0 reduce-scatter.14
  1052.4 56.0 reduce-scatter.16
  1111.2 27.2 reduce-scatter.22
  1140.7 58.8 reduce-scatter.18
